TPU v7x, 512 devices: a whole 4x4x16 slice. The times are simulated.
512 devices in a mesh: dp: 64 (over z, x_lo, core), tensor: 8 (over y, x_hi).
Axes of the slice: x: 4 (x_hi: 2, x_lo: 2; x = x_hi * 2 + x_lo), y: 4, z: 16, core: 2. Of those that a mesh axis runs over, the one named last changes fastest.
Arguments:
- activations: bfloat16 [32768, 1024], P('dp', 'tensor'), may hold values from -16 to 16
- cotangent: bfloat16 [32768, 2, 1024], P('dp'), may hold values from -16 to 16
- weight: bfloat16 [1024, 2, 1024], P('tensor'), may hold values from -0.125 to 0.125
- owners: int32 [3], replicated, may hold values from 0 to 63
- worker_group: int32 [64], replicated, may hold values from 0 to 1, as said below
- basis_a: bfloat16 [64, 1024, 1024], P('dp', None, 'tensor'), may hold values from -0.1875 to 0.1875
- values_a: bfloat16 [64, 1024], P('dp', 'tensor'), may hold values from 0.0099487305 to 0.29882812
- basis_g: bfloat16 [64, 2, 1024, 1024], P('dp', None, None, 'tensor'), may hold values from -0.1875 to 0.1875
- values_g: bfloat16 [64, 2, 1024], P('dp', None, 'tensor'), may hold values from 0.0099487305 to 0.29882812
Outputs:
- grad_input: bfloat16 [32768, 1024], P('dp', 'tensor')
- factor_a: float32 [1024, 1024], P('dp', 'tensor')
- factor_g: float32 [1024, 2, 1024], P('dp', None, 'tensor')
- preconditioned: bfloat16 [1024, 2, 1024], P(None, None, 'tensor')
- worker_block: bfloat16 [64, 1024, 1024], P('dp', None, 'tensor')
Inputs may be any that keep to these rules, and one draw needn't show every extreme that they name: `worker_group`: each of the 2 groups holds at least one replica.
All inputs are finite; a program needn't handle non-finite values.
Results may differ from a plain program's by a relative error of at most 0.01.
Values may be sent and summed in bfloat16 or wider, within the bound.
No kernel may reach another device: no remote copies, remote signals or barrier semaphores. Data moves between devices by JAX's collectives and lax.ppermute only.
A program may use at most 64 MiB of HBM per device.

v0:
```python
from functools import partial

import jax
import jax.numpy as jnp
from jax import lax
from jax.sharding import PartitionSpec as P

damping = 0.001


def broadcast(array, axis, root):
    mine = lax.axis_index(axis) == root
    return lax.psum(jnp.where(mine, array, jnp.zeros_like(array)), axis)


def accumulate(rotated_rows, eigen_rows, running, pieces, offset):
    basis_piece, value_piece = pieces
    spectral = jnp.dot(rotated_rows, basis_piece, preferred_element_type=jnp.float32)
    denominator = eigen_rows[:, None] * value_piece.astype(jnp.float32) + damping
    scaled = (spectral / denominator).astype(jnp.bfloat16)
    return lax.dot_general(
        scaled, basis_piece, (((1,), (1,)), ((), ())), preferred_element_type=jnp.float32
    )


def precondition(grad_rows, stacked_basis, stacked_values, whole_a, eigen_rows):
    block_count = grad_rows.shape[1]
    slab_width = grad_rows.shape[0]
    full_width = grad_rows.shape[2]
    grad_cols = lax.all_to_all(grad_rows, "tensor", split_axis=2, concat_axis=0, tiled=True)
    rotated = jnp.einsum(
        "re,rkc->ekc", whole_a, grad_cols, preferred_element_type=jnp.float32
    ).astype(jnp.bfloat16)
    rotated_rows = lax.all_to_all(rotated, "tensor", split_axis=0, concat_axis=2, tiled=True)
    mixed_list = []
    for block_index in range(block_count):
        start_value = jnp.zeros((slab_width, full_width), jnp.float32)
        folder = partial(accumulate, rotated_rows[:, block_index, :], eigen_rows)
        mixed = folder(
            start_value,
            (
                lax.all_gather(stacked_basis[block_index], "tensor", axis=1, tiled=True),
                lax.all_gather(stacked_values[block_index][None, :], "tensor", axis=1, tiled=True),
            ),
            jnp.int32(0),
        )
        mixed_list.append(mixed.astype(jnp.bfloat16))
    mixed_rows = jnp.stack(mixed_list, 1)
    mixed_cols = lax.all_to_all(mixed_rows, "tensor", split_axis=2, concat_axis=0, tiled=True)
    return jnp.einsum(
        "re,ekc->rkc", whole_a, mixed_cols, preferred_element_type=jnp.float32
    ).astype(jnp.bfloat16)


def local(
    activations, cotangent, weight, owners, worker_group, basis_a, values_a, basis_g, values_g
):
    tok_rows = activations.shape[0]
    slab_width = activations.shape[1]
    block_count = cotangent.shape[1]
    full_width = cotangent.shape[2]
    tokens_all = tok_rows * lax.axis_size("dp")
    flat_cot = cotangent.reshape(tok_rows, block_count * full_width)
    flat_weight = weight.reshape(slab_width, block_count * full_width)
    grad_input = lax.dot_general(
        flat_cot, flat_weight, (((1,), (1,)), ((), ())), preferred_element_type=jnp.float32
    ).astype(jnp.bfloat16)
    grad_term = (
        lax.dot_general(
            activations, flat_cot, (((0,), (0,)), ((), ())), preferred_element_type=jnp.float32
        )
        / tokens_all
    )
    grad_term = grad_term.reshape(slab_width, block_count, full_width)
    a_term = (
        lax.dot_general(
            lax.all_gather(activations, "tensor", axis=1, tiled=True),
            activations,
            (((0,), (0,)), ((), ())),
            preferred_element_type=jnp.float32,
        )
        / tokens_all
    )
    own_cols = lax.dynamic_slice_in_dim(
        cotangent, lax.axis_index("tensor") * slab_width, slab_width, 2
    )
    g_term = (
        jnp.einsum("tja,tjb->ajb", cotangent, own_cols, preferred_element_type=jnp.float32)
        / tokens_all
    )
    row_count = full_width // lax.axis_size("dp")
    first_row = lax.axis_index("dp") * row_count
    grad_sum, a_sum, g_sum = lax.psum((grad_term, a_term, g_term), "dp")
    factor_a = lax.dynamic_slice_in_dim(a_sum, first_row, row_count, 0)
    factor_g = lax.dynamic_slice_in_dim(g_sum, first_row, row_count, 0)
    grad_rows = grad_sum.astype(jnp.bfloat16)
    basis_a_cols, values_a_cols = (
        broadcast(basis_a[0], "dp", owners[0]),
        broadcast(values_a[0], "dp", owners[0]),
    )
    whole_a, eigen_whole = (
        lax.all_gather(basis_a_cols, "tensor", axis=1, tiled=True),
        lax.all_gather(values_a_cols[None, :], "tensor", axis=1, tiled=True),
    )
    eigen_rows = values_a_cols.astype(jnp.float32)
    basis_list = []
    value_list = []
    for block_index in range(block_count):
        basis_cols, value_cols = (
            broadcast(basis_g[0, block_index], "dp", owners[1 + block_index]),
            broadcast(values_g[0, block_index], "dp", owners[1 + block_index]),
        )
        basis_list.append(basis_cols)
        value_list.append(value_cols)
    stacked_basis = jnp.stack(basis_list, 0)
    stacked_values = jnp.stack(value_list, 0)
    group_id = worker_group[lax.axis_index("dp")]
    preconditioned = precondition(grad_rows, stacked_basis, stacked_values, whole_a, eigen_rows)
    worker_block = lax.dynamic_index_in_dim(preconditioned, group_id, 1, keepdims=False)[None]
    return (grad_input, factor_a, factor_g, preconditioned, worker_block)


def solution(mesh):
    return jax.shard_map(
        local,
        mesh=mesh,
        in_specs=(
            P("dp", "tensor"),
            P("dp", None, None),
            P("tensor", None, None),
            P(),
            P(),
            P("dp", None, "tensor"),
            P("dp", "tensor"),
            P("dp", None, None, "tensor"),
            P("dp", None, "tensor"),
        ),
        out_specs=(
            P("dp", "tensor"),
            P("dp", "tensor"),
            P("dp", None, "tensor"),
            P(None, None, "tensor"),
            P("dp", None, "tensor"),
        ),
        check_vma=False,
    )
```

profile of v0, /device:TPU:1, one launch (start us, length us, event | category | flops | bytes accessed | tf_op | source)
XLA Modules:
  0.0 1184.4 jit_solution(11311916232444734345)
XLA Ops:
  7.2 1.4 fusion.47
  12.4 1.9 select_bitcast_fusion.1
  14.4 424.8 %all-reduce.9.cloned.1.call-done = (bf16[1024,128]{1,0:T(8,128)(2,1)}, bf16[1024,128]{0,1:T(8,128)(2,1)}, bf16[1024,128]{1,0:T(8,128)(2,1)}) async-done(((bf16[1024,128]{1,0:T(8,128)(2,1)}, bf16[1024,128]{0,1:T(8,128)(2,1)}, bf16[1024,128]{1,0:T(8,128)(2,1)}), (bf16[1024,128]{1,0:T(8,128)(2,1)}, bf16[1024,128]{0,1:T(8,128)(2,1)}, bf16[1024,128]{1,0:T(8,128)(2,1)})) %all-reduce.9.cloned.1.call-update) | async-done | bytes 786448 | tf_op jit(solution)/shard_map/psum | solution.py:13
  442.0 1.5 convolution_multiply_fusion
  443.5 3.1 reshape.38
  446.6 3.2 copy.74
  449.8 215.3 %all-reduce.10 = bf16[128,2,1024]{0,1,2:T(2,128)(2,1)} all-reduce(f32[128,2,1024]{0,1,2:T(2,128)} %copy.74), channel_id=1, replica_groups=mesh['dp'=64,'tensor'=8] {'dp'}, use_global_device_ids=true, to_apply=%region_3.4 | all-reduce | flops 262144 | bytes 1572864 | tf_op jit(solution)/shard_map/psum | solution.py:93
  665.1 7.6 all-to-all-start
  672.9 1.9 fusion.11
  674.8 7.0 all-to-all-done
  682.9 2.4 fusion.17
  685.3 1.3 copy.76
  686.6 4.4 all-to-all-start.1
  691.1 2.5 convolution_multiply_fusion.1
  693.7 110.4 %all-reduce.1 = (bf16[1,128]{1,0:T(2,128)(2,1)S(1)}, bf16[128]{0:T(256)(128)(2,1)S(1)}, bf16[1,128]{1,0:T(2,128)(2,1)S(1)}) all-reduce(bf16[1,128]{1,0:T(2,128)(2,1)S(1)} %get-tuple-element.41, bf16[128]{0:T(256)(128)(2,1)S(1)} %fusion.42, bf16[1,128]{1,0:T(2,128)(2,1)S(1)} %get-tuple-element.40), channel_id=1, replica_groups=mesh['dp'=64,'tensor'=8] {'dp'}, use_global_device_ids=true, to_apply=%region_8.9 | all-reduce | flops 384 | bytes 1536 | tf_op jit(solution)/shard_map/psum | solution.py:13
  804.1 20.4 %all_gather.21 = bf16[1,1024]{1,0:T(2,128)(2,1)S(1)} all-gather(bf16[1,128]{1,0:T(2,128)(2,1)S(1)} %get-tuple-element.34), channel_id=1, replica_groups=mesh['dp'=64,'tensor'=8] {'tensor'}, dimensions={1}, use_global_device_ids=true | all-gather | bytes 2304 | tf_op jit(solution)/shard_map/all_gather | solution.py:43
  824.5 14.5 %all_gather.23 = bf16[1,1024]{1,0:T(2,128)(2,1)S(1)} all-gather(bf16[1,128]{1,0:T(2,128)(2,1)S(1)} %get-tuple-element.32), channel_id=1, replica_groups=mesh['dp'=64,'tensor'=8] {'tensor'}, dimensions={1}, use_global_device_ids=true | all-gather | bytes 2304 | tf_op jit(solution)/shard_map/all_gather | solution.py:43
  843.8 3.4 fusion.22
  847.2 4.1 fusion.23
  853.4 4.4 all-to-all-start.2
  857.9 1.4 fusion.27
  859.2 310.4 %all-reduce.7.cloned.1.call-done = (f32[1024,128]{1,0:T(8,128)}, f32[1024,2,128]{0,2,1:T(8,128)}) async-done(((f32[1024,128]{1,0:T(8,128)}, f32[1024,2,128]{0,2,1:T(8,128)}), (f32[1024,128]{1,0:T(8,128)}, f32[1024,2,128]{0,2,1:T(8,128)})) %all-reduce.7.cloned.1.call-update) | async-done | bytes 1572880 | tf_op jit(solution)/shard_map/psum | solution.py:93
  1173.1 2.3 fusion.14
  1175.5 1.3 copy.85
  (50 shorter events, 15.2 us)
Async XLA Ops:
  7.2 850.7 %copy-start = (bf16[128,2,1024]{2,1,0:T(2,128)(2,1)S(1)}, bf16[128,2,1024]{2,1,0:T(2,128)(2,1)}, u32[]{:S(2)}) copy-start(bf16[128,2,1024]{2,1,0:T(2,128)(2,1)} %param.11) | copy-start | bytes 1572868
  7.2 433.9 %copy-start.1 = (bf16[512,2,1024]{2,1,0:T(2,128)(2,1)S(1)}, bf16[512,2,1024]{2,1,0:T(2,128)(2,1)}, u32[]{:S(2)}) copy-start(bf16[512,2,1024]{2,1,0:T(2,128)(2,1)} %param.10) | copy-start | bytes 6291460
  7.2 432.0 %all-reduce.9.cloned.1.call-start = ((), (), s32[]{:S(2)}) async-start(), calls=%async_computation.8 | async-start | bytes 1572864 | tf_op jit(solution)/shard_map/psum | solution.py:13
  14.3 668.6 %all-gather.7.cloned.1.call-start = ((), (), s32[]{:S(2)}) async-start(), calls=%async_computation.4 | async-start | bytes 2359296 | tf_op jit(solution)/shard_map/all_gather | solution.py:102
  439.2 251.9 %all-gather.5.cloned.1.call-start = ((), (), s32[]{:S(2)}) async-start(), calls=%async_computation.3 | async-start | bytes 1179648 | tf_op jit(solution)/shard_map/all_gather | solution.py:77
  439.9 403.8 %all-gather.9.cloned.1.call-start = ((), (), s32[]{:S(2)}) async-start(), calls=%async_computation.5 | async-start | bytes 2359296 | tf_op jit(solution)/shard_map/all_gather | solution.py:42
  440.5 406.7 %all-gather.11.cloned.1.call-start = ((), (), s32[]{:S(2)}) async-start(), calls=%async_computation.6 | async-start | bytes 2359296 | tf_op jit(solution)/shard_map/all_gather | solution.py:42
  441.1 0.9 copy-start.2
  665.1 16.7 %all-to-all-start = ((bf16[128,2,1024]{0,1,2:T(2,128)(2,1)}), bf16[128,2,1024]{0,1,2:T(2,128)(2,1)S(1)}, u32[]{:S(2)}, u32[]{:S(2)}) async-start(bf16[128,2,1024]{0,1,2:T(2,128)(2,1)} %all-reduce.10), calls=%async_computation | async-start | bytes 1048576 | tf_op jit(solution)/shard_map/all_to_all | solution.py:30
  686.6 7.0 copy-start.4
  686.6 7.0 copy-start.3
  686.6 152.4 %copy-start.5 = (s32[64]{0:T(128)S(1)}, s32[64]{0:T(128)}, u32[]{:S(2)}) copy-start(s32[64]{0:T(128)} %param.13) | copy-start | bytes 772
  686.6 154.9 %all-to-all-start.1 = ((bf16[1024,2,128]{2,1,0:T(2,128)(2,1)}), bf16[1024,2,128]{2,1,0:T(2,128)(2,1)S(1)}, u32[]{:S(2)}, u32[]{:S(2)}) async-start(bf16[1024,2,128]{2,1,0:T(2,128)(2,1)} %copy.76), calls=%async_computation.1 | async-start | bytes 1048576 | tf_op jit(solution)/shard_map/all_to_all | solution.py:34
  691.0 478.6 %all-reduce.7.cloned.1.call-start = ((), (), s32[]{:S(2)}) async-start(), calls=%async_computation.7 | async-start | bytes 3145728 | tf_op jit(solution)/shard_map/psum | solution.py:93
  853.4 319.2 %all-to-all-start.2 = ((bf16[128,2,1024]{0,1,2:T(2,128)(2,1)}), bf16[128,2,1024]{0,1,2:T(2,128)(2,1)S(1)}, u32[]{:S(2)}, u32[]{:S(2)}) async-start(bf16[128,2,1024]{0,1,2:T(2,128)(2,1)} %copy.81), calls=%async_computation.2 | async-start | bytes 1048576 | tf_op jit(solution)/shard_map/all_to_all | solution.py:49
Sparse Core Ops, SparseCore 0:
  14.4 424.6 all-reduce.8
  442.9 70.4 all-gather.6
  516.8 59.1 all-gather.4
  579.4 70.2 all-gather.8
  653.1 71.2 all-gather.10
  728.0 441.5 all-reduce.6
where the time goes:
time: 1190 us; the launch traced here: 1180 us
  waiting for transfers between devices  744 us (63%)
  blocking collectives  361 us (30%)
  local copies, waits for them, and re-layouts  21.7 us (2%)
  matrix products  19.5 us (2%)
  between operations  18.2 us (2%)
  starting transfers between devices  16.6 us (1%)
    psum x1, waiting for transfers between devices, broadcast(): return lax.psum(jnp.where(mine, array, jnp.zeros_like(array)), axis)  425 us
    psum x1, waiting for transfers between devices, local(): grad_sum, a_sum, g_sum = lax.psum((grad_term, a_term, g_term), 'dp')  310 us
    psum x1, blocking collectives, local(): grad_sum, a_sum, g_sum = lax.psum((grad_term, a_term, g_term), 'dp')  215 us
    psum x1, blocking collectives, broadcast(): return lax.psum(jnp.where(mine, array, jnp.zeros_like(array)), axis)  110 us
    all_gather x2, blocking collectives, precondition(): lax.all_gather(stacked_values[block_index][None, :], 'tensor', axis=1, ti...  34.9 us
  transfers between devices with their start and end apart: 9, of which 3 were waited for; matrix products, arithmetic and copies ran while one was open for 3% of the time, Pallas kernels for 0%

commit v1 on v0

v1 whole, which is shorter than its diff:
```python
import jax
import jax.numpy as jnp
from jax import lax
from jax.sharding import Mesh, PartitionSpec as P

damping = 0.001
f32 = jnp.float32
bf16 = jnp.bfloat16


def exchange(array, axis):
    return lax.all_to_all(array, axis, 0, 0, tiled=True)


def swap(array, axis):
    return lax.ppermute(array, axis, [(0, 1), (1, 0)])


def pick(array, index, axis=0):
    return lax.dynamic_index_in_dim(array, index, axis, keepdims=False)


def add(left, right):
    return (left.astype(f32) + right.astype(f32)).astype(bf16)


def rows(array):
    return array.reshape(-1, array.shape[-1])


def cut(array, sizes):
    out, start = [], 0
    for size in sizes:
        out.append(lax.slice_in_dim(array, start, start + size, axis=array.ndim - 2))
        start += size
    return out


def repeat(array, count):
    return jnp.broadcast_to(array[None], (count,) + array.shape)


def local(act, cot, weight, owners, worker_group, basis_a, values_a, basis_g, values_g):
    tok, slab = act.shape
    blocks, full = cot.shape[1:]
    nz, nt = lax.axis_size("z"), lax.axis_size("t")
    z, xl, core, t = (lax.axis_index(name) for name in ("z", "xl", "c", "t"))
    scale = 1.0 / (tok * nz * 4)
    group = full // (nz * 4)
    half = full // 2
    piece = slab // 2

    owner_z, owner_x, owner_c = owners // 4, (owners // 2) % 2, owners % 2
    here_c, here_x = owner_c == core, owner_x == xl
    j_own = 1 + xl

    whole_act = exchange(jnp.broadcast_to(act[None], (nt, tok, slab)).reshape(nt * tok, slab), "t")
    whole_act = whole_act.reshape(nt, tok, slab)

    grad = jnp.einsum("tjb,ta->jba", cot, act, preferred_element_type=f32) * scale
    grad = grad.astype(bf16).reshape(blocks, nt, 2, piece, slab)
    own_cols = lax.dynamic_slice_in_dim(cot, t * slab, slab, 2)
    g_term = jnp.einsum("tja,tjb->jab", cot, own_cols, preferred_element_type=f32) * scale
    g_term = g_term.astype(bf16).reshape(blocks, nz, 2, 2, group, slab)

    qa = basis_a[0].reshape(2, half, slab)
    qg = basis_g[0].reshape(blocks, 2, half, slab)
    vals = jnp.concatenate(
        [values_a.reshape(1, slab), values_g.reshape(blocks, slab), jnp.zeros((5, slab), bf16)], 0
    )

    def for_core(index):
        return (
            pick(grad, index, 2).reshape(-1, slab),
            pick(g_term, index, 3).reshape(-1, slab),
            pick(qa, index, 0),
            pick(qg, index, 1).reshape(-1, slab),
        )

    sent = for_core(1 - core)
    mine = for_core(core)
    sizes = [part.shape[0] for part in sent]
    got = swap(jnp.concatenate(sent + (vals,), 0), "c")
    got_grad, got_g, got_qa, got_qg, got_vals = cut(got, sizes + [8])
    grad = add(mine[0], got_grad).reshape(blocks, nt * piece, slab)
    g_term = add(mine[1], got_g).reshape(blocks, nz, 2, group, slab)
    qa = jnp.where(here_c[0], mine[2], got_qa)
    qg = jnp.where(here_c[1:, None, None], mine[3].reshape(blocks, half, slab), got_qg.reshape(blocks, half, slab))
    flags = lambda here: jnp.concatenate([here, jnp.zeros((5,), here.dtype)])[:, None]
    vals = jnp.where(flags(here_c), vals, got_vals)

    def for_x(index):
        return (
            pick(grad, index),
            pick(g_term, index, 2).reshape(-1, slab),
            pick(qg, index),
        )

    sent = for_x(1 - xl)
    mine = for_x(xl)
    sizes = [part.shape[0] for part in sent]
    got = swap(jnp.concatenate(sent + (qa, vals), 0), "xl")
    got_grad, got_g, got_qg, got_qa, got_vals = cut(got, sizes + [half, 8])
    grad = add(mine[0], got_grad)
    g_term = add(mine[1], got_g).reshape(blocks, nz, group, slab)
    qg = jnp.where(pick(here_x, j_own), mine[2], got_qg)
    qa = jnp.where(here_x[0], qa, got_qa)
    vals = jnp.where(flags(here_x), vals, got_vals)

    per = half // nz
    sent = jnp.concatenate(
        [
            grad.reshape(nz, per, slab),
            g_term.transpose(1, 0, 2, 3).reshape(nz, blocks * group, slab),
            qa.reshape(nz, per, slab),
            qg.reshape(nz, per, slab),
            repeat(vals, nz),
        ],
        1,
    )
    got = exchange(sent, "z")
    got_grad, got_g, got_qa, got_qg, got_vals = cut(got, [per, blocks * group, per, per, 8])
    grad = jnp.sum(got_grad.astype(f32), 0).astype(bf16)
    factor_g = jnp.sum(got_g.astype(f32), 0).reshape(blocks, group, slab).transpose(1, 0, 2)
    qa = pick(got_qa, owner_z[0])
    qg = pick(got_qg, pick(owner_z, j_own))
    vals = jnp.stack(
        [pick(got_vals[:, 0], owner_z[0])]
        + [pick(got_vals[:, 1 + j], owner_z[1 + j]) for j in range(blocks)]
        + [jnp.zeros((slab,), bf16)] * 5,
        0,
    )

    a_term = jnp.einsum("ntf,tb->nfb", whole_act, act, preferred_element_type=f32) * scale
    a_term = a_term.astype(bf16).reshape(nz, 2, 2, group, slab)
    got = swap(pick(a_term, 1 - core, 2), "c")
    a_term = add(pick(a_term, core, 2), got)
    got = swap(pick(a_term, 1 - xl, 1), "xl")
    a_term = add(pick(a_term, xl, 1), got)

    sent = jnp.concatenate([repeat(jnp.concatenate([grad, qa, qg], 0), nz), a_term], 1)
    got = exchange(sent, "z")
    got_grad, got_qa, got_qg, got_a = cut(got, [per, per, per, group])
    factor_a = jnp.sum(got_a.astype(f32), 0)
    grad, qa, qg = rows(got_grad), rows(got_qa), rows(got_qg)

    sent = jnp.concatenate(
        [grad.reshape(nt, piece, slab), repeat(qa, nt), repeat(vals, nt)], 1
    )
    got = lax.all_gather(exchange(sent, "t"), "c", axis=0)
    grad, qa, vals = cut(got, [piece, half, 8])
    vals = vals[0].transpose(1, 0, 2).reshape(8, full).astype(f32)
    grad = grad.transpose(0, 2, 1, 3).reshape(slab, full)
    qa = qa.transpose(0, 2, 1, 3).reshape(full, full)
    qa_cols = lax.dynamic_slice_in_dim(qa, core * half, half, 1)
    rotated = lax.dot_general(
        qa_cols, grad, (((0,), (1,)), ((), ())), preferred_element_type=f32
    ).astype(bf16)

    sent = jnp.concatenate([rotated.reshape(nt, piece, slab), repeat(qg, nt)], 1)
    got_rot, got_qg = cut(exchange(sent, "t"), [piece, half])
    qg = lax.all_gather(got_qg, "c", axis=0).transpose(0, 2, 1, 3).reshape(full, full)
    rotated = got_rot.transpose(1, 0, 2).reshape(piece, full)
    spectral = jnp.dot(rotated, qg, preferred_element_type=f32)
    la = lax.dynamic_slice_in_dim(vals[0], core * half + t * piece, piece, 0)
    lg = pick(vals, j_own)
    scaled = (spectral / (la[:, None] * lg[None, :] + damping)).astype(bf16)
    mixed = lax.dot_general(
        scaled, qg, (((1,), (1,)), ((), ())), preferred_element_type=f32
    ).astype(bf16)

    sent = mixed.reshape(piece, nt, slab).transpose(1, 0, 2)
    got = exchange(repeat(sent, blocks).reshape(blocks * nt, piece, slab), ("xl", "t"))
    got = lax.all_gather(got.reshape(blocks, nt * piece, slab), "c", axis=0)
    mixed = got.transpose(0, 2, 1, 3).reshape(full, blocks * slab)
    pre = jnp.dot(qa, mixed, preferred_element_type=f32).astype(bf16).reshape(full, blocks, slab)
    worker = pick(pre, worker_group[(z * 2 + xl) * 2 + core], 1)[None]

    grad_input = lax.dot_general(
        cot, weight, (((1, 2), (1, 2)), ((), ())), preferred_element_type=f32
    ).astype(bf16)
    return grad_input, factor_a, factor_g, pre, worker


def solution(mesh):
    dp, tensor = mesh.devices.shape
    fine = Mesh(mesh.devices.reshape(dp // 4, 2, 2, tensor), ("z", "xl", "c", "t"))
    dp = ("z", "xl", "c")
    return jax.shard_map(
        local,
        mesh=fine,
        in_specs=(
            P(dp, "t"),
            P(dp, None, None),
            P("t", None, None),
            P(),
            P(),
            P(dp, None, "t"),
            P(dp, "t"),
            P(dp, None, None, "t"),
            P(dp, None, "t"),
        ),
        out_specs=(
            P(dp, "t"),
            P(dp, "t"),
            P(dp, None, "t"),
            P(None, None, "t"),
            P(dp, None, "t"),
        ),
        check_vma=False,
    )
```

time: 1190 us -> 275 us (0.23)
  waiting for transfers between devices: 744 us -> 83.8 us
  blocking collectives: 361 us -> 43 us
  starting transfers between devices: 16.6 us -> 52.3 us
  local copies, waits for them, and re-layouts: 21.7 us -> 47.9 us
    psum x2 -> x0, waiting for transfers between devices: 735 us -> none  [the longest x1 425 us: broadcast(): return lax.psum(jnp.where(mine, array, jnp.zeros_like(array)), axis)]
    psum x2 -> x0, blocking collectives: 326 us -> none  [the longest x1 215 us: local(): grad_sum, a_sum, g_sum = lax.psum((grad_term, a_term, g_term), 'dp')]
    all_gather x4 -> x2, waiting for transfers between devices: 0.06 us -> 46.4 us  [the longest x1 26.5 us: local(): got = lax.all_gather(exchange(sent, 't'), 'c', axis=0)]
    all_to_all x0 -> x2, blocking collectives: none -> 39.3 us  [exchange(): return lax.all_to_all(array, axis, 0, 0, tiled=True)]
    all_gather x2 -> x1, blocking collectives: 34.9 us -> 3.63 us  [local(): got = lax.all_gather(got.reshape(blocks, nt * piece, slab), 'c', axis=0)]
    all_to_all x3 -> x4, waiting for transfers between devices: 7.04 us -> 33.3 us  [exchange(): return lax.all_to_all(array, axis, 0, 0, tiled=True)]
    all_to_all x3 -> x4, starting transfers between devices: 16.4 us -> 36.3 us  [exchange(): return lax.all_to_all(array, axis, 0, 0, tiled=True)]
    ppermute x0 -> x4, starting transfers between devices: none -> 15.9 us  [swap(): return lax.ppermute(array, axis, [(0, 1), (1, 0)])]
  transfers between devices with their start and end apart: 9 -> 10, of which waited for: 3 -> 8; matrix products, arithmetic and copies ran while one was open for 3% -> 9% of each run, Pallas kernels for 0% -> 0%
where the time goes in v1:
time: 275 us; the launch traced here: 274 us
  waiting for transfers between devices  83.8 us (30%)
  starting transfers between devices  52.3 us (19%)
  local copies, waits for them, and re-layouts  47.9 us (17%)
  blocking collectives  43 us (16%)
  between operations  24.3 us (9%)
  other arithmetic  11.5 us (4%)
  matrix products  10.9 us (4%)
    all_to_all x2, blocking collectives, exchange(): return lax.all_to_all(array, axis, 0, 0, tiled=True)  39.3 us
    all_to_all x4, starting transfers between devices, exchange(): return lax.all_to_all(array, axis, 0, 0, tiled=True)  36.3 us
    all_to_all x4, waiting for transfers between devices, exchange(): return lax.all_to_all(array, axis, 0, 0, tiled=True)  33.3 us
    all_gather x1, waiting for transfers between devices, local(): got = lax.all_gather(exchange(sent, 't'), 'c', axis=0)  26.5 us
    all_gather x1, waiting for transfers between devices, local(): lax.all_gather(got_qg, 'c', axis=0).transpose(0, 2, 1, 3)  19.8 us
    ppermute x4, starting transfers between devices, swap(): return lax.ppermute(array, axis, [(0, 1), (1, 0)])  15.9 us
    unnamed x47, local copies, waits for them, and re-layouts  15.4 us
    dynamic_slice x10, local copies, waits for them, and re-layouts, pick(): return lax.dynamic_index_in_dim(array, index, axis, keepdims=False)  7.06 us
  transfers between devices with their start and end apart: 10, of which 8 were waited for; matrix products, arithmetic and copies ran while one was open for 9% of the time, Pallas kernels for 0%

profile of v1, /device:TPU:1, one launch (start us, length us, event | category | flops | bytes accessed | tf_op | source)
XLA Modules:
  0.0 273.6 jit_solution(2620482853834263592)
XLA Ops:
  9.8 4.7 %copy.62 = bf16[512,2,1024]{0,2,1:T(8,128)(2,1)S(1)} copy(bf16[512,2,1024]{2,1,0:T(2,128)(2,1)} %param.10) | data formatting | bytes 4194304 | tf_op args[1]
  19.8 1.8 constant_dynamic-slice_fusion.12
  21.6 4.4 %concatenate.31 = bf16[3592,128]{1,0:T(8,128)(2,1)} concatenate(bf16[1024,128]{1,0:T(8,128)(2,1)S(1)} %bitcast.201, bf16[1024,128]{1,0:T(8,128)(2,1)S(1)} %bitcast.200, bf16[512,128]{1,0:T(8,128)(2,1)S(1)} %dynamic-slice_bitcast_fusion.1, bf16[1024,128]{1,0:T(8,128)(2,1)} %bitcast.202, bf16[1,128]{1,0:T(2,128)(2,1)S(1)} %copy-done.9, bf16[2,128]{1,0:T(2,128)(2,1)S(1)} %bitcast.234, ...), dimensions={0} | concatenate | bytes 1839104 | tf_op jit(solution)/shard_map/concatenate | solution.py:83
  25.9 8.8 %collective-permute-start = (bf16[3592,128]{1,0:T(8,128)(2,1)}, bf16[3592,128]{1,0:T(8,128)(2,1)S(1)}, u32[]{:S(2)}, u32[]{:S(2)}) collective-permute-start(bf16[3592,128]{1,0:T(8,128)(2,1)} %concatenate.31), channel_id=1, source_target_pairs={{0,8},{8,0},{1,9},{9,1},{2,10},{10,2},{3,11},{11,3},{4,12},{12,4},... | collective-permute-start | bytes 2758664 | tf_op jit(solution)/shard_map/ppermute | solution.py:16
  42.7 1.9 collective-permute-start.1
  46.3 2.0 broadcast_in_dim.82
  48.2 4.2 %all-to-all-start.1 = ((bf16[8,512,128]{1,2,0:T(8,128)(2,1)}), bf16[8,512,128]{1,2,0:T(8,128)(2,1)}, u32[]{:S(2)}, u32[]{:S(2)}) async-start(bf16[8,512,128]{1,2,0:T(8,128)(2,1)} %broadcast_in_dim.82), calls=%async_computation.1 | async-start | bytes 2097152 | tf_op jit(solution)/shard_map/all_to_all | solution.py:12
  55.0 3.2 %collective-permute-done.1 = bf16[2056,128]{1,0:T(8,128)(2,1)} collective-permute-done((bf16[2056,128]{1,0:T(8,128)(2,1)}, bf16[2056,128]{1,0:T(8,128)(2,1)}, u32[]{:S(2)}, u32[]{:S(2)}) %collective-permute-start.1) | collective-permute-done | bytes 526368 | tf_op jit(solution)/shard_map/ppermute | solution.py:16
  60.8 2.4 slice_select_fusion
  66.0 3.6 %all-to-all-done.1 = bf16[8,512,128]{1,2,0:T(8,128)(2,1)} async-done(((bf16[8,512,128]{1,2,0:T(8,128)(2,1)}), bf16[8,512,128]{1,2,0:T(8,128)(2,1)}, u32[]{:S(2)}, u32[]{:S(2)}) %all-to-all-start.1) | async-done | bytes 1048608 | tf_op jit(solution)/shard_map/all_to_all | solution.py:12
  69.6 14.0 %all-to-all-start = ((bf16[16,136,128]{2,1,0:T(8,128)(2,1)}), bf16[16,136,128]{2,1,0:T(8,128)(2,1)S(1)}, u32[]{:S(2)}, u32[]{:S(2)}) async-start(bf16[16,136,128]{2,1,0:T(8,128)(2,1)} %constant_dynamic-update-slice_fusion.3), calls=%async_computation | async-start | bytes 1114112 | tf_op jit(solution)/shard_map/all_to_all | solution.py:12
  85.3 3.3 %collective-permute-start.2 = (bf16[16,2,16,128]{3,2,1,0:T(8,128)(2,1)S(1)}, bf16[16,2,16,128]{3,2,1,0:T(8,128)(2,1)S(1)}, u32[]{:S(2)}, u32[]{:S(2)}) collective-permute-start(bf16[16,2,16,128]{3,2,1,0:T(8,128)(2,1)S(1)} %dynamic-slice_bitcast_fusion), channel_id=1, source_target_pairs={{0,8},{8,0},{1,9},{9,1},{2,10},{10,2},{3,11},{11,3},{4,12},{12,4},... | collective-permute-start | bytes 393224 | tf_op jit(solution)/shard_map/ppermute | solution.py:16
  89.6 1.9 collective-permute-start.3
  96.1 11.4 %all-to-all-done = bf16[16,136,128]{2,1,0:T(8,128)(2,1)S(1)} async-done(((bf16[16,136,128]{2,1,0:T(8,128)(2,1)}), bf16[16,136,128]{2,1,0:T(8,128)(2,1)S(1)}, u32[]{:S(2)}, u32[]{:S(2)}) %all-to-all-start) | async-done | bytes 557088 | tf_op jit(solution)/shard_map/all_to_all | solution.py:12
  108.4 12.5 %all-to-all-start.2 = ((bf16[16,112,128]{2,1,0:T(8,128)(2,1)}), bf16[16,112,128]{2,1,0:T(8,128)(2,1)}, u32[]{:S(2)}, u32[]{:S(2)}) async-start(bf16[16,112,128]{2,1,0:T(8,128)(2,1)} %pad_maximum_fusion.2), calls=%async_computation.2 | async-start | bytes 917504 | tf_op jit(solution)/shard_map/all_to_all | solution.py:12
  125.0 16.7 %all-to-all-done.2 = bf16[16,112,128]{2,1,0:T(8,128)(2,1)} async-done(((bf16[16,112,128]{2,1,0:T(8,128)(2,1)}), bf16[16,112,128]{2,1,0:T(8,128)(2,1)}, u32[]{:S(2)}, u32[]{:S(2)}) %all-to-all-start.2) | async-done | bytes 458784 | tf_op jit(solution)/shard_map/all_to_all | solution.py:12
  143.0 15.9 %all_to_all.31 = bf16[8,584,128]{2,1,0:T(8,128)(2,1)} all-to-all(bf16[8,584,128]{2,1,0:T(8,128)(2,1)S(1)} %pad_maximum_fusion), channel_id=1, replica_groups=mesh['z'=16,'xl'=2,'c'=2,'t'=8] {'t'}, dimensions={0} | all-to-all | bytes 2392064 | tf_op jit(solution)/shard_map/all_to_all | solution.py:12
  158.9 26.5 %all-gather.5.cloned.1.call-done = bf16[16,584,128]{2,1,0:T(8,128)(2,1)} async-done(((bf16[8,584,128]{2,1,0:T(8,128)(2,1)}), bf16[16,584,128]{2,1,0:T(8,128)(2,1)}) %all-gather.5.cloned.1.call-update) | async-done | bytes 2392080 | tf_op jit(solution)/shard_map/all_gather | solution.py:150
  191.7 23.4 %all_to_all.32 = bf16[8,576,128]{2,1,0:T(8,128)(2,1)S(1)} all-to-all(bf16[8,576,128]{2,1,0:T(8,128)(2,1)S(1)} %pad_maximum_fusion.1), channel_id=1, replica_groups=mesh['z'=16,'xl'=2,'c'=2,'t'=8] {'t'}, dimensions={0} | all-to-all | bytes 2359296 | tf_op jit(solution)/shard_map/all_to_all | solution.py:12
  218.2 19.8 %all-gather.7.cloned.1.call-done = bf16[16,512,128]{2,1,0:T(8,128)(2,1)} async-done(((bf16[8,512,128]{2,1,0:T(8,128)(2,1)}), bf16[16,512,128]{2,1,0:T(8,128)(2,1)}) %all-gather.7.cloned.1.call-update) | async-done | bytes 2097168 | tf_op jit(solution)/shard_map/all_gather | solution.py:162
  238.0 4.3 %copy.74 = bf16[2,512,8,128]{3,2,1,0:T(8,128)(2,1)} copy(bf16[2,512,8,128]{3,1,2,0:T(8,128)(2,1)} %bitcast.193) | data formatting | bytes 4194304 | tf_op jit(solution)/shard_map/transpose | solution.py:162
  242.3 3.4 %fusion.24 = bf16[8,8,8,128]{3,1,2,0:T(8,128)(2,1)S(1)} fusion(bf16[128,8,8,128]{3,2,1,0:T(8,128)(2,1)} %bitcast.194, f32[1024]{0:T(1024)S(1)} %bitcast.236, f32[64]{0:T(128)S(1)} %fusion.61, bf16[8,576,128]{2,1,0:T(8,128)(2,1)} %copy-done.3), kind=kOutput, calls=%fused_computation.24 | convolution fusion | flops 268763136 | bytes 4460800 | tf_op jit(solution)/shard_map/dot_general | solution.py:168
  246.6 5.5 %all-to-all-start.5 = ((bf16[16,64,128]{2,1,0:T(8,128)(2,1)}), bf16[16,64,128]{2,1,0:T(8,128)(2,1)S(1)}, u32[]{:S(2)}, u32[]{:S(2)}) async-start(bf16[16,64,128]{2,1,0:T(8,128)(2,1)} %bitcast.204), calls=%async_computation.5 | async-start | bytes 524288 | tf_op jit(solution)/shard_map/all_to_all | solution.py:12
  259.8 3.6 %all_gather.19 = bf16[2,2,512,128]{3,2,1,0:T(8,128)(2,1)S(1)} all-gather(bf16[1,2,512,128]{3,2,1,0:T(8,128)(2,1)S(1)} %bitcast.203), channel_id=1, replica_groups=mesh['z'=16,'xl'=2,'c'=2,'t'=8] {'c'}, dimensions={0}, use_global_device_ids=true | all-gather | bytes 786432 | tf_op jit(solution)/shard_map/all_gather | solution.py:174
  (120 shorter events, 49.9 us)
Async XLA Ops:
  7.2 244.9 %copy-start = (bf16[128,2,1024]{2,1,0:T(2,128)(2,1)S(1)}, bf16[128,2,1024]{2,1,0:T(2,128)(2,1)}, u32[]{:S(2)}) copy-start(bf16[128,2,1024]{2,1,0:T(2,128)(2,1)} %param.11) | copy-start | bytes 1572868
  14.6 1.6 copy-start.4
  17.7 3.9 %copy-start.9 = (bf16[1,128]{1,0:T(2,128)(2,1)S(1)}, bf16[1,128]{1,0:T(2,128)(2,1)}, u32[]{:S(2)}) copy-start(bf16[1,128]{1,0:T(2,128)(2,1)} %param.15) | copy-start | bytes 772
  17.7 3.9 %copy-start.10 = (bf16[1,2,128]{2,1,0:T(2,128)(2,1)S(1)}, bf16[1,2,128]{2,1,0:T(2,128)(2,1)}, u32[]{:S(2)}) copy-start(bf16[1,2,128]{2,1,0:T(2,128)(2,1)} %param.17) | copy-start | bytes 1540
  25.9 11.1 %collective-permute-start = (bf16[3592,128]{1,0:T(8,128)(2,1)}, bf16[3592,128]{1,0:T(8,128)(2,1)S(1)}, u32[]{:S(2)}, u32[]{:S(2)}) collective-permute-start(bf16[3592,128]{1,0:T(8,128)(2,1)} %concatenate.31), channel_id=1, source_target_pairs={{0,8},{8,0},{1,9},{9,1},{2,10},{10,2},{3,11},{11,3},{4,12},{12,4},... | collective-permute-start | bytes 2758664 | tf_op jit(solution)/shard_map/ppermute | solution.py:16
  37.1 2.7 copy-start.8
  37.1 2.7 copy-start.13
  37.1 4.2 %copy-start.7 = (bf16[1,1024,128]{2,1,0:T(8,128)(2,1)S(1)}, bf16[1,1024,128]{2,1,0:T(8,128)(2,1)}, u32[]{:S(2)}) copy-start(bf16[1,1024,128]{2,1,0:T(8,128)(2,1)} %param.14) | copy-start | bytes 786436
  37.1 4.9 %copy-start.11 = (bf16[1,2,128]{2,1,0:T(2,128)(2,1)S(1)}, bf16[1,2,128]{2,1,0:T(2,128)(2,1)}, u32[]{:S(2)}) copy-start(bf16[1,2,128]{2,1,0:T(2,128)(2,1)} %param.17) | copy-start | bytes 1540
  37.1 4.9 %copy-start.12 = (pred[8]{0:T(512)(128)(4,1)S(1)}, pred[8]{0:T(512)(128)(4,1)}, u32[]{:S(2)}) copy-start(pred[8]{0:T(512)(128)(4,1)} %concatenate.32) | copy-start | bytes 28
  38.4 3.0 %copy-start.6 = (bf16[1024,128]{1,0:T(8,128)(2,1)}, bf16[1024,128]{1,0:T(8,128)(2,1)S(1)}, u32[]{:S(2)}) copy-start(bf16[1024,128]{1,0:T(8,128)(2,1)S(1)} %get-tuple-element.28) | copy-start | bytes 786436
  42.7 15.5 %collective-permute-start.1 = (bf16[2056,128]{1,0:T(8,128)(2,1)}, bf16[2056,128]{1,0:T(8,128)(2,1)}, u32[]{:S(2)}, u32[]{:S(2)}) collective-permute-start(bf16[2056,128]{1,0:T(8,128)(2,1)} %constant_dynamic-update-slice_fusion), channel_id=1, source_target_pairs={{0,16},{16,0},{1,17},{17,1},{2,18},{18,2},{3,19},{19,3},{4,20},{20... | collective-permute-start | bytes 1579016 | tf_op jit(solution)/shard_map/ppermute | solution.py:16
  48.2 21.3 %all-to-all-start.1 = ((bf16[8,512,128]{1,2,0:T(8,128)(2,1)}), bf16[8,512,128]{1,2,0:T(8,128)(2,1)}, u32[]{:S(2)}, u32[]{:S(2)}) async-start(bf16[8,512,128]{1,2,0:T(8,128)(2,1)} %broadcast_in_dim.82), calls=%async_computation.1 | async-start | bytes 2097152 | tf_op jit(solution)/shard_map/all_to_all | solution.py:12
  53.7 10.9 %copy-start.15 = (pred[8]{0:T(512)(128)(4,1)S(1)}, pred[8]{0:T(512)(128)(4,1)}, u32[]{:S(2)}) copy-start(pred[8]{0:T(512)(128)(4,1)} %concatenate.35) | copy-start | bytes 28
  63.2 25.4 %copy-start.14 = (s32[3]{0:T(128)S(1)}, s32[3]{0:T(128)}, u32[]{:S(2)}) copy-start(s32[3]{0:T(128)} %param.12) | copy-start | bytes 40
  69.6 37.9 %all-to-all-start = ((bf16[16,136,128]{2,1,0:T(8,128)(2,1)}), bf16[16,136,128]{2,1,0:T(8,128)(2,1)S(1)}, u32[]{:S(2)}, u32[]{:S(2)}) async-start(bf16[16,136,128]{2,1,0:T(8,128)(2,1)} %constant_dynamic-update-slice_fusion.3), calls=%async_computation | async-start | bytes 1114112 | tf_op jit(solution)/shard_map/all_to_all | solution.py:12
  85.3 4.2 %collective-permute-start.2 = (bf16[16,2,16,128]{3,2,1,0:T(8,128)(2,1)S(1)}, bf16[16,2,16,128]{3,2,1,0:T(8,128)(2,1)S(1)}, u32[]{:S(2)}, u32[]{:S(2)}) collective-permute-start(bf16[16,2,16,128]{3,2,1,0:T(8,128)(2,1)S(1)} %dynamic-slice_bitcast_fusion), channel_id=1, source_target_pairs={{0,8},{8,0},{1,9},{9,1},{2,10},{10,2},{3,11},{11,3},{4,12},{12,4},... | collective-permute-start | bytes 393224 | tf_op jit(solution)/shard_map/ppermute | solution.py:16
  89.6 6.4 %collective-permute-start.3 = (bf16[16,16,128]{2,1,0:T(8,128)(2,1)S(1)}, bf16[16,16,128]{2,1,0:T(8,128)(2,1)S(1)}, u32[]{:S(2)}, u32[]{:S(2)}) collective-permute-start(bf16[16,16,128]{2,1,0:T(8,128)(2,1)S(1)} %dynamic-slice_bitcast_fusion.2), channel_id=1, source_target_pairs={{0,16},{16,0},{1,17},{17,1},{2,18},{18,2},{3,19},{19,3},{4,20},{20... | collective-permute-start | bytes 196616 | tf_op jit(solution)/shard_map/ppermute | solution.py:16
  108.4 33.3 %all-to-all-start.2 = ((bf16[16,112,128]{2,1,0:T(8,128)(2,1)}), bf16[16,112,128]{2,1,0:T(8,128)(2,1)}, u32[]{:S(2)}, u32[]{:S(2)}) async-start(bf16[16,112,128]{2,1,0:T(8,128)(2,1)} %pad_maximum_fusion.2), calls=%async_computation.2 | async-start | bytes 917504 | tf_op jit(solution)/shard_map/all_to_all | solution.py:12
  120.9 64.5 %all-gather.5.cloned.1.call-start = ((), (), s32[]{:S(2)}) async-start(), calls=%async_computation.6 | async-start | bytes 3588096 | tf_op jit(solution)/shard_map/all_gather | solution.py:150
  158.9 79.1 %all-gather.7.cloned.1.call-start = ((), (), s32[]{:S(2)}) async-start(), calls=%async_computation.7 | async-start | bytes 3145728 | tf_op jit(solution)/shard_map/all_gather | solution.py:162
  246.6 13.3 %all-to-all-start.5 = ((bf16[16,64,128]{2,1,0:T(8,128)(2,1)}), bf16[16,64,128]{2,1,0:T(8,128)(2,1)S(1)}, u32[]{:S(2)}, u32[]{:S(2)}) async-start(bf16[16,64,128]{2,1,0:T(8,128)(2,1)} %bitcast.204), calls=%async_computation.5 | async-start | bytes 524288 | tf_op jit(solution)/shard_map/all_to_all | solution.py:12
  252.1 1.4 copy-start.16
  253.5 10.5 %copy-start.2 = (bf16[2,512,8,128]{3,2,1,0:T(8,128)(2,1)S(1)}, bf16[2,512,8,128]{3,2,1,0:T(8,128)(2,1)}, u32[]{:S(2)}) copy-start(bf16[2,512,8,128]{3,2,1,0:T(8,128)(2,1)} %copy-done.1) | copy-start | bytes 6291460
  (3 other events, 3.2 us)
Sparse Core Ops, SparseCore 0:
  159.0 26.4 all-gather.4
  217.5 20.5 all-gather.6

commit v2 on v1

v2 whole, which is shorter than its diff:
```python
import functools

import jax
import jax.numpy as jnp
from jax import lax
from jax.experimental import pallas as pl
from jax.experimental.pallas import tpu as pltpu
from jax.sharding import Mesh, PartitionSpec as P

damping = 0.001
f32 = jnp.float32
bf16 = jnp.bfloat16
VALS = 16

Z, XL, CORE, T, OWNER, GROUP = 0, 1, 2, 3, 4, 7


def exchange(array, axis):
    return lax.all_to_all(array, axis, 0, 0, tiled=True)


def swap(array, axis):
    return lax.ppermute(array, axis, [(0, 1), (1, 0)])


def call(body, outs, info, *args, scratch=(), flops=0):
    bytes_all = sum(a.size * a.dtype.itemsize for a in args) + sum(
        o.size * o.dtype.itemsize for o in outs
    )
    return pl.pallas_call(
        body,
        out_shape=outs,
        in_specs=[pl.BlockSpec(memory_space=pltpu.SMEM)]
        + [pl.BlockSpec(memory_space=pltpu.VMEM)] * len(args),
        out_specs=[pl.BlockSpec(memory_space=pltpu.VMEM)] * len(outs),
        scratch_shapes=list(scratch),
        compiler_params=pltpu.CompilerParams(vmem_limit_bytes=40 * 1024 * 1024),
        cost_estimate=pl.CostEstimate(flops=flops, bytes_accessed=bytes_all, transcendentals=0),
    )(info, *args)


def out(shape, dtype=bf16):
    return jax.ShapeDtypeStruct(shape, dtype)


def dot(left, right, dims=((1,), (0,))):
    return lax.dot_general(left, right, (dims, ((), ())), preferred_element_type=f32)


def value_rows(flags, own, other):
    place = lax.broadcasted_iota(jnp.int32, own.shape, 0)
    take = jnp.zeros(own.shape, jnp.int32)
    for row, flag in enumerate(flags):
        take = jnp.where(place == row, flag.astype(jnp.int32), take)
    return jnp.where(take > 0, own.astype(f32), other.astype(f32)).astype(bf16)


def pack_bases(info, ba, bg, vals, sent):
    half = ba.shape[0] // 2
    start = pl.multiple_of((1 - info[CORE]) * half, half)
    sent[0:half] = ba[pl.ds(start, half)]
    for j in range(bg.shape[0]):
        sent[(1 + j) * half : (2 + j) * half] = bg[j, pl.ds(start, half)]
    sent[(1 + bg.shape[0]) * half :] = vals[...]


def select_core(info, ba, bg, vals, got, sent):
    half = ba.shape[0] // 2
    nz, _, slab = sent.shape
    per = half // nz
    core = info[CORE]
    start = pl.multiple_of(core * half, half)
    count = 1 + bg.shape[0]
    flags = [info[OWNER + i] % 2 == core for i in range(count)]
    for i in range(count):
        span = slice(i * per, (i + 1) * per)

        @pl.when(flags[i])
        def _():
            own = ba[pl.ds(start, half)] if i == 0 else bg[i - 1, pl.ds(start, half)]
            sent[:, span] = own.reshape(nz, per, slab)

        @pl.when(jnp.logical_not(flags[i]))
        def _():
            sent[:, span] = got[i * half : (i + 1) * half].reshape(nz, per, slab)

    chosen = value_rows(flags, vals[...], got[count * half :])
    for k in range(nz):
        sent[k, count * per :] = chosen


def select_z(info, got, sent, keep):
    per = (got.shape[1] - VALS) // 3
    xl = info[XL]
    source = [info[OWNER + i] // 4 for i in range(3)]

    def part(i):
        return got[source[i], i * per : (i + 1) * per]

    chosen = got[source[0], 3 * per :]
    for i in (1, 2):
        other = got[source[i], 3 * per :]
        place = lax.broadcasted_iota(jnp.int32, chosen.shape, 0)
        chosen = jnp.where(place == i, other.astype(f32), chosen.astype(f32)).astype(bf16)
    for ref in (sent, keep):
        ref[0:per] = part(0)
        ref[2 * per :] = chosen

    @pl.when(xl == 0)
    def _():
        keep[per : 2 * per] = part(1)
        sent[per : 2 * per] = part(2)

    @pl.when(xl == 1)
    def _():
        keep[per : 2 * per] = part(2)
        sent[per : 2 * per] = part(1)


def terms(info, x0, x1, act, own0, own1, sent, keep, packed):
    _, _, nz, height, slab = packed.shape
    full = x0.shape[1]
    nt = full // slab
    per = full // 2 // nz
    group = (height - per) // 2
    scale = 1.0 / (x0.shape[0] * nz * 4)
    for j, (x, own) in enumerate(((x0, own0), (x1, own1))):
        right = jnp.concatenate([act[...], own[...]], 1)
        both = dot(x[...], right, ((0,), (0,))) * scale
        grad = both[:, :slab].reshape(nt, 2, slab // 2, slab)
        cov = both[:, slab:].reshape(nz, 2, 2, group, slab)
        for c in range(2):
            packed[c, j, :, 0:per] = grad[:, c].reshape(nz, per, slab)
            for xl in range(2):
                packed[c, xl, :, per + j * group : per + (j + 1) * group] = cov[:, xl, c]
    core = info[CORE]
    sent[...] = packed[1 - core].astype(bf16)
    keep[...] = packed[core]


def add_core(info, keep, got, sent, rest):
    xl = info[XL]
    sent[...] = (keep[1 - xl] + got[1 - xl].astype(f32)).astype(bf16)
    rest[...] = keep[xl] + got[xl].astype(f32)


def pack_z(info, keep, got, base, other, sent, vals):
    nz, height, slab = keep.shape
    per = (base.shape[0] - VALS) // 2
    xl = info[XL]
    sent[:, 0:height] = (keep[...] + got[...].astype(f32)).astype(bf16)
    here = [(info[OWNER + i] // 2) % 2 == xl for i in range(3)]
    flag_a = here[0]
    flag_g = (info[OWNER + 1 + xl] // 2) % 2 == xl
    for i, flag in enumerate((flag_a, flag_g)):
        span = slice(i * per, (i + 1) * per)
        place = slice(height + i * per, height + (i + 1) * per)

        @pl.when(flag)
        def _():
            for k in range(nz):
                sent[k, place] = base[span]

        @pl.when(jnp.logical_not(flag))
        def _():
            for k in range(nz):
                sent[k, place] = other[span]

    vals[...] = value_rows(here, base[2 * per :], other[2 * per :])


def reduce_z(info, got, a_keep, a_got, sent, factor_g, qa, qg):
    nz, _, slab = got.shape
    half = qa.shape[0]
    per = half // nz
    group = factor_g.shape[1]
    total = got[0, 0 : per + 2 * group].astype(f32)
    for k in range(1, nz):
        total = total + got[k, 0 : per + 2 * group].astype(f32)
    grad = total[0:per].astype(bf16)
    for j in range(2):
        factor_g[j] = total[per + j * group : per + (j + 1) * group]
    for k in range(nz):
        sent[k, 0:per] = grad
    sent[:, per:] = (a_keep[...] + a_got[...].astype(f32)).astype(bf16)
    start = per + 2 * group
    qa[...] = got[:, start : start + per].reshape(half, slab)
    qg[...] = got[:, start + per : start + 2 * per].reshape(half, slab)


def pack_t(info, got, qa, vals, sent, factor_a):
    nz, _, slab = got.shape
    half = qa.shape[0]
    per = half // nz
    nt = sent.shape[0]
    piece = half // nt
    sent[:, 0:piece] = got[:, 0:per].reshape(half, slab).reshape(nt, piece, slab)
    for k in range(nt):
        sent[k, piece : piece + half] = qa[...]
        sent[k, piece + half :] = vals[...]
    total = got[0, per:].astype(f32)
    for k in range(1, nz):
        total = total + got[k, per:].astype(f32)
    factor_a[...] = total


def rotate(info, own, other, qg, sent, grad):
    nt, _, slab = own.shape
    half = qg.shape[0]
    piece = half // nt
    core = info[CORE]
    mine = pl.multiple_of(core * piece, piece)
    theirs = pl.multiple_of((1 - core) * piece, piece)
    for k in range(nt):
        grad[pl.ds(mine, piece), k * slab : (k + 1) * slab] = own[k, 0:piece]
        grad[pl.ds(theirs, piece), k * slab : (k + 1) * slab] = other[k, 0:piece]
    near = grad[:, pl.ds(pl.multiple_of(core * half, half), half)]
    far = grad[:, pl.ds(pl.multiple_of((1 - core) * half, half), half)]
    for i in range(nt // 2):
        k = core * (nt // 2) + i
        turned = dot(near, own[k, piece : piece + half]) + dot(far, other[k, piece : piece + half])
        turned = turned.T.astype(bf16)
        sent[2 * i, 0:piece] = turned[0:piece]
        sent[2 * i + 1, 0:piece] = turned[piece:]
    for k in range(nt):
        sent[k, piece:] = qg[...]


def scale_rows(info, own, other, gathered, sent, rot, scaled, column):
    nt, height, slab = own.shape
    piece = sent.shape[2]
    half = height - piece
    core, xl, t = info[CORE], info[XL], info[T]
    first = gathered.shape[1] - VALS
    row = gathered[core * (nt // 2) + t // 2, first:].astype(f32)[0:1]
    column[...] = jnp.broadcast_to(row, (slab, slab)).T
    la = column[pl.ds(pl.multiple_of((t % 2) * piece, piece), piece)]
    for k in range(nt):
        rot[:, k * slab : (k + 1) * slab] = own[k, 0:piece]
    near = rot[:, pl.ds(pl.multiple_of(core * half, half), half)]
    far = rot[:, pl.ds(pl.multiple_of((1 - core) * half, half), half)]
    for k in range(nt):
        spectral = dot(near, own[k, piece:]) + dot(far, other[k, piece:])
        values = gathered[k, first:].astype(f32)
        lg = jnp.where(xl == 0, values[1:2], values[2:3])
        scaled[k] = (spectral / (la * lg + damping)).astype(bf16)
    for side, ref in ((core, own), (1 - core, other)):
        mixed = dot(scaled[0], ref[0, piece:], ((1,), (1,)))
        for k in range(1, nt):
            mixed = mixed + dot(scaled[k], ref[k, piece:], ((1,), (1,)))
        mixed = mixed.astype(bf16)
        for i in range(nt // 2):
            for copy in range(2):
                sent[copy, side * (nt // 2) + i] = mixed[:, i * slab : (i + 1) * slab]


def finish(info, own, other, own_mixed, other_mixed, pre, worker):
    blocks, nt, piece, slab = own_mixed.shape
    half = pre.shape[1] // 2
    core = info[CORE]
    for side, ref in ((core, own), (1 - core, other)):
        total = jnp.zeros((half, blocks * slab), f32)
        for part, mixed in ((core, own_mixed), (1 - core, other_mixed)):
            for i in range(nt // 2):
                right = jnp.concatenate(
                    [mixed[j, 2 * i : 2 * i + 2].reshape(2 * piece, slab) for j in range(blocks)], 1
                )
                total = total + dot(ref[part * (nt // 2) + i, piece : piece + half], right)
        total = total.astype(bf16)
        place = pl.ds(pl.multiple_of(side * half, half), half)
        for j in range(blocks):
            pre[j, place] = total[:, j * slab : (j + 1) * slab]

        @pl.when(info[GROUP] == 0)
        def _():
            worker[0, place] = total[:, :slab]

        @pl.when(info[GROUP] == 1)
        def _():
            worker[0, place] = total[:, slab:]


def local(act, cot, weight, owners, worker_group, basis_a, values_a, basis_g, values_g):
    tok, slab = act.shape
    blocks, full = cot.shape[1:]
    nz, nt = lax.axis_size("z"), lax.axis_size("t")
    z, xl, core, t = (lax.axis_index(name) for name in ("z", "xl", "c", "t"))
    group = full // (nz * 4)
    half, piece = full // 2, slab // 2
    per = half // nz
    height = per + blocks * group
    replica = (z * 2 + xl) * 2 + core
    info = jnp.concatenate(
        [
            jnp.stack([z, xl, core, t]).astype(jnp.int32),
            owners,
            lax.dynamic_slice_in_dim(worker_group, replica, 1),
        ]
    )

    ba, bg = basis_a[0], basis_g[0]
    vals = jnp.concatenate([values_a, values_g[0], jnp.zeros((VALS - 3, slab), bf16)], 0)
    (sent,) = call(pack_bases, [out((3 * half + VALS, slab))], info, ba, bg, vals)
    got = swap(sent, "c")
    (sent,) = call(select_core, [out((nz, 3 * per + VALS, slab))], info, ba, bg, vals, got)
    got_bases = exchange(sent, "z")

    whole_act = lax.all_gather(act, "t", axis=1, tiled=True)

    x0, x1 = cot[:, 0], cot[:, 1]
    own0 = lax.dynamic_slice_in_dim(x0, t * slab, slab, 1)
    own1 = lax.dynamic_slice_in_dim(x1, t * slab, slab, 1)
    block = (2, nz, height, slab)
    sent, keep = call(
        terms,
        [out(block), out(block, f32)],
        info,
        x0,
        x1,
        act,
        own0,
        own1,
        scratch=[pltpu.VMEM((2,) + block, f32)],
        flops=8 * tok * full * slab,
    )
    got = swap(sent, "c")
    sent, keep = call(add_core, [out(block[1:]), out(block[1:], f32)], info, keep, got)
    got = swap(sent, "xl")

    shape = (2 * per + VALS, slab)
    base_sent, base_keep = call(select_z, [out(shape), out(shape)], info, got_bases)
    base_got = swap(base_sent, "xl")

    sent, vals = call(
        pack_z,
        [out((nz, height + 2 * per, slab)), out((VALS, slab))],
        info,
        keep,
        got,
        base_keep,
        base_got,
    )
    got = exchange(sent, "z")

    scale = 1.0 / (tok * nz * 4)
    a_term = dot(whole_act, act, ((0,), (0,))) * scale
    a_term = a_term.reshape(nz, 2, 2, group, slab)
    pick = functools.partial(lax.dynamic_index_in_dim, keepdims=False)
    a_got = swap(pick(a_term, 1 - core, 2).astype(bf16), "c")
    a_term = pick(a_term, core, 2) + a_got.astype(f32)
    a_got = swap(pick(a_term, 1 - xl, 1).astype(bf16), "xl")
    a_keep = pick(a_term, xl, 1)

    sent, factor_g, qa, qg = call(
        reduce_z,
        [out((nz, per + group, slab)), out((blocks, group, slab), f32), out((half, slab)), out((half, slab))],
        info,
        got,
        a_keep,
        a_got,
    )
    got = exchange(sent, "z")
    sent, factor_a = call(
        pack_t,
        [out((nt, piece + half + VALS, slab)), out((group, slab), f32)],
        info,
        got,
        qa,
        vals,
    )
    own = exchange(sent, "t")
    other = swap(own, "c")
    (sent,) = call(
        rotate,
        [out((nt, piece + half, slab))],
        info,
        own,
        other,
        qg,
        scratch=[pltpu.VMEM((slab, full), bf16)],
        flops=2 * slab * full * half,
    )
    own_rows = exchange(sent, "t")
    other_rows = swap(own_rows, "c")
    (sent,) = call(
        scale_rows,
        [out((blocks, nt, piece, slab))],
        info,
        own_rows,
        other_rows,
        own,
        scratch=[
            pltpu.VMEM((piece, full), bf16),
            pltpu.VMEM((nt, piece, slab), bf16),
            pltpu.VMEM((slab, slab), f32),
        ],
        flops=4 * piece * full * full,
    )
    own_mixed = exchange(sent.reshape(blocks * nt, piece, slab), ("xl", "t"))
    own_mixed = own_mixed.reshape(blocks, nt, piece, slab)
    other_mixed = swap(own_mixed, "c")
    pre, worker = call(
        finish,
        [out((blocks, full, slab)), out((1, full, slab))],
        info,
        own,
        other,
        own_mixed,
        other_mixed,
        flops=4 * full * full * slab,
    )

    grad_input = (dot(x0, weight[:, 0], ((1,), (1,))) + dot(x1, weight[:, 1], ((1,), (1,)))).astype(
        bf16
    )
    return (
        grad_input,
        factor_a,
        factor_g.transpose(1, 0, 2),
        pre.transpose(1, 0, 2),
        worker,
    )


def solution(mesh):
    dp, tensor = mesh.devices.shape
    fine = Mesh(mesh.devices.reshape(dp // 4, 2, 2, tensor), ("z", "xl", "c", "t"))
    dp = ("z", "xl", "c")
    return jax.shard_map(
        local,
        mesh=fine,
        in_specs=(
            P(dp, "t"),
            P(dp, None, None),
            P("t", None, None),
            P(),
            P(),
            P(dp, None, "t"),
            P(dp, "t"),
            P(dp, None, None, "t"),
            P(dp, None, "t"),
        ),
        out_specs=(
            P(dp, "t"),
            P(dp, "t"),
            P(dp, None, "t"),
            P(None, None, "t"),
            P(dp, None, "t"),
        ),
        check_vma=False,
    )
```

time: 275 us -> 222 us (0.81)
  waiting for transfers between devices: 83.8 us -> 31.4 us
  local copies, waits for them, and re-layouts: 47.9 us -> 23.9 us
  blocking collectives: 43 us -> 65.2 us
  Pallas kernels: 0 us -> 15.1 us
  other arithmetic: 11.5 us -> 0.78 us
  starting transfers between devices: 52.3 us -> 62.4 us
  between operations: 24.3 us -> 14.3 us
  matrix products: 10.9 us -> 5.83 us
    all_gather x2 -> x1, waiting for transfers between devices: 46.4 us -> 1.57 us  [local(): whole_act = lax.all_gather(act, 't', axis=1, tiled=True)]
    all_to_all x2 -> x3, blocking collectives: 39.3 us -> 65.2 us  [exchange(): return lax.all_to_all(array, axis, 0, 0, tiled=True)]
    ppermute x4 -> x9, starting transfers between devices: 15.9 us -> 37.5 us  [swap(): return lax.ppermute(array, axis, [(0, 1), (1, 0)])]
    all_to_all x4 -> x3, waiting for transfers between devices: 33.3 us -> 15.6 us  [exchange(): return lax.all_to_all(array, axis, 0, 0, tiled=True)]
    pallas_call x0 -> x11, Pallas kernels: none -> 15.1 us  [call(): pl.pallas_call(body, out_shape=outs, in_specs=[pl.BlockSpec(memory_space=...]
    all_to_all x4 -> x3, starting transfers between devices: 36.3 us -> 24.8 us  [exchange(): return lax.all_to_all(array, axis, 0, 0, tiled=True)]
    ppermute x4 -> x9, waiting for transfers between devices: 4.1 us -> 14.2 us  [swap(): return lax.ppermute(array, axis, [(0, 1), (1, 0)])]
    transpose x8 -> x0, local copies, waits for them, and re-layouts: 9.12 us -> none  [the longest x1 4.3 us: local(): lax.all_gather(got_qg, 'c', axis=0).transpose(0, 2, 1, 3)]
  transfers between devices with their start and end apart: 10 -> 13, of which waited for: 8 -> 11; matrix products, arithmetic and copies ran while one was open for 9% -> 9% of each run, Pallas kernels for 0% -> 2%
where the time goes in v2:
time: 222 us; the launch traced here: 219 us
  blocking collectives  65.2 us (29%)
  starting transfers between devices  62.4 us (28%)
  waiting for transfers between devices  31.4 us (14%)
  local copies, waits for them, and re-layouts  23.9 us (11%)
  Pallas kernels  15.1 us (7%)
  between operations  14.3 us (6%)
  matrix products  5.83 us (3%)
    all_to_all x3, blocking collectives, exchange(): return lax.all_to_all(array, axis, 0, 0, tiled=True)  65.2 us
    ppermute x9, starting transfers between devices, swap(): return lax.ppermute(array, axis, [(0, 1), (1, 0)])  37.5 us
    all_to_all x3, starting transfers between devices, exchange(): return lax.all_to_all(array, axis, 0, 0, tiled=True)  24.8 us
    all_to_all x3, waiting for transfers between devices, exchange(): return lax.all_to_all(array, axis, 0, 0, tiled=True)  15.6 us
    pallas_call x11, Pallas kernels, call(): pl.pallas_call(body, out_shape=outs, in_specs=[pl.BlockSpec(memory_space=...  15.1 us
    ppermute x9, waiting for transfers between devices, swap(): return lax.ppermute(array, axis, [(0, 1), (1, 0)])  14.2 us
    unnamed x24, local copies, waits for them, and re-layouts  12.8 us
    dot_general x3, matrix products, dot(): lax.dot_general(left, right, (dims, ((), ())), preferred_element_type=f32)  5.83 us
  transfers between devices with their start and end apart: 13, of which 11 were waited for; matrix products, arithmetic and copies ran while one was open for 9% of the time, Pallas kernels for 2%

profile of v2, /device:TPU:1, one launch (start us, length us, event | category | flops | bytes accessed | tf_op | source)
XLA Modules:
  0.0 219.0 jit_solution(16626693720214498821)
XLA Ops:
  13.2 8.8 %collective-permute-start.2 = (bf16[1552,128]{1,0:T(8,128)(2,1)S(1)}, bf16[1552,128]{1,0:T(8,128)(2,1)S(1)}, u32[]{:S(2)}, u32[]{:S(2)}) collective-permute-start(bf16[1552,128]{1,0:T(8,128)(2,1)S(1)} %shard_map.130), channel_id=1, source_target_pairs={{0,8},{8,0},{1,9},{9,1},{2,10},{10,2},{3,11},{11,3},{4,12},{12,4},... | collective-permute-start | bytes 1191944 | tf_op jit(solution)/shard_map/ppermute | solution.py:23
  26.7 9.5 %all-to-all-start = ((bf16[16,112,128]{2,1,0:T(8,128)(2,1)}), bf16[16,112,128]{2,1,0:T(8,128)(2,1)S(1)}, u32[]{:S(2)}, u32[]{:S(2)}) async-start(bf16[16,112,128]{2,1,0:T(8,128)(2,1)} %shard_map.131), calls=%async_computation | async-start | bytes 917504 | tf_op jit(solution)/shard_map/all_to_all | solution.py:19
  36.3 5.6 %fusion.6 = (bf16[512,1,1024]{2,1,0:T(2,128)(2,1)S(1)}, bf16[512,1,1024]{2,1,0:T(2,128)(2,1)S(1)}) fusion(bf16[512,2,1024]{2,1,0:T(2,128)(2,1)} %param.10), kind=kLoop, calls=%fused_computation.19 | loop fusion | bytes 4194304 | tf_op jit(solution)/shard_map/slice | solution.py:310
  51.5 2.6 %collective-permute-start = (bf16[2,16,64,128]{3,2,1,0:T(8,128)(2,1)S(1)}, bf16[2,16,64,128]{3,2,1,0:T(8,128)(2,1)S(1)}, u32[]{:S(2)}, u32[]{:S(2)}) collective-permute-start(bf16[2,16,64,128]{3,2,1,0:T(8,128)(2,1)S(1)} %get-tuple-element.22), channel_id=1, source_target_pairs={{0,8},{8,0},{1,9},{9,1},{2,10},{10,2},{3,11},{11,3},{4,12},{12,4},... | collective-permute-start | bytes 1572872 | tf_op jit(solution)/shard_map/ppermute | solution.py:23
  56.2 3.1 %collective-permute-start.1 = (bf16[16,64,128]{2,1,0:T(8,128)(2,1)S(1)}, bf16[16,64,128]{2,1,0:T(8,128)(2,1)S(1)}, u32[]{:S(2)}, u32[]{:S(2)}) collective-permute-start(bf16[16,64,128]{2,1,0:T(8,128)(2,1)S(1)} %get-tuple-element.24), channel_id=1, source_target_pairs={{0,16},{16,0},{1,17},{17,1},{2,18},{18,2},{3,19},{19,3},{4,20},{20... | collective-permute-start | bytes 786440 | tf_op jit(solution)/shard_map/ppermute | solution.py:23
  59.9 2.2 collective-permute-start.3
  62.1 3.5 %collective-permute-done.1.got = bf16[16,64,128]{2,1,0:T(8,128)(2,1)S(1)} collective-permute-done((bf16[16,64,128]{2,1,0:T(8,128)(2,1)S(1)}, bf16[16,64,128]{2,1,0:T(8,128)(2,1)S(1)}, u32[]{:S(2)}, u32[]{:S(2)}) %collective-permute-start.1) | collective-permute-done | bytes 262176 | tf_op jit(solution)/shard_map/ppermute | solution.py:23
  67.5 11.7 %all-to-all-start.1 = ((bf16[16,128,128]{2,1,0:T(8,128)(2,1)}), bf16[16,128,128]{2,1,0:T(8,128)(2,1)S(1)}, u32[]{:S(2)}, u32[]{:S(2)}) async-start(bf16[16,128,128]{2,1,0:T(8,128)(2,1)} %get-tuple-element.27), calls=%async_computation.1 | async-start | bytes 1048576 | tf_op jit(solution)/shard_map/all_to_all | solution.py:19
  82.5 3.4 %collective-permute-start.4 = (bf16[16,2,16,128]{3,2,0,1:T(8,128)(2,1)S(1)}, bf16[16,2,16,128]{3,2,0,1:T(8,128)(2,1)S(1)}, u32[]{:S(2)}, u32[]{:S(2)}) collective-permute-start(bf16[16,2,16,128]{3,2,0,1:T(8,128)(2,1)S(1)} %fusion.2), channel_id=1, source_target_pairs={{0,8},{8,0},{1,9},{9,1},{2,10},{10,2},{3,11},{11,3},{4,12},{12,4},... | collective-permute-start | bytes 393224 | tf_op jit(solution)/shard_map/ppermute | solution.py:23
  87.0 2.2 %collective-permute-start.5 = (bf16[16,16,128]{2,1,0:T(8,128)(2,1)S(1)}, bf16[16,16,128]{2,1,0:T(8,128)(2,1)S(1)}, u32[]{:S(2)}, u32[]{:S(2)}) collective-permute-start(bf16[16,16,128]{2,1,0:T(8,128)(2,1)S(1)} %fusion.3), channel_id=1, source_target_pairs={{0,16},{16,0},{1,17},{17,1},{2,18},{18,2},{3,19},{19,3},{4,20},{20... | collective-permute-start | bytes 196616 | tf_op jit(solution)/shard_map/ppermute | solution.py:23
  89.2 3.1 %collective-permute-done.5.a_got = bf16[16,16,128]{2,1,0:T(8,128)(2,1)S(1)} collective-permute-done((bf16[16,16,128]{2,1,0:T(8,128)(2,1)S(1)}, bf16[16,16,128]{2,1,0:T(8,128)(2,1)S(1)}, u32[]{:S(2)}, u32[]{:S(2)}) %collective-permute-start.5) | collective-permute-done | bytes 65568 | tf_op jit(solution)/shard_map/ppermute | solution.py:23
  92.3 9.8 %all-to-all-done.1.got = bf16[16,128,128]{2,1,0:T(8,128)(2,1)S(1)} async-done(((bf16[16,128,128]{2,1,0:T(8,128)(2,1)}), bf16[16,128,128]{2,1,0:T(8,128)(2,1)S(1)}, u32[]{:S(2)}, u32[]{:S(2)}) %all-to-all-start.1) | async-done | bytes 524320 | tf_op jit(solution)/shard_map/all_to_all | solution.py:19
  102.6 24.3 %all_to_all.30.got = bf16[16,48,128]{2,1,0:T(8,128)(2,1)S(1)} all-to-all(bf16[16,48,128]{2,1,0:T(8,128)(2,1)S(1)} %get-tuple-element.28), channel_id=1, replica_groups=mesh['z'=16,'xl'=2,'c'=2,'t'=8] {'z'}, dimensions={0} | all-to-all | bytes 393216 | tf_op jit(solution)/shard_map/all_to_all | solution.py:19
  128.3 20.0 %all_to_all.31.own.gathered = bf16[8,592,128]{2,1,0:T(8,128)(2,1)S(1)} all-to-all(bf16[8,592,128]{2,1,0:T(8,128)(2,1)S(1)} %get-tuple-element.33), channel_id=1, replica_groups=mesh['z'=16,'xl'=2,'c'=2,'t'=8] {'t'}, dimensions={0} | all-to-all | bytes 2424832 | tf_op jit(solution)/shard_map/all_to_all | solution.py:19
  148.3 8.3 %collective-permute-start.6 = (bf16[8,592,128]{2,1,0:T(8,128)(2,1)S(1)}, bf16[8,592,128]{2,1,0:T(8,128)(2,1)S(1)}, u32[]{:S(2)}, u32[]{:S(2)}) collective-permute-start(bf16[8,592,128]{2,1,0:T(8,128)(2,1)S(1)} %all_to_all.31.own.gathered), channel_id=1, source_target_pairs={{0,8},{8,0},{1,9},{9,1},{2,10},{10,2},{3,11},{11,3},{4,12},{12,4},... | collective-permute-start | bytes 3637256 | tf_op jit(solution)/shard_map/ppermute | solution.py:23
  156.6 2.5 %collective-permute-done.6.other = bf16[8,592,128]{2,1,0:T(8,128)(2,1)S(1)} collective-permute-done((bf16[8,592,128]{2,1,0:T(8,128)(2,1)S(1)}, bf16[8,592,128]{2,1,0:T(8,128)(2,1)S(1)}, u32[]{:S(2)}, u32[]{:S(2)}) %collective-permute-start.6) | collective-permute-done | bytes 1212448 | tf_op jit(solution)/shard_map/ppermute | solution.py:23
  160.3 20.8 %all_to_all.32.own = bf16[8,576,128]{2,1,0:T(8,128)(2,1)S(1)} all-to-all(bf16[8,576,128]{2,1,0:T(8,128)(2,1)S(1)} %shard_map.136), channel_id=1, replica_groups=mesh['z'=16,'xl'=2,'c'=2,'t'=8] {'t'}, dimensions={0} | all-to-all | bytes 2359296 | tf_op jit(solution)/shard_map/all_to_all | solution.py:19
  181.1 3.3 %collective-permute-start.7 = (bf16[8,576,128]{2,1,0:T(8,128)(2,1)S(1)}, bf16[8,576,128]{2,1,0:T(8,128)(2,1)S(1)}, u32[]{:S(2)}, u32[]{:S(2)}) collective-permute-start(bf16[8,576,128]{2,1,0:T(8,128)(2,1)S(1)} %all_to_all.32.own), channel_id=1, source_target_pairs={{0,8},{8,0},{1,9},{9,1},{2,10},{10,2},{3,11},{11,3},{4,12},{12,4},... | collective-permute-start | bytes 3538952 | tf_op jit(solution)/shard_map/ppermute | solution.py:23
  186.8 2.4 %shard_map.137 = bf16[2,8,64,128]{3,2,1,0:T(8,128)(2,1)} custom-call(s32[8]{0:T(128)S(1)} %concatenate.6.info, bf16[8,576,128]{2,1,0:T(8,128)(2,1)S(1)} %all_to_all.32.own, bf16[8,576,128]{2,1,0:T(8,128)(2,1)S(1)} %collective-permute-done.7.other, bf16[8,592,128]{2,1,0:T(8,128)(2,1)S(1)} %all_to_all.31.own.gathered), custom_call_target="tpu_custom_call" | custom-call | flops 268435456 | bytes 3833856 | tf_op jit(solution)/shard_map/pallas_call | solution.py:30
  189.3 3.5 %all-to-all-start.5 = ((bf16[16,64,128]{2,1,0:T(8,128)(2,1)}), bf16[16,64,128]{2,1,0:T(8,128)(2,1)S(1)}, u32[]{:S(2)}, u32[]{:S(2)}) async-start(bf16[16,64,128]{2,1,0:T(8,128)(2,1)} %bitcast.19), calls=%async_computation.5 | async-start | bytes 524288 | tf_op jit(solution)/shard_map/all_to_all | solution.py:19
  194.6 5.8 %all-to-all-done.5 = bf16[16,64,128]{2,1,0:T(8,128)(2,1)S(1)} async-done(((bf16[16,64,128]{2,1,0:T(8,128)(2,1)}), bf16[16,64,128]{2,1,0:T(8,128)(2,1)S(1)}, u32[]{:S(2)}, u32[]{:S(2)}) %all-to-all-start.5) | async-done | bytes 262176 | tf_op jit(solution)/shard_map/all_to_all | solution.py:19
  200.4 3.7 %collective-permute-start.8 = (bf16[2,8,64,128]{3,2,1,0:T(8,128)(2,1)S(1)}, bf16[2,8,64,128]{3,2,1,0:T(8,128)(2,1)S(1)}, u32[]{:S(2)}, u32[]{:S(2)}) collective-permute-start(bf16[2,8,64,128]{3,2,1,0:T(8,128)(2,1)S(1)} %bitcast.46), channel_id=1, source_target_pairs={{0,8},{8,0},{1,9},{9,1},{2,10},{10,2},{3,11},{11,3},{4,12},{12,4},... | collective-permute-start | bytes 786440 | tf_op jit(solution)/shard_map/ppermute | solution.py:23
  204.2 2.3 %fusion = bf16[512,128]{1,0:T(8,128)(2,1)} fusion(f32[512,128]{1,0:T(8,128)S(1)} %fusion.1, bf16[128,1,1024]{2,1,0:T(2,128)(2,1)S(1)} %get-tuple-element.49, bf16[512,1,1024]{2,0,1:T(8,128)(2,1)} %copy.28), kind=kOutput, calls=%fused_computation.2 | convolution fusion | flops 134348800 | bytes 1703936 | tf_op jit(solution)/shard_map/dot_general | solution.py:47
  207.1 3.7 %shard_map.138 = (bf16[2,1024,128]{2,1,0:T(8,128)(2,1)S(1)}, bf16[1,1024,128]{2,1,0:T(8,128)(2,1)}) custom-call(s32[8]{0:T(128)S(1)} %concatenate.6.info, bf16[8,592,128]{2,1,0:T(8,128)(2,1)S(1)} %all_to_all.31.own.gathered, bf16[8,592,128]{2,1,0:T(8,128)(2,1)S(1)} %collective-permute-done.6.other, bf16[2,8,64,128]{3,2,1,0:T(8,128)(2,1)S(1)} %bitcast.47, ...), custom_call_target="tpu_custom_call" | custom-call | flops 536870912 | bytes 3735552 | tf_op jit(solution)/shard_map/pallas_call | solution.py:30
  (56 shorter events, 38.4 us)
Async XLA Ops:
  7.2 73.6 %all-gather.2.cloned.1.call-start = ((), (), s32[]{:S(2)}) async-start(), calls=%async_computation.6 | async-start | bytes 1179648 | tf_op jit(solution)/shard_map/all_gather | solution.py:308
  10.7 1.0 copy-start
  11.7 0.9 copy-start.3
  13.2 10.1 %collective-permute-start.2 = (bf16[1552,128]{1,0:T(8,128)(2,1)S(1)}, bf16[1552,128]{1,0:T(8,128)(2,1)S(1)}, u32[]{:S(2)}, u32[]{:S(2)}) collective-permute-start(bf16[1552,128]{1,0:T(8,128)(2,1)S(1)} %shard_map.130), channel_id=1, source_target_pairs={{0,8},{8,0},{1,9},{9,1},{2,10},{10,2},{3,11},{11,3},{4,12},{12,4},... | collective-permute-start | bytes 1191944 | tf_op jit(solution)/shard_map/ppermute | solution.py:23
  23.4 1.0 copy-start.1
  24.4 0.9 copy-start.4
  26.7 32.6 %all-to-all-start = ((bf16[16,112,128]{2,1,0:T(8,128)(2,1)}), bf16[16,112,128]{2,1,0:T(8,128)(2,1)S(1)}, u32[]{:S(2)}, u32[]{:S(2)}) async-start(bf16[16,112,128]{2,1,0:T(8,128)(2,1)} %shard_map.131), calls=%async_computation | async-start | bytes 917504 | tf_op jit(solution)/shard_map/all_to_all | solution.py:19
  41.9 1.3 copy-start.7
  41.9 4.1 %copy-start.5 = (bf16[512,1,1024]{2,1,0:T(2,128)(2,1)}, bf16[512,1,1024]{2,1,0:T(2,128)(2,1)S(1)}, u32[]{:S(2)}) copy-start(bf16[512,1,1024]{2,1,0:T(2,128)(2,1)S(1)} %get-tuple-element.47) | copy-start | bytes 3145732
  46.0 3.1 %copy-start.6 = (bf16[512,1,1024]{2,1,0:T(2,128)(2,1)S(1)}, bf16[512,1,1024]{2,1,0:T(2,128)(2,1)}, u32[]{:S(2)}) copy-start(bf16[512,1,1024]{2,1,0:T(2,128)(2,1)} %copy-done.5) | copy-start | bytes 3145732
  49.1 0.9 copy-start.2
  51.5 4.1 %collective-permute-start = (bf16[2,16,64,128]{3,2,1,0:T(8,128)(2,1)S(1)}, bf16[2,16,64,128]{3,2,1,0:T(8,128)(2,1)S(1)}, u32[]{:S(2)}, u32[]{:S(2)}) collective-permute-start(bf16[2,16,64,128]{3,2,1,0:T(8,128)(2,1)S(1)} %get-tuple-element.22), channel_id=1, source_target_pairs={{0,8},{8,0},{1,9},{9,1},{2,10},{10,2},{3,11},{11,3},{4,12},{12,4},... | collective-permute-start | bytes 1572872 | tf_op jit(solution)/shard_map/ppermute | solution.py:23
  56.2 9.4 %collective-permute-start.1 = (bf16[16,64,128]{2,1,0:T(8,128)(2,1)S(1)}, bf16[16,64,128]{2,1,0:T(8,128)(2,1)S(1)}, u32[]{:S(2)}, u32[]{:S(2)}) collective-permute-start(bf16[16,64,128]{2,1,0:T(8,128)(2,1)S(1)} %get-tuple-element.24), channel_id=1, source_target_pairs={{0,16},{16,0},{1,17},{17,1},{2,18},{18,2},{3,19},{19,3},{4,20},{20... | collective-permute-start | bytes 786440 | tf_op jit(solution)/shard_map/ppermute | solution.py:23
  59.9 6.1 %collective-permute-start.3 = (bf16[80,128]{1,0:T(8,128)(2,1)S(1)}, bf16[80,128]{1,0:T(8,128)(2,1)S(1)}, u32[]{:S(2)}, u32[]{:S(2)}) collective-permute-start(bf16[80,128]{1,0:T(8,128)(2,1)S(1)} %get-tuple-element.26), channel_id=1, source_target_pairs={{0,16},{16,0},{1,17},{17,1},{2,18},{18,2},{3,19},{19,3},{4,20},{20... | collective-permute-start | bytes 61448 | tf_op jit(solution)/shard_map/ppermute | solution.py:23
  67.5 34.6 %all-to-all-start.1 = ((bf16[16,128,128]{2,1,0:T(8,128)(2,1)}), bf16[16,128,128]{2,1,0:T(8,128)(2,1)S(1)}, u32[]{:S(2)}, u32[]{:S(2)}) async-start(bf16[16,128,128]{2,1,0:T(8,128)(2,1)} %get-tuple-element.27), calls=%async_computation.1 | async-start | bytes 1048576 | tf_op jit(solution)/shard_map/all_to_all | solution.py:19
  82.5 4.4 %collective-permute-start.4 = (bf16[16,2,16,128]{3,2,0,1:T(8,128)(2,1)S(1)}, bf16[16,2,16,128]{3,2,0,1:T(8,128)(2,1)S(1)}, u32[]{:S(2)}, u32[]{:S(2)}) collective-permute-start(bf16[16,2,16,128]{3,2,0,1:T(8,128)(2,1)S(1)} %fusion.2), channel_id=1, source_target_pairs={{0,8},{8,0},{1,9},{9,1},{2,10},{10,2},{3,11},{11,3},{4,12},{12,4},... | collective-permute-start | bytes 393224 | tf_op jit(solution)/shard_map/ppermute | solution.py:23
  87.0 5.3 %collective-permute-start.5 = (bf16[16,16,128]{2,1,0:T(8,128)(2,1)S(1)}, bf16[16,16,128]{2,1,0:T(8,128)(2,1)S(1)}, u32[]{:S(2)}, u32[]{:S(2)}) collective-permute-start(bf16[16,16,128]{2,1,0:T(8,128)(2,1)S(1)} %fusion.3), channel_id=1, source_target_pairs={{0,16},{16,0},{1,17},{17,1},{2,18},{18,2},{3,19},{19,3},{4,20},{20... | collective-permute-start | bytes 196616 | tf_op jit(solution)/shard_map/ppermute | solution.py:23
  148.3 10.8 %collective-permute-start.6 = (bf16[8,592,128]{2,1,0:T(8,128)(2,1)S(1)}, bf16[8,592,128]{2,1,0:T(8,128)(2,1)S(1)}, u32[]{:S(2)}, u32[]{:S(2)}) collective-permute-start(bf16[8,592,128]{2,1,0:T(8,128)(2,1)S(1)} %all_to_all.31.own.gathered), channel_id=1, source_target_pairs={{0,8},{8,0},{1,9},{9,1},{2,10},{10,2},{3,11},{11,3},{4,12},{12,4},... | collective-permute-start | bytes 3637256 | tf_op jit(solution)/shard_map/ppermute | solution.py:23
  160.3 24.1 %copy-start.8 = (bf16[128,2,1024]{2,1,0:T(2,128)(2,1)S(1)}, bf16[128,2,1024]{2,1,0:T(2,128)(2,1)}, u32[]{:S(2)}) copy-start(bf16[128,2,1024]{2,1,0:T(2,128)(2,1)} %param.11) | copy-start | bytes 1572868
  181.1 5.7 %collective-permute-start.7 = (bf16[8,576,128]{2,1,0:T(8,128)(2,1)S(1)}, bf16[8,576,128]{2,1,0:T(8,128)(2,1)S(1)}, u32[]{:S(2)}, u32[]{:S(2)}) collective-permute-start(bf16[8,576,128]{2,1,0:T(8,128)(2,1)S(1)} %all_to_all.32.own), channel_id=1, source_target_pairs={{0,8},{8,0},{1,9},{9,1},{2,10},{10,2},{3,11},{11,3},{4,12},{12,4},... | collective-permute-start | bytes 3538952 | tf_op jit(solution)/shard_map/ppermute | solution.py:23
  189.3 11.2 %all-to-all-start.5 = ((bf16[16,64,128]{2,1,0:T(8,128)(2,1)}), bf16[16,64,128]{2,1,0:T(8,128)(2,1)S(1)}, u32[]{:S(2)}, u32[]{:S(2)}) async-start(bf16[16,64,128]{2,1,0:T(8,128)(2,1)} %bitcast.19), calls=%async_computation.5 | async-start | bytes 524288 | tf_op jit(solution)/shard_map/all_to_all | solution.py:19
  200.4 6.7 %collective-permute-start.8 = (bf16[2,8,64,128]{3,2,1,0:T(8,128)(2,1)S(1)}, bf16[2,8,64,128]{3,2,1,0:T(8,128)(2,1)S(1)}, u32[]{:S(2)}, u32[]{:S(2)}) collective-permute-start(bf16[2,8,64,128]{3,2,1,0:T(8,128)(2,1)S(1)} %bitcast.46), channel_id=1, source_target_pairs={{0,8},{8,0},{1,9},{9,1},{2,10},{10,2},{3,11},{11,3},{4,12},{12,4},... | collective-permute-start | bytes 786440 | tf_op jit(solution)/shard_map/ppermute | solution.py:23
Sparse Core Ops, SparseCore 0:
  22.2 58.5 all-gather.1

commit v3 on v2

v3 whole, which is shorter than its diff:
```python
import functools

import jax
import jax.numpy as jnp
from jax import lax
from jax.experimental import pallas as pl
from jax.experimental.pallas import tpu as pltpu
from jax.sharding import Mesh, PartitionSpec as P

damping = 0.001
f32 = jnp.float32
bf16 = jnp.bfloat16
VALS = 16


def exchange(array, axis):
    return lax.all_to_all(array, axis, 0, 0, tiled=True)


def swap(array, axis):
    return lax.ppermute(array, axis, [(0, 1), (1, 0)])


def across(array, axis, step):
    pairs = [(i, i ^ step) for i in range(lax.axis_size(axis))]
    return lax.ppermute(array, axis, pairs)


def call(body, outs, scalars, args, places=None, scratch=(), flops=0):
    bytes_all = sum(a.size * a.dtype.itemsize for a in args) + sum(
        o.size * o.dtype.itemsize for o in outs
    )
    places = places or [pltpu.VMEM] * len(args)
    return pl.pallas_call(
        body,
        out_shape=outs,
        in_specs=[pl.BlockSpec(memory_space=pltpu.SMEM)] * len(scalars)
        + [pl.BlockSpec(memory_space=place) for place in places],
        out_specs=[pl.BlockSpec(memory_space=pltpu.VMEM)] * len(outs),
        scratch_shapes=list(scratch),
        compiler_params=pltpu.CompilerParams(vmem_limit_bytes=40 * 1024 * 1024),
        cost_estimate=pl.CostEstimate(flops=flops, bytes_accessed=bytes_all, transcendentals=0),
    )(*scalars, *args)


def out(shape, dtype=bf16):
    return jax.ShapeDtypeStruct(shape, dtype)


def dot(left, right, dims=((1,), (0,))):
    return lax.dot_general(left, right, (dims, ((), ())), preferred_element_type=f32)


def value_rows(flags, own, other):
    place = lax.broadcasted_iota(jnp.int32, own.shape, 0)
    take = jnp.zeros(own.shape, jnp.int32)
    for row, flag in enumerate(flags):
        take = jnp.where(place == row, flag.astype(jnp.int32), take)
    return jnp.where(take > 0, own.astype(f32), other.astype(f32)).astype(bf16)


def choose(flag, ref, place, own, other):
    @pl.when(flag)
    def _():
        ref[place] = own()

    @pl.when(jnp.logical_not(flag))
    def _():
        ref[place] = other()


def pack_bases(ba, bg, va, vg, sent, keep, sem):
    half = ba.shape[1] // 2
    core = lax.axis_index("c")
    place = lax.broadcasted_iota(jnp.int32, (VALS, ba.shape[2]), 0)
    vals = jnp.where(place == 0, va[...].astype(f32), 0.0)
    for j in range(2):
        row = vg[0].astype(f32)[j : j + 1]
        vals = jnp.where(place == 1 + j, row, vals)
    copies = []
    for side, (ref, who) in enumerate(((sent, 1 - core), (keep, core))):
        rows = pl.ds(pl.multiple_of(who * half, half), half)
        for i in range(3):
            source = ba.at[0, rows] if i == 0 else bg.at[0, i - 1, rows]
            copies.append(
                pltpu.make_async_copy(source, ref.at[i * half : (i + 1) * half], sem.at[side, i])
            )
            copies[-1].start()
    sent[3 * half :] = vals.astype(bf16)
    keep[3 * half :] = vals.astype(bf16)
    for copy in copies:
        copy.wait()


def select_core(owners, own, got, sent, keep):
    half = (own.shape[0] - VALS) // 3
    core, xl = lax.axis_index("c"), lax.axis_index("xl")
    flags = [owners[i] % 2 == core for i in range(3)]

    def fill(ref, slot, i):
        start = pl.multiple_of(i * half, half)
        choose(
            owners[i] % 2 == core,
            ref,
            slice(slot * half, (slot + 1) * half),
            lambda: own[pl.ds(start, half)],
            lambda: got[pl.ds(start, half)],
        )

    vals = value_rows(flags, own[3 * half :], got[3 * half :])
    for ref, block in ((sent, 2 - xl), (keep, 1 + xl)):
        fill(ref, 0, 0)
        fill(ref, 1, block)
        ref[2 * half :] = vals


def select_x(owners, own, got, sent):
    nz, _, slab = sent.shape
    half = (own.shape[0] - VALS) // 2
    per = half // nz
    xl = lax.axis_index("xl")
    here = [(owners[i] // 2) % 2 == xl for i in range(3)]
    flags = (here[0], (owners[1 + xl] // 2) % 2 == xl)
    for i, flag in enumerate(flags):
        rows = slice(i * half, (i + 1) * half)
        choose(
            flag,
            sent,
            (slice(None), slice(i * per, (i + 1) * per)),
            lambda: own[rows].reshape(nz, per, slab),
            lambda: got[rows].reshape(nz, per, slab),
        )
    vals = value_rows(here, own[2 * half :], got[2 * half :])
    for k in range(nz):
        sent[k, 2 * per :] = vals


def terms(cot, act, sent, keep, packed, flat):
    _, _, nz, height, slab = packed.shape
    tok, blocks, full = cot.shape
    nt = full // slab
    per = full // 2 // nz
    group = (height - per) // 2
    scale = 1.0 / (tok * nz * 4)
    flat[...] = cot[...].reshape(tok, blocks * full)
    t = lax.axis_index("t")
    for j in range(2):
        own = flat[:, pl.ds(pl.multiple_of(j * full + t * slab, slab), slab)]
        right = jnp.concatenate([act[...], own], 1)
        both = dot(flat[:, j * full : (j + 1) * full], right, ((0,), (0,))) * scale
        grad = both[:, :slab].reshape(nt, 2, slab // 2, slab)
        cov = both[:, slab:].reshape(nz, 2, 2, group, slab)
        for c in range(2):
            packed[c, j, :, 0:per] = grad[:, c].reshape(nz, per, slab)
            for xl in range(2):
                packed[c, xl, :, per + j * group : per + (j + 1) * group] = cov[:, xl, c]
    core = lax.axis_index("c")
    sent[...] = packed[1 - core].astype(bf16)
    keep[...] = packed[core]


def add_core(keep, got, sent, rest):
    xl = lax.axis_index("xl")
    sent[...] = (keep[1 - xl] + got[1 - xl].astype(f32)).astype(bf16)
    rest[...] = keep[xl] + got[xl].astype(f32)


def pack_z(owners, keep, got, bases, sent, vals, cov):
    nz, height, slab = keep.shape
    per = (bases.shape[1] - VALS) // 2
    xl = lax.axis_index("xl")
    source = [owners[i] // 4 for i in range(3)]
    sent[:, 0:per] = (keep[:, 0:per] + got[:, 0:per].astype(f32)).astype(bf16)
    cov[...] = keep[:, per:] + got[:, per:].astype(f32)
    for i, src in enumerate((source[0], owners[1 + xl] // 4)):
        part = bases[src, i * per : (i + 1) * per]
        for k in range(nz):
            sent[k, (1 + i) * per : (2 + i) * per] = part
    chosen = bases[source[0], 2 * per :].astype(f32)
    place = lax.broadcasted_iota(jnp.int32, chosen.shape, 0)
    for i in (1, 2):
        chosen = jnp.where(place == i, bases[source[i], 2 * per :].astype(f32), chosen)
    vals[...] = chosen.astype(bf16)


def reduce_z(got, sent, bases):
    nz, height, slab = got.shape
    per = height // 3
    total = got[0, 0:per].astype(f32)
    for k in range(1, nz):
        total = total + got[k, 0:per].astype(f32)
    total = total.astype(bf16)
    for k in range(nz):
        sent[k] = total
    half = nz * per
    bases[0:half] = got[:, per : 2 * per].reshape(half, slab)
    bases[half:] = got[:, 2 * per :].reshape(half, slab)


def stack_bases(*refs):
    pieces, whole = refs[:-1], refs[-1]
    t = lax.axis_index("t")
    for k, piece in enumerate(pieces):
        whole[t ^ k] = piece[...]


def pack_t(got, vals, sent):
    nz, per, slab = got.shape
    nt, height, _ = sent.shape[1:]
    piece = height - VALS
    grad = got[...].reshape(nz * per, slab).reshape(nt, piece, slab)
    for c in range(2):
        sent[c, :, 0:piece] = grad
        for k in range(nt):
            sent[c, k, piece:] = vals[...]


def rotate(got, own, other, sent, grad):
    nt, height, slab = own.shape
    half = height // 2
    piece = half // nt
    core = lax.axis_index("c")
    for c in range(2):
        for k in range(nt):
            grad[c * piece : (c + 1) * piece, k * slab : (k + 1) * slab] = got[c, k, 0:piece]
    near = grad[:, pl.ds(pl.multiple_of(core * half, half), half)]
    far = grad[:, pl.ds(pl.multiple_of((1 - core) * half, half), half)]
    for i in range(nt // 2):
        k = core * (nt // 2) + i
        turned = dot(near, own[k, 0:half]) + dot(far, other[k, 0:half])
        turned = turned.T.astype(bf16)
        sent[2 * i] = turned[0:piece]
        sent[2 * i + 1] = turned[piece:]


def scale_rows(rows, own, other, got, sent, rot, scaled, column):
    nt, piece, slab = rows.shape
    half = own.shape[1] // 2
    core, xl, t = lax.axis_index("c"), lax.axis_index("xl"), lax.axis_index("t")
    row = got[0, core * (nt // 2) + t // 2, piece:].astype(f32)[0:1]
    column[...] = jnp.broadcast_to(row, (slab, slab)).T
    la = column[pl.ds(pl.multiple_of((t % 2) * piece, piece), piece)]
    for k in range(nt):
        rot[:, k * slab : (k + 1) * slab] = rows[k]
    near = rot[:, pl.ds(pl.multiple_of(core * half, half), half)]
    far = rot[:, pl.ds(pl.multiple_of((1 - core) * half, half), half)]
    for k in range(nt):
        spectral = dot(near, own[k, half:]) + dot(far, other[k, half:])
        values = got[0, k, piece:].astype(f32)
        lg = jnp.where(xl == 0, values[1:2], values[2:3])
        scaled[k] = (spectral / (la * lg + damping)).astype(bf16)
    for side, ref in ((core, own), (1 - core, other)):
        mixed = dot(scaled[0], ref[0, half:], ((1,), (1,)))
        for k in range(1, nt):
            mixed = mixed + dot(scaled[k], ref[k, half:], ((1,), (1,)))
        mixed = mixed.astype(bf16)
        for i in range(nt // 2):
            for copy in range(2):
                sent[copy, side * (nt // 2) + i] = mixed[:, i * slab : (i + 1) * slab]


def finish(groups, own, other, own_mixed, other_mixed, pre, worker):
    blocks, nt, piece, slab = own_mixed.shape
    half = own.shape[1] // 2
    core = lax.axis_index("c")
    replica = (lax.axis_index("z") * 2 + lax.axis_index("xl")) * 2 + core
    group = groups[replica]
    for side, ref in ((core, own), (1 - core, other)):
        total = jnp.zeros((half, blocks * slab), f32)
        for part, mixed in ((core, own_mixed), (1 - core, other_mixed)):
            for i in range(nt // 2):
                right = jnp.concatenate(
                    [mixed[j, 2 * i : 2 * i + 2].reshape(2 * piece, slab) for j in range(blocks)], 1
                )
                total = total + dot(ref[part * (nt // 2) + i, 0:half], right)
        total = total.astype(bf16)
        place = pl.ds(pl.multiple_of(side * half, half), half)
        pre[place] = total.reshape(half, blocks, slab)
        choose(
            group == 0,
            worker,
            (0, place),
            lambda: total[:, :slab],
            lambda: total[:, slab:],
        )


def input_grad(cot, weight, grad):
    tok, blocks, full = cot.shape
    left = cot[...].reshape(tok, blocks * full)
    right = weight[...].reshape(weight.shape[0], blocks * full)
    grad[...] = dot(left, right, ((1,), (1,))).astype(bf16)


def input_factor(whole, act, sent, keep, packed):
    nz, _, _, group, slab = packed.shape
    scale = 1.0 / (act.shape[0] * nz * 4)
    packed[...] = (dot(whole[...], act[...], ((0,), (0,))) * scale).reshape(packed.shape)
    core = lax.axis_index("c")
    sent[...] = packed[:, :, 1 - core].astype(bf16)
    keep[...] = packed[:, :, core]


def input_factor_core(keep, got, sent, rest):
    xl = lax.axis_index("xl")
    sent[...] = (keep[:, 1 - xl] + got[:, 1 - xl].astype(f32)).astype(bf16)
    rest[...] = keep[:, xl] + got[:, xl].astype(f32)


def pack_factors(cov, keep, got, sent):
    group = keep.shape[1]
    sent[:, 0 : 2 * group] = cov[...].astype(bf16)
    sent[:, 2 * group :] = (keep[...] + got[...].astype(f32)).astype(bf16)


def local(act, cot, weight, owners, worker_group, basis_a, values_a, basis_g, values_g):
    tok, slab = act.shape
    blocks, full = cot.shape[1:]
    nz, nt = lax.axis_size("z"), lax.axis_size("t")
    group = full // (nz * 4)
    half, piece = full // 2, slab // 2
    per = half // nz
    height = per + blocks * group

    shape = (3 * half + VALS, slab)
    sent, keep = call(
        pack_bases,
        [out(shape), out(shape)],
        [],
        [basis_a, basis_g, values_a, values_g],
        [pl.ANY, pl.ANY, pltpu.VMEM, pltpu.VMEM],
        scratch=[pltpu.SemaphoreType.DMA((2, 3))],
    )
    got = swap(sent, "c")
    shape = (2 * half + VALS, slab)
    sent, keep = call(select_core, [out(shape), out(shape)], [owners], [keep, got])
    got = swap(sent, "xl")
    (sent,) = call(select_x, [out((nz, 2 * per + VALS, slab))], [owners], [keep, got])
    got_bases = exchange(sent, "z")

    whole_act = lax.all_gather(act, "t", axis=1, tiled=True)

    block = (2, nz, height, slab)
    sent, keep = call(
        terms,
        [out(block), out(block, f32)],
        [],
        [cot, act],
        scratch=[pltpu.VMEM((2,) + block, f32), pltpu.VMEM((tok, blocks * full), bf16)],
        flops=8 * tok * full * slab,
    )
    got = swap(sent, "c")
    sent, keep = call(add_core, [out(block[1:]), out(block[1:], f32)], [], [keep, got])
    got = swap(sent, "xl")

    sent, vals, cov = call(
        pack_z,
        [out((nz, 3 * per, slab)), out((VALS, slab)), out((nz, 2 * group, slab), f32)],
        [owners],
        [keep, got, got_bases],
    )
    got = exchange(sent, "z")

    block = (nz, 2, group, slab)
    sent, keep = call(
        input_factor,
        [out(block), out(block, f32)],
        [],
        [whole_act, act],
        scratch=[pltpu.VMEM((nz, 2, 2, group, slab), f32)],
        flops=2 * tok * full * slab,
    )
    a_got = swap(sent, "c")
    block = (nz, group, slab)
    sent, keep = call(input_factor_core, [out(block), out(block, f32)], [], [keep, a_got])
    a_got = swap(sent, "xl")
    (sent,) = call(pack_factors, [out((nz, 3 * group, slab))], [], [cov, keep, a_got])
    factors = lax.psum_scatter(sent, "z", scatter_dimension=0, tiled=False).astype(f32)
    factor_g = factors[: 2 * group].reshape(blocks, group, slab).transpose(1, 0, 2)
    factor_a = factors[2 * group :]

    sent, bases = call(
        reduce_z, [out((nz, per, slab)), out((2 * half, slab))], [], [got]
    )
    got = exchange(sent, "z")
    pieces = [bases] + [across(bases, "t", k) for k in range(1, nt)]
    (own,) = call(stack_bases, [out((nt, 2 * half, slab))], [], pieces)
    other = swap(own, "c")

    (sent,) = call(pack_t, [out((2, nt, piece + VALS, slab))], [], [got, vals])
    columns = exchange(sent.reshape(2 * nt, piece + VALS, slab), ("c", "t"))
    columns = columns.reshape(2, nt, piece + VALS, slab)
    (sent,) = call(
        rotate,
        [out((nt, piece, slab))],
        [],
        [columns, own, other],
        scratch=[pltpu.VMEM((slab, full), bf16)],
        flops=2 * slab * full * half,
    )
    rows = exchange(sent, "t")
    (sent,) = call(
        scale_rows,
        [out((blocks, nt, piece, slab))],
        [],
        [rows, own, other, columns],
        scratch=[
            pltpu.VMEM((piece, full), bf16),
            pltpu.VMEM((nt, piece, slab), bf16),
            pltpu.VMEM((slab, slab), f32),
        ],
        flops=4 * piece * full * full,
    )
    own_mixed = exchange(sent.reshape(blocks * nt, piece, slab), ("xl", "t"))
    own_mixed = own_mixed.reshape(blocks, nt, piece, slab)
    other_mixed = swap(own_mixed, "c")
    pre, worker = call(
        finish,
        [out((full, blocks, slab)), out((1, full, slab))],
        [worker_group],
        [own, other, own_mixed, other_mixed],
        flops=4 * full * full * slab,
    )

    (grad_input,) = call(
        input_grad, [out((tok, slab))], [], [cot, weight], flops=4 * tok * full * slab
    )
    return grad_input, factor_a, factor_g, pre, worker


def solution(mesh):
    dp, tensor = mesh.devices.shape
    fine = Mesh(mesh.devices.reshape(dp // 4, 2, 2, tensor), ("z", "xl", "c", "t"))
    dp = ("z", "xl", "c")
    return jax.shard_map(
        local,
        mesh=fine,
        in_specs=(
            P(dp, "t"),
            P(dp, None, None),
            P("t", None, None),
            P(),
            P(),
            P(dp, None, "t"),
            P(dp, "t"),
            P(dp, None, None, "t"),
            P(dp, None, "t"),
        ),
        out_specs=(
            P(dp, "t"),
            P(dp, "t"),
            P(dp, None, "t"),
            P(None, None, "t"),
            P(dp, None, "t"),
        ),
        check_vma=False,
    )
```

time: 222 us -> 299 us (1.35)
  the two profiles are of different devices: /device:TPU:1 before, /device:TPU:4 now
where the time goes in v3:
time: 299 us; the launch traced here: 298 us
  waiting for transfers between devices  114 us (38%)
  starting transfers between devices  73.4 us (25%)
  blocking collectives  68.3 us (23%)
  Pallas kernels  20 us (7%)
  between operations  14.3 us (5%)
  local copies, waits for them, and re-layouts  7.28 us (2%)
    all_to_all x3, blocking collectives, exchange(): return lax.all_to_all(array, axis, 0, 0, tiled=True)  68.3 us
    reduce_scatter x1, waiting for transfers between devices, local(): lax.psum_scatter(sent, 'z', scatter_dimension=0, tiled=False).astype(f32)  50.7 us
    all_gather x1, waiting for transfers between devices, local(): whole_act = lax.all_gather(act, 't', axis=1, tiled=True)  27.8 us
    ppermute x7, starting transfers between devices, across(): return lax.ppermute(array, axis, pairs)  27.7 us
    all_to_all x3, starting transfers between devices, exchange(): return lax.all_to_all(array, axis, 0, 0, tiled=True)  26 us
    pallas_call x16, Pallas kernels, call(): pl.pallas_call(body, out_shape=outs, in_specs=[pl.BlockSpec(memory_space=...  20 us
    ppermute x8, starting transfers between devices, swap(): return lax.ppermute(array, axis, [(0, 1), (1, 0)])  19.8 us
    ppermute x8, waiting for transfers between devices, swap(): return lax.ppermute(array, axis, [(0, 1), (1, 0)])  19.2 us
  transfers between devices with their start and end apart: 20, of which 11 were waited for; matrix products, arithmetic and copies ran while one was open for 1% of the time, Pallas kernels for 4%

profile of v3, /device:TPU:4, one launch (start us, length us, event | category | flops | bytes accessed | tf_op | source)
XLA Modules:
  0.0 297.9 jit_solution(15089034551000581086)
XLA Ops:
  16.7 3.1 %collective-permute-start.3 = (bf16[1040,128]{1,0:T(8,128)(2,1)S(1)}, bf16[1040,128]{1,0:T(8,128)(2,1)S(1)}, u32[]{:S(2)}, u32[]{:S(2)}) collective-permute-start(bf16[1040,128]{1,0:T(8,128)(2,1)S(1)} %get-tuple-element.31), channel_id=1, source_target_pairs={{0,16},{16,0},{1,17},{17,1},{2,18},{18,2},{3,19},{19,3},{4,20},{20... | collective-permute-start | bytes 798728 | tf_op jit(solution)/shard_map/ppermute | solution.py:21
  19.8 7.2 %collective-permute-done.3.got = bf16[1040,128]{1,0:T(8,128)(2,1)S(1)} collective-permute-done((bf16[1040,128]{1,0:T(8,128)(2,1)S(1)}, bf16[1040,128]{1,0:T(8,128)(2,1)S(1)}, u32[]{:S(2)}, u32[]{:S(2)}) %collective-permute-start.3) | collective-permute-done | bytes 266272 | tf_op jit(solution)/shard_map/ppermute | solution.py:21
  28.3 15.3 %all-to-all-start = ((bf16[16,80,128]{2,1,0:T(8,128)(2,1)}), bf16[16,80,128]{2,1,0:T(8,128)(2,1)S(1)}, u32[]{:S(2)}, u32[]{:S(2)}) async-start(bf16[16,80,128]{2,1,0:T(8,128)(2,1)} %shard_map.133), calls=%async_computation | async-start | bytes 655360 | tf_op jit(solution)/shard_map/all_to_all | solution.py:17
  49.4 3.1 %collective-permute-start.1 = (bf16[16,64,128]{2,1,0:T(8,128)(2,1)S(1)}, bf16[16,64,128]{2,1,0:T(8,128)(2,1)S(1)}, u32[]{:S(2)}, u32[]{:S(2)}) collective-permute-start(bf16[16,64,128]{2,1,0:T(8,128)(2,1)S(1)} %get-tuple-element.27), channel_id=1, source_target_pairs={{0,16},{16,0},{1,17},{17,1},{2,18},{18,2},{3,19},{19,3},{4,20},{20... | collective-permute-start | bytes 786440 | tf_op jit(solution)/shard_map/ppermute | solution.py:21
  52.5 7.1 %collective-permute-done.1.got = bf16[16,64,128]{2,1,0:T(8,128)(2,1)S(1)} collective-permute-done((bf16[16,64,128]{2,1,0:T(8,128)(2,1)S(1)}, bf16[16,64,128]{2,1,0:T(8,128)(2,1)S(1)}, u32[]{:S(2)}, u32[]{:S(2)}) %collective-permute-start.1) | collective-permute-done | bytes 262176 | tf_op jit(solution)/shard_map/ppermute | solution.py:21
  59.6 4.5 %all-to-all-done.bases = bf16[16,80,128]{2,1,0:T(8,128)(2,1)S(1)} async-done(((bf16[16,80,128]{2,1,0:T(8,128)(2,1)}), bf16[16,80,128]{2,1,0:T(8,128)(2,1)S(1)}, u32[]{:S(2)}, u32[]{:S(2)}) %all-to-all-start) | async-done | bytes 327712 | tf_op jit(solution)/shard_map/all_to_all | solution.py:17
  64.7 30.1 %all_to_all.30.got = bf16[16,96,128]{2,1,0:T(8,128)(2,1)S(1)} all-to-all(bf16[16,96,128]{2,1,0:T(8,128)(2,1)S(1)} %get-tuple-element.37), channel_id=1, replica_groups=mesh['z'=16,'xl'=2,'c'=2,'t'=8] {'z'}, dimensions={0} | all-to-all | bytes 786432 | tf_op jit(solution)/shard_map/all_to_all | solution.py:17
  94.8 5.0 %collective-permute-start.12 = (bf16[1024,128]{1,0:T(8,128)(2,1)S(1)}, bf16[1024,128]{1,0:T(8,128)(2,1)S(1)}, u32[]{:S(2)}, u32[]{:S(2)}) collective-permute-start(bf16[1024,128]{1,0:T(8,128)(2,1)S(1)} %get-tuple-element.38.refs_0_), channel_id=1, source_target_pairs={{0,7},{1,6},{2,5},{3,4},{4,3},{5,2},{6,1},{7,0},{8,15},{9,14},{10,... | collective-permute-start | bytes 786440 | tf_op jit(solution)/shard_map/ppermute | solution.py:26
  101.9 6.4 %collective-permute-start.10 = (bf16[1024,128]{1,0:T(8,128)(2,1)S(1)}, bf16[1024,128]{1,0:T(8,128)(2,1)S(1)}, u32[]{:S(2)}, u32[]{:S(2)}) collective-permute-start(bf16[1024,128]{1,0:T(8,128)(2,1)S(1)} %get-tuple-element.38.refs_0_), channel_id=1, source_target_pairs={{0,5},{1,4},{2,7},{3,6},{4,1},{5,0},{6,3},{7,2},{8,13},{9,12},{10,... | collective-permute-start | bytes 786440 | tf_op jit(solution)/shard_map/ppermute | solution.py:26
  108.3 3.4 %collective-permute-start.9 = (bf16[1024,128]{1,0:T(8,128)(2,1)S(1)}, bf16[1024,128]{1,0:T(8,128)(2,1)S(1)}, u32[]{:S(2)}, u32[]{:S(2)}) collective-permute-start(bf16[1024,128]{1,0:T(8,128)(2,1)S(1)} %get-tuple-element.38.refs_0_), channel_id=1, source_target_pairs={{0,4},{1,5},{2,6},{3,7},{4,0},{5,1},{6,2},{7,3},{8,12},{9,13},{10,... | collective-permute-start | bytes 786440 | tf_op jit(solution)/shard_map/ppermute | solution.py:26
  114.1 3.5 %collective-permute-start.7 = (bf16[1024,128]{1,0:T(8,128)(2,1)S(1)}, bf16[1024,128]{1,0:T(8,128)(2,1)S(1)}, u32[]{:S(2)}, u32[]{:S(2)}) collective-permute-start(bf16[1024,128]{1,0:T(8,128)(2,1)S(1)} %get-tuple-element.38.refs_0_), channel_id=1, source_target_pairs={{0,2},{1,3},{2,0},{3,1},{4,6},{5,7},{6,4},{7,5},{8,10},{9,11},{10,... | collective-permute-start | bytes 786440 | tf_op jit(solution)/shard_map/ppermute | solution.py:26
  117.6 4.9 %collective-permute-start.6 = (bf16[1024,128]{1,0:T(8,128)(2,1)S(1)}, bf16[1024,128]{1,0:T(8,128)(2,1)S(1)}, u32[]{:S(2)}, u32[]{:S(2)}) collective-permute-start(bf16[1024,128]{1,0:T(8,128)(2,1)S(1)} %get-tuple-element.38.refs_0_), channel_id=1, source_target_pairs={{0,1},{1,0},{2,3},{3,2},{4,5},{5,4},{6,7},{7,6},{8,9},{9,8},{10,11... | collective-permute-start | bytes 786440 | tf_op jit(solution)/shard_map/ppermute | solution.py:26
  122.5 3.0 collective-permute-done.9.refs_4_
  125.5 4.0 %collective-permute-done.7.refs_2_ = bf16[1024,128]{1,0:T(8,128)(2,1)S(1)} collective-permute-done((bf16[1024,128]{1,0:T(8,128)(2,1)S(1)}, bf16[1024,128]{1,0:T(8,128)(2,1)S(1)}, u32[]{:S(2)}, u32[]{:S(2)}) %collective-permute-start.7) | collective-permute-done | bytes 262176 | tf_op jit(solution)/shard_map/ppermute | solution.py:26
  131.6 26.5 %all_to_all.31.got = bf16[16,32,128]{2,1,0:T(8,128)(2,1)S(1)} all-to-all(bf16[16,32,128]{2,1,0:T(8,128)(2,1)S(1)} %get-tuple-element.39), channel_id=1, replica_groups=mesh['z'=16,'xl'=2,'c'=2,'t'=8] {'z'}, dimensions={0} | all-to-all | bytes 262144 | tf_op jit(solution)/shard_map/all_to_all | solution.py:17
  158.9 4.8 %all-to-all-start.3 = ((bf16[16,80,128]{2,1,0:T(8,128)(2,1)}), bf16[16,80,128]{2,1,0:T(8,128)(2,1)S(1)}, u32[]{:S(2)}, u32[]{:S(2)}) async-start(bf16[16,80,128]{2,1,0:T(8,128)(2,1)} %bitcast.3), calls=%async_computation.4 | async-start | bytes 655360 | tf_op jit(solution)/shard_map/all_to_all | solution.py:17
  163.7 27.8 %all-gather.2.cloned.1.call-done.whole = bf16[512,1024]{1,0:T(8,128)(2,1)} async-done(((bf16[512,128]{1,0:T(8,128)(2,1)}), bf16[512,1024]{1,0:T(8,128)(2,1)}) %all-gather.2.cloned.1.call-update) | async-done | bytes 1048592 | tf_op jit(solution)/shard_map/all_gather | solution.py:341
  196.7 4.0 %collective-permute-start.5 = (bf16[16,16,128]{2,1,0:T(8,128)(2,1)S(1)}, bf16[16,16,128]{2,1,0:T(8,128)(2,1)S(1)}, u32[]{:S(2)}, u32[]{:S(2)}) collective-permute-start(bf16[16,16,128]{2,1,0:T(8,128)(2,1)S(1)} %get-tuple-element.36), channel_id=1, source_target_pairs={{0,16},{16,0},{1,17},{17,1},{2,18},{18,2},{3,19},{19,3},{4,20},{20... | collective-permute-start | bytes 196616 | tf_op jit(solution)/shard_map/ppermute | solution.py:21
  203.5 5.8 %all-to-all-start.4 = ((bf16[8,64,128]{2,1,0:T(8,128)(2,1)}), bf16[8,64,128]{2,1,0:T(8,128)(2,1)S(1)}, u32[]{:S(2)}, u32[]{:S(2)}) async-start(bf16[8,64,128]{2,1,0:T(8,128)(2,1)} %shard_map.141), calls=%async_computation.5 | async-start | bytes 262144 | tf_op jit(solution)/shard_map/all_to_all | solution.py:17
  210.1 4.7 %all-to-all-done.4.rows = bf16[8,64,128]{2,1,0:T(8,128)(2,1)S(1)} async-done(((bf16[8,64,128]{2,1,0:T(8,128)(2,1)}), bf16[8,64,128]{2,1,0:T(8,128)(2,1)S(1)}, u32[]{:S(2)}, u32[]{:S(2)}) %all-to-all-start.4) | async-done | bytes 131104 | tf_op jit(solution)/shard_map/all_to_all | solution.py:17
  214.7 2.9 shard_map.142
  217.7 11.7 %all_to_all.32 = bf16[16,64,128]{2,1,0:T(8,128)(2,1)S(1)} all-to-all(bf16[16,64,128]{2,1,0:T(8,128)(2,1)S(1)} %bitcast.14), channel_id=1, replica_groups=mesh['z'=16,'xl'=2,'c'=2,'t'=8] {'xl','t'}, dimensions={0} | all-to-all | bytes 524288 | tf_op jit(solution)/shard_map/all_to_all | solution.py:17
  232.9 50.7 %reduce-scatter.2.cloned.1.call-done = bf16[1,48,128]{2,1,0:T(8,128)(2,1)} async-done(((bf16[16,48,128]{2,1,0:T(8,128)(2,1)}), bf16[1,48,128]{2,1,0:T(8,128)(2,1)}) %reduce-scatter.2.cloned.1.call-update) | async-done | bytes 12304 | tf_op jit(solution)/shard_map/reduce_scatter | solution.py:378
  286.2 4.9 %shard_map.143 = (bf16[1024,2,128]{2,1,0:T(2,128)(2,1)}, bf16[1,1024,128]{2,1,0:T(8,128)(2,1)}) custom-call(s32[64]{0:T(128)S(1)} %copy-done.12, bf16[8,1024,128]{2,1,0:T(8,128)(2,1)S(1)} %shard_map.139.own, bf16[8,1024,128]{2,1,0:T(8,128)(2,1)} %collective-permute-done.13.other, bf16[2,8,64,128]{3,2,1,0:T(8,128)(2,1)S(1)} %bitcast.13, ...), custom_call_target="tpu_custom_call" | custom-call | flops 536870912 | bytes 5505024 | tf_op jit(solution)/shard_map/pallas_call | solution.py:34
  (67 shorter events, 39.1 us)
Async XLA Ops:
  7.2 36.5 %copy-start.2 = (bf16[512,128]{1,0:T(8,128)(2,1)S(1)}, bf16[512,128]{1,0:T(8,128)(2,1)}, u32[]{:S(2)}) copy-start(bf16[512,128]{1,0:T(8,128)(2,1)} %act.3) | copy-start | bytes 393220
  7.2 36.5 %copy-start = (bf16[512,2,1024]{2,1,0:T(2,128)(2,1)S(1)}, bf16[512,2,1024]{2,1,0:T(2,128)(2,1)}, u32[]{:S(2)}) copy-start(bf16[512,2,1024]{2,1,0:T(2,128)(2,1)} %cot.3) | copy-start | bytes 6291460
  11.7 3.6 %collective-permute-start.2 = (bf16[1552,128]{1,0:T(8,128)(2,1)S(1)}, bf16[1552,128]{1,0:T(8,128)(2,1)S(1)}, u32[]{:S(2)}, u32[]{:S(2)}) collective-permute-start(bf16[1552,128]{1,0:T(8,128)(2,1)S(1)} %get-tuple-element.29), channel_id=1, source_target_pairs={{0,8},{8,0},{1,9},{9,1},{2,10},{10,2},{3,11},{11,3},{4,12},{12,4},... | collective-permute-start | bytes 1191944 | tf_op jit(solution)/shard_map/ppermute | solution.py:21
  16.7 10.3 %collective-permute-start.3 = (bf16[1040,128]{1,0:T(8,128)(2,1)S(1)}, bf16[1040,128]{1,0:T(8,128)(2,1)S(1)}, u32[]{:S(2)}, u32[]{:S(2)}) collective-permute-start(bf16[1040,128]{1,0:T(8,128)(2,1)S(1)} %get-tuple-element.31), channel_id=1, source_target_pairs={{0,16},{16,0},{1,17},{17,1},{2,18},{18,2},{3,19},{19,3},{4,20},{20... | collective-permute-start | bytes 798728 | tf_op jit(solution)/shard_map/ppermute | solution.py:21
  28.3 35.7 %all-to-all-start = ((bf16[16,80,128]{2,1,0:T(8,128)(2,1)}), bf16[16,80,128]{2,1,0:T(8,128)(2,1)S(1)}, u32[]{:S(2)}, u32[]{:S(2)}) async-start(bf16[16,80,128]{2,1,0:T(8,128)(2,1)} %shard_map.133), calls=%async_computation | async-start | bytes 655360 | tf_op jit(solution)/shard_map/all_to_all | solution.py:17
  43.7 147.9 %all-gather.2.cloned.1.call-start = ((), (), s32[]{:S(2)}) async-start(), calls=%async_computation.7 | async-start | bytes 1179648 | tf_op jit(solution)/shard_map/all_gather | solution.py:341
  45.5 3.8 %collective-permute-start = (bf16[2,16,64,128]{3,2,1,0:T(8,128)(2,1)S(1)}, bf16[2,16,64,128]{3,2,1,0:T(8,128)(2,1)S(1)}, u32[]{:S(2)}, u32[]{:S(2)}) collective-permute-start(bf16[2,16,64,128]{3,2,1,0:T(8,128)(2,1)S(1)} %get-tuple-element.25), channel_id=1, source_target_pairs={{0,8},{8,0},{1,9},{9,1},{2,10},{10,2},{3,11},{11,3},{4,12},{12,4},... | collective-permute-start | bytes 1572872 | tf_op jit(solution)/shard_map/ppermute | solution.py:21
  49.4 10.2 %collective-permute-start.1 = (bf16[16,64,128]{2,1,0:T(8,128)(2,1)S(1)}, bf16[16,64,128]{2,1,0:T(8,128)(2,1)S(1)}, u32[]{:S(2)}, u32[]{:S(2)}) collective-permute-start(bf16[16,64,128]{2,1,0:T(8,128)(2,1)S(1)} %get-tuple-element.27), channel_id=1, source_target_pairs={{0,16},{16,0},{1,17},{17,1},{2,18},{18,2},{3,19},{19,3},{4,20},{20... | collective-permute-start | bytes 786440 | tf_op jit(solution)/shard_map/ppermute | solution.py:21
  94.8 96.8 %copy-start.3 = (bf16[512,128]{1,0:T(8,128)(2,1)S(1)}, bf16[512,128]{1,0:T(8,128)(2,1)}, u32[]{:S(2)}) copy-start(bf16[512,128]{1,0:T(8,128)(2,1)} %act.3) | copy-start | bytes 393220
  94.8 19.2 %collective-permute-start.12 = (bf16[1024,128]{1,0:T(8,128)(2,1)S(1)}, bf16[1024,128]{1,0:T(8,128)(2,1)S(1)}, u32[]{:S(2)}, u32[]{:S(2)}) collective-permute-start(bf16[1024,128]{1,0:T(8,128)(2,1)S(1)} %get-tuple-element.38.refs_0_), channel_id=1, source_target_pairs={{0,7},{1,6},{2,5},{3,4},{4,3},{5,2},{6,1},{7,0},{8,15},{9,14},{10,... | collective-permute-start | bytes 786440 | tf_op jit(solution)/shard_map/ppermute | solution.py:26
  99.8 17.8 %collective-permute-start.11 = (bf16[1024,128]{1,0:T(8,128)(2,1)S(1)}, bf16[1024,128]{1,0:T(8,128)(2,1)S(1)}, u32[]{:S(2)}, u32[]{:S(2)}) collective-permute-start(bf16[1024,128]{1,0:T(8,128)(2,1)S(1)} %get-tuple-element.38.refs_0_), channel_id=1, source_target_pairs={{0,6},{1,7},{2,4},{3,5},{4,2},{5,3},{6,0},{7,1},{8,14},{9,15},{10,... | collective-permute-start | bytes 786440 | tf_op jit(solution)/shard_map/ppermute | solution.py:26
  101.9 20.6 %collective-permute-start.10 = (bf16[1024,128]{1,0:T(8,128)(2,1)S(1)}, bf16[1024,128]{1,0:T(8,128)(2,1)S(1)}, u32[]{:S(2)}, u32[]{:S(2)}) collective-permute-start(bf16[1024,128]{1,0:T(8,128)(2,1)S(1)} %get-tuple-element.38.refs_0_), channel_id=1, source_target_pairs={{0,5},{1,4},{2,7},{3,6},{4,1},{5,0},{6,3},{7,2},{8,13},{9,12},{10,... | collective-permute-start | bytes 786440 | tf_op jit(solution)/shard_map/ppermute | solution.py:26
  108.3 17.2 %collective-permute-start.9 = (bf16[1024,128]{1,0:T(8,128)(2,1)S(1)}, bf16[1024,128]{1,0:T(8,128)(2,1)S(1)}, u32[]{:S(2)}, u32[]{:S(2)}) collective-permute-start(bf16[1024,128]{1,0:T(8,128)(2,1)S(1)} %get-tuple-element.38.refs_0_), channel_id=1, source_target_pairs={{0,4},{1,5},{2,6},{3,7},{4,0},{5,1},{6,2},{7,3},{8,12},{9,13},{10,... | collective-permute-start | bytes 786440 | tf_op jit(solution)/shard_map/ppermute | solution.py:26
  111.8 13.8 %collective-permute-start.8 = (bf16[1024,128]{1,0:T(8,128)(2,1)S(1)}, bf16[1024,128]{1,0:T(8,128)(2,1)S(1)}, u32[]{:S(2)}, u32[]{:S(2)}) collective-permute-start(bf16[1024,128]{1,0:T(8,128)(2,1)S(1)} %get-tuple-element.38.refs_0_), channel_id=1, source_target_pairs={{0,3},{1,2},{2,1},{3,0},{4,7},{5,6},{6,5},{7,4},{8,11},{9,10},{10,... | collective-permute-start | bytes 786440 | tf_op jit(solution)/shard_map/ppermute | solution.py:26
  114.1 15.5 %collective-permute-start.7 = (bf16[1024,128]{1,0:T(8,128)(2,1)S(1)}, bf16[1024,128]{1,0:T(8,128)(2,1)S(1)}, u32[]{:S(2)}, u32[]{:S(2)}) collective-permute-start(bf16[1024,128]{1,0:T(8,128)(2,1)S(1)} %get-tuple-element.38.refs_0_), channel_id=1, source_target_pairs={{0,2},{1,3},{2,0},{3,1},{4,6},{5,7},{6,4},{7,5},{8,10},{9,11},{10,... | collective-permute-start | bytes 786440 | tf_op jit(solution)/shard_map/ppermute | solution.py:26
  117.6 11.9 %collective-permute-start.6 = (bf16[1024,128]{1,0:T(8,128)(2,1)S(1)}, bf16[1024,128]{1,0:T(8,128)(2,1)S(1)}, u32[]{:S(2)}, u32[]{:S(2)}) collective-permute-start(bf16[1024,128]{1,0:T(8,128)(2,1)S(1)} %get-tuple-element.38.refs_0_), channel_id=1, source_target_pairs={{0,1},{1,0},{2,3},{3,2},{4,5},{5,4},{6,7},{7,6},{8,9},{9,8},{10,11... | collective-permute-start | bytes 786440 | tf_op jit(solution)/shard_map/ppermute | solution.py:26
  129.7 71.0 %collective-permute-start.13 = (bf16[8,1024,128]{2,1,0:T(8,128)(2,1)S(1)}, bf16[8,1024,128]{2,1,0:T(8,128)(2,1)}, u32[]{:S(2)}, u32[]{:S(2)}) collective-permute-start(bf16[8,1024,128]{2,1,0:T(8,128)(2,1)S(1)} %shard_map.139.own), channel_id=1, source_target_pairs={{0,8},{8,0},{1,9},{9,1},{2,10},{10,2},{3,11},{11,3},{4,12},{12,4},... | collective-permute-start | bytes 6291464 | tf_op jit(solution)/shard_map/ppermute | solution.py:21
  158.9 41.8 %all-to-all-start.3 = ((bf16[16,80,128]{2,1,0:T(8,128)(2,1)}), bf16[16,80,128]{2,1,0:T(8,128)(2,1)S(1)}, u32[]{:S(2)}, u32[]{:S(2)}) async-start(bf16[16,80,128]{2,1,0:T(8,128)(2,1)} %bitcast.3), calls=%async_computation.4 | async-start | bytes 655360 | tf_op jit(solution)/shard_map/all_to_all | solution.py:17
  193.4 3.2 %collective-permute-start.4 = (bf16[16,2,16,128]{3,2,1,0:T(8,128)(2,1)S(1)}, bf16[16,2,16,128]{3,2,1,0:T(8,128)(2,1)S(1)}, u32[]{:S(2)}, u32[]{:S(2)}) collective-permute-start(bf16[16,2,16,128]{3,2,1,0:T(8,128)(2,1)S(1)} %get-tuple-element.34), channel_id=1, source_target_pairs={{0,8},{8,0},{1,9},{9,1},{2,10},{10,2},{3,11},{11,3},{4,12},{12,4},... | collective-permute-start | bytes 393224 | tf_op jit(solution)/shard_map/ppermute | solution.py:21
  196.7 12.6 %collective-permute-start.5 = (bf16[16,16,128]{2,1,0:T(8,128)(2,1)S(1)}, bf16[16,16,128]{2,1,0:T(8,128)(2,1)S(1)}, u32[]{:S(2)}, u32[]{:S(2)}) collective-permute-start(bf16[16,16,128]{2,1,0:T(8,128)(2,1)S(1)} %get-tuple-element.36), channel_id=1, source_target_pairs={{0,16},{16,0},{1,17},{17,1},{2,18},{18,2},{3,19},{19,3},{4,20},{20... | collective-permute-start | bytes 196616 | tf_op jit(solution)/shard_map/ppermute | solution.py:21
  203.5 11.2 %all-to-all-start.4 = ((bf16[8,64,128]{2,1,0:T(8,128)(2,1)}), bf16[8,64,128]{2,1,0:T(8,128)(2,1)S(1)}, u32[]{:S(2)}, u32[]{:S(2)}) async-start(bf16[8,64,128]{2,1,0:T(8,128)(2,1)} %shard_map.141), calls=%async_computation.5 | async-start | bytes 262144 | tf_op jit(solution)/shard_map/all_to_all | solution.py:17
  209.3 74.2 %reduce-scatter.2.cloned.1.call-start = ((), (), s32[]{:S(2)}) async-start(), calls=%async_computation.8 | async-start | bytes 208896 | tf_op jit(solution)/shard_map/reduce_scatter | solution.py:378
  217.6 68.6 %copy-start.12 = (s32[64]{0:T(128)S(1)}, s32[64]{0:T(128)}, u32[]{:S(2)}) copy-start(s32[64]{0:T(128)} %groups.1) | copy-start | bytes 772
  229.4 56.8 %collective-permute-start.14 = (bf16[2,8,64,128]{3,2,1,0:T(8,128)(2,1)S(1)}, bf16[2,8,64,128]{3,2,1,0:T(8,128)(2,1)S(1)}, u32[]{:S(2)}, u32[]{:S(2)}) collective-permute-start(bf16[2,8,64,128]{3,2,1,0:T(8,128)(2,1)S(1)} %bitcast.12), channel_id=1, source_target_pairs={{0,8},{8,0},{1,9},{9,1},{2,10},{10,2},{3,11},{11,3},{4,12},{12,4},... | collective-permute-start | bytes 786440 | tf_op jit(solution)/shard_map/ppermute | solution.py:21
  (9 other events, 78.9 us)
Sparse Core Ops, SparseCore 0:
  131.7 59.7 all-gather.1
  213.5 70.0 reduce-scatter.1

commit v4 on v3

--- a/solution.py
+++ b/solution.py
@@ -165,17 +165,16 @@
     rest[...] = keep[xl] + got[xl].astype(f32)
 
 
-def pack_z(owners, keep, got, bases, sent, vals, cov):
+def pack_z(owners, keep, got, bases, sent, vals):
     nz, height, slab = keep.shape
     per = (bases.shape[1] - VALS) // 2
     xl = lax.axis_index("xl")
     source = [owners[i] // 4 for i in range(3)]
-    sent[:, 0:per] = (keep[:, 0:per] + got[:, 0:per].astype(f32)).astype(bf16)
-    cov[...] = keep[:, per:] + got[:, per:].astype(f32)
+    sent[:, 0:height] = (keep[...] + got[...].astype(f32)).astype(bf16)
     for i, src in enumerate((source[0], owners[1 + xl] // 4)):
         part = bases[src, i * per : (i + 1) * per]
         for k in range(nz):
-            sent[k, (1 + i) * per : (2 + i) * per] = part
+            sent[k, height + i * per : height + (i + 1) * per] = part
     chosen = bases[source[0], 2 * per :].astype(f32)
     place = lax.broadcasted_iota(jnp.int32, chosen.shape, 0)
     for i in (1, 2):
@@ -183,41 +182,60 @@
     vals[...] = chosen.astype(bf16)
 
 
-def reduce_z(got, sent, bases):
+def reduce_z(got, a_keep, a_got, sent, factor_g, bases):
+    nz, _, slab = got.shape
+    group = a_keep.shape[1]
+    half = bases.shape[0] // 2
+    per = half // nz
+    height = per + 2 * group
+    total = got[0, 0:height].astype(f32)
+    for k in range(1, nz):
+        total = total + got[k, 0:height].astype(f32)
+    grad = total[0:per].astype(bf16)
+    for k in range(nz):
+        sent[k, 0:per] = grad
+    sent[:, per:] = (a_keep[...] + a_got[...].astype(f32)).astype(bf16)
+    for j in range(2):
+        factor_g[j] = total[per + j * group : per + (j + 1) * group]
+    bases[0:half] = got[:, height : height + per].reshape(half, slab)
+    bases[half:] = got[:, height + per :].reshape(half, slab)
+
+
+def pair_bases(own, got, qa, qg):
+    half = own.shape[0] // 2
+    side = lax.axis_index("t") % 2
+    for slot, ref in ((side, own), (1 - side, got)):
+        qa[slot] = ref[0:half]
+        qg[slot] = ref[half:]
+
+
+def stack_pairs(own, one, two, three, after, whole):
+    first = lax.axis_index("t") // 2
+    for k, pair in enumerate((own, one, two, three)):
+        for side in range(2):
+            whole[2 * (first ^ k) + side] = pair[side]
+
+
+def pack_t(got, vals, pair, sent, factor_a, same):
     nz, height, slab = got.shape
-    per = height // 3
-    total = got[0, 0:per].astype(f32)
-    for k in range(1, nz):
-        total = total + got[k, 0:per].astype(f32)
-    total = total.astype(bf16)
-    for k in range(nz):
-        sent[k] = total
-    half = nz * per
-    bases[0:half] = got[:, per : 2 * per].reshape(half, slab)
-    bases[half:] = got[:, 2 * per :].reshape(half, slab)
-
-
-def stack_bases(*refs):
-    pieces, whole = refs[:-1], refs[-1]
-    t = lax.axis_index("t")
-    for k, piece in enumerate(pieces):
-        whole[t ^ k] = piece[...]
-
-
-def pack_t(got, vals, sent):
-    nz, per, slab = got.shape
-    nt, height, _ = sent.shape[1:]
-    piece = height - VALS
-    grad = got[...].reshape(nz * per, slab).reshape(nt, piece, slab)
+    group = factor_a.shape[0]
+    per = height - group
+    nt, width, _ = sent.shape[1:]
+    piece = width - VALS
+    grad = got[:, 0:per].reshape(nz * per, slab).reshape(nt, piece, slab)
     for c in range(2):
         sent[c, :, 0:piece] = grad
         for k in range(nt):
             sent[c, k, piece:] = vals[...]
+    total = got[0, per:].astype(f32)
+    for k in range(1, nz):
+        total = total + got[k, per:].astype(f32)
+    factor_a[...] = total
+    same[...] = pair[...]
 
 
 def rotate(got, own, other, sent, grad):
-    nt, height, slab = own.shape
-    half = height // 2
+    nt, half, slab = own.shape
     piece = half // nt
     core = lax.axis_index("c")
     for c in range(2):
@@ -227,7 +245,7 @@
     far = grad[:, pl.ds(pl.multiple_of((1 - core) * half, half), half)]
     for i in range(nt // 2):
         k = core * (nt // 2) + i
-        turned = dot(near, own[k, 0:half]) + dot(far, other[k, 0:half])
+        turned = dot(near, own[k]) + dot(far, other[k])
         turned = turned.T.astype(bf16)
         sent[2 * i] = turned[0:piece]
         sent[2 * i + 1] = turned[piece:]
@@ -235,7 +253,7 @@
 
 def scale_rows(rows, own, other, got, sent, rot, scaled, column):
     nt, piece, slab = rows.shape
-    half = own.shape[1] // 2
+    half = own.shape[1]
     core, xl, t = lax.axis_index("c"), lax.axis_index("xl"), lax.axis_index("t")
     row = got[0, core * (nt // 2) + t // 2, piece:].astype(f32)[0:1]
     column[...] = jnp.broadcast_to(row, (slab, slab)).T
@@ -245,14 +263,14 @@
     near = rot[:, pl.ds(pl.multiple_of(core * half, half), half)]
     far = rot[:, pl.ds(pl.multiple_of((1 - core) * half, half), half)]
     for k in range(nt):
-        spectral = dot(near, own[k, half:]) + dot(far, other[k, half:])
+        spectral = dot(near, own[k]) + dot(far, other[k])
         values = got[0, k, piece:].astype(f32)
         lg = jnp.where(xl == 0, values[1:2], values[2:3])
         scaled[k] = (spectral / (la * lg + damping)).astype(bf16)
     for side, ref in ((core, own), (1 - core, other)):
-        mixed = dot(scaled[0], ref[0, half:], ((1,), (1,)))
+        mixed = dot(scaled[0], ref[0], ((1,), (1,)))
         for k in range(1, nt):
-            mixed = mixed + dot(scaled[k], ref[k, half:], ((1,), (1,)))
+            mixed = mixed + dot(scaled[k], ref[k], ((1,), (1,)))
         mixed = mixed.astype(bf16)
         for i in range(nt // 2):
             for copy in range(2):
@@ -261,7 +279,7 @@
 
 def finish(groups, own, other, own_mixed, other_mixed, pre, worker):
     blocks, nt, piece, slab = own_mixed.shape
-    half = own.shape[1] // 2
+    half = own.shape[1]
     core = lax.axis_index("c")
     replica = (lax.axis_index("z") * 2 + lax.axis_index("xl")) * 2 + core
     group = groups[replica]
@@ -272,7 +290,7 @@
                 right = jnp.concatenate(
                     [mixed[j, 2 * i : 2 * i + 2].reshape(2 * piece, slab) for j in range(blocks)], 1
                 )
-                total = total + dot(ref[part * (nt // 2) + i, 0:half], right)
+                total = total + dot(ref[part * (nt // 2) + i], right)
         total = total.astype(bf16)
         place = pl.ds(pl.multiple_of(side * half, half), half)
         pre[place] = total.reshape(half, blocks, slab)
@@ -307,12 +325,6 @@
     rest[...] = keep[:, xl] + got[:, xl].astype(f32)
 
 
-def pack_factors(cov, keep, got, sent):
-    group = keep.shape[1]
-    sent[:, 0 : 2 * group] = cov[...].astype(bf16)
-    sent[:, 2 * group :] = (keep[...] + got[...].astype(f32)).astype(bf16)
-
-
 def local(act, cot, weight, owners, worker_group, basis_a, values_a, basis_g, values_g):
     tok, slab = act.shape
     blocks, full = cot.shape[1:]
@@ -328,7 +340,7 @@
         [out(shape), out(shape)],
         [],
         [basis_a, basis_g, values_a, values_g],
-        [pl.ANY, pl.ANY, pltpu.VMEM, pltpu.VMEM],
+        [pltpu.HBM, pltpu.HBM, pltpu.VMEM, pltpu.VMEM],
         scratch=[pltpu.SemaphoreType.DMA((2, 3))],
     )
     got = swap(sent, "c")
@@ -353,9 +365,9 @@
     sent, keep = call(add_core, [out(block[1:]), out(block[1:], f32)], [], [keep, got])
     got = swap(sent, "xl")
 
-    sent, vals, cov = call(
+    sent, vals = call(
         pack_z,
-        [out((nz, 3 * per, slab)), out((VALS, slab)), out((nz, 2 * group, slab), f32)],
+        [out((nz, height + 2 * per, slab)), out((VALS, slab))],
         [owners],
         [keep, got, got_bases],
     )
@@ -374,27 +386,39 @@
     block = (nz, group, slab)
     sent, keep = call(input_factor_core, [out(block), out(block, f32)], [], [keep, a_got])
     a_got = swap(sent, "xl")
-    (sent,) = call(pack_factors, [out((nz, 3 * group, slab))], [], [cov, keep, a_got])
-    factors = lax.psum_scatter(sent, "z", scatter_dimension=0, tiled=False).astype(f32)
-    factor_g = factors[: 2 * group].reshape(blocks, group, slab).transpose(1, 0, 2)
-    factor_a = factors[2 * group :]
-
-    sent, bases = call(
-        reduce_z, [out((nz, per, slab)), out((2 * half, slab))], [], [got]
-    )
+
+    sent, factor_g, bases = call(
+        reduce_z,
+        [out((nz, per + group, slab)), out((blocks, group, slab), f32), out((2 * half, slab))],
+        [],
+        [got, keep, a_got],
+    )
+    pair = out((2, half, slab))
+    whole = out((nt, half, slab))
+    orders = [pltpu.VMEM] * 4 + [pl.ANY]
     got = exchange(sent, "z")
-    pieces = [bases] + [across(bases, "t", k) for k in range(1, nt)]
-    (own,) = call(stack_bases, [out((nt, 2 * half, slab))], [], pieces)
-    other = swap(own, "c")
-
-    (sent,) = call(pack_t, [out((2, nt, piece + VALS, slab))], [], [got, vals])
+    near = across(bases, "t", 1)
+    qa, qg = call(pair_bases, [pair, pair], [], [bases, near])
+    pairs = [qa] + [across(qa, "t", 2 * k) for k in range(1, nt // 2)]
+    (qa_own,) = call(stack_pairs, [whole], [], pairs + [got], orders)
+    qa_other = swap(qa_own, "c")
+
+    sent, factor_a, qg = call(
+        pack_t,
+        [out((2, nt, piece + VALS, slab)), out((group, slab), f32), pair],
+        [],
+        [got, vals, qg],
+    )
     columns = exchange(sent.reshape(2 * nt, piece + VALS, slab), ("c", "t"))
     columns = columns.reshape(2, nt, piece + VALS, slab)
+    pairs = [qg] + [across(qg, "t", 2 * k) for k in range(1, nt // 2)]
+    (qg_own,) = call(stack_pairs, [whole], [], pairs + [columns], orders)
+    qg_other = swap(qg_own, "c")
     (sent,) = call(
         rotate,
         [out((nt, piece, slab))],
         [],
-        [columns, own, other],
+        [columns, qa_own, qa_other],
         scratch=[pltpu.VMEM((slab, full), bf16)],
         flops=2 * slab * full * half,
     )
@@ -403,7 +427,7 @@
         scale_rows,
         [out((blocks, nt, piece, slab))],
         [],
-        [rows, own, other, columns],
+        [rows, qg_own, qg_other, columns],
         scratch=[
             pltpu.VMEM((piece, full), bf16),
             pltpu.VMEM((nt, piece, slab), bf16),
@@ -418,14 +442,14 @@
         finish,
         [out((full, blocks, slab)), out((1, full, slab))],
         [worker_group],
-        [own, other, own_mixed, other_mixed],
+        [qa_own, qa_other, own_mixed, other_mixed],
         flops=4 * full * full * slab,
     )
 
     (grad_input,) = call(
         input_grad, [out((tok, slab))], [], [cot, weight], flops=4 * tok * full * slab
     )
-    return grad_input, factor_a, factor_g, pre, worker
+    return grad_input, factor_a, factor_g.transpose(1, 0, 2), pre, worker
 
 
 def solution(mesh):

time: 299 us -> 242 us (0.81)
  the two profiles are of different devices: /device:TPU:4 before, /device:TPU:1 now
where the time goes in v4:
time: 242 us; the launch traced here: 240 us
  starting transfers between devices  95.2 us (39%)
  waiting for transfers between devices  73.2 us (30%)
  blocking collectives  20.9 us (9%)
  Pallas kernels  20.5 us (8%)
  local copies, waits for them, and re-layouts  16.1 us (7%)
  between operations  14.4 us (6%)
    all_gather x1, waiting for transfers between devices, local(): whole_act = lax.all_gather(act, 't', axis=1, tiled=True)  41.3 us
    all_to_all x4, starting transfers between devices, exchange(): return lax.all_to_all(array, axis, 0, 0, tiled=True)  40.2 us
    ppermute x9, starting transfers between devices, swap(): return lax.ppermute(array, axis, [(0, 1), (1, 0)])  32.8 us
    ppermute x7, starting transfers between devices, across(): return lax.ppermute(array, axis, pairs)  22.2 us
    all_to_all x2, blocking collectives, exchange(): return lax.all_to_all(array, axis, 0, 0, tiled=True)  20.9 us
    ppermute x9, waiting for transfers between devices, swap(): return lax.ppermute(array, axis, [(0, 1), (1, 0)])  20.7 us
    pallas_call x17, Pallas kernels, call(): pl.pallas_call(body, out_shape=outs, in_specs=[pl.BlockSpec(memory_space=...  20.5 us
    unnamed x53, local copies, waits for them, and re-layouts  16.1 us
  transfers between devices with their start and end apart: 21, of which 9 were waited for; matrix products, arithmetic and copies ran while one was open for 0% of the time, Pallas kernels for 5%

profile of v4, /device:TPU:1, one launch (start us, length us, event | category | flops | bytes accessed | tf_op | source)
XLA Modules:
  0.0 240.4 jit_solution(9224628803688466209)
XLA Ops:
  11.7 8.8 %collective-permute-start.2 = (bf16[1552,128]{1,0:T(8,128)(2,1)S(1)}, bf16[1552,128]{1,0:T(8,128)(2,1)S(1)}, u32[]{:S(2)}, u32[]{:S(2)}) collective-permute-start(bf16[1552,128]{1,0:T(8,128)(2,1)S(1)} %get-tuple-element.34), channel_id=1, source_target_pairs={{0,8},{8,0},{1,9},{9,1},{2,10},{10,2},{3,11},{11,3},{4,12},{12,4},... | collective-permute-start | bytes 1191944 | tf_op jit(solution)/shard_map/ppermute | solution.py:21
  25.1 7.6 %collective-permute-done.3.got = bf16[1040,128]{1,0:T(8,128)(2,1)S(1)} collective-permute-done((bf16[1040,128]{1,0:T(8,128)(2,1)S(1)}, bf16[1040,128]{1,0:T(8,128)(2,1)S(1)}, u32[]{:S(2)}, u32[]{:S(2)}) %collective-permute-start.3) | collective-permute-done | bytes 266272 | tf_op jit(solution)/shard_map/ppermute | solution.py:21
  34.0 9.5 %all-to-all-start = ((bf16[16,80,128]{2,1,0:T(8,128)(2,1)}), bf16[16,80,128]{2,1,0:T(8,128)(2,1)S(1)}, u32[]{:S(2)}, u32[]{:S(2)}) async-start(bf16[16,80,128]{2,1,0:T(8,128)(2,1)} %shard_map.133), calls=%async_computation | async-start | bytes 655360 | tf_op jit(solution)/shard_map/all_to_all | solution.py:17
  45.4 3.5 %collective-permute-start = (bf16[2,16,64,128]{3,2,1,0:T(8,128)(2,1)S(1)}, bf16[2,16,64,128]{3,2,1,0:T(8,128)(2,1)S(1)}, u32[]{:S(2)}, u32[]{:S(2)}) collective-permute-start(bf16[2,16,64,128]{3,2,1,0:T(8,128)(2,1)S(1)} %get-tuple-element.30), channel_id=1, source_target_pairs={{0,8},{8,0},{1,9},{9,1},{2,10},{10,2},{3,11},{11,3},{4,12},{12,4},... | collective-permute-start | bytes 1572872 | tf_op jit(solution)/shard_map/ppermute | solution.py:21
  51.2 3.1 %collective-permute-start.1 = (bf16[16,64,128]{2,1,0:T(8,128)(2,1)}, bf16[16,64,128]{2,1,0:T(8,128)(2,1)S(1)}, u32[]{:S(2)}, u32[]{:S(2)}) collective-permute-start(bf16[16,64,128]{2,1,0:T(8,128)(2,1)} %get-tuple-element.32), channel_id=1, source_target_pairs={{0,16},{16,0},{1,17},{17,1},{2,18},{18,2},{3,19},{19,3},{4,20},{20... | collective-permute-start | bytes 786440 | tf_op jit(solution)/shard_map/ppermute | solution.py:21
  54.3 6.5 %collective-permute-done.1.got = bf16[16,64,128]{2,1,0:T(8,128)(2,1)S(1)} collective-permute-done((bf16[16,64,128]{2,1,0:T(8,128)(2,1)}, bf16[16,64,128]{2,1,0:T(8,128)(2,1)S(1)}, u32[]{:S(2)}, u32[]{:S(2)}) %collective-permute-start.1) | collective-permute-done | bytes 262176 | tf_op jit(solution)/shard_map/ppermute | solution.py:21
  62.2 11.7 %all-to-all-start.1 = ((bf16[16,128,128]{2,1,0:T(8,128)(2,1)}), bf16[16,128,128]{2,1,0:T(8,128)(2,1)S(1)}, u32[]{:S(2)}, u32[]{:S(2)}) async-start(bf16[16,128,128]{2,1,0:T(8,128)(2,1)} %get-tuple-element.37), calls=%async_computation.1 | async-start | bytes 1048576 | tf_op jit(solution)/shard_map/all_to_all | solution.py:17
  74.0 41.3 %all-gather.2.cloned.1.call-done.whole = bf16[512,1024]{1,0:T(8,128)(2,1)} async-done(((bf16[512,128]{1,0:T(8,128)(2,1)}), bf16[512,1024]{1,0:T(8,128)(2,1)}) %all-gather.2.cloned.1.call-update) | async-done | bytes 1048592 | tf_op jit(solution)/shard_map/all_gather | solution.py:353
  117.1 3.4 %collective-permute-start.4 = (bf16[16,2,16,128]{3,2,1,0:T(8,128)(2,1)S(1)}, bf16[16,2,16,128]{3,2,1,0:T(8,128)(2,1)S(1)}, u32[]{:S(2)}, u32[]{:S(2)}) collective-permute-start(bf16[16,2,16,128]{3,2,1,0:T(8,128)(2,1)S(1)} %get-tuple-element.39), channel_id=1, source_target_pairs={{0,8},{8,0},{1,9},{9,1},{2,10},{10,2},{3,11},{11,3},{4,12},{12,4},... | collective-permute-start | bytes 393224 | tf_op jit(solution)/shard_map/ppermute | solution.py:21
  123.7 2.8 %collective-permute-done.5.a_got = bf16[16,16,128]{2,1,0:T(8,128)(2,1)S(1)} collective-permute-done((bf16[16,16,128]{2,1,0:T(8,128)(2,1)S(1)}, bf16[16,16,128]{2,1,0:T(8,128)(2,1)S(1)}, u32[]{:S(2)}, u32[]{:S(2)}) %collective-permute-start.5) | collective-permute-done | bytes 65568 | tf_op jit(solution)/shard_map/ppermute | solution.py:21
  127.3 12.0 %all-to-all-start.2 = ((bf16[16,48,128]{2,1,0:T(8,128)(2,1)}), bf16[16,48,128]{2,1,0:T(8,128)(2,1)S(1)}, u32[]{:S(2)}, u32[]{:S(2)}) async-start(bf16[16,48,128]{2,1,0:T(8,128)(2,1)} %get-tuple-element.42), calls=%async_computation.2 | async-start | bytes 393216 | tf_op jit(solution)/shard_map/all_to_all | solution.py:17
  139.3 3.0 %collective-permute-start.6 = (bf16[1024,128]{1,0:T(8,128)(2,1)S(1)}, bf16[1024,128]{1,0:T(8,128)(2,1)S(1)}, u32[]{:S(2)}, u32[]{:S(2)}) collective-permute-start(bf16[1024,128]{1,0:T(8,128)(2,1)S(1)} %get-tuple-element.44.own), channel_id=1, source_target_pairs={{0,1},{1,0},{2,3},{3,2},{4,5},{5,4},{6,7},{7,6},{8,9},{9,8},{10,11... | collective-permute-start | bytes 786440 | tf_op jit(solution)/shard_map/ppermute | solution.py:26
  142.3 6.4 %collective-permute-done.6.got = bf16[1024,128]{1,0:T(8,128)(2,1)S(1)} collective-permute-done((bf16[1024,128]{1,0:T(8,128)(2,1)S(1)}, bf16[1024,128]{1,0:T(8,128)(2,1)S(1)}, u32[]{:S(2)}, u32[]{:S(2)}) %collective-permute-start.6) | collective-permute-done | bytes 262176 | tf_op jit(solution)/shard_map/ppermute | solution.py:26
  150.7 3.6 %collective-permute-start.8 = (bf16[2,512,128]{2,1,0:T(8,128)(2,1)S(1)}, bf16[2,512,128]{2,1,0:T(8,128)(2,1)S(1)}, u32[]{:S(2)}, u32[]{:S(2)}) collective-permute-start(bf16[2,512,128]{2,1,0:T(8,128)(2,1)S(1)} %get-tuple-element.48.own), channel_id=1, source_target_pairs={{0,4},{1,5},{2,6},{3,7},{4,0},{5,1},{6,2},{7,3},{8,12},{9,13},{10,... | collective-permute-start | bytes 786440 | tf_op jit(solution)/shard_map/ppermute | solution.py:26
  154.3 4.0 %collective-permute-start.9 = (bf16[2,512,128]{2,1,0:T(8,128)(2,1)S(1)}, bf16[2,512,128]{2,1,0:T(8,128)(2,1)}, u32[]{:S(2)}, u32[]{:S(2)}) collective-permute-start(bf16[2,512,128]{2,1,0:T(8,128)(2,1)S(1)} %get-tuple-element.48.own), channel_id=1, source_target_pairs={{0,6},{1,7},{2,4},{3,5},{4,2},{5,3},{6,0},{7,1},{8,14},{9,15},{10,... | collective-permute-start | bytes 786440 | tf_op jit(solution)/shard_map/ppermute | solution.py:26
  159.3 6.9 %all-to-all-start.3 = ((bf16[16,80,128]{2,1,0:T(8,128)(2,1)}), bf16[16,80,128]{2,1,0:T(8,128)(2,1)S(1)}, u32[]{:S(2)}, u32[]{:S(2)}) async-start(bf16[16,80,128]{2,1,0:T(8,128)(2,1)} %bitcast.1), calls=%async_computation.3 | async-start | bytes 655360 | tf_op jit(solution)/shard_map/all_to_all | solution.py:17
  166.2 3.3 %collective-permute-start.11 = (bf16[2,512,128]{2,1,0:T(8,128)(2,1)}, bf16[2,512,128]{2,1,0:T(8,128)(2,1)S(1)}, u32[]{:S(2)}, u32[]{:S(2)}) collective-permute-start(bf16[2,512,128]{2,1,0:T(8,128)(2,1)} %get-tuple-element.50.own), channel_id=1, source_target_pairs={{0,2},{1,3},{2,0},{3,1},{4,6},{5,7},{6,4},{7,5},{8,10},{9,11},{10,... | collective-permute-start | bytes 786440 | tf_op jit(solution)/shard_map/ppermute | solution.py:26
  169.5 4.3 %collective-permute-start.12 = (bf16[2,512,128]{2,1,0:T(8,128)(2,1)}, bf16[2,512,128]{2,1,0:T(8,128)(2,1)S(1)}, u32[]{:S(2)}, u32[]{:S(2)}) collective-permute-start(bf16[2,512,128]{2,1,0:T(8,128)(2,1)} %get-tuple-element.50.own), channel_id=1, source_target_pairs={{0,4},{1,5},{2,6},{3,7},{4,0},{5,1},{6,2},{7,3},{8,12},{9,13},{10,... | collective-permute-start | bytes 786440 | tf_op jit(solution)/shard_map/ppermute | solution.py:26
  182.1 2.9 %collective-permute-start.10 = (bf16[8,512,128]{2,1,0:T(8,128)(2,1)S(1)}, bf16[8,512,128]{2,1,0:T(8,128)(2,1)}, u32[]{:S(2)}, u32[]{:S(2)}) collective-permute-start(bf16[8,512,128]{2,1,0:T(8,128)(2,1)S(1)} %shard_map.140.own), channel_id=1, source_target_pairs={{0,8},{8,0},{1,9},{9,1},{2,10},{10,2},{3,11},{11,3},{4,12},{12,4},... | collective-permute-start | bytes 3145736 | tf_op jit(solution)/shard_map/ppermute | solution.py:21
  186.5 4.9 %collective-permute-done.13.three = bf16[2,512,128]{2,1,0:T(8,128)(2,1)S(1)} collective-permute-done((bf16[2,512,128]{2,1,0:T(8,128)(2,1)}, bf16[2,512,128]{2,1,0:T(8,128)(2,1)S(1)}, u32[]{:S(2)}, u32[]{:S(2)}) %collective-permute-start.13) | collective-permute-done | bytes 262176 | tf_op jit(solution)/shard_map/ppermute | solution.py:26
  200.2 10.8 %all_to_all.30.rows = bf16[8,64,128]{2,1,0:T(8,128)(2,1)S(1)} all-to-all(bf16[8,64,128]{2,1,0:T(8,128)(2,1)S(1)} %shard_map.141), channel_id=1, replica_groups=mesh['z'=16,'xl'=2,'c'=2,'t'=8] {'t'}, dimensions={0} | all-to-all | bytes 262144 | tf_op jit(solution)/shard_map/all_to_all | solution.py:17
  212.2 10.1 %all_to_all.31 = bf16[16,64,128]{2,1,0:T(8,128)(2,1)S(1)} all-to-all(bf16[16,64,128]{2,1,0:T(8,128)(2,1)S(1)} %bitcast.10), channel_id=1, replica_groups=mesh['z'=16,'xl'=2,'c'=2,'t'=8] {'xl','t'}, dimensions={0} | all-to-all | bytes 524288 | tf_op jit(solution)/shard_map/all_to_all | solution.py:17
  222.3 4.4 %collective-permute-start.15 = (bf16[2,8,64,128]{3,2,1,0:T(8,128)(2,1)S(1)}, bf16[2,8,64,128]{3,2,1,0:T(8,128)(2,1)S(1)}, u32[]{:S(2)}, u32[]{:S(2)}) collective-permute-start(bf16[2,8,64,128]{3,2,1,0:T(8,128)(2,1)S(1)} %bitcast.8), channel_id=1, source_target_pairs={{0,8},{8,0},{1,9},{9,1},{2,10},{10,2},{3,11},{11,3},{4,12},{12,4},... | collective-permute-start | bytes 786440 | tf_op jit(solution)/shard_map/ppermute | solution.py:21
  229.0 4.6 %shard_map.144 = (bf16[1024,2,128]{2,1,0:T(2,128)(2,1)}, bf16[1,1024,128]{2,1,0:T(8,128)(2,1)}) custom-call(s32[64]{0:T(128)S(1)} %copy-done.25, bf16[8,512,128]{2,1,0:T(8,128)(2,1)S(1)} %shard_map.140.own, bf16[8,512,128]{2,1,0:T(8,128)(2,1)} %collective-permute-done.10.other, bf16[2,8,64,128]{3,2,1,0:T(8,128)(2,1)S(1)} %bitcast.9, ...), custom_call_target="tpu_custom_call" | custom-call | flops 536870912 | bytes 3407872 | tf_op jit(solution)/shard_map/pallas_call | solution.py:34
  (91 shorter events, 46.4 us)
Async XLA Ops:
  7.2 36.4 %copy-start = (bf16[512,2,1024]{2,1,0:T(2,128)(2,1)S(1)}, bf16[512,2,1024]{2,1,0:T(2,128)(2,1)}, u32[]{:S(2)}) copy-start(bf16[512,2,1024]{2,1,0:T(2,128)(2,1)} %cot.3) | copy-start | bytes 6291460
  7.2 36.4 %copy-start.3 = (bf16[512,128]{1,0:T(8,128)(2,1)S(1)}, bf16[512,128]{1,0:T(8,128)(2,1)}, u32[]{:S(2)}) copy-start(bf16[512,128]{1,0:T(8,128)(2,1)} %act.3) | copy-start | bytes 393220
  11.7 10.1 %collective-permute-start.2 = (bf16[1552,128]{1,0:T(8,128)(2,1)S(1)}, bf16[1552,128]{1,0:T(8,128)(2,1)S(1)}, u32[]{:S(2)}, u32[]{:S(2)}) collective-permute-start(bf16[1552,128]{1,0:T(8,128)(2,1)S(1)} %get-tuple-element.34), channel_id=1, source_target_pairs={{0,8},{8,0},{1,9},{9,1},{2,10},{10,2},{3,11},{11,3},{4,12},{12,4},... | collective-permute-start | bytes 1191944 | tf_op jit(solution)/shard_map/ppermute | solution.py:21
  23.2 9.5 %collective-permute-start.3 = (bf16[1040,128]{1,0:T(8,128)(2,1)S(1)}, bf16[1040,128]{1,0:T(8,128)(2,1)S(1)}, u32[]{:S(2)}, u32[]{:S(2)}) collective-permute-start(bf16[1040,128]{1,0:T(8,128)(2,1)S(1)} %get-tuple-element.36), channel_id=1, source_target_pairs={{0,16},{16,0},{1,17},{17,1},{2,18},{18,2},{3,19},{19,3},{4,20},{20... | collective-permute-start | bytes 798728 | tf_op jit(solution)/shard_map/ppermute | solution.py:21
  34.0 26.8 %all-to-all-start = ((bf16[16,80,128]{2,1,0:T(8,128)(2,1)}), bf16[16,80,128]{2,1,0:T(8,128)(2,1)S(1)}, u32[]{:S(2)}, u32[]{:S(2)}) async-start(bf16[16,80,128]{2,1,0:T(8,128)(2,1)} %shard_map.133), calls=%async_computation | async-start | bytes 655360 | tf_op jit(solution)/shard_map/all_to_all | solution.py:17
  43.6 71.7 %all-gather.2.cloned.1.call-start = ((), (), s32[]{:S(2)}) async-start(), calls=%async_computation.6 | async-start | bytes 1179648 | tf_op jit(solution)/shard_map/all_gather | solution.py:353
  45.4 69.9 %copy-start.4 = (bf16[512,128]{1,0:T(8,128)(2,1)S(1)}, bf16[512,128]{1,0:T(8,128)(2,1)}, u32[]{:S(2)}) copy-start(bf16[512,128]{1,0:T(8,128)(2,1)} %act.3) | copy-start | bytes 393220
  45.4 5.0 %collective-permute-start = (bf16[2,16,64,128]{3,2,1,0:T(8,128)(2,1)S(1)}, bf16[2,16,64,128]{3,2,1,0:T(8,128)(2,1)S(1)}, u32[]{:S(2)}, u32[]{:S(2)}) collective-permute-start(bf16[2,16,64,128]{3,2,1,0:T(8,128)(2,1)S(1)} %get-tuple-element.30), channel_id=1, source_target_pairs={{0,8},{8,0},{1,9},{9,1},{2,10},{10,2},{3,11},{11,3},{4,12},{12,4},... | collective-permute-start | bytes 1572872 | tf_op jit(solution)/shard_map/ppermute | solution.py:21
  51.2 9.6 %collective-permute-start.1 = (bf16[16,64,128]{2,1,0:T(8,128)(2,1)}, bf16[16,64,128]{2,1,0:T(8,128)(2,1)S(1)}, u32[]{:S(2)}, u32[]{:S(2)}) collective-permute-start(bf16[16,64,128]{2,1,0:T(8,128)(2,1)} %get-tuple-element.32), channel_id=1, source_target_pairs={{0,16},{16,0},{1,17},{17,1},{2,18},{18,2},{3,19},{19,3},{4,20},{20... | collective-permute-start | bytes 786440 | tf_op jit(solution)/shard_map/ppermute | solution.py:21
  62.2 64.3 %all-to-all-start.1 = ((bf16[16,128,128]{2,1,0:T(8,128)(2,1)}), bf16[16,128,128]{2,1,0:T(8,128)(2,1)S(1)}, u32[]{:S(2)}, u32[]{:S(2)}) async-start(bf16[16,128,128]{2,1,0:T(8,128)(2,1)} %get-tuple-element.37), calls=%async_computation.1 | async-start | bytes 1048576 | tf_op jit(solution)/shard_map/all_to_all | solution.py:17
  117.1 4.4 %collective-permute-start.4 = (bf16[16,2,16,128]{3,2,1,0:T(8,128)(2,1)S(1)}, bf16[16,2,16,128]{3,2,1,0:T(8,128)(2,1)S(1)}, u32[]{:S(2)}, u32[]{:S(2)}) collective-permute-start(bf16[16,2,16,128]{3,2,1,0:T(8,128)(2,1)S(1)} %get-tuple-element.39), channel_id=1, source_target_pairs={{0,8},{8,0},{1,9},{9,1},{2,10},{10,2},{3,11},{11,3},{4,12},{12,4},... | collective-permute-start | bytes 393224 | tf_op jit(solution)/shard_map/ppermute | solution.py:21
  121.5 5.0 %collective-permute-start.5 = (bf16[16,16,128]{2,1,0:T(8,128)(2,1)S(1)}, bf16[16,16,128]{2,1,0:T(8,128)(2,1)S(1)}, u32[]{:S(2)}, u32[]{:S(2)}) collective-permute-start(bf16[16,16,128]{2,1,0:T(8,128)(2,1)S(1)} %get-tuple-element.41), channel_id=1, source_target_pairs={{0,16},{16,0},{1,17},{17,1},{2,18},{18,2},{3,19},{19,3},{4,20},{20... | collective-permute-start | bytes 196616 | tf_op jit(solution)/shard_map/ppermute | solution.py:21
  127.3 31.1 %all-to-all-start.2 = ((bf16[16,48,128]{2,1,0:T(8,128)(2,1)}), bf16[16,48,128]{2,1,0:T(8,128)(2,1)S(1)}, u32[]{:S(2)}, u32[]{:S(2)}) async-start(bf16[16,48,128]{2,1,0:T(8,128)(2,1)} %get-tuple-element.42), calls=%async_computation.2 | async-start | bytes 393216 | tf_op jit(solution)/shard_map/all_to_all | solution.py:17
  139.3 9.4 %collective-permute-start.6 = (bf16[1024,128]{1,0:T(8,128)(2,1)S(1)}, bf16[1024,128]{1,0:T(8,128)(2,1)S(1)}, u32[]{:S(2)}, u32[]{:S(2)}) collective-permute-start(bf16[1024,128]{1,0:T(8,128)(2,1)S(1)} %get-tuple-element.44.own), channel_id=1, source_target_pairs={{0,1},{1,0},{2,3},{3,2},{4,5},{5,4},{6,7},{7,6},{8,9},{9,8},{10,11... | collective-permute-start | bytes 786440 | tf_op jit(solution)/shard_map/ppermute | solution.py:26
  148.7 25.1 %collective-permute-start.7 = (bf16[2,512,128]{2,1,0:T(8,128)(2,1)S(1)}, bf16[2,512,128]{2,1,0:T(8,128)(2,1)S(1)}, u32[]{:S(2)}, u32[]{:S(2)}) collective-permute-start(bf16[2,512,128]{2,1,0:T(8,128)(2,1)S(1)} %get-tuple-element.48.own), channel_id=1, source_target_pairs={{0,2},{1,3},{2,0},{3,1},{4,6},{5,7},{6,4},{7,5},{8,10},{9,11},{10,... | collective-permute-start | bytes 786440 | tf_op jit(solution)/shard_map/ppermute | solution.py:26
  150.7 25.9 %collective-permute-start.8 = (bf16[2,512,128]{2,1,0:T(8,128)(2,1)S(1)}, bf16[2,512,128]{2,1,0:T(8,128)(2,1)S(1)}, u32[]{:S(2)}, u32[]{:S(2)}) collective-permute-start(bf16[2,512,128]{2,1,0:T(8,128)(2,1)S(1)} %get-tuple-element.48.own), channel_id=1, source_target_pairs={{0,4},{1,5},{2,6},{3,7},{4,0},{5,1},{6,2},{7,3},{8,12},{9,13},{10,... | collective-permute-start | bytes 786440 | tf_op jit(solution)/shard_map/ppermute | solution.py:26
  154.3 23.0 %collective-permute-start.9 = (bf16[2,512,128]{2,1,0:T(8,128)(2,1)S(1)}, bf16[2,512,128]{2,1,0:T(8,128)(2,1)}, u32[]{:S(2)}, u32[]{:S(2)}) collective-permute-start(bf16[2,512,128]{2,1,0:T(8,128)(2,1)S(1)} %get-tuple-element.48.own), channel_id=1, source_target_pairs={{0,6},{1,7},{2,4},{3,5},{4,2},{5,3},{6,0},{7,1},{8,14},{9,15},{10,... | collective-permute-start | bytes 786440 | tf_op jit(solution)/shard_map/ppermute | solution.py:26
  159.3 32.8 %all-to-all-start.3 = ((bf16[16,80,128]{2,1,0:T(8,128)(2,1)}), bf16[16,80,128]{2,1,0:T(8,128)(2,1)S(1)}, u32[]{:S(2)}, u32[]{:S(2)}) async-start(bf16[16,80,128]{2,1,0:T(8,128)(2,1)} %bitcast.1), calls=%async_computation.3 | async-start | bytes 655360 | tf_op jit(solution)/shard_map/all_to_all | solution.py:17
  166.2 18.8 %collective-permute-start.11 = (bf16[2,512,128]{2,1,0:T(8,128)(2,1)}, bf16[2,512,128]{2,1,0:T(8,128)(2,1)S(1)}, u32[]{:S(2)}, u32[]{:S(2)}) collective-permute-start(bf16[2,512,128]{2,1,0:T(8,128)(2,1)} %get-tuple-element.50.own), channel_id=1, source_target_pairs={{0,2},{1,3},{2,0},{3,1},{4,6},{5,7},{6,4},{7,5},{8,10},{9,11},{10,... | collective-permute-start | bytes 786440 | tf_op jit(solution)/shard_map/ppermute | solution.py:26
  169.5 16.3 %collective-permute-start.12 = (bf16[2,512,128]{2,1,0:T(8,128)(2,1)}, bf16[2,512,128]{2,1,0:T(8,128)(2,1)S(1)}, u32[]{:S(2)}, u32[]{:S(2)}) collective-permute-start(bf16[2,512,128]{2,1,0:T(8,128)(2,1)} %get-tuple-element.50.own), channel_id=1, source_target_pairs={{0,4},{1,5},{2,6},{3,7},{4,0},{5,1},{6,2},{7,3},{8,12},{9,13},{10,... | collective-permute-start | bytes 786440 | tf_op jit(solution)/shard_map/ppermute | solution.py:26
  174.6 16.8 %collective-permute-start.13 = (bf16[2,512,128]{2,1,0:T(8,128)(2,1)}, bf16[2,512,128]{2,1,0:T(8,128)(2,1)S(1)}, u32[]{:S(2)}, u32[]{:S(2)}) collective-permute-start(bf16[2,512,128]{2,1,0:T(8,128)(2,1)} %get-tuple-element.50.own), channel_id=1, source_target_pairs={{0,6},{1,7},{2,4},{3,5},{4,2},{5,3},{6,0},{7,1},{8,14},{9,15},{10,... | collective-permute-start | bytes 786440 | tf_op jit(solution)/shard_map/ppermute | solution.py:26
  182.1 16.3 %collective-permute-start.10 = (bf16[8,512,128]{2,1,0:T(8,128)(2,1)S(1)}, bf16[8,512,128]{2,1,0:T(8,128)(2,1)}, u32[]{:S(2)}, u32[]{:S(2)}) collective-permute-start(bf16[8,512,128]{2,1,0:T(8,128)(2,1)S(1)} %shard_map.140.own), channel_id=1, source_target_pairs={{0,8},{8,0},{1,9},{9,1},{2,10},{10,2},{3,11},{11,3},{4,12},{12,4},... | collective-permute-start | bytes 3145736 | tf_op jit(solution)/shard_map/ppermute | solution.py:21
  196.0 15.1 %collective-permute-start.14 = (bf16[8,512,128]{2,1,0:T(8,128)(2,1)S(1)}, bf16[8,512,128]{2,1,0:T(8,128)(2,1)S(1)}, u32[]{:S(2)}, u32[]{:S(2)}) collective-permute-start(bf16[8,512,128]{2,1,0:T(8,128)(2,1)S(1)} %shard_map.142.own), channel_id=1, source_target_pairs={{0,8},{8,0},{1,9},{9,1},{2,10},{10,2},{3,11},{11,3},{4,12},{12,4},... | collective-permute-start | bytes 3145736 | tf_op jit(solution)/shard_map/ppermute | solution.py:21
  222.3 6.7 %collective-permute-start.15 = (bf16[2,8,64,128]{3,2,1,0:T(8,128)(2,1)S(1)}, bf16[2,8,64,128]{3,2,1,0:T(8,128)(2,1)S(1)}, u32[]{:S(2)}, u32[]{:S(2)}) collective-permute-start(bf16[2,8,64,128]{3,2,1,0:T(8,128)(2,1)S(1)} %bitcast.8), channel_id=1, source_target_pairs={{0,8},{8,0},{1,9},{9,1},{2,10},{10,2},{3,11},{11,3},{4,12},{12,4},... | collective-permute-start | bytes 786440 | tf_op jit(solution)/shard_map/ppermute | solution.py:21
  (23 other events, 122.1 us)
Sparse Core Ops, SparseCore 0:
  54.5 60.7 all-gather.1

commit v5 on v4

--- a/solution.py
+++ b/solution.py
@@ -21,26 +21,29 @@
     return lax.ppermute(array, axis, [(0, 1), (1, 0)])
 
 
-def across(array, axis, step):
-    pairs = [(i, i ^ step) for i in range(lax.axis_size(axis))]
-    return lax.ppermute(array, axis, pairs)
-
-
-def call(body, outs, scalars, args, places=None, scratch=(), flops=0):
-    bytes_all = sum(a.size * a.dtype.itemsize for a in args) + sum(
-        o.size * o.dtype.itemsize for o in outs
-    )
+def call(body, outs, scalars, args, places=None, scratch=(), flops=0, limit=40):
     places = places or [pltpu.VMEM] * len(args)
+    specs, arrays = [], []
+    for arg, place in zip(args, places):
+        if isinstance(arg, tuple):
+            array, rows, block = arg
+            shape = (array.shape[0], rows, array.shape[2])
+            specs.append(pl.BlockSpec(shape, functools.partial(lambda k, i: (0, k, 0), block)))
+        else:
+            array = arg
+            specs.append(pl.BlockSpec(memory_space=place))
+        arrays.append(array)
+    bytes_all = sum(a.size * a.dtype.itemsize for a in arrays + list(outs))
     return pl.pallas_call(
         body,
+        grid=(1,),
         out_shape=outs,
-        in_specs=[pl.BlockSpec(memory_space=pltpu.SMEM)] * len(scalars)
-        + [pl.BlockSpec(memory_space=place) for place in places],
+        in_specs=[pl.BlockSpec(memory_space=pltpu.SMEM)] * len(scalars) + specs,
         out_specs=[pl.BlockSpec(memory_space=pltpu.VMEM)] * len(outs),
         scratch_shapes=list(scratch),
-        compiler_params=pltpu.CompilerParams(vmem_limit_bytes=40 * 1024 * 1024),
+        compiler_params=pltpu.CompilerParams(vmem_limit_bytes=limit * 1024 * 1024),
         cost_estimate=pl.CostEstimate(flops=flops, bytes_accessed=bytes_all, transcendentals=0),
-    )(*scalars, *args)
+    )(*scalars, *arrays)
 
 
 def out(shape, dtype=bf16):
@@ -135,25 +138,31 @@
         sent[k, 2 * per :] = vals
 
 
-def terms(cot, act, sent, keep, packed, flat):
+def terms(cot, act, whole, sent, keep, packed, flat, cov):
     _, _, nz, height, slab = packed.shape
     tok, blocks, full = cot.shape
     nt = full // slab
     per = full // 2 // nz
-    group = (height - per) // 2
+    group = (height - per) // 3
     scale = 1.0 / (tok * nz * 4)
     flat[...] = cot[...].reshape(tok, blocks * full)
     t = lax.axis_index("t")
+    for k in range(nt):
+        cov[k * slab : (k + 1) * slab] = dot(whole[k], act[...], ((0,), (0,))) * scale
+    place = slice(per + 2 * group, height)
+    for c in range(2):
+        for xl in range(2):
+            packed[c, xl, :, place] = cov[...].reshape(nz, 2, 2, group, slab)[:, xl, c]
     for j in range(2):
         own = flat[:, pl.ds(pl.multiple_of(j * full + t * slab, slab), slab)]
         right = jnp.concatenate([act[...], own], 1)
         both = dot(flat[:, j * full : (j + 1) * full], right, ((0,), (0,))) * scale
         grad = both[:, :slab].reshape(nt, 2, slab // 2, slab)
-        cov = both[:, slab:].reshape(nz, 2, 2, group, slab)
+        out_cov = both[:, slab:].reshape(nz, 2, 2, group, slab)
         for c in range(2):
             packed[c, j, :, 0:per] = grad[:, c].reshape(nz, per, slab)
             for xl in range(2):
-                packed[c, xl, :, per + j * group : per + (j + 1) * group] = cov[:, xl, c]
+                packed[c, xl, :, per + j * group : per + (j + 1) * group] = out_cov[:, xl, c]
     core = lax.axis_index("c")
     sent[...] = packed[1 - core].astype(bf16)
     keep[...] = packed[core]
@@ -182,56 +191,29 @@
     vals[...] = chosen.astype(bf16)
 
 
-def reduce_z(got, a_keep, a_got, sent, factor_g, bases):
+def reduce_z(got, vals, grad, factor_a, factor_g, sent):
     nz, _, slab = got.shape
-    group = a_keep.shape[1]
-    half = bases.shape[0] // 2
-    per = half // nz
-    height = per + 2 * group
+    group = factor_a.shape[0]
+    per = grad.shape[0]
+    half = nz * per
+    height = per + 3 * group
     total = got[0, 0:height].astype(f32)
     for k in range(1, nz):
         total = total + got[k, 0:height].astype(f32)
-    grad = total[0:per].astype(bf16)
-    for k in range(nz):
-        sent[k, 0:per] = grad
-    sent[:, per:] = (a_keep[...] + a_got[...].astype(f32)).astype(bf16)
+    grad[...] = total[0:per].astype(bf16)
     for j in range(2):
         factor_g[j] = total[per + j * group : per + (j + 1) * group]
-    bases[0:half] = got[:, height : height + per].reshape(half, slab)
-    bases[half:] = got[:, height + per :].reshape(half, slab)
-
-
-def pair_bases(own, got, qa, qg):
-    half = own.shape[0] // 2
-    side = lax.axis_index("t") % 2
-    for slot, ref in ((side, own), (1 - side, got)):
-        qa[slot] = ref[0:half]
-        qg[slot] = ref[half:]
-
-
-def stack_pairs(own, one, two, three, after, whole):
-    first = lax.axis_index("t") // 2
-    for k, pair in enumerate((own, one, two, three)):
-        for side in range(2):
-            whole[2 * (first ^ k) + side] = pair[side]
-
-
-def pack_t(got, vals, pair, sent, factor_a, same):
-    nz, height, slab = got.shape
-    group = factor_a.shape[0]
-    per = height - group
-    nt, width, _ = sent.shape[1:]
-    piece = width - VALS
-    grad = got[:, 0:per].reshape(nz * per, slab).reshape(nt, piece, slab)
+    factor_a[...] = total[per + 2 * group :]
+    for k in range(sent.shape[0]):
+        sent[k, 0:half] = got[:, height : height + per].reshape(half, slab)
+        sent[k, half : 2 * half] = got[:, height + per :].reshape(half, slab)
+        sent[k, 2 * half :] = vals[...]
+
+
+def pack_t(grad, sent):
+    nt, piece, slab = sent.shape[1:]
     for c in range(2):
-        sent[c, :, 0:piece] = grad
-        for k in range(nt):
-            sent[c, k, piece:] = vals[...]
-    total = got[0, per:].astype(f32)
-    for k in range(1, nz):
-        total = total + got[k, per:].astype(f32)
-    factor_a[...] = total
-    same[...] = pair[...]
+        sent[c] = grad[...].reshape(nt, piece, slab)
 
 
 def rotate(got, own, other, sent, grad):
@@ -251,11 +233,11 @@
         sent[2 * i + 1] = turned[piece:]
 
 
-def scale_rows(rows, own, other, got, sent, rot, scaled, column):
+def scale_rows(rows, own, other, vals, sent, rot, scaled, column):
     nt, piece, slab = rows.shape
     half = own.shape[1]
     core, xl, t = lax.axis_index("c"), lax.axis_index("xl"), lax.axis_index("t")
-    row = got[0, core * (nt // 2) + t // 2, piece:].astype(f32)[0:1]
+    row = vals[core * (nt // 2) + t // 2].astype(f32)[0:1]
     column[...] = jnp.broadcast_to(row, (slab, slab)).T
     la = column[pl.ds(pl.multiple_of((t % 2) * piece, piece), piece)]
     for k in range(nt):
@@ -264,7 +246,7 @@
     far = rot[:, pl.ds(pl.multiple_of((1 - core) * half, half), half)]
     for k in range(nt):
         spectral = dot(near, own[k]) + dot(far, other[k])
-        values = got[0, k, piece:].astype(f32)
+        values = vals[k].astype(f32)
         lg = jnp.where(xl == 0, values[1:2], values[2:3])
         scaled[k] = (spectral / (la * lg + damping)).astype(bf16)
     for side, ref in ((core, own), (1 - core, other)):
@@ -310,21 +292,6 @@
     grad[...] = dot(left, right, ((1,), (1,))).astype(bf16)
 
 
-def input_factor(whole, act, sent, keep, packed):
-    nz, _, _, group, slab = packed.shape
-    scale = 1.0 / (act.shape[0] * nz * 4)
-    packed[...] = (dot(whole[...], act[...], ((0,), (0,))) * scale).reshape(packed.shape)
-    core = lax.axis_index("c")
-    sent[...] = packed[:, :, 1 - core].astype(bf16)
-    keep[...] = packed[:, :, core]
-
-
-def input_factor_core(keep, got, sent, rest):
-    xl = lax.axis_index("xl")
-    sent[...] = (keep[:, 1 - xl] + got[:, 1 - xl].astype(f32)).astype(bf16)
-    rest[...] = keep[:, xl] + got[:, xl].astype(f32)
-
-
 def local(act, cot, weight, owners, worker_group, basis_a, values_a, basis_g, values_g):
     tok, slab = act.shape
     blocks, full = cot.shape[1:]
@@ -332,7 +299,9 @@
     group = full // (nz * 4)
     half, piece = full // 2, slab // 2
     per = half // nz
-    height = per + blocks * group
+    height = per + (blocks + 1) * group
+
+    whole_act = exchange(jnp.broadcast_to(act[None], (nt, tok, slab)), "t")
 
     shape = (3 * half + VALS, slab)
     sent, keep = call(
@@ -340,8 +309,9 @@
         [out(shape), out(shape)],
         [],
         [basis_a, basis_g, values_a, values_g],
-        [pltpu.HBM, pltpu.HBM, pltpu.VMEM, pltpu.VMEM],
+        [pl.ANY, pl.ANY, pltpu.VMEM, pltpu.VMEM],
         scratch=[pltpu.SemaphoreType.DMA((2, 3))],
+        limit=56,
     )
     got = swap(sent, "c")
     shape = (2 * half + VALS, slab)
@@ -350,16 +320,18 @@
     (sent,) = call(select_x, [out((nz, 2 * per + VALS, slab))], [owners], [keep, got])
     got_bases = exchange(sent, "z")
 
-    whole_act = lax.all_gather(act, "t", axis=1, tiled=True)
-
     block = (2, nz, height, slab)
     sent, keep = call(
         terms,
         [out(block), out(block, f32)],
         [],
-        [cot, act],
-        scratch=[pltpu.VMEM((2,) + block, f32), pltpu.VMEM((tok, blocks * full), bf16)],
-        flops=8 * tok * full * slab,
+        [cot, act, whole_act],
+        scratch=[
+            pltpu.VMEM((2,) + block, f32),
+            pltpu.VMEM((tok, blocks * full), bf16),
+            pltpu.VMEM((full, slab), f32),
+        ],
+        flops=10 * tok * full * slab,
     )
     got = swap(sent, "c")
     sent, keep = call(add_core, [out(block[1:]), out(block[1:], f32)], [], [keep, got])
@@ -373,52 +345,30 @@
     )
     got = exchange(sent, "z")
 
-    block = (nz, 2, group, slab)
-    sent, keep = call(
-        input_factor,
-        [out(block), out(block, f32)],
+    width = 2 * half + VALS
+    grad, factor_a, factor_g, sent = call(
+        reduce_z,
+        [
+            out((per, slab)),
+            out((group, slab), f32),
+            out((blocks, group, slab), f32),
+            out((nt, width, slab)),
+        ],
         [],
-        [whole_act, act],
-        scratch=[pltpu.VMEM((nz, 2, 2, group, slab), f32)],
-        flops=2 * tok * full * slab,
-    )
-    a_got = swap(sent, "c")
-    block = (nz, group, slab)
-    sent, keep = call(input_factor_core, [out(block), out(block, f32)], [], [keep, a_got])
-    a_got = swap(sent, "xl")
-
-    sent, factor_g, bases = call(
-        reduce_z,
-        [out((nz, per + group, slab)), out((blocks, group, slab), f32), out((2 * half, slab))],
-        [],
-        [got, keep, a_got],
-    )
-    pair = out((2, half, slab))
-    whole = out((nt, half, slab))
-    orders = [pltpu.VMEM] * 4 + [pl.ANY]
-    got = exchange(sent, "z")
-    near = across(bases, "t", 1)
-    qa, qg = call(pair_bases, [pair, pair], [], [bases, near])
-    pairs = [qa] + [across(qa, "t", 2 * k) for k in range(1, nt // 2)]
-    (qa_own,) = call(stack_pairs, [whole], [], pairs + [got], orders)
-    qa_other = swap(qa_own, "c")
-
-    sent, factor_a, qg = call(
-        pack_t,
-        [out((2, nt, piece + VALS, slab)), out((group, slab), f32), pair],
-        [],
-        [got, vals, qg],
-    )
-    columns = exchange(sent.reshape(2 * nt, piece + VALS, slab), ("c", "t"))
-    columns = columns.reshape(2, nt, piece + VALS, slab)
-    pairs = [qg] + [across(qg, "t", 2 * k) for k in range(1, nt // 2)]
-    (qg_own,) = call(stack_pairs, [whole], [], pairs + [columns], orders)
-    qg_other = swap(qg_own, "c")
+        [got, vals],
+    )
+    own = exchange(sent, "t")
+    grad = lax.all_gather(grad, "z", axis=0, tiled=True)
+    other = swap(own, "c")
+
+    (sent,) = call(pack_t, [out((2, nt, piece, slab))], [], [grad])
+    columns = exchange(sent.reshape(2 * nt, piece, slab), ("c", "t"))
+    columns = columns.reshape(2, nt, piece, slab)
     (sent,) = call(
         rotate,
         [out((nt, piece, slab))],
         [],
-        [columns, qa_own, qa_other],
+        [columns, (own, half, 0), (other, half, 0)],
         scratch=[pltpu.VMEM((slab, full), bf16)],
         flops=2 * slab * full * half,
     )
@@ -427,7 +377,7 @@
         scale_rows,
         [out((blocks, nt, piece, slab))],
         [],
-        [rows, qg_own, qg_other, columns],
+        [rows, (own, half, 1), (other, half, 1), (own, VALS, 2 * half // VALS)],
         scratch=[
             pltpu.VMEM((piece, full), bf16),
             pltpu.VMEM((nt, piece, slab), bf16),
@@ -442,7 +392,7 @@
         finish,
         [out((full, blocks, slab)), out((1, full, slab))],
         [worker_group],
-        [qa_own, qa_other, own_mixed, other_mixed],
+        [(own, half, 0), (other, half, 0), own_mixed, other_mixed],
         flops=4 * full * full * slab,
     )
 

time: 242 us -> 223 us (0.921)
  blocking collectives: 20.9 us -> 135 us
  waiting for transfers between devices: 73.2 us -> 19.3 us
  starting transfers between devices: 95.2 us -> 45.9 us
  between operations: 14.4 us -> 0.78 us
  local copies, waits for them, and re-layouts: 16.1 us -> 4.57 us
  Pallas kernels: 20.5 us -> 16.9 us
    all_to_all x2 -> x5, blocking collectives: 20.9 us -> 112 us  [exchange(): return lax.all_to_all(array, axis, 0, 0, tiled=True)]
    all_gather x1 -> x0, waiting for transfers between devices: 41.3 us -> none  [local(): whole_act = lax.all_gather(act, 't', axis=1, tiled=True)]
    all_gather x0 -> x1, blocking collectives: none -> 22.9 us  [local(): grad = lax.all_gather(grad, 'z', axis=0, tiled=True)]
    ppermute x7 -> x0, starting transfers between devices: 22.2 us -> none  [across(): return lax.ppermute(array, axis, pairs)]
    all_to_all x4 -> x2, starting transfers between devices: 40.2 us -> 20.5 us  [exchange(): return lax.all_to_all(array, axis, 0, 0, tiled=True)]
    unnamed x53 -> x13, local copies, waits for them, and re-layouts: 16.1 us -> 2.53 us
    ppermute x7 -> x0, waiting for transfers between devices: 11.3 us -> none  [across(): return lax.ppermute(array, axis, pairs)]
    ppermute x9 -> x6, starting transfers between devices: 32.8 us -> 25.4 us  [swap(): return lax.ppermute(array, axis, [(0, 1), (1, 0)])]
  transfers between devices with their start and end apart: 21 -> 8, of which waited for: 9 -> 5; matrix products, arithmetic and copies ran while one was open for 0% -> 0% of each run, Pallas kernels for 5% -> 4%
where the time goes in v5:
time: 223 us; the launch traced here: 222 us
  blocking collectives  135 us (61%)
  starting transfers between devices  45.9 us (21%)
  waiting for transfers between devices  19.3 us (9%)
  Pallas kernels  16.9 us (8%)
  local copies, waits for them, and re-layouts  4.57 us (2%)
    all_to_all x5, blocking collectives, exchange(): return lax.all_to_all(array, axis, 0, 0, tiled=True)  112 us
    ppermute x6, starting transfers between devices, swap(): return lax.ppermute(array, axis, [(0, 1), (1, 0)])  25.4 us
    all_gather x1, blocking collectives, local(): grad = lax.all_gather(grad, 'z', axis=0, tiled=True)  22.9 us
    all_to_all x2, starting transfers between devices, exchange(): return lax.all_to_all(array, axis, 0, 0, tiled=True)  20.5 us
    pallas_call x12, Pallas kernels, call(): pl.pallas_call(body, grid=(1,), out_shape=outs, in_specs=[pl.BlockSpec(me...  16.9 us
    ppermute x6, waiting for transfers between devices, swap(): return lax.ppermute(array, axis, [(0, 1), (1, 0)])  16.6 us
  transfers between devices with their start and end apart: 8, of which 5 were waited for; matrix products, arithmetic and copies ran while one was open for 0% of the time, Pallas kernels for 4%

profile of v5, /device:TPU:1, one launch (start us, length us, event | category | flops | bytes accessed | tf_op | source)
XLA Modules:
  0.0 222.4 jit_solution(18216039735918119245)
XLA Ops:
  0.6 2.0 broadcast_in_dim.2
  2.7 7.6 %all-to-all-start = ((bf16[8,512,128]{2,1,0:T(8,128)(2,1)}), bf16[8,512,128]{2,1,0:T(8,128)(2,1)S(1)}, u32[]{:S(2)}, u32[]{:S(2)}) async-start(bf16[8,512,128]{2,1,0:T(8,128)(2,1)} %broadcast_in_dim.2), calls=%async_computation | async-start | bytes 2097152 | tf_op jit(solution)/shard_map/all_to_all | solution.py:17
  10.3 2.8 %shard_map.131 = (bf16[1552,128]{1,0:T(8,128)(2,1)}, bf16[1552,128]{1,0:T(8,128)(2,1)}) custom-call(bf16[1,1024,128]{2,1,0:T(8,128)(2,1)} %ba.1, bf16[1,2,1024,128]{3,2,1,0:T(8,128)(2,1)} %bg.1, bf16[1,128]{1,0:T(2,128)(2,1)} %va.1, bf16[1,2,128]{2,1,0:T(2,128)(2,1)} %vg.1), custom_call_target="tpu_custom_call" | custom-call | bytes 1581824 | tf_op jit(solution)/shard_map/pallas_call | solution.py:37
  13.1 4.9 %collective-permute-start.2 = (bf16[1552,128]{1,0:T(8,128)(2,1)}, bf16[1552,128]{1,0:T(8,128)(2,1)S(1)}, u32[]{:S(2)}, u32[]{:S(2)}) collective-permute-start(bf16[1552,128]{1,0:T(8,128)(2,1)} %get-tuple-element.26), channel_id=1, source_target_pairs={{0,8},{8,0},{1,9},{9,1},{2,10},{10,2},{3,11},{11,3},{4,12},{12,4},... | collective-permute-start | bytes 1191944 | tf_op jit(solution)/shard_map/ppermute | solution.py:21
  18.0 1.5 collective-permute-done.2.got
  21.2 1.9 collective-permute-start.3
  23.1 7.6 %collective-permute-done.3.got = bf16[1040,128]{1,0:T(8,128)(2,1)S(1)} collective-permute-done((bf16[1040,128]{1,0:T(8,128)(2,1)S(1)}, bf16[1040,128]{1,0:T(8,128)(2,1)S(1)}, u32[]{:S(2)}, u32[]{:S(2)}) %collective-permute-start.3) | collective-permute-done | bytes 266272 | tf_op jit(solution)/shard_map/ppermute | solution.py:21
  32.1 12.9 %all-to-all-start.1 = ((bf16[16,80,128]{2,1,0:T(8,128)(2,1)}), bf16[16,80,128]{2,1,0:T(8,128)(2,1)S(1)}, u32[]{:S(2)}, u32[]{:S(2)}) async-start(bf16[16,80,128]{2,1,0:T(8,128)(2,1)} %shard_map.133), calls=%async_computation.1 | async-start | bytes 655360 | tf_op jit(solution)/shard_map/all_to_all | solution.py:17
  45.9 2.2 shard_map.129
  48.1 3.4 %collective-permute-start = (bf16[2,16,80,128]{3,2,1,0:T(8,128)(2,1)S(1)}, bf16[2,16,80,128]{3,2,1,0:T(8,128)(2,1)S(1)}, u32[]{:S(2)}, u32[]{:S(2)}) collective-permute-start(bf16[2,16,80,128]{3,2,1,0:T(8,128)(2,1)S(1)} %get-tuple-element.22), channel_id=1, source_target_pairs={{0,8},{8,0},{1,9},{9,1},{2,10},{10,2},{3,11},{11,3},{4,12},{12,4},... | collective-permute-start | bytes 1966088 | tf_op jit(solution)/shard_map/ppermute | solution.py:21
  51.5 1.7 collective-permute-done.got
  54.0 2.5 %collective-permute-start.1 = (bf16[16,80,128]{2,1,0:T(8,128)(2,1)}, bf16[16,80,128]{2,1,0:T(8,128)(2,1)S(1)}, u32[]{:S(2)}, u32[]{:S(2)}) collective-permute-start(bf16[16,80,128]{2,1,0:T(8,128)(2,1)} %get-tuple-element.24), channel_id=1, source_target_pairs={{0,16},{16,0},{1,17},{17,1},{2,18},{18,2},{3,19},{19,3},{4,20},{20... | collective-permute-start | bytes 983048 | tf_op jit(solution)/shard_map/ppermute | solution.py:21
  56.5 2.7 %all-to-all-done.1.bases = bf16[16,80,128]{2,1,0:T(8,128)(2,1)S(1)} async-done(((bf16[16,80,128]{2,1,0:T(8,128)(2,1)}), bf16[16,80,128]{2,1,0:T(8,128)(2,1)S(1)}, u32[]{:S(2)}, u32[]{:S(2)}) %all-to-all-start.1) | async-done | bytes 327712 | tf_op jit(solution)/shard_map/all_to_all | solution.py:17
  59.2 5.8 %collective-permute-done.1.got = bf16[16,80,128]{2,1,0:T(8,128)(2,1)S(1)} collective-permute-done((bf16[16,80,128]{2,1,0:T(8,128)(2,1)}, bf16[16,80,128]{2,1,0:T(8,128)(2,1)S(1)}, u32[]{:S(2)}, u32[]{:S(2)}) %collective-permute-start.1) | collective-permute-done | bytes 327712 | tf_op jit(solution)/shard_map/ppermute | solution.py:21
  65.6 43.4 %all_to_all.35.got = bf16[16,144,128]{2,1,0:T(8,128)(2,1)S(1)} all-to-all(bf16[16,144,128]{2,1,0:T(8,128)(2,1)S(1)} %get-tuple-element.29), channel_id=1, replica_groups=mesh['z'=16,'xl'=2,'c'=2,'t'=8] {'z'}, dimensions={0} | all-to-all | bytes 1179648 | tf_op jit(solution)/shard_map/all_to_all | solution.py:17
  109.9 31.1 %all_to_all.36.own.vals = bf16[8,1040,128]{2,1,0:T(8,128)(2,1)S(1)} all-to-all(bf16[8,1040,128]{2,1,0:T(8,128)(2,1)S(1)} %get-tuple-element.33), channel_id=1, replica_groups=mesh['z'=16,'xl'=2,'c'=2,'t'=8] {'t'}, dimensions={0} | all-to-all | bytes 4259840 | tf_op jit(solution)/shard_map/all_to_all | solution.py:17
  141.0 7.4 %collective-permute-start.4 = (bf16[8,1040,128]{2,1,0:T(8,128)(2,1)S(1)}, bf16[8,1040,128]{2,1,0:T(8,128)(2,1)S(1)}, u32[]{:S(2)}, u32[]{:S(2)}) collective-permute-start(bf16[8,1040,128]{2,1,0:T(8,128)(2,1)S(1)} %all_to_all.36.own.vals), channel_id=1, source_target_pairs={{0,8},{8,0},{1,9},{9,1},{2,10},{10,2},{3,11},{11,3},{4,12},{12,4},... | collective-permute-start | bytes 6389768 | tf_op jit(solution)/shard_map/ppermute | solution.py:21
  148.5 22.9 %all_gather.3.grad = bf16[512,128]{1,0:T(8,128)(2,1)S(1)} all-gather(bf16[32,128]{1,0:T(8,128)(2,1)S(1)} %get-tuple-element.34), channel_id=1, replica_groups=mesh['z'=16,'xl'=2,'c'=2,'t'=8] {'z'}, dimensions={0}, use_global_device_ids=true | all-gather | bytes 139264 | tf_op jit(solution)/shard_map/all_gather | solution.py:361
  171.4 17.5 %all_to_all.37 = bf16[16,64,128]{2,1,0:T(8,128)(2,1)S(1)} all-to-all(bf16[16,64,128]{2,1,0:T(8,128)(2,1)S(1)} %bitcast.9), channel_id=1, replica_groups=mesh['z'=16,'xl'=2,'c'=2,'t'=8] {'c','t'}, dimensions={0} | all-to-all | bytes 524288 | tf_op jit(solution)/shard_map/all_to_all | solution.py:17
  189.6 10.0 %all_to_all.38.rows = bf16[8,64,128]{2,1,0:T(8,128)(2,1)S(1)} all-to-all(bf16[8,64,128]{2,1,0:T(8,128)(2,1)S(1)} %shard_map.137), channel_id=1, replica_groups=mesh['z'=16,'xl'=2,'c'=2,'t'=8] {'t'}, dimensions={0} | all-to-all | bytes 262144 | tf_op jit(solution)/shard_map/all_to_all | solution.py:17
  201.0 10.1 %all_to_all.39 = bf16[16,64,128]{2,1,0:T(8,128)(2,1)S(1)} all-to-all(bf16[16,64,128]{2,1,0:T(8,128)(2,1)S(1)} %bitcast.8), channel_id=1, replica_groups=mesh['z'=16,'xl'=2,'c'=2,'t'=8] {'xl','t'}, dimensions={0} | all-to-all | bytes 524288 | tf_op jit(solution)/shard_map/all_to_all | solution.py:17
  211.0 5.3 %collective-permute-start.5 = (bf16[2,8,64,128]{3,2,1,0:T(8,128)(2,1)S(1)}, bf16[2,8,64,128]{3,2,1,0:T(8,128)(2,1)S(1)}, u32[]{:S(2)}, u32[]{:S(2)}) collective-permute-start(bf16[2,8,64,128]{3,2,1,0:T(8,128)(2,1)S(1)} %bitcast.5), channel_id=1, source_target_pairs={{0,8},{8,0},{1,9},{9,1},{2,10},{10,2},{3,11},{11,3},{4,12},{12,4},... | collective-permute-start | bytes 786440 | tf_op jit(solution)/shard_map/ppermute | solution.py:21
  216.4 1.6 shard_map.128
  218.6 3.9 %shard_map.139 = (bf16[1024,2,128]{2,1,0:T(2,128)(2,1)}, bf16[1,1024,128]{2,1,0:T(8,128)(2,1)}) custom-call(s32[64]{0:T(128)S(1)} %copy-done.5, bf16[8,1040,128]{2,1,0:T(8,128)(2,1)S(1)} %all_to_all.36.own.vals, bf16[8,1040,128]{2,1,0:T(8,128)(2,1)S(1)} %collective-permute-done.4.other, bf16[2,8,64,128]{3,2,1,0:T(8,128)(2,1)S(1)} %bitcast.6, ...), custom_call_target="tpu_custom_call" | custom-call | flops 536870912 | bytes 5570560 | tf_op jit(solution)/shard_map/pallas_call | solution.py:37
  (24 shorter events, 8.9 us)
Async XLA Ops:
  0.6 18.9 %copy-start.4 = (s32[3]{0:T(128)S(1)}, s32[3]{0:T(128)}, u32[]{:S(2)}) copy-start(s32[3]{0:T(128)} %owners.5) | copy-start | bytes 40
  2.7 42.3 %copy-start = (bf16[512,2,1024]{2,1,0:T(2,128)(2,1)S(1)}, bf16[512,2,1024]{2,1,0:T(2,128)(2,1)}, u32[]{:S(2)}) copy-start(bf16[512,2,1024]{2,1,0:T(2,128)(2,1)} %cot.3) | copy-start | bytes 6291460
  2.7 29.4 %all-to-all-start = ((bf16[8,512,128]{2,1,0:T(8,128)(2,1)}), bf16[8,512,128]{2,1,0:T(8,128)(2,1)S(1)}, u32[]{:S(2)}, u32[]{:S(2)}) async-start(bf16[8,512,128]{2,1,0:T(8,128)(2,1)} %broadcast_in_dim.2), calls=%async_computation | async-start | bytes 2097152 | tf_op jit(solution)/shard_map/all_to_all | solution.py:17
  13.1 6.4 %collective-permute-start.2 = (bf16[1552,128]{1,0:T(8,128)(2,1)}, bf16[1552,128]{1,0:T(8,128)(2,1)S(1)}, u32[]{:S(2)}, u32[]{:S(2)}) collective-permute-start(bf16[1552,128]{1,0:T(8,128)(2,1)} %get-tuple-element.26), channel_id=1, source_target_pairs={{0,8},{8,0},{1,9},{9,1},{2,10},{10,2},{3,11},{11,3},{4,12},{12,4},... | collective-permute-start | bytes 1191944 | tf_op jit(solution)/shard_map/ppermute | solution.py:21
  19.6 1.0 copy-start.3
  21.2 9.5 %collective-permute-start.3 = (bf16[1040,128]{1,0:T(8,128)(2,1)S(1)}, bf16[1040,128]{1,0:T(8,128)(2,1)S(1)}, u32[]{:S(2)}, u32[]{:S(2)}) collective-permute-start(bf16[1040,128]{1,0:T(8,128)(2,1)S(1)} %get-tuple-element.28), channel_id=1, source_target_pairs={{0,16},{16,0},{1,17},{17,1},{2,18},{18,2},{3,19},{19,3},{4,20},{20... | collective-permute-start | bytes 798728 | tf_op jit(solution)/shard_map/ppermute | solution.py:21
  32.1 27.2 %all-to-all-start.1 = ((bf16[16,80,128]{2,1,0:T(8,128)(2,1)}), bf16[16,80,128]{2,1,0:T(8,128)(2,1)S(1)}, u32[]{:S(2)}, u32[]{:S(2)}) async-start(bf16[16,80,128]{2,1,0:T(8,128)(2,1)} %shard_map.133), calls=%async_computation.1 | async-start | bytes 655360 | tf_op jit(solution)/shard_map/all_to_all | solution.py:17
  45.0 0.9 copy-start.1
  48.1 5.1 %collective-permute-start = (bf16[2,16,80,128]{3,2,1,0:T(8,128)(2,1)S(1)}, bf16[2,16,80,128]{3,2,1,0:T(8,128)(2,1)S(1)}, u32[]{:S(2)}, u32[]{:S(2)}) collective-permute-start(bf16[2,16,80,128]{3,2,1,0:T(8,128)(2,1)S(1)} %get-tuple-element.22), channel_id=1, source_target_pairs={{0,8},{8,0},{1,9},{9,1},{2,10},{10,2},{3,11},{11,3},{4,12},{12,4},... | collective-permute-start | bytes 1966088 | tf_op jit(solution)/shard_map/ppermute | solution.py:21
  54.0 11.0 %collective-permute-start.1 = (bf16[16,80,128]{2,1,0:T(8,128)(2,1)}, bf16[16,80,128]{2,1,0:T(8,128)(2,1)S(1)}, u32[]{:S(2)}, u32[]{:S(2)}) collective-permute-start(bf16[16,80,128]{2,1,0:T(8,128)(2,1)} %get-tuple-element.24), channel_id=1, source_target_pairs={{0,16},{16,0},{1,17},{17,1},{2,18},{18,2},{3,19},{19,3},{4,20},{20... | collective-permute-start | bytes 983048 | tf_op jit(solution)/shard_map/ppermute | solution.py:21
  141.0 47.9 %collective-permute-start.4 = (bf16[8,1040,128]{2,1,0:T(8,128)(2,1)S(1)}, bf16[8,1040,128]{2,1,0:T(8,128)(2,1)S(1)}, u32[]{:S(2)}, u32[]{:S(2)}) collective-permute-start(bf16[8,1040,128]{2,1,0:T(8,128)(2,1)S(1)} %all_to_all.36.own.vals), channel_id=1, source_target_pairs={{0,8},{8,0},{1,9},{9,1},{2,10},{10,2},{3,11},{11,3},{4,12},{12,4},... | collective-permute-start | bytes 6389768 | tf_op jit(solution)/shard_map/ppermute | solution.py:21
  199.6 16.8 %copy-start.2 = (bf16[128,2,1024]{2,1,0:T(2,128)(2,1)S(1)}, bf16[128,2,1024]{2,1,0:T(2,128)(2,1)}, u32[]{:S(2)}) copy-start(bf16[128,2,1024]{2,1,0:T(2,128)(2,1)} %weight.1) | copy-start | bytes 1572868
  201.0 17.6 %copy-start.5 = (s32[64]{0:T(128)S(1)}, s32[64]{0:T(128)}, u32[]{:S(2)}) copy-start(s32[64]{0:T(128)} %groups.1) | copy-start | bytes 772
  211.0 7.5 %collective-permute-start.5 = (bf16[2,8,64,128]{3,2,1,0:T(8,128)(2,1)S(1)}, bf16[2,8,64,128]{3,2,1,0:T(8,128)(2,1)S(1)}, u32[]{:S(2)}, u32[]{:S(2)}) collective-permute-start(bf16[2,8,64,128]{3,2,1,0:T(8,128)(2,1)S(1)} %bitcast.5), channel_id=1, source_target_pairs={{0,8},{8,0},{1,9},{9,1},{2,10},{10,2},{3,11},{11,3},{4,12},{12,4},... | collective-permute-start | bytes 786440 | tf_op jit(solution)/shard_map/ppermute | solution.py:21

commit v6 on v5

--- a/solution.py
+++ b/solution.py
@@ -174,16 +174,13 @@
     rest[...] = keep[xl] + got[xl].astype(f32)
 
 
-def pack_z(owners, keep, got, bases, sent, vals):
-    nz, height, slab = keep.shape
+def pack_z(owners, keep, got, bases, sent, part, vals):
     per = (bases.shape[1] - VALS) // 2
     xl = lax.axis_index("xl")
     source = [owners[i] // 4 for i in range(3)]
-    sent[:, 0:height] = (keep[...] + got[...].astype(f32)).astype(bf16)
+    sent[...] = (keep[...] + got[...].astype(f32)).astype(bf16)
     for i, src in enumerate((source[0], owners[1 + xl] // 4)):
-        part = bases[src, i * per : (i + 1) * per]
-        for k in range(nz):
-            sent[k, height + i * per : height + (i + 1) * per] = part
+        part[i * per : (i + 1) * per] = bases[src, i * per : (i + 1) * per]
     chosen = bases[source[0], 2 * per :].astype(f32)
     place = lax.broadcasted_iota(jnp.int32, chosen.shape, 0)
     for i in (1, 2):
@@ -191,29 +188,32 @@
     vals[...] = chosen.astype(bf16)
 
 
-def reduce_z(got, vals, grad, factor_a, factor_g, sent):
-    nz, _, slab = got.shape
+def reduce_z(got, bases, vals, grad, factor_a, factor_g, sent):
+    nz, height, slab = got.shape
     group = factor_a.shape[0]
     per = grad.shape[0]
     half = nz * per
-    height = per + 3 * group
-    total = got[0, 0:height].astype(f32)
+    total = got[0].astype(f32)
     for k in range(1, nz):
-        total = total + got[k, 0:height].astype(f32)
+        total = total + got[k].astype(f32)
     grad[...] = total[0:per].astype(bf16)
     for j in range(2):
         factor_g[j] = total[per + j * group : per + (j + 1) * group]
     factor_a[...] = total[per + 2 * group :]
     for k in range(sent.shape[0]):
-        sent[k, 0:half] = got[:, height : height + per].reshape(half, slab)
-        sent[k, half : 2 * half] = got[:, height + per :].reshape(half, slab)
+        sent[k, 0:half] = bases[:, 0:per].reshape(half, slab)
+        sent[k, half : 2 * half] = bases[:, per:].reshape(half, slab)
         sent[k, 2 * half :] = vals[...]
 
 
-def pack_t(grad, sent):
+def pack_t(grad, own, sent, qa, qg, vals):
     nt, piece, slab = sent.shape[1:]
+    half = qa.shape[1]
     for c in range(2):
         sent[c] = grad[...].reshape(nt, piece, slab)
+    qa[...] = own[:, 0:half]
+    qg[...] = own[:, half : 2 * half]
+    vals[...] = own[:, 2 * half :]
 
 
 def rotate(got, own, other, sent, grad):
@@ -337,13 +337,14 @@
     sent, keep = call(add_core, [out(block[1:]), out(block[1:], f32)], [], [keep, got])
     got = swap(sent, "xl")
 
-    sent, vals = call(
+    sent, part, vals = call(
         pack_z,
-        [out((nz, height + 2 * per, slab)), out((VALS, slab))],
+        [out((nz, height, slab)), out((2 * per, slab)), out((VALS, slab))],
         [owners],
         [keep, got, got_bases],
     )
     got = exchange(sent, "z")
+    bases = lax.all_gather(part, "z", axis=0)
 
     width = 2 * half + VALS
     grad, factor_a, factor_g, sent = call(
@@ -355,20 +356,29 @@
             out((nt, width, slab)),
         ],
         [],
-        [got, vals],
+        [got, bases, vals],
     )
     own = exchange(sent, "t")
     grad = lax.all_gather(grad, "z", axis=0, tiled=True)
-    other = swap(own, "c")
-
-    (sent,) = call(pack_t, [out((2, nt, piece, slab))], [], [grad])
+    sent, qa, qg, vals = call(
+        pack_t,
+        [
+            out((2, nt, piece, slab)),
+            out((nt, half, slab)),
+            out((nt, half, slab)),
+            out((nt, VALS, slab)),
+        ],
+        [],
+        [grad, own],
+    )
+    qa_other, qg_other = swap(qa, "c"), swap(qg, "c")
     columns = exchange(sent.reshape(2 * nt, piece, slab), ("c", "t"))
     columns = columns.reshape(2, nt, piece, slab)
     (sent,) = call(
         rotate,
         [out((nt, piece, slab))],
         [],
-        [columns, (own, half, 0), (other, half, 0)],
+        [columns, qa, qa_other],
         scratch=[pltpu.VMEM((slab, full), bf16)],
         flops=2 * slab * full * half,
     )
@@ -377,7 +387,7 @@
         scale_rows,
         [out((blocks, nt, piece, slab))],
         [],
-        [rows, (own, half, 1), (other, half, 1), (own, VALS, 2 * half // VALS)],
+        [rows, qg, qg_other, vals],
         scratch=[
             pltpu.VMEM((piece, full), bf16),
             pltpu.VMEM((nt, piece, slab), bf16),
@@ -392,7 +402,7 @@
         finish,
         [out((full, blocks, slab)), out((1, full, slab))],
         [worker_group],
-        [(own, half, 0), (other, half, 0), own_mixed, other_mixed],
+        [qa, qa_other, own_mixed, other_mixed],
         flops=4 * full * full * slab,
     )
 

time: 223 us -> 215 us (0.964)
  blocking collectives: 135 us -> 82.9 us
  starting transfers between devices: 45.9 us -> 78 us
  waiting for transfers between devices: 19.3 us -> 26.1 us
  Pallas kernels: 16.9 us -> 19.8 us
  local copies, waits for them, and re-layouts: 4.57 us -> 6.88 us
    all_to_all x5 -> x2, blocking collectives: 112 us -> 25.8 us  [exchange(): return lax.all_to_all(array, axis, 0, 0, tiled=True)]
    all_gather x0 -> x1, blocking collectives: none -> 35.4 us  [local(): bases = lax.all_gather(part, 'z', axis=0)]
    all_to_all x2 -> x5, starting transfers between devices: 20.5 us -> 42.7 us  [exchange(): return lax.all_to_all(array, axis, 0, 0, tiled=True)]
    ppermute x6 -> x7, starting transfers between devices: 25.4 us -> 35.3 us  [swap(): return lax.ppermute(array, axis, [(0, 1), (1, 0)])]
    all_to_all x2 -> x5, waiting for transfers between devices: 2.71 us -> 10.4 us  [exchange(): return lax.all_to_all(array, axis, 0, 0, tiled=True)]
    pallas_call x12, Pallas kernels: 16.9 us -> 19.8 us  [call(): pl.pallas_call(body, grid=(1,), out_shape=outs, in_specs=[pl.BlockSpec(me...]
    unnamed x13 -> x21, local copies, waits for them, and re-layouts: 2.53 us -> 4.85 us
    ppermute x6 -> x7, waiting for transfers between devices: 16.6 us -> 15.6 us  [swap(): return lax.ppermute(array, axis, [(0, 1), (1, 0)])]
  transfers between devices with their start and end apart: 8 -> 12, of which waited for: 5 -> 6; matrix products, arithmetic and copies ran while one was open for 0% -> 0% of each run, Pallas kernels for 4% -> 5%
where the time goes in v6:
time: 215 us
  blocking collectives  82.9 us (39%)
  starting transfers between devices  78 us (36%)
  waiting for transfers between devices  26.1 us (12%)
  Pallas kernels  19.8 us (9%)
  local copies, waits for them, and re-layouts  6.88 us (3%)
    all_to_all x5, starting transfers between devices, exchange(): return lax.all_to_all(array, axis, 0, 0, tiled=True)  42.7 us
    all_gather x1, blocking collectives, local(): bases = lax.all_gather(part, 'z', axis=0)  35.4 us
    ppermute x7, starting transfers between devices, swap(): return lax.ppermute(array, axis, [(0, 1), (1, 0)])  35.3 us
    all_to_all x2, blocking collectives, exchange(): return lax.all_to_all(array, axis, 0, 0, tiled=True)  25.8 us
    all_gather x1, blocking collectives, local(): grad = lax.all_gather(grad, 'z', axis=0, tiled=True)  21.7 us
    pallas_call x12, Pallas kernels, call(): pl.pallas_call(body, grid=(1,), out_shape=outs, in_specs=[pl.BlockSpec(me...  19.8 us
    ppermute x7, waiting for transfers between devices, swap(): return lax.ppermute(array, axis, [(0, 1), (1, 0)])  15.6 us
    all_to_all x5, waiting for transfers between devices, exchange(): return lax.all_to_all(array, axis, 0, 0, tiled=True)  10.4 us
  transfers between devices with their start and end apart: 12, of which 6 were waited for; matrix products, arithmetic and copies ran while one was open for 0% of the time, Pallas kernels for 5%

profile of v6, /device:TPU:1, one launch (start us, length us, event | category | flops | bytes accessed | tf_op | source)
XLA Modules:
  0.0 214.5 jit_solution(5803301334184881513)
XLA Ops:
  0.6 2.0 broadcast_in_dim.2
  2.7 7.6 %all-to-all-start = ((bf16[8,512,128]{2,1,0:T(8,128)(2,1)}), bf16[8,512,128]{2,1,0:T(8,128)(2,1)S(1)}, u32[]{:S(2)}, u32[]{:S(2)}) async-start(bf16[8,512,128]{2,1,0:T(8,128)(2,1)} %broadcast_in_dim.2), calls=%async_computation | async-start | bytes 2097152 | tf_op jit(solution)/shard_map/all_to_all | solution.py:17
  10.3 2.8 %shard_map.131 = (bf16[1552,128]{1,0:T(8,128)(2,1)}, bf16[1552,128]{1,0:T(8,128)(2,1)}) custom-call(bf16[1,1024,128]{2,1,0:T(8,128)(2,1)} %ba.1, bf16[1,2,1024,128]{3,2,1,0:T(8,128)(2,1)} %bg.1, bf16[1,128]{1,0:T(2,128)(2,1)} %va.1, bf16[1,2,128]{2,1,0:T(2,128)(2,1)} %vg.1), custom_call_target="tpu_custom_call" | custom-call | bytes 1581824 | tf_op jit(solution)/shard_map/pallas_call | solution.py:37
  13.1 4.9 %collective-permute-start.2 = (bf16[1552,128]{1,0:T(8,128)(2,1)}, bf16[1552,128]{1,0:T(8,128)(2,1)S(1)}, u32[]{:S(2)}, u32[]{:S(2)}) collective-permute-start(bf16[1552,128]{1,0:T(8,128)(2,1)} %get-tuple-element.31), channel_id=1, source_target_pairs={{0,8},{8,0},{1,9},{9,1},{2,10},{10,2},{3,11},{11,3},{4,12},{12,4},... | collective-permute-start | bytes 1191944 | tf_op jit(solution)/shard_map/ppermute | solution.py:21
  23.1 7.6 %collective-permute-done.3.got = bf16[1040,128]{1,0:T(8,128)(2,1)S(1)} collective-permute-done((bf16[1040,128]{1,0:T(8,128)(2,1)S(1)}, bf16[1040,128]{1,0:T(8,128)(2,1)S(1)}, u32[]{:S(2)}, u32[]{:S(2)}) %collective-permute-start.3) | collective-permute-done | bytes 266272 | tf_op jit(solution)/shard_map/ppermute | solution.py:21
  32.0 12.9 %all-to-all-start.1 = ((bf16[16,80,128]{2,1,0:T(8,128)(2,1)}), bf16[16,80,128]{2,1,0:T(8,128)(2,1)S(1)}, u32[]{:S(2)}, u32[]{:S(2)}) async-start(bf16[16,80,128]{2,1,0:T(8,128)(2,1)} %shard_map.133), calls=%async_computation.1 | async-start | bytes 655360 | tf_op jit(solution)/shard_map/all_to_all | solution.py:17
  45.9 2.2 %shard_map.129 = (bf16[2,16,80,128]{3,2,1,0:T(8,128)(2,1)S(1)}, f32[2,16,80,128]{3,2,1,0:T(8,128)S(1)}) custom-call(bf16[512,2,1024]{2,1,0:T(2,128)(2,1)S(1)} %copy-done, bf16[512,128]{1,0:T(8,128)(2,1)S(1)} %copy-done.5, bf16[8,512,128]{2,1,0:T(8,128)(2,1)S(1)} %all-to-all-done.whole), custom_call_target="tpu_custom_call" | custom-call | flops 671088640 | bytes 5242880 | tf_op jit(solution)/shard_map/pallas_call | solution.py:37
  48.0 3.4 %collective-permute-start = (bf16[2,16,80,128]{3,2,1,0:T(8,128)(2,1)S(1)}, bf16[2,16,80,128]{3,2,1,0:T(8,128)(2,1)S(1)}, u32[]{:S(2)}, u32[]{:S(2)}) collective-permute-start(bf16[2,16,80,128]{3,2,1,0:T(8,128)(2,1)S(1)} %get-tuple-element.27), channel_id=1, source_target_pairs={{0,8},{8,0},{1,9},{9,1},{2,10},{10,2},{3,11},{11,3},{4,12},{12,4},... | collective-permute-start | bytes 1966088 | tf_op jit(solution)/shard_map/ppermute | solution.py:21
  53.2 2.6 %collective-permute-start.1 = (bf16[16,80,128]{2,1,0:T(8,128)(2,1)S(1)}, bf16[16,80,128]{2,1,0:T(8,128)(2,1)S(1)}, u32[]{:S(2)}, u32[]{:S(2)}) collective-permute-start(bf16[16,80,128]{2,1,0:T(8,128)(2,1)S(1)} %get-tuple-element.29), channel_id=1, source_target_pairs={{0,16},{16,0},{1,17},{17,1},{2,18},{18,2},{3,19},{19,3},{4,20},{20... | collective-permute-start | bytes 983048 | tf_op jit(solution)/shard_map/ppermute | solution.py:21
  55.8 3.4 %all-to-all-done.1.bases = bf16[16,80,128]{2,1,0:T(8,128)(2,1)S(1)} async-done(((bf16[16,80,128]{2,1,0:T(8,128)(2,1)}), bf16[16,80,128]{2,1,0:T(8,128)(2,1)S(1)}, u32[]{:S(2)}, u32[]{:S(2)}) %all-to-all-start.1) | async-done | bytes 327712 | tf_op jit(solution)/shard_map/all_to_all | solution.py:17
  59.2 4.8 %collective-permute-done.1.got = bf16[16,80,128]{2,1,0:T(8,128)(2,1)S(1)} collective-permute-done((bf16[16,80,128]{2,1,0:T(8,128)(2,1)S(1)}, bf16[16,80,128]{2,1,0:T(8,128)(2,1)S(1)}, u32[]{:S(2)}, u32[]{:S(2)}) %collective-permute-start.1) | collective-permute-done | bytes 327712 | tf_op jit(solution)/shard_map/ppermute | solution.py:21
  65.4 11.7 %all-to-all-start.2 = ((bf16[16,80,128]{2,1,0:T(8,128)(2,1)}), bf16[16,80,128]{2,1,0:T(8,128)(2,1)S(1)}, u32[]{:S(2)}, u32[]{:S(2)}) async-start(bf16[16,80,128]{2,1,0:T(8,128)(2,1)} %get-tuple-element.34), calls=%async_computation.2 | async-start | bytes 655360 | tf_op jit(solution)/shard_map/all_to_all | solution.py:17
  77.1 35.4 %all-gather = bf16[1024,128]{1,0:T(8,128)(2,1)S(1)} all-gather(bf16[64,128]{1,0:T(8,128)(2,1)S(1)} %get-tuple-element.35), channel_id=2, replica_groups=mesh['z'=16,'xl'=2,'c'=2,'t'=8] {'z'}, dimensions={0}, use_global_device_ids=true | all-gather | bytes 278528 | tf_op jit(solution)/shard_map/all_gather | solution.py:347
  114.8 6.9 %all-to-all-start.3 = ((bf16[8,1040,128]{2,1,0:T(8,128)(2,1)}), bf16[8,1040,128]{2,1,0:T(8,128)(2,1)S(1)}, u32[]{:S(2)}, u32[]{:S(2)}) async-start(bf16[8,1040,128]{2,1,0:T(8,128)(2,1)} %copy-done.4), calls=%async_computation.3 | async-start | bytes 4259840 | tf_op jit(solution)/shard_map/all_to_all | solution.py:17
  121.7 21.7 %all_gather.11.grad = bf16[512,128]{1,0:T(8,128)(2,1)S(1)} all-gather(bf16[32,128]{1,0:T(8,128)(2,1)S(1)} %get-tuple-element.39), channel_id=1, replica_groups=mesh['z'=16,'xl'=2,'c'=2,'t'=8] {'z'}, dimensions={0}, use_global_device_ids=true | all-gather | bytes 139264 | tf_op jit(solution)/shard_map/all_gather | solution.py:362
  144.6 15.0 %collective-permute-start.4 = (bf16[8,512,128]{2,1,0:T(8,128)(2,1)S(1)}, bf16[8,512,128]{2,1,0:T(8,128)(2,1)S(1)}, u32[]{:S(2)}, u32[]{:S(2)}) collective-permute-start(bf16[8,512,128]{2,1,0:T(8,128)(2,1)S(1)} %get-tuple-element.41.own), channel_id=1, source_target_pairs={{0,8},{8,0},{1,9},{9,1},{2,10},{10,2},{3,11},{11,3},{4,12},{12,4},... | collective-permute-start | bytes 3145736 | tf_op jit(solution)/shard_map/ppermute | solution.py:21
  159.6 1.9 collective-permute-start.5
  161.5 15.6 %all_to_all.35 = bf16[16,64,128]{2,1,0:T(8,128)(2,1)S(1)} all-to-all(bf16[16,64,128]{2,1,0:T(8,128)(2,1)S(1)} %bitcast.11), channel_id=1, replica_groups=mesh['z'=16,'xl'=2,'c'=2,'t'=8] {'c','t'}, dimensions={0} | all-to-all | bytes 524288 | tf_op jit(solution)/shard_map/all_to_all | solution.py:17
  179.3 3.5 %all-to-all-start.5 = ((bf16[8,64,128]{2,1,0:T(8,128)(2,1)}), bf16[8,64,128]{2,1,0:T(8,128)(2,1)S(1)}, u32[]{:S(2)}, u32[]{:S(2)}) async-start(bf16[8,64,128]{2,1,0:T(8,128)(2,1)} %shard_map.137), calls=%async_computation.5 | async-start | bytes 262144 | tf_op jit(solution)/shard_map/all_to_all | solution.py:17
  182.8 7.0 %all-to-all-done.5.rows = bf16[8,64,128]{2,1,0:T(8,128)(2,1)S(1)} async-done(((bf16[8,64,128]{2,1,0:T(8,128)(2,1)}), bf16[8,64,128]{2,1,0:T(8,128)(2,1)S(1)}, u32[]{:S(2)}, u32[]{:S(2)}) %all-to-all-start.5) | async-done | bytes 131104 | tf_op jit(solution)/shard_map/all_to_all | solution.py:17
  189.8 2.8 %shard_map.138 = bf16[2,8,64,128]{3,2,1,0:T(8,128)(2,1)S(1)} custom-call(bf16[8,64,128]{2,1,0:T(8,128)(2,1)S(1)} %all-to-all-done.5.rows, bf16[8,512,128]{2,1,0:T(8,128)(2,1)} %get-tuple-element.43.own, bf16[8,512,128]{2,1,0:T(8,128)(2,1)} %collective-permute-done.5.other, bf16[8,16,128]{2,1,0:T(8,128)(2,1)S(1)} %get-tuple-element.44.vals), custom_call_target="tpu_custom_call" | custom-call | flops 268435456 | bytes 2523136 | tf_op jit(solution)/shard_map/pallas_call | solution.py:37
  192.5 10.2 %all_to_all.36 = bf16[16,64,128]{2,1,0:T(8,128)(2,1)S(1)} all-to-all(bf16[16,64,128]{2,1,0:T(8,128)(2,1)S(1)} %bitcast.7), channel_id=1, replica_groups=mesh['z'=16,'xl'=2,'c'=2,'t'=8] {'xl','t'}, dimensions={0} | all-to-all | bytes 524288 | tf_op jit(solution)/shard_map/all_to_all | solution.py:17
  202.7 5.7 %collective-permute-start.6 = (bf16[2,8,64,128]{3,2,1,0:T(8,128)(2,1)S(1)}, bf16[2,8,64,128]{3,2,1,0:T(8,128)(2,1)S(1)}, u32[]{:S(2)}, u32[]{:S(2)}) collective-permute-start(bf16[2,8,64,128]{3,2,1,0:T(8,128)(2,1)S(1)} %bitcast.9), channel_id=1, source_target_pairs={{0,8},{8,0},{1,9},{9,1},{2,10},{10,2},{3,11},{11,3},{4,12},{12,4},... | collective-permute-start | bytes 786440 | tf_op jit(solution)/shard_map/ppermute | solution.py:21
  210.7 3.9 %shard_map.139 = (bf16[1024,2,128]{2,1,0:T(2,128)(2,1)}, bf16[1,1024,128]{2,1,0:T(8,128)(2,1)}) custom-call(s32[64]{0:T(128)S(1)} %copy-done.9, bf16[8,512,128]{2,1,0:T(8,128)(2,1)S(1)} %get-tuple-element.41.own, bf16[8,512,128]{2,1,0:T(8,128)(2,1)S(1)} %copy-done.3, bf16[2,8,64,128]{3,2,1,0:T(8,128)(2,1)S(1)} %bitcast.10, ...), custom_call_target="tpu_custom_call" | custom-call | flops 536870912 | bytes 3407872 | tf_op jit(solution)/shard_map/pallas_call | solution.py:37
  (38 shorter events, 18.3 us)
Async XLA Ops:
  0.6 18.9 %copy-start.8 = (s32[3]{0:T(128)S(1)}, s32[3]{0:T(128)}, u32[]{:S(2)}) copy-start(s32[3]{0:T(128)} %owners.5) | copy-start | bytes 40
  2.7 42.3 %copy-start = (bf16[512,2,1024]{2,1,0:T(2,128)(2,1)S(1)}, bf16[512,2,1024]{2,1,0:T(2,128)(2,1)}, u32[]{:S(2)}) copy-start(bf16[512,2,1024]{2,1,0:T(2,128)(2,1)} %cot.3) | copy-start | bytes 6291460
  2.7 29.4 %all-to-all-start = ((bf16[8,512,128]{2,1,0:T(8,128)(2,1)}), bf16[8,512,128]{2,1,0:T(8,128)(2,1)S(1)}, u32[]{:S(2)}, u32[]{:S(2)}) async-start(bf16[8,512,128]{2,1,0:T(8,128)(2,1)} %broadcast_in_dim.2), calls=%async_computation | async-start | bytes 2097152 | tf_op jit(solution)/shard_map/all_to_all | solution.py:17
  13.1 6.4 %collective-permute-start.2 = (bf16[1552,128]{1,0:T(8,128)(2,1)}, bf16[1552,128]{1,0:T(8,128)(2,1)S(1)}, u32[]{:S(2)}, u32[]{:S(2)}) collective-permute-start(bf16[1552,128]{1,0:T(8,128)(2,1)} %get-tuple-element.31), channel_id=1, source_target_pairs={{0,8},{8,0},{1,9},{9,1},{2,10},{10,2},{3,11},{11,3},{4,12},{12,4},... | collective-permute-start | bytes 1191944 | tf_op jit(solution)/shard_map/ppermute | solution.py:21
  19.5 1.0 copy-start.7
  21.2 9.5 %collective-permute-start.3 = (bf16[1040,128]{1,0:T(8,128)(2,1)S(1)}, bf16[1040,128]{1,0:T(8,128)(2,1)S(1)}, u32[]{:S(2)}, u32[]{:S(2)}) collective-permute-start(bf16[1040,128]{1,0:T(8,128)(2,1)S(1)} %get-tuple-element.33), channel_id=1, source_target_pairs={{0,16},{16,0},{1,17},{17,1},{2,18},{18,2},{3,19},{19,3},{4,20},{20... | collective-permute-start | bytes 798728 | tf_op jit(solution)/shard_map/ppermute | solution.py:21
  32.0 27.2 %all-to-all-start.1 = ((bf16[16,80,128]{2,1,0:T(8,128)(2,1)}), bf16[16,80,128]{2,1,0:T(8,128)(2,1)S(1)}, u32[]{:S(2)}, u32[]{:S(2)}) async-start(bf16[16,80,128]{2,1,0:T(8,128)(2,1)} %shard_map.133), calls=%async_computation.1 | async-start | bytes 655360 | tf_op jit(solution)/shard_map/all_to_all | solution.py:17
  45.0 0.9 copy-start.5
  48.0 5.1 %collective-permute-start = (bf16[2,16,80,128]{3,2,1,0:T(8,128)(2,1)S(1)}, bf16[2,16,80,128]{3,2,1,0:T(8,128)(2,1)S(1)}, u32[]{:S(2)}, u32[]{:S(2)}) collective-permute-start(bf16[2,16,80,128]{3,2,1,0:T(8,128)(2,1)S(1)} %get-tuple-element.27), channel_id=1, source_target_pairs={{0,8},{8,0},{1,9},{9,1},{2,10},{10,2},{3,11},{11,3},{4,12},{12,4},... | collective-permute-start | bytes 1966088 | tf_op jit(solution)/shard_map/ppermute | solution.py:21
  53.2 10.8 %collective-permute-start.1 = (bf16[16,80,128]{2,1,0:T(8,128)(2,1)S(1)}, bf16[16,80,128]{2,1,0:T(8,128)(2,1)S(1)}, u32[]{:S(2)}, u32[]{:S(2)}) collective-permute-start(bf16[16,80,128]{2,1,0:T(8,128)(2,1)S(1)} %get-tuple-element.29), channel_id=1, source_target_pairs={{0,16},{16,0},{1,17},{17,1},{2,18},{18,2},{3,19},{19,3},{4,20},{20... | collective-permute-start | bytes 983048 | tf_op jit(solution)/shard_map/ppermute | solution.py:21
  65.4 47.2 %all-to-all-start.2 = ((bf16[16,80,128]{2,1,0:T(8,128)(2,1)}), bf16[16,80,128]{2,1,0:T(8,128)(2,1)S(1)}, u32[]{:S(2)}, u32[]{:S(2)}) async-start(bf16[16,80,128]{2,1,0:T(8,128)(2,1)} %get-tuple-element.34), calls=%async_computation.2 | async-start | bytes 655360 | tf_op jit(solution)/shard_map/all_to_all | solution.py:17
  113.4 1.4 copy-start.4
  114.8 28.6 %all-to-all-start.3 = ((bf16[8,1040,128]{2,1,0:T(8,128)(2,1)}), bf16[8,1040,128]{2,1,0:T(8,128)(2,1)S(1)}, u32[]{:S(2)}, u32[]{:S(2)}) async-start(bf16[8,1040,128]{2,1,0:T(8,128)(2,1)} %copy-done.4), calls=%async_computation.3 | async-start | bytes 4259840 | tf_op jit(solution)/shard_map/all_to_all | solution.py:17
  144.6 32.5 %collective-permute-start.4 = (bf16[8,512,128]{2,1,0:T(8,128)(2,1)S(1)}, bf16[8,512,128]{2,1,0:T(8,128)(2,1)S(1)}, u32[]{:S(2)}, u32[]{:S(2)}) collective-permute-start(bf16[8,512,128]{2,1,0:T(8,128)(2,1)S(1)} %get-tuple-element.41.own), channel_id=1, source_target_pairs={{0,8},{8,0},{1,9},{9,1},{2,10},{10,2},{3,11},{11,3},{4,12},{12,4},... | collective-permute-start | bytes 3145736 | tf_op jit(solution)/shard_map/ppermute | solution.py:21
  159.6 23.2 %collective-permute-start.5 = (bf16[8,512,128]{2,1,0:T(8,128)(2,1)}, bf16[8,512,128]{2,1,0:T(8,128)(2,1)}, u32[]{:S(2)}, u32[]{:S(2)}) collective-permute-start(bf16[8,512,128]{2,1,0:T(8,128)(2,1)} %get-tuple-element.43.own), channel_id=1, source_target_pairs={{0,8},{8,0},{1,9},{9,1},{2,10},{10,2},{3,11},{11,3},{4,12},{12,4},... | collective-permute-start | bytes 3145736 | tf_op jit(solution)/shard_map/ppermute | solution.py:21
  178.3 1.0 copy-start.2
  179.3 29.2 %copy-start.1 = (bf16[512,2,1024]{2,1,0:T(2,128)(2,1)S(1)}, bf16[512,2,1024]{2,1,0:T(2,128)(2,1)}, u32[]{:S(2)}) copy-start(bf16[512,2,1024]{2,1,0:T(2,128)(2,1)} %cot.3) | copy-start | bytes 6291460
  179.3 10.5 %all-to-all-start.5 = ((bf16[8,64,128]{2,1,0:T(8,128)(2,1)}), bf16[8,64,128]{2,1,0:T(8,128)(2,1)S(1)}, u32[]{:S(2)}, u32[]{:S(2)}) async-start(bf16[8,64,128]{2,1,0:T(8,128)(2,1)} %shard_map.137), calls=%async_computation.5 | async-start | bytes 262144 | tf_op jit(solution)/shard_map/all_to_all | solution.py:17
  189.8 18.7 %copy-start.6 = (bf16[128,2,1024]{2,1,0:T(2,128)(2,1)S(1)}, bf16[128,2,1024]{2,1,0:T(2,128)(2,1)}, u32[]{:S(2)}) copy-start(bf16[128,2,1024]{2,1,0:T(2,128)(2,1)} %weight.1) | copy-start | bytes 1572868
  192.5 18.1 %copy-start.3 = (bf16[8,512,128]{2,1,0:T(8,128)(2,1)S(1)}, bf16[8,512,128]{2,1,0:T(8,128)(2,1)}, u32[]{:S(2)}) copy-start(bf16[8,512,128]{2,1,0:T(8,128)(2,1)} %copy-done.2) | copy-start | bytes 3145732
  192.5 18.1 %copy-start.9 = (s32[64]{0:T(128)S(1)}, s32[64]{0:T(128)}, u32[]{:S(2)}) copy-start(s32[64]{0:T(128)} %groups.1) | copy-start | bytes 772
  202.7 7.9 %collective-permute-start.6 = (bf16[2,8,64,128]{3,2,1,0:T(8,128)(2,1)S(1)}, bf16[2,8,64,128]{3,2,1,0:T(8,128)(2,1)S(1)}, u32[]{:S(2)}, u32[]{:S(2)}) collective-permute-start(bf16[2,8,64,128]{3,2,1,0:T(8,128)(2,1)S(1)} %bitcast.9), channel_id=1, source_target_pairs={{0,8},{8,0},{1,9},{9,1},{2,10},{10,2},{3,11},{11,3},{4,12},{12,4},... | collective-permute-start | bytes 786440 | tf_op jit(solution)/shard_map/ppermute | solution.py:21

commit v7 on v5

--- a/solution.py
+++ b/solution.py
@@ -19,6 +19,11 @@
 
 def swap(array, axis):
     return lax.ppermute(array, axis, [(0, 1), (1, 0)])
+
+
+def across(array, axis, step):
+    pairs = [(i, i ^ step) for i in range(lax.axis_size(axis))]
+    return lax.ppermute(array, axis, pairs)
 
 
 def call(body, outs, scalars, args, places=None, scratch=(), flops=0, limit=40):
@@ -72,7 +77,7 @@
         ref[place] = other()
 
 
-def pack_bases(ba, bg, va, vg, sent, keep, sem):
+def pack_bases(ba, bg, va, vg, act, sent, keep, every, sem):
     half = ba.shape[1] // 2
     core = lax.axis_index("c")
     place = lax.broadcasted_iota(jnp.int32, (VALS, ba.shape[2]), 0)
@@ -91,6 +96,8 @@
             copies[-1].start()
     sent[3 * half :] = vals.astype(bf16)
     keep[3 * half :] = vals.astype(bf16)
+    for k in range(every.shape[0]):
+        every[k] = act[...]
     for copy in copies:
         copy.wait()
 
@@ -117,11 +124,41 @@
         ref[2 * half :] = vals
 
 
-def select_x(owners, own, got, sent):
+def grad_terms(cot, act, sent, keep, flat):
+    blocks, half, slab = keep.shape
+    tok, _, full = cot.shape
+    nt = full // slab
+    scale = 1.0 / (tok * lax.axis_size("z") * 4)
+    core = lax.axis_index("c")
+    flat[...] = cot[...].reshape(tok, blocks * full)
+    for j in range(blocks):
+        term = dot(flat[:, j * full : (j + 1) * full], act[...], ((0,), (0,))) * scale
+        term = term.reshape(nt, 2, slab // 2, slab)
+        for c in range(2):
+            part = term[:, c].reshape(half, slab)
+
+            @pl.when(core == c)
+            def _():
+                keep[j] = part
+
+            @pl.when(core != c)
+            def _():
+                sent[j] = part.astype(bf16)
+
+
+def add_core(keep, got, sent, rest):
+    xl = lax.axis_index("xl")
+    sent[...] = (keep[1 - xl] + got[1 - xl].astype(f32)).astype(bf16)
+    rest[...] = keep[xl] + got[xl].astype(f32)
+
+
+def pack_z(owners, keep, got, own, other, after, sent):
     nz, _, slab = sent.shape
     half = (own.shape[0] - VALS) // 2
     per = half // nz
     xl = lax.axis_index("xl")
+    total = (keep[...] + got[...].astype(f32)).astype(bf16)
+    sent[:, 0:per] = total.reshape(nz, per, slab)
     here = [(owners[i] // 2) % 2 == xl for i in range(3)]
     flags = (here[0], (owners[1 + xl] // 2) % 2 == xl)
     for i, flag in enumerate(flags):
@@ -129,105 +166,128 @@
         choose(
             flag,
             sent,
-            (slice(None), slice(i * per, (i + 1) * per)),
+            (slice(None), slice((1 + i) * per, (2 + i) * per)),
             lambda: own[rows].reshape(nz, per, slab),
-            lambda: got[rows].reshape(nz, per, slab),
+            lambda: other[rows].reshape(nz, per, slab),
         )
-    vals = value_rows(here, own[2 * half :], got[2 * half :])
+    vals = value_rows(here, own[2 * half :], other[2 * half :])
     for k in range(nz):
-        sent[k, 2 * per :] = vals
-
-
-def terms(cot, act, whole, sent, keep, packed, flat, cov):
-    _, _, nz, height, slab = packed.shape
+        sent[k, 3 * per :] = vals
+
+
+def reduce_z(owners, got, sent, vals):
+    nz, height, _ = sent.shape
+    per = height // 3
+    xl = lax.axis_index("xl")
+    source = [owners[i] // 4 for i in range(3)]
+    total = got[0, 0:per].astype(f32)
+    for k in range(1, nz):
+        total = total + got[k, 0:per].astype(f32)
+    parts = [total.astype(bf16)]
+    for i, src in enumerate((source[0], owners[1 + xl] // 4)):
+        parts.append(got[src, (1 + i) * per : (2 + i) * per])
+    for i, part in enumerate(parts):
+        for k in range(nz):
+            sent[k, i * per : (i + 1) * per] = part
+    chosen = got[source[0], 3 * per :].astype(f32)
+    place = lax.broadcasted_iota(jnp.int32, chosen.shape, 0)
+    for i in (1, 2):
+        chosen = jnp.where(place == i, got[source[i], 3 * per :].astype(f32), chosen)
+    vals[...] = chosen.astype(bf16)
+
+
+def factor_terms(cot, act, whole, sent, keep, flat, both):
+    nz, _, height, slab = keep.shape
+    group = height // 3
     tok, blocks, full = cot.shape
     nt = full // slab
-    per = full // 2 // nz
-    group = (height - per) // 3
     scale = 1.0 / (tok * nz * 4)
+    core, t = lax.axis_index("c"), lax.axis_index("t")
     flat[...] = cot[...].reshape(tok, blocks * full)
-    t = lax.axis_index("t")
+    for j in range(blocks):
+        own = flat[:, pl.ds(pl.multiple_of(j * full + t * slab, slab), slab)]
+        both[j] = dot(flat[:, j * full : (j + 1) * full], own, ((0,), (0,))) * scale
     for k in range(nt):
-        cov[k * slab : (k + 1) * slab] = dot(whole[k], act[...], ((0,), (0,))) * scale
-    place = slice(per + 2 * group, height)
-    for c in range(2):
-        for xl in range(2):
-            packed[c, xl, :, place] = cov[...].reshape(nz, 2, 2, group, slab)[:, xl, c]
+        both[blocks, k * slab : (k + 1) * slab] = dot(whole[k], act[...], ((0,), (0,))) * scale
+    for i in range(blocks + 1):
+        term = both[i].reshape(nz, 2, 2, group, slab)
+        rows = slice(i * group, (i + 1) * group)
+        for c in range(2):
+
+            @pl.when(core == c)
+            def _():
+                keep[:, :, rows] = term[:, :, c]
+
+            @pl.when(core != c)
+            def _():
+                sent[:, :, rows] = term[:, :, c].astype(bf16)
+
+
+def factor_core(keep, got, sent, rest):
+    xl = lax.axis_index("xl")
+    sent[...] = (keep[:, 1 - xl] + got[:, 1 - xl].astype(f32)).astype(bf16)
+    rest[...] = keep[:, xl] + got[:, xl].astype(f32)
+
+
+def factor_z(bit, keep, got, sent, rest):
+    count, height, slab = keep.shape
+    total = keep[...] + got[...].astype(f32)
+    if count == 1:
+        rest[...] = total
+    else:
+        mine = (lax.axis_index("z") // bit) % 2
+        total = total.reshape(count // 2, 2, height, slab)
+        for side in range(2):
+
+            @pl.when(mine == side)
+            def _():
+                rest[...] = total[:, side]
+                sent[...] = total[:, 1 - side].astype(bf16)
+
+
+def pack_t(got, vals, keep, f_got, sent, f_sent, f_rest):
+    nz, height, slab = got.shape
+    nt = sent.shape[0]
+    per = height // 3
+    half = nz * per
+    piece = half // nt
+    sent[:, 0:piece] = got[:, 0:per].reshape(nt, piece, slab)
+    for k in range(nt):
+        for i in range(2):
+            rows = got[:, (1 + i) * per : (2 + i) * per].reshape(half, slab)
+            sent[k, piece + i * half : piece + (i + 1) * half] = rows
+        sent[k, piece + 2 * half :] = vals[...]
+    factor_z(1, keep, f_got, f_sent, f_rest)
+
+
+def split(own, keep, f_got, near, qg, vals, factor_a, factor_g):
+    nt, height, slab = near.shape
+    half = qg.shape[1]
+    near[...] = own[:, 0:height]
+    qg[...] = own[:, height : height + half]
+    vals[...] = own[:, height + half :]
+    group = factor_a.shape[0]
+    total = keep[0] + f_got[0].astype(f32)
     for j in range(2):
-        own = flat[:, pl.ds(pl.multiple_of(j * full + t * slab, slab), slab)]
-        right = jnp.concatenate([act[...], own], 1)
-        both = dot(flat[:, j * full : (j + 1) * full], right, ((0,), (0,))) * scale
-        grad = both[:, :slab].reshape(nt, 2, slab // 2, slab)
-        out_cov = both[:, slab:].reshape(nz, 2, 2, group, slab)
-        for c in range(2):
-            packed[c, j, :, 0:per] = grad[:, c].reshape(nz, per, slab)
-            for xl in range(2):
-                packed[c, xl, :, per + j * group : per + (j + 1) * group] = out_cov[:, xl, c]
+        factor_g[j] = total[j * group : (j + 1) * group]
+    factor_a[...] = total[2 * group :]
+
+
+def rotate(own, other, sent, grad):
+    nt, height, slab = own.shape
+    piece = slab // 2
+    half = height - piece
     core = lax.axis_index("c")
-    sent[...] = packed[1 - core].astype(bf16)
-    keep[...] = packed[core]
-
-
-def add_core(keep, got, sent, rest):
-    xl = lax.axis_index("xl")
-    sent[...] = (keep[1 - xl] + got[1 - xl].astype(f32)).astype(bf16)
-    rest[...] = keep[xl] + got[xl].astype(f32)
-
-
-def pack_z(owners, keep, got, bases, sent, vals):
-    nz, height, slab = keep.shape
-    per = (bases.shape[1] - VALS) // 2
-    xl = lax.axis_index("xl")
-    source = [owners[i] // 4 for i in range(3)]
-    sent[:, 0:height] = (keep[...] + got[...].astype(f32)).astype(bf16)
-    for i, src in enumerate((source[0], owners[1 + xl] // 4)):
-        part = bases[src, i * per : (i + 1) * per]
-        for k in range(nz):
-            sent[k, height + i * per : height + (i + 1) * per] = part
-    chosen = bases[source[0], 2 * per :].astype(f32)
-    place = lax.broadcasted_iota(jnp.int32, chosen.shape, 0)
-    for i in (1, 2):
-        chosen = jnp.where(place == i, bases[source[i], 2 * per :].astype(f32), chosen)
-    vals[...] = chosen.astype(bf16)
-
-
-def reduce_z(got, vals, grad, factor_a, factor_g, sent):
-    nz, _, slab = got.shape
-    group = factor_a.shape[0]
-    per = grad.shape[0]
-    half = nz * per
-    height = per + 3 * group
-    total = got[0, 0:height].astype(f32)
-    for k in range(1, nz):
-        total = total + got[k, 0:height].astype(f32)
-    grad[...] = total[0:per].astype(bf16)
-    for j in range(2):
-        factor_g[j] = total[per + j * group : per + (j + 1) * group]
-    factor_a[...] = total[per + 2 * group :]
-    for k in range(sent.shape[0]):
-        sent[k, 0:half] = got[:, height : height + per].reshape(half, slab)
-        sent[k, half : 2 * half] = got[:, height + per :].reshape(half, slab)
-        sent[k, 2 * half :] = vals[...]
-
-
-def pack_t(grad, sent):
-    nt, piece, slab = sent.shape[1:]
-    for c in range(2):
-        sent[c] = grad[...].reshape(nt, piece, slab)
-
-
-def rotate(got, own, other, sent, grad):
-    nt, half, slab = own.shape
-    piece = half // nt
-    core = lax.axis_index("c")
-    for c in range(2):
-        for k in range(nt):
-            grad[c * piece : (c + 1) * piece, k * slab : (k + 1) * slab] = got[c, k, 0:piece]
+    mine = pl.multiple_of(core * piece, piece)
+    theirs = pl.multiple_of((1 - core) * piece, piece)
+    for k in range(nt):
+        grad[pl.ds(mine, piece), k * slab : (k + 1) * slab] = own[k, 0:piece]
+        grad[pl.ds(theirs, piece), k * slab : (k + 1) * slab] = other[k, 0:piece]
     near = grad[:, pl.ds(pl.multiple_of(core * half, half), half)]
     far = grad[:, pl.ds(pl.multiple_of((1 - core) * half, half), half)]
     for i in range(nt // 2):
         k = core * (nt // 2) + i
-        turned = dot(near, own[k]) + dot(far, other[k])
+        turned = dot(near, own[k, piece:]) + dot(far, other[k, piece:])
         turned = turned.T.astype(bf16)
         sent[2 * i] = turned[0:piece]
         sent[2 * i + 1] = turned[piece:]
@@ -261,7 +321,7 @@
 
 def finish(groups, own, other, own_mixed, other_mixed, pre, worker):
     blocks, nt, piece, slab = own_mixed.shape
-    half = own.shape[1]
+    half = own.shape[1] - piece
     core = lax.axis_index("c")
     replica = (lax.axis_index("z") * 2 + lax.axis_index("xl")) * 2 + core
     group = groups[replica]
@@ -272,7 +332,7 @@
                 right = jnp.concatenate(
                     [mixed[j, 2 * i : 2 * i + 2].reshape(2 * piece, slab) for j in range(blocks)], 1
                 )
-                total = total + dot(ref[part * (nt // 2) + i], right)
+                total = total + dot(ref[part * (nt // 2) + i, piece:], right)
         total = total.astype(bf16)
         place = pl.ds(pl.multiple_of(side * half, half), half)
         pre[place] = total.reshape(half, blocks, slab)
@@ -299,76 +359,101 @@
     group = full // (nz * 4)
     half, piece = full // 2, slab // 2
     per = half // nz
-    height = per + (blocks + 1) * group
-
-    whole_act = exchange(jnp.broadcast_to(act[None], (nt, tok, slab)), "t")
 
     shape = (3 * half + VALS, slab)
-    sent, keep = call(
+    sent, keep, every = call(
         pack_bases,
-        [out(shape), out(shape)],
-        [],
-        [basis_a, basis_g, values_a, values_g],
-        [pl.ANY, pl.ANY, pltpu.VMEM, pltpu.VMEM],
+        [out(shape), out(shape), out((nt, tok, slab))],
+        [],
+        [basis_a, basis_g, values_a, values_g, act],
+        [pl.ANY, pl.ANY, pltpu.VMEM, pltpu.VMEM, pltpu.VMEM],
         scratch=[pltpu.SemaphoreType.DMA((2, 3))],
         limit=56,
     )
     got = swap(sent, "c")
+    whole_act = exchange(every, "t")
     shape = (2 * half + VALS, slab)
-    sent, keep = call(select_core, [out(shape), out(shape)], [owners], [keep, got])
+    sent, base = call(select_core, [out(shape), out(shape)], [owners], [keep, got])
+    base_got = swap(sent, "xl")
+
+    flat = pltpu.VMEM((tok, blocks * full), bf16)
+    shape = (blocks, half, slab)
+    sent, keep = call(
+        grad_terms,
+        [out(shape), out(shape, f32)],
+        [],
+        [cot, act],
+        scratch=[flat],
+        flops=4 * tok * full * slab,
+    )
+    got = swap(sent, "c")
+    sent, keep = call(add_core, [out(shape[1:]), out(shape[1:], f32)], [], [keep, got])
     got = swap(sent, "xl")
-    (sent,) = call(select_x, [out((nz, 2 * per + VALS, slab))], [owners], [keep, got])
-    got_bases = exchange(sent, "z")
-
-    block = (2, nz, height, slab)
+
+    (sent,) = call(
+        pack_z,
+        [out((nz, 3 * per + VALS, slab))],
+        [owners],
+        [keep, got, base, base_got, whole_act],
+        [pltpu.VMEM] * 4 + [pl.ANY],
+    )
+    got = exchange(sent, "z")
+    sent, vals = call(
+        reduce_z, [out((nz, 3 * per, slab)), out((VALS, slab))], [owners], [got]
+    )
+    got = exchange(sent, "z")
+
+    height = (blocks + 1) * group
+    shape = (nz, 2, height, slab)
     sent, keep = call(
-        terms,
-        [out(block), out(block, f32)],
+        factor_terms,
+        [out(shape), out(shape, f32)],
         [],
         [cot, act, whole_act],
-        scratch=[
-            pltpu.VMEM((2,) + block, f32),
-            pltpu.VMEM((tok, blocks * full), bf16),
-            pltpu.VMEM((full, slab), f32),
-        ],
-        flops=10 * tok * full * slab,
-    )
-    got = swap(sent, "c")
-    sent, keep = call(add_core, [out(block[1:]), out(block[1:], f32)], [], [keep, got])
-    got = swap(sent, "xl")
-
-    sent, vals = call(
-        pack_z,
-        [out((nz, height + 2 * per, slab)), out((VALS, slab))],
-        [owners],
-        [keep, got, got_bases],
-    )
-    got = exchange(sent, "z")
-
-    width = 2 * half + VALS
-    grad, factor_a, factor_g, sent = call(
-        reduce_z,
+        scratch=[flat, pltpu.VMEM((blocks + 1, full, slab), f32)],
+        flops=6 * tok * full * slab,
+    )
+    f_got = swap(sent, "c")
+    shape = (nz, height, slab)
+    sent, keep = call(factor_core, [out(shape), out(shape, f32)], [], [keep, f_got])
+    f_got = swap(sent, "xl")
+
+    width = piece + 2 * half + VALS
+    shape = (nz // 2, height, slab)
+    sent, f_sent, f_keep = call(
+        pack_t,
+        [out((nt, width, slab)), out(shape), out(shape, f32)],
+        [],
+        [got, vals, keep, f_got],
+    )
+    own = exchange(sent, "t")
+    f_got = across(f_sent, "z", 1)
+    bit = 2
+    while bit < nz:
+        shape = (nz // 2 // bit, height, slab)
+        f_sent, f_keep = call(
+            functools.partial(factor_z, bit), [out(shape), out(shape, f32)], [], [f_keep, f_got]
+        )
+        f_got = across(f_sent, "z", bit)
+        bit *= 2
+    near, qg, vals, factor_a, factor_g = call(
+        split,
         [
-            out((per, slab)),
+            out((nt, piece + half, slab)),
+            out((nt, half, slab)),
+            out((nt, VALS, slab)),
             out((group, slab), f32),
             out((blocks, group, slab), f32),
-            out((nt, width, slab)),
         ],
         [],
-        [got, vals],
-    )
-    own = exchange(sent, "t")
-    grad = lax.all_gather(grad, "z", axis=0, tiled=True)
-    other = swap(own, "c")
-
-    (sent,) = call(pack_t, [out((2, nt, piece, slab))], [], [grad])
-    columns = exchange(sent.reshape(2 * nt, piece, slab), ("c", "t"))
-    columns = columns.reshape(2, nt, piece, slab)
+        [own, f_keep, f_got],
+    )
+    near_other, qg_other = swap(near, "c"), swap(qg, "c")
     (sent,) = call(
         rotate,
         [out((nt, piece, slab))],
         [],
-        [columns, (own, half, 0), (other, half, 0)],
+        [near, near_other],
         scratch=[pltpu.VMEM((slab, full), bf16)],
         flops=2 * slab * full * half,
     )
@@ -377,7 +462,7 @@
         scale_rows,
         [out((blocks, nt, piece, slab))],
         [],
-        [rows, (own, half, 1), (other, half, 1), (own, VALS, 2 * half // VALS)],
+        [rows, qg, qg_other, vals],
         scratch=[
             pltpu.VMEM((piece, full), bf16),
             pltpu.VMEM((nt, piece, slab), bf16),
@@ -392,7 +477,7 @@
         finish,
         [out((full, blocks, slab)), out((1, full, slab))],
         [worker_group],
-        [(own, half, 0), (other, half, 0), own_mixed, other_mixed],
+        [near, near_other, own_mixed, other_mixed],
         flops=4 * full * full * slab,
     )
 

time: 223 us -> 203 us (0.910)
  blocking collectives: 135 us -> 44.8 us
  starting transfers between devices: 45.9 us -> 92.6 us
  waiting for transfers between devices: 19.3 us -> 34 us
  Pallas kernels: 16.9 us -> 21.7 us
  local copies, waits for them, and re-layouts: 4.57 us -> 8.02 us
    all_to_all x5 -> x2, blocking collectives: 112 us -> 44.8 us  [exchange(): return lax.all_to_all(array, axis, 0, 0, tiled=True)]
    ppermute x0 -> x4, starting transfers between devices: none -> 27 us  [across(): return lax.ppermute(array, axis, pairs)]
    all_gather x1 -> x0, blocking collectives: 22.9 us -> none  [local(): grad = lax.all_gather(grad, 'z', axis=0, tiled=True)]
    ppermute x0 -> x4, waiting for transfers between devices: none -> 10.9 us  [across(): return lax.ppermute(array, axis, pairs)]
    all_to_all x2 -> x4, starting transfers between devices: 20.5 us -> 31.4 us  [exchange(): return lax.all_to_all(array, axis, 0, 0, tiled=True)]
    ppermute x6 -> x9, starting transfers between devices: 25.4 us -> 34.2 us  [swap(): return lax.ppermute(array, axis, [(0, 1), (1, 0)])]
    all_to_all x2 -> x4, waiting for transfers between devices: 2.71 us -> 9.89 us  [exchange(): return lax.all_to_all(array, axis, 0, 0, tiled=True)]
    unnamed x13 -> x31, local copies, waits for them, and re-layouts: 2.53 us -> 8.02 us
  transfers between devices with their start and end apart: 8 -> 17, of which waited for: 5 -> 10; matrix products, arithmetic and copies ran while one was open for 0% -> 0% of each run, Pallas kernels for 4% -> 4%
where the time goes in v7:
time: 203 us; the launch traced here: 202 us
  starting transfers between devices  92.6 us (46%)
  blocking collectives  44.8 us (22%)
  waiting for transfers between devices  34 us (17%)
  Pallas kernels  21.7 us (11%)
  local copies, waits for them, and re-layouts  8.02 us (4%)
    all_to_all x2, blocking collectives, exchange(): return lax.all_to_all(array, axis, 0, 0, tiled=True)  44.8 us
    ppermute x9, starting transfers between devices, swap(): return lax.ppermute(array, axis, [(0, 1), (1, 0)])  34.2 us
    all_to_all x4, starting transfers between devices, exchange(): return lax.all_to_all(array, axis, 0, 0, tiled=True)  31.4 us
    ppermute x4, starting transfers between devices, across(): return lax.ppermute(array, axis, pairs)  27 us
    pallas_call x17, Pallas kernels, call(): pl.pallas_call(body, grid=(1,), out_shape=outs, in_specs=[pl.BlockSpec(me...  21.7 us
    ppermute x9, waiting for transfers between devices, swap(): return lax.ppermute(array, axis, [(0, 1), (1, 0)])  13.2 us
    ppermute x4, waiting for transfers between devices, across(): return lax.ppermute(array, axis, pairs)  10.9 us
    all_to_all x4, waiting for transfers between devices, exchange(): return lax.all_to_all(array, axis, 0, 0, tiled=True)  9.89 us
  transfers between devices with their start and end apart: 17, of which 10 were waited for; matrix products, arithmetic and copies ran while one was open for 0% of the time, Pallas kernels for 4%

profile of v7, /device:TPU:1, one launch (start us, length us, event | category | flops | bytes accessed | tf_op | source)
XLA Modules:
  0.0 202.2 jit_solution(10234512284761651797)
XLA Ops:
  0.7 3.6 %shard_map.131 = (bf16[1552,128]{1,0:T(8,128)(2,1)}, bf16[1552,128]{1,0:T(8,128)(2,1)}, bf16[8,512,128]{2,1,0:T(8,128)(2,1)}) custom-call(bf16[1,1024,128]{2,1,0:T(8,128)(2,1)} %ba.1, bf16[1,2,1024,128]{3,2,1,0:T(8,128)(2,1)} %bg.1, bf16[1,128]{1,0:T(2,128)(2,1)} %va.1, bf16[1,2,128]{2,1,0:T(2,128)(2,1)} %vg.1, bf16[512,128]{1,0:T(8,128)(2,1)} %act.5), custom_call_target="tpu_custom_call" | custom-call | bytes 2761472 | tf_op jit(solution)/shard_map/pallas_call | solution.py:42
  4.3 7.5 %all-to-all-start = ((bf16[8,512,128]{2,1,0:T(8,128)(2,1)}), bf16[8,512,128]{2,1,0:T(8,128)(2,1)S(1)}, u32[]{:S(2)}, u32[]{:S(2)}) async-start(bf16[8,512,128]{2,1,0:T(8,128)(2,1)} %get-tuple-element.44), calls=%async_computation | async-start | bytes 2097152 | tf_op jit(solution)/shard_map/all_to_all | solution.py:17
  11.8 5.0 %collective-permute-start.2 = (bf16[1552,128]{1,0:T(8,128)(2,1)}, bf16[1552,128]{1,0:T(8,128)(2,1)S(1)}, u32[]{:S(2)}, u32[]{:S(2)}) collective-permute-start(bf16[1552,128]{1,0:T(8,128)(2,1)} %get-tuple-element.41), channel_id=1, source_target_pairs={{0,8},{8,0},{1,9},{9,1},{2,10},{10,2},{3,11},{11,3},{4,12},{12,4},... | collective-permute-start | bytes 1191944 | tf_op jit(solution)/shard_map/ppermute | solution.py:21
  24.0 3.4 %collective-permute-start.1 = (bf16[512,128]{1,0:T(8,128)(2,1)S(1)}, bf16[512,128]{1,0:T(8,128)(2,1)S(1)}, u32[]{:S(2)}, u32[]{:S(2)}) collective-permute-start(bf16[512,128]{1,0:T(8,128)(2,1)S(1)} %get-tuple-element.39), channel_id=1, source_target_pairs={{0,16},{16,0},{1,17},{17,1},{2,18},{18,2},{3,19},{19,3},{4,20},{20... | collective-permute-start | bytes 393224 | tf_op jit(solution)/shard_map/ppermute | solution.py:21
  27.3 6.1 %collective-permute-done.1.got = bf16[512,128]{1,0:T(8,128)(2,1)S(1)} collective-permute-done((bf16[512,128]{1,0:T(8,128)(2,1)S(1)}, bf16[512,128]{1,0:T(8,128)(2,1)S(1)}, u32[]{:S(2)}, u32[]{:S(2)}) %collective-permute-start.1) | collective-permute-done | bytes 131104 | tf_op jit(solution)/shard_map/ppermute | solution.py:21
  36.7 34.3 %all_to_all.30.got = bf16[16,112,128]{2,1,0:T(8,128)(2,1)S(1)} all-to-all(bf16[16,112,128]{2,1,0:T(8,128)(2,1)S(1)} %shard_map.133), channel_id=1, replica_groups=mesh['z'=16,'xl'=2,'c'=2,'t'=8] {'z'}, dimensions={0} | all-to-all | bytes 917504 | tf_op jit(solution)/shard_map/all_to_all | solution.py:17
  72.4 11.7 %all-to-all-start.2 = ((bf16[16,96,128]{2,1,0:T(8,128)(2,1)}), bf16[16,96,128]{2,1,0:T(8,128)(2,1)S(1)}, u32[]{:S(2)}, u32[]{:S(2)}) async-start(bf16[16,96,128]{2,1,0:T(8,128)(2,1)} %copy-done.8), calls=%async_computation.2 | async-start | bytes 786432 | tf_op jit(solution)/shard_map/all_to_all | solution.py:17
  86.8 3.1 %collective-permute-start.4 = (bf16[16,2,48,128]{3,2,1,0:T(8,128)(2,1)S(1)}, bf16[16,2,48,128]{3,2,1,0:T(8,128)(2,1)S(1)}, u32[]{:S(2)}, u32[]{:S(2)}) collective-permute-start(bf16[16,2,48,128]{3,2,1,0:T(8,128)(2,1)S(1)} %get-tuple-element.48), channel_id=1, source_target_pairs={{0,8},{8,0},{1,9},{9,1},{2,10},{10,2},{3,11},{11,3},{4,12},{12,4},... | collective-permute-start | bytes 1179656 | tf_op jit(solution)/shard_map/ppermute | solution.py:21
  91.3 2.8 %collective-permute-start.5 = (bf16[16,48,128]{2,1,0:T(8,128)(2,1)S(1)}, bf16[16,48,128]{2,1,0:T(8,128)(2,1)S(1)}, u32[]{:S(2)}, u32[]{:S(2)}) collective-permute-start(bf16[16,48,128]{2,1,0:T(8,128)(2,1)S(1)} %get-tuple-element.50), channel_id=1, source_target_pairs={{0,16},{16,0},{1,17},{17,1},{2,18},{18,2},{3,19},{19,3},{4,20},{20... | collective-permute-start | bytes 589832 | tf_op jit(solution)/shard_map/ppermute | solution.py:21
  94.1 5.2 %collective-permute-done.5.f_got = bf16[16,48,128]{2,1,0:T(8,128)(2,1)S(1)} collective-permute-done((bf16[16,48,128]{2,1,0:T(8,128)(2,1)S(1)}, bf16[16,48,128]{2,1,0:T(8,128)(2,1)S(1)}, u32[]{:S(2)}, u32[]{:S(2)}) %collective-permute-start.5) | collective-permute-done | bytes 196640 | tf_op jit(solution)/shard_map/ppermute | solution.py:21
  99.3 2.8 %all-to-all-done.2.got = bf16[16,96,128]{2,1,0:T(8,128)(2,1)S(1)} async-done(((bf16[16,96,128]{2,1,0:T(8,128)(2,1)}), bf16[16,96,128]{2,1,0:T(8,128)(2,1)S(1)}, u32[]{:S(2)}, u32[]{:S(2)}) %all-to-all-start.2) | async-done | bytes 393248 | tf_op jit(solution)/shard_map/all_to_all | solution.py:17
  103.9 5.2 %all-to-all-start.3 = ((bf16[8,1104,128]{2,1,0:T(8,128)(2,1)}), bf16[8,1104,128]{2,1,0:T(8,128)(2,1)}, u32[]{:S(2)}, u32[]{:S(2)}) async-start(bf16[8,1104,128]{2,1,0:T(8,128)(2,1)} %copy-done.3), calls=%async_computation.3 | async-start | bytes 4521984 | tf_op jit(solution)/shard_map/all_to_all | solution.py:17
  109.2 7.6 %collective-permute-start.6 = (bf16[8,48,128]{2,1,0:T(8,128)(2,1)S(1)}, bf16[8,48,128]{2,1,0:T(8,128)(2,1)S(1)}, u32[]{:S(2)}, u32[]{:S(2)}) collective-permute-start(bf16[8,48,128]{2,1,0:T(8,128)(2,1)S(1)} %get-tuple-element.53), channel_id=1, source_target_pairs={{0,32},{32,0},{64,96},{96,64},{128,160},{160,128},{192,224},{224,1... | collective-permute-start | bytes 294920 | tf_op jit(solution)/shard_map/ppermute | solution.py:26
  118.8 4.5 %collective-permute-start.7 = (bf16[4,48,128]{2,1,0:T(8,128)(2,1)S(1)}, bf16[4,48,128]{2,1,0:T(8,128)(2,1)S(1)}, u32[]{:S(2)}, u32[]{:S(2)}) collective-permute-start(bf16[4,48,128]{2,1,0:T(8,128)(2,1)S(1)} %get-tuple-element.55), channel_id=1, source_target_pairs={{0,64},{32,96},{64,0},{96,32},{128,192},{160,224},{192,128},{224,1... | collective-permute-start | bytes 147464 | tf_op jit(solution)/shard_map/ppermute | solution.py:26
  125.2 6.1 %collective-permute-start.8 = (bf16[2,48,128]{2,1,0:T(8,128)(2,1)S(1)}, bf16[2,48,128]{2,1,0:T(8,128)(2,1)S(1)}, u32[]{:S(2)}, u32[]{:S(2)}) collective-permute-start(bf16[2,48,128]{2,1,0:T(8,128)(2,1)S(1)} %get-tuple-element.57), channel_id=1, source_target_pairs={{0,128},{32,160},{64,192},{96,224},{128,0},{160,32},{192,64},{224,... | collective-permute-start | bytes 73736 | tf_op jit(solution)/shard_map/ppermute | solution.py:26
  134.1 8.8 %collective-permute-start.9 = (bf16[1,48,128]{2,1,0:T(8,128)(2,1)S(1)}, bf16[1,48,128]{2,1,0:T(8,128)(2,1)S(1)}, u32[]{:S(2)}, u32[]{:S(2)}) collective-permute-start(bf16[1,48,128]{2,1,0:T(8,128)(2,1)S(1)} %get-tuple-element.59), channel_id=1, source_target_pairs={{0,256},{32,288},{64,320},{96,352},{128,384},{160,416},{192,448},{... | collective-permute-start | bytes 36872 | tf_op jit(solution)/shard_map/ppermute | solution.py:26
  142.9 4.4 %collective-permute-done.9.f_got = bf16[1,48,128]{2,1,0:T(8,128)(2,1)S(1)} collective-permute-done((bf16[1,48,128]{2,1,0:T(8,128)(2,1)S(1)}, bf16[1,48,128]{2,1,0:T(8,128)(2,1)S(1)}, u32[]{:S(2)}, u32[]{:S(2)}) %collective-permute-start.9) | collective-permute-done | bytes 12320 | tf_op jit(solution)/shard_map/ppermute | solution.py:26
  149.9 9.6 %collective-permute-start.10 = (bf16[8,576,128]{2,1,0:T(8,128)(2,1)S(1)}, bf16[8,576,128]{2,1,0:T(8,128)(2,1)S(1)}, u32[]{:S(2)}, u32[]{:S(2)}) collective-permute-start(bf16[8,576,128]{2,1,0:T(8,128)(2,1)S(1)} %get-tuple-element.62.own), channel_id=1, source_target_pairs={{0,8},{8,0},{1,9},{9,1},{2,10},{10,2},{3,11},{11,3},{4,12},{12,4},... | collective-permute-start | bytes 3538952 | tf_op jit(solution)/shard_map/ppermute | solution.py:21
  164.2 6.9 %all-to-all-start.4 = ((bf16[8,64,128]{2,1,0:T(8,128)(2,1)}), bf16[8,64,128]{2,1,0:T(8,128)(2,1)S(1)}, u32[]{:S(2)}, u32[]{:S(2)}) async-start(bf16[8,64,128]{2,1,0:T(8,128)(2,1)} %shard_map.142), calls=%async_computation.4 | async-start | bytes 262144 | tf_op jit(solution)/shard_map/all_to_all | solution.py:17
  171.1 7.0 %all-to-all-done.4.rows = bf16[8,64,128]{2,1,0:T(8,128)(2,1)S(1)} async-done(((bf16[8,64,128]{2,1,0:T(8,128)(2,1)}), bf16[8,64,128]{2,1,0:T(8,128)(2,1)S(1)}, u32[]{:S(2)}, u32[]{:S(2)}) %all-to-all-start.4) | async-done | bytes 131104 | tf_op jit(solution)/shard_map/all_to_all | solution.py:17
  178.2 2.8 %shard_map.143 = bf16[2,8,64,128]{3,2,1,0:T(8,128)(2,1)S(1)} custom-call(bf16[8,64,128]{2,1,0:T(8,128)(2,1)S(1)} %all-to-all-done.4.rows, bf16[8,512,128]{2,1,0:T(8,128)(2,1)} %get-tuple-element.63.own, bf16[8,512,128]{2,1,0:T(8,128)(2,1)} %collective-permute-done.11.other, bf16[8,16,128]{2,1,0:T(8,128)(2,1)S(1)} %get-tuple-element.64.vals), custom_call_target="tpu_custom_call" | custom-call | flops 268435456 | bytes 2523136 | tf_op jit(solution)/shard_map/pallas_call | solution.py:42
  181.0 10.5 %all_to_all.31 = bf16[16,64,128]{2,1,0:T(8,128)(2,1)S(1)} all-to-all(bf16[16,64,128]{2,1,0:T(8,128)(2,1)S(1)} %bitcast.5), channel_id=1, replica_groups=mesh['z'=16,'xl'=2,'c'=2,'t'=8] {'xl','t'}, dimensions={0} | all-to-all | bytes 524288 | tf_op jit(solution)/shard_map/all_to_all | solution.py:17
  191.4 4.7 %collective-permute-start.12 = (bf16[2,8,64,128]{3,2,1,0:T(8,128)(2,1)S(1)}, bf16[2,8,64,128]{3,2,1,0:T(8,128)(2,1)S(1)}, u32[]{:S(2)}, u32[]{:S(2)}) collective-permute-start(bf16[2,8,64,128]{3,2,1,0:T(8,128)(2,1)S(1)} %bitcast.3), channel_id=1, source_target_pairs={{0,8},{8,0},{1,9},{9,1},{2,10},{10,2},{3,11},{11,3},{4,12},{12,4},... | collective-permute-start | bytes 786440 | tf_op jit(solution)/shard_map/ppermute | solution.py:21
  198.4 3.9 %shard_map.144 = (bf16[1024,2,128]{2,1,0:T(2,128)(2,1)}, bf16[1,1024,128]{2,1,0:T(8,128)(2,1)}) custom-call(s32[64]{0:T(128)S(1)} %copy-done.14, bf16[8,576,128]{2,1,0:T(8,128)(2,1)S(1)} %get-tuple-element.62.own, bf16[8,576,128]{2,1,0:T(8,128)(2,1)S(1)} %copy-done.2, bf16[2,8,64,128]{3,2,1,0:T(8,128)(2,1)S(1)} %bitcast.4, ...), custom_call_target="tpu_custom_call" | custom-call | flops 536870912 | bytes 3670016 | tf_op jit(solution)/shard_map/pallas_call | solution.py:42
  (60 shorter events, 33.7 us)
Async XLA Ops:
  0.6 16.2 %copy-start.4 = (bf16[512,128]{1,0:T(8,128)(2,1)S(1)}, bf16[512,128]{1,0:T(8,128)(2,1)}, u32[]{:S(2)}) copy-start(bf16[512,128]{1,0:T(8,128)(2,1)} %act.5) | copy-start | bytes 393220
  0.6 16.2 %copy-start = (bf16[512,2,1024]{2,1,0:T(2,128)(2,1)S(1)}, bf16[512,2,1024]{2,1,0:T(2,128)(2,1)}, u32[]{:S(2)}) copy-start(bf16[512,2,1024]{2,1,0:T(2,128)(2,1)} %cot.5) | copy-start | bytes 6291460
  4.3 16.3 %copy-start.13 = (s32[3]{0:T(128)S(1)}, s32[3]{0:T(128)}, u32[]{:S(2)}) copy-start(s32[3]{0:T(128)} %owners.5) | copy-start | bytes 40
  4.3 29.8 %all-to-all-start = ((bf16[8,512,128]{2,1,0:T(8,128)(2,1)}), bf16[8,512,128]{2,1,0:T(8,128)(2,1)S(1)}, u32[]{:S(2)}, u32[]{:S(2)}) async-start(bf16[8,512,128]{2,1,0:T(8,128)(2,1)} %get-tuple-element.44), calls=%async_computation | async-start | bytes 2097152 | tf_op jit(solution)/shard_map/all_to_all | solution.py:17
  11.8 8.8 %copy-start.7 = (bf16[1552,128]{1,0:T(8,128)(2,1)S(1)}, bf16[1552,128]{1,0:T(8,128)(2,1)}, u32[]{:S(2)}) copy-start(bf16[1552,128]{1,0:T(8,128)(2,1)} %get-tuple-element.40.own) | copy-start | bytes 1191940
  11.8 8.8 %collective-permute-start.2 = (bf16[1552,128]{1,0:T(8,128)(2,1)}, bf16[1552,128]{1,0:T(8,128)(2,1)S(1)}, u32[]{:S(2)}, u32[]{:S(2)}) collective-permute-start(bf16[1552,128]{1,0:T(8,128)(2,1)} %get-tuple-element.41), channel_id=1, source_target_pairs={{0,8},{8,0},{1,9},{9,1},{2,10},{10,2},{3,11},{11,3},{4,12},{12,4},... | collective-permute-start | bytes 1191944 | tf_op jit(solution)/shard_map/ppermute | solution.py:21
  18.6 4.5 %collective-permute-start = (bf16[2,512,128]{2,1,0:T(8,128)(2,1)S(1)}, bf16[2,512,128]{2,1,0:T(8,128)(2,1)S(1)}, u32[]{:S(2)}, u32[]{:S(2)}) collective-permute-start(bf16[2,512,128]{2,1,0:T(8,128)(2,1)S(1)} %get-tuple-element.37), channel_id=1, source_target_pairs={{0,8},{8,0},{1,9},{9,1},{2,10},{10,2},{3,11},{11,3},{4,12},{12,4},... | collective-permute-start | bytes 786440 | tf_op jit(solution)/shard_map/ppermute | solution.py:21
  21.3 12.2 %collective-permute-start.3 = (bf16[1040,128]{1,0:T(8,128)(2,1)S(1)}, bf16[1040,128]{1,0:T(8,128)(2,1)S(1)}, u32[]{:S(2)}, u32[]{:S(2)}) collective-permute-start(bf16[1040,128]{1,0:T(8,128)(2,1)S(1)} %get-tuple-element.43), channel_id=1, source_target_pairs={{0,16},{16,0},{1,17},{17,1},{2,18},{18,2},{3,19},{19,3},{4,20},{20... | collective-permute-start | bytes 798728 | tf_op jit(solution)/shard_map/ppermute | solution.py:21
  24.0 9.5 %collective-permute-start.1 = (bf16[512,128]{1,0:T(8,128)(2,1)S(1)}, bf16[512,128]{1,0:T(8,128)(2,1)S(1)}, u32[]{:S(2)}, u32[]{:S(2)}) collective-permute-start(bf16[512,128]{1,0:T(8,128)(2,1)S(1)} %get-tuple-element.39), channel_id=1, source_target_pairs={{0,16},{16,0},{1,17},{17,1},{2,18},{18,2},{3,19},{19,3},{4,20},{20... | collective-permute-start | bytes 393224 | tf_op jit(solution)/shard_map/ppermute | solution.py:21
  72.4 29.8 %all-to-all-start.2 = ((bf16[16,96,128]{2,1,0:T(8,128)(2,1)}), bf16[16,96,128]{2,1,0:T(8,128)(2,1)S(1)}, u32[]{:S(2)}, u32[]{:S(2)}) async-start(bf16[16,96,128]{2,1,0:T(8,128)(2,1)} %copy-done.8), calls=%async_computation.2 | async-start | bytes 786432 | tf_op jit(solution)/shard_map/all_to_all | solution.py:17
  86.8 4.4 %collective-permute-start.4 = (bf16[16,2,48,128]{3,2,1,0:T(8,128)(2,1)S(1)}, bf16[16,2,48,128]{3,2,1,0:T(8,128)(2,1)S(1)}, u32[]{:S(2)}, u32[]{:S(2)}) collective-permute-start(bf16[16,2,48,128]{3,2,1,0:T(8,128)(2,1)S(1)} %get-tuple-element.48), channel_id=1, source_target_pairs={{0,8},{8,0},{1,9},{9,1},{2,10},{10,2},{3,11},{11,3},{4,12},{12,4},... | collective-permute-start | bytes 1179656 | tf_op jit(solution)/shard_map/ppermute | solution.py:21
  91.3 8.0 %collective-permute-start.5 = (bf16[16,48,128]{2,1,0:T(8,128)(2,1)S(1)}, bf16[16,48,128]{2,1,0:T(8,128)(2,1)S(1)}, u32[]{:S(2)}, u32[]{:S(2)}) collective-permute-start(bf16[16,48,128]{2,1,0:T(8,128)(2,1)S(1)} %get-tuple-element.50), channel_id=1, source_target_pairs={{0,16},{16,0},{1,17},{17,1},{2,18},{18,2},{3,19},{19,3},{4,20},{20... | collective-permute-start | bytes 589832 | tf_op jit(solution)/shard_map/ppermute | solution.py:21
  103.9 43.3 %all-to-all-start.3 = ((bf16[8,1104,128]{2,1,0:T(8,128)(2,1)}), bf16[8,1104,128]{2,1,0:T(8,128)(2,1)}, u32[]{:S(2)}, u32[]{:S(2)}) async-start(bf16[8,1104,128]{2,1,0:T(8,128)(2,1)} %copy-done.3), calls=%async_computation.3 | async-start | bytes 4521984 | tf_op jit(solution)/shard_map/all_to_all | solution.py:17
  109.2 9.6 %collective-permute-start.6 = (bf16[8,48,128]{2,1,0:T(8,128)(2,1)S(1)}, bf16[8,48,128]{2,1,0:T(8,128)(2,1)S(1)}, u32[]{:S(2)}, u32[]{:S(2)}) collective-permute-start(bf16[8,48,128]{2,1,0:T(8,128)(2,1)S(1)} %get-tuple-element.53), channel_id=1, source_target_pairs={{0,32},{32,0},{64,96},{96,64},{128,160},{160,128},{192,224},{224,1... | collective-permute-start | bytes 294920 | tf_op jit(solution)/shard_map/ppermute | solution.py:26
  118.8 6.4 %collective-permute-start.7 = (bf16[4,48,128]{2,1,0:T(8,128)(2,1)S(1)}, bf16[4,48,128]{2,1,0:T(8,128)(2,1)S(1)}, u32[]{:S(2)}, u32[]{:S(2)}) collective-permute-start(bf16[4,48,128]{2,1,0:T(8,128)(2,1)S(1)} %get-tuple-element.55), channel_id=1, source_target_pairs={{0,64},{32,96},{64,0},{96,32},{128,192},{160,224},{192,128},{224,1... | collective-permute-start | bytes 147464 | tf_op jit(solution)/shard_map/ppermute | solution.py:26
  125.2 8.9 %collective-permute-start.8 = (bf16[2,48,128]{2,1,0:T(8,128)(2,1)S(1)}, bf16[2,48,128]{2,1,0:T(8,128)(2,1)S(1)}, u32[]{:S(2)}, u32[]{:S(2)}) collective-permute-start(bf16[2,48,128]{2,1,0:T(8,128)(2,1)S(1)} %get-tuple-element.57), channel_id=1, source_target_pairs={{0,128},{32,160},{64,192},{96,224},{128,0},{160,32},{192,64},{224,... | collective-permute-start | bytes 73736 | tf_op jit(solution)/shard_map/ppermute | solution.py:26
  134.1 13.2 %collective-permute-start.9 = (bf16[1,48,128]{2,1,0:T(8,128)(2,1)S(1)}, bf16[1,48,128]{2,1,0:T(8,128)(2,1)S(1)}, u32[]{:S(2)}, u32[]{:S(2)}) collective-permute-start(bf16[1,48,128]{2,1,0:T(8,128)(2,1)S(1)} %get-tuple-element.59), channel_id=1, source_target_pairs={{0,256},{32,288},{64,320},{96,352},{128,384},{160,416},{192,448},{... | collective-permute-start | bytes 36872 | tf_op jit(solution)/shard_map/ppermute | solution.py:26
  149.9 12.0 %collective-permute-start.10 = (bf16[8,576,128]{2,1,0:T(8,128)(2,1)S(1)}, bf16[8,576,128]{2,1,0:T(8,128)(2,1)S(1)}, u32[]{:S(2)}, u32[]{:S(2)}) collective-permute-start(bf16[8,576,128]{2,1,0:T(8,128)(2,1)S(1)} %get-tuple-element.62.own), channel_id=1, source_target_pairs={{0,8},{8,0},{1,9},{9,1},{2,10},{10,2},{3,11},{11,3},{4,12},{12,4},... | collective-permute-start | bytes 3538952 | tf_op jit(solution)/shard_map/ppermute | solution.py:21
  159.5 11.6 %collective-permute-start.11 = (bf16[8,512,128]{2,1,0:T(8,128)(2,1)}, bf16[8,512,128]{2,1,0:T(8,128)(2,1)}, u32[]{:S(2)}, u32[]{:S(2)}) collective-permute-start(bf16[8,512,128]{2,1,0:T(8,128)(2,1)} %get-tuple-element.63.own), channel_id=1, source_target_pairs={{0,8},{8,0},{1,9},{9,1},{2,10},{10,2},{3,11},{11,3},{4,12},{12,4},... | collective-permute-start | bytes 3145736 | tf_op jit(solution)/shard_map/ppermute | solution.py:21
  164.2 14.0 %all-to-all-start.4 = ((bf16[8,64,128]{2,1,0:T(8,128)(2,1)}), bf16[8,64,128]{2,1,0:T(8,128)(2,1)S(1)}, u32[]{:S(2)}, u32[]{:S(2)}) async-start(bf16[8,64,128]{2,1,0:T(8,128)(2,1)} %shard_map.142), calls=%async_computation.4 | async-start | bytes 262144 | tf_op jit(solution)/shard_map/all_to_all | solution.py:17
  178.2 18.0 %copy-start.6 = (bf16[128,2,1024]{2,1,0:T(2,128)(2,1)S(1)}, bf16[128,2,1024]{2,1,0:T(2,128)(2,1)}, u32[]{:S(2)}) copy-start(bf16[128,2,1024]{2,1,0:T(2,128)(2,1)} %weight.1) | copy-start | bytes 1572868
  180.9 17.4 %copy-start.2 = (bf16[8,576,128]{2,1,0:T(8,128)(2,1)S(1)}, bf16[8,576,128]{2,1,0:T(8,128)(2,1)}, u32[]{:S(2)}) copy-start(bf16[8,576,128]{2,1,0:T(8,128)(2,1)} %copy-done.1) | copy-start | bytes 3538948
  180.9 17.4 %copy-start.14 = (s32[64]{0:T(128)S(1)}, s32[64]{0:T(128)}, u32[]{:S(2)}) copy-start(s32[64]{0:T(128)} %groups.1) | copy-start | bytes 772
  191.4 6.9 %collective-permute-start.12 = (bf16[2,8,64,128]{3,2,1,0:T(8,128)(2,1)S(1)}, bf16[2,8,64,128]{3,2,1,0:T(8,128)(2,1)S(1)}, u32[]{:S(2)}, u32[]{:S(2)}) collective-permute-start(bf16[2,8,64,128]{3,2,1,0:T(8,128)(2,1)S(1)} %bitcast.3), channel_id=1, source_target_pairs={{0,8},{8,0},{1,9},{9,1},{2,10},{10,2},{3,11},{11,3},{4,12},{12,4},... | collective-permute-start | bytes 786440 | tf_op jit(solution)/shard_map/ppermute | solution.py:21
  (8 other events, 7.4 us)

commit v8 on v7

--- a/solution.py
+++ b/solution.py
@@ -26,7 +26,7 @@
     return lax.ppermute(array, axis, pairs)
 
 
-def call(body, outs, scalars, args, places=None, scratch=(), flops=0, limit=40):
+def call(body, outs, scalars, args, places=None, scratch=(), flops=0, limit=20):
     places = places or [pltpu.VMEM] * len(args)
     specs, arrays = [], []
     for arg, place in zip(args, places):
@@ -49,6 +49,16 @@
         compiler_params=pltpu.CompilerParams(vmem_limit_bytes=limit * 1024 * 1024),
         cost_estimate=pl.CostEstimate(flops=flops, bytes_accessed=bytes_all, transcendentals=0),
     )(*scalars, *arrays)
+
+
+def follow(array, after):
+    return pl.pallas_call(
+        lambda *refs: None,
+        out_shape=jax.ShapeDtypeStruct(array.shape, array.dtype),
+        in_specs=[pl.BlockSpec(memory_space=pl.ANY)] * 2,
+        out_specs=pl.BlockSpec(memory_space=pl.ANY),
+        input_output_aliases={0: 0},
+    )(array, after)
 
 
 def out(shape, dtype=bf16):
@@ -251,49 +261,43 @@
     per = height // 3
     half = nz * per
     piece = half // nt
-    sent[:, 0:piece] = got[:, 0:per].reshape(nt, piece, slab)
     for k in range(nt):
         for i in range(2):
             rows = got[:, (1 + i) * per : (2 + i) * per].reshape(half, slab)
-            sent[k, piece + i * half : piece + (i + 1) * half] = rows
-        sent[k, piece + 2 * half :] = vals[...]
+            sent[k, i * half : (i + 1) * half] = rows
+        sent[k, 2 * half + piece :] = vals[...]
+    sent[:, 2 * half : 2 * half + piece] = got[:, 0:per].reshape(nt, piece, slab)
     factor_z(1, keep, f_got, f_sent, f_rest)
 
 
-def split(own, keep, f_got, near, qg, vals, factor_a, factor_g):
-    nt, height, slab = near.shape
-    half = qg.shape[1]
-    near[...] = own[:, 0:height]
-    qg[...] = own[:, height : height + half]
-    vals[...] = own[:, height + half :]
+def factor_out(keep, got, factor_a, factor_g):
     group = factor_a.shape[0]
-    total = keep[0] + f_got[0].astype(f32)
+    total = keep[0] + got[0].astype(f32)
     for j in range(2):
         factor_g[j] = total[j * group : (j + 1) * group]
     factor_a[...] = total[2 * group :]
 
 
-def rotate(own, other, sent, grad):
-    nt, height, slab = own.shape
+def rotate(own, other, own_grad, other_grad, sent, grad):
+    nt, half, slab = own.shape
     piece = slab // 2
-    half = height - piece
     core = lax.axis_index("c")
     mine = pl.multiple_of(core * piece, piece)
     theirs = pl.multiple_of((1 - core) * piece, piece)
     for k in range(nt):
-        grad[pl.ds(mine, piece), k * slab : (k + 1) * slab] = own[k, 0:piece]
-        grad[pl.ds(theirs, piece), k * slab : (k + 1) * slab] = other[k, 0:piece]
+        grad[pl.ds(mine, piece), k * slab : (k + 1) * slab] = own_grad[k]
+        grad[pl.ds(theirs, piece), k * slab : (k + 1) * slab] = other_grad[k]
     near = grad[:, pl.ds(pl.multiple_of(core * half, half), half)]
     far = grad[:, pl.ds(pl.multiple_of((1 - core) * half, half), half)]
     for i in range(nt // 2):
         k = core * (nt // 2) + i
-        turned = dot(near, own[k, piece:]) + dot(far, other[k, piece:])
+        turned = dot(near, own[k]) + dot(far, other[k])
         turned = turned.T.astype(bf16)
         sent[2 * i] = turned[0:piece]
         sent[2 * i + 1] = turned[piece:]
 
 
-def scale_rows(rows, own, other, vals, sent, rot, scaled, column):
+def scale_rows(rows, own, other, vals, after, sent, rot, scaled, column):
     nt, piece, slab = rows.shape
     half = own.shape[1]
     core, xl, t = lax.axis_index("c"), lax.axis_index("xl"), lax.axis_index("t")
@@ -321,7 +325,7 @@
 
 def finish(groups, own, other, own_mixed, other_mixed, pre, worker):
     blocks, nt, piece, slab = own_mixed.shape
-    half = own.shape[1] - piece
+    half = own.shape[1]
     core = lax.axis_index("c")
     replica = (lax.axis_index("z") * 2 + lax.axis_index("xl")) * 2 + core
     group = groups[replica]
@@ -332,7 +336,7 @@
                 right = jnp.concatenate(
                     [mixed[j, 2 * i : 2 * i + 2].reshape(2 * piece, slab) for j in range(blocks)], 1
                 )
-                total = total + dot(ref[part * (nt // 2) + i, piece:], right)
+                total = total + dot(ref[part * (nt // 2) + i], right)
         total = total.astype(bf16)
         place = pl.ds(pl.multiple_of(side * half, half), half)
         pre[place] = total.reshape(half, blocks, slab)
@@ -436,24 +440,23 @@
         )
         f_got = across(f_sent, "z", bit)
         bit *= 2
-    near, qg, vals, factor_a, factor_g = call(
-        split,
-        [
-            out((nt, piece + half, slab)),
-            out((nt, half, slab)),
-            out((nt, VALS, slab)),
-            out((group, slab), f32),
-            out((blocks, group, slab), f32),
-        ],
-        [],
-        [own, f_keep, f_got],
-    )
-    near_other, qg_other = swap(near, "c"), swap(qg, "c")
+    factor_a, factor_g = call(
+        factor_out,
+        [out((group, slab), f32), out((blocks, group, slab), f32)],
+        [],
+        [f_keep, f_got],
+    )
+    own = follow(own, f_sent)
+    other = swap(own, "c")
+    qa, qa_other = (own, half, 0), (other, half, 0)
+    qg, qg_other = (own, half, 1), (other, half, 1)
+    columns, columns_other = (own, piece, 2 * half // piece), (other, piece, 2 * half // piece)
+    vals = (own, VALS, (2 * half + piece) // VALS)
     (sent,) = call(
         rotate,
         [out((nt, piece, slab))],
         [],
-        [near, near_other],
+        [qa, qa_other, columns, columns_other],
         scratch=[pltpu.VMEM((slab, full), bf16)],
         flops=2 * slab * full * half,
     )
@@ -462,7 +465,8 @@
         scale_rows,
         [out((blocks, nt, piece, slab))],
         [],
-        [rows, qg, qg_other, vals],
+        [rows, qg, qg_other, vals, factor_a],
+        [pltpu.VMEM] * 4 + [pl.ANY],
         scratch=[
             pltpu.VMEM((piece, full), bf16),
             pltpu.VMEM((nt, piece, slab), bf16),
@@ -477,7 +481,7 @@
         finish,
         [out((full, blocks, slab)), out((1, full, slab))],
         [worker_group],
-        [near, near_other, own_mixed, other_mixed],
+        [qa, qa_other, own_mixed, other_mixed],
         flops=4 * full * full * slab,
     )
 

time: 203 us -> 205 us (level)
  local copies, waits for them, and re-layouts: 8.02 us -> 14.3 us
  blocking collectives: 44.8 us -> 48.6 us
  Pallas kernels: 21.7 us -> 18.4 us
  waiting for transfers between devices: 34 us -> 30.7 us
  starting transfers between devices: 92.6 us -> 90.3 us
    all_to_all x4, waiting for transfers between devices: 9.89 us -> 2.84 us  [exchange(): return lax.all_to_all(array, axis, 0, 0, tiled=True)]
    unnamed x31 -> x47, local copies, waits for them, and re-layouts: 8.02 us -> 14.3 us
    all_to_all x2, blocking collectives: 44.8 us -> 48.6 us  [exchange(): return lax.all_to_all(array, axis, 0, 0, tiled=True)]
    ppermute x9 -> x8, waiting for transfers between devices: 13.2 us -> 16.8 us  [swap(): return lax.ppermute(array, axis, [(0, 1), (1, 0)])]
    pallas_call x17, Pallas kernels: 21.7 us -> 18.4 us  [call(): pl.pallas_call(body, grid=(1,), out_shape=outs, in_specs=[pl.BlockSpec(me...]
    ppermute x9 -> x8, starting transfers between devices: 34.2 us -> 32.2 us  [swap(): return lax.ppermute(array, axis, [(0, 1), (1, 0)])]
  transfers between devices with their start and end apart: 17 -> 16, of which waited for: 10 -> 9; matrix products, arithmetic and copies ran while one was open for 0% -> 0% of each run, Pallas kernels for 4% -> 3%
where the time goes in v8:
time: 205 us; the launch traced here: 203 us
  starting transfers between devices  90.3 us (44%)
  blocking collectives  48.6 us (24%)
  waiting for transfers between devices  30.7 us (15%)
  Pallas kernels  18.4 us (9%)
  local copies, waits for them, and re-layouts  14.3 us (7%)
    all_to_all x2, blocking collectives, exchange(): return lax.all_to_all(array, axis, 0, 0, tiled=True)  48.6 us
    ppermute x8, starting transfers between devices, swap(): return lax.ppermute(array, axis, [(0, 1), (1, 0)])  32.2 us
    all_to_all x4, starting transfers between devices, exchange(): return lax.all_to_all(array, axis, 0, 0, tiled=True)  31.4 us
    ppermute x4, starting transfers between devices, across(): return lax.ppermute(array, axis, pairs)  26.7 us
    pallas_call x17, Pallas kernels, call(): pl.pallas_call(body, grid=(1,), out_shape=outs, in_specs=[pl.BlockSpec(me...  18.4 us
    ppermute x8, waiting for transfers between devices, swap(): return lax.ppermute(array, axis, [(0, 1), (1, 0)])  16.8 us
    unnamed x47, local copies, waits for them, and re-layouts  14.3 us
    ppermute x4, waiting for transfers between devices, across(): return lax.ppermute(array, axis, pairs)  11.1 us
  transfers between devices with their start and end apart: 16, of which 9 were waited for; matrix products, arithmetic and copies ran while one was open for 0% of the time, Pallas kernels for 3%

profile of v8, /device:TPU:1, one launch (start us, length us, event | category | flops | bytes accessed | tf_op | source)
XLA Modules:
  0.0 203.4 jit_solution(1214946444461347103)
XLA Ops:
  0.7 3.6 %shard_map.131 = (bf16[1552,128]{1,0:T(8,128)(2,1)}, bf16[1552,128]{1,0:T(8,128)(2,1)}, bf16[8,512,128]{2,1,0:T(8,128)(2,1)}) custom-call(bf16[1,1024,128]{2,1,0:T(8,128)(2,1)} %ba.1, bf16[1,2,1024,128]{3,2,1,0:T(8,128)(2,1)} %bg.1, bf16[1,128]{1,0:T(2,128)(2,1)} %va.1, bf16[1,2,128]{2,1,0:T(2,128)(2,1)} %vg.1, bf16[512,128]{1,0:T(8,128)(2,1)} %act.5), custom_call_target="tpu_custom_call" | custom-call | bytes 2761472 | tf_op jit(solution)/shard_map/pallas_call | solution.py:42
  4.3 7.5 %all-to-all-start = ((bf16[8,512,128]{2,1,0:T(8,128)(2,1)}), bf16[8,512,128]{2,1,0:T(8,128)(2,1)S(1)}, u32[]{:S(2)}, u32[]{:S(2)}) async-start(bf16[8,512,128]{2,1,0:T(8,128)(2,1)} %get-tuple-element.41), calls=%async_computation | async-start | bytes 2097152 | tf_op jit(solution)/shard_map/all_to_all | solution.py:17
  11.8 5.0 %collective-permute-start.2 = (bf16[1552,128]{1,0:T(8,128)(2,1)}, bf16[1552,128]{1,0:T(8,128)(2,1)S(1)}, u32[]{:S(2)}, u32[]{:S(2)}) collective-permute-start(bf16[1552,128]{1,0:T(8,128)(2,1)} %get-tuple-element.38), channel_id=1, source_target_pairs={{0,8},{8,0},{1,9},{9,1},{2,10},{10,2},{3,11},{11,3},{4,12},{12,4},... | collective-permute-start | bytes 1191944 | tf_op jit(solution)/shard_map/ppermute | solution.py:21
  24.0 3.4 %collective-permute-start.1 = (bf16[512,128]{1,0:T(8,128)(2,1)S(1)}, bf16[512,128]{1,0:T(8,128)(2,1)S(1)}, u32[]{:S(2)}, u32[]{:S(2)}) collective-permute-start(bf16[512,128]{1,0:T(8,128)(2,1)S(1)} %get-tuple-element.36), channel_id=1, source_target_pairs={{0,16},{16,0},{1,17},{17,1},{2,18},{18,2},{3,19},{19,3},{4,20},{20... | collective-permute-start | bytes 393224 | tf_op jit(solution)/shard_map/ppermute | solution.py:21
  27.3 6.1 %collective-permute-done.1.got = bf16[512,128]{1,0:T(8,128)(2,1)S(1)} collective-permute-done((bf16[512,128]{1,0:T(8,128)(2,1)S(1)}, bf16[512,128]{1,0:T(8,128)(2,1)S(1)}, u32[]{:S(2)}, u32[]{:S(2)}) %collective-permute-start.1) | collective-permute-done | bytes 131104 | tf_op jit(solution)/shard_map/ppermute | solution.py:21
  36.7 34.3 %all_to_all.30.got = bf16[16,112,128]{2,1,0:T(8,128)(2,1)S(1)} all-to-all(bf16[16,112,128]{2,1,0:T(8,128)(2,1)S(1)} %shard_map.133), channel_id=1, replica_groups=mesh['z'=16,'xl'=2,'c'=2,'t'=8] {'z'}, dimensions={0} | all-to-all | bytes 917504 | tf_op jit(solution)/shard_map/all_to_all | solution.py:17
  72.3 11.8 %all-to-all-start.2 = ((bf16[16,96,128]{2,1,0:T(8,128)(2,1)}), bf16[16,96,128]{2,1,0:T(8,128)(2,1)S(1)}, u32[]{:S(2)}, u32[]{:S(2)}) async-start(bf16[16,96,128]{2,1,0:T(8,128)(2,1)} %copy-done.13), calls=%async_computation.2 | async-start | bytes 786432 | tf_op jit(solution)/shard_map/all_to_all | solution.py:17
  86.8 3.1 %collective-permute-start.4 = (bf16[16,2,48,128]{3,2,1,0:T(8,128)(2,1)S(1)}, bf16[16,2,48,128]{3,2,1,0:T(8,128)(2,1)S(1)}, u32[]{:S(2)}, u32[]{:S(2)}) collective-permute-start(bf16[16,2,48,128]{3,2,1,0:T(8,128)(2,1)S(1)} %get-tuple-element.45), channel_id=1, source_target_pairs={{0,8},{8,0},{1,9},{9,1},{2,10},{10,2},{3,11},{11,3},{4,12},{12,4},... | collective-permute-start | bytes 1179656 | tf_op jit(solution)/shard_map/ppermute | solution.py:21
  91.3 2.8 %collective-permute-start.5 = (bf16[16,48,128]{2,1,0:T(8,128)(2,1)S(1)}, bf16[16,48,128]{2,1,0:T(8,128)(2,1)S(1)}, u32[]{:S(2)}, u32[]{:S(2)}) collective-permute-start(bf16[16,48,128]{2,1,0:T(8,128)(2,1)S(1)} %get-tuple-element.47), channel_id=1, source_target_pairs={{0,16},{16,0},{1,17},{17,1},{2,18},{18,2},{3,19},{19,3},{4,20},{20... | collective-permute-start | bytes 589832 | tf_op jit(solution)/shard_map/ppermute | solution.py:21
  94.1 5.2 %collective-permute-done.5.f_got = bf16[16,48,128]{2,1,0:T(8,128)(2,1)S(1)} collective-permute-done((bf16[16,48,128]{2,1,0:T(8,128)(2,1)S(1)}, bf16[16,48,128]{2,1,0:T(8,128)(2,1)S(1)}, u32[]{:S(2)}, u32[]{:S(2)}) %collective-permute-start.5) | collective-permute-done | bytes 196640 | tf_op jit(solution)/shard_map/ppermute | solution.py:21
  99.3 2.8 %all-to-all-done.2.got = bf16[16,96,128]{2,1,0:T(8,128)(2,1)S(1)} async-done(((bf16[16,96,128]{2,1,0:T(8,128)(2,1)}), bf16[16,96,128]{2,1,0:T(8,128)(2,1)S(1)}, u32[]{:S(2)}, u32[]{:S(2)}) %all-to-all-start.2) | async-done | bytes 393248 | tf_op jit(solution)/shard_map/all_to_all | solution.py:17
  103.9 5.2 %all-to-all-start.3 = ((bf16[8,1104,128]{2,1,0:T(8,128)(2,1)}), bf16[8,1104,128]{2,1,0:T(8,128)(2,1)S(1)}, u32[]{:S(2)}, u32[]{:S(2)}) async-start(bf16[8,1104,128]{2,1,0:T(8,128)(2,1)} %copy-done.8), calls=%async_computation.3 | async-start | bytes 4521984 | tf_op jit(solution)/shard_map/all_to_all | solution.py:17
  109.2 7.6 %collective-permute-start.6 = (bf16[8,48,128]{2,1,0:T(8,128)(2,1)S(1)}, bf16[8,48,128]{2,1,0:T(8,128)(2,1)S(1)}, u32[]{:S(2)}, u32[]{:S(2)}) collective-permute-start(bf16[8,48,128]{2,1,0:T(8,128)(2,1)S(1)} %get-tuple-element.49), channel_id=1, source_target_pairs={{0,32},{32,0},{64,96},{96,64},{128,160},{160,128},{192,224},{224,1... | collective-permute-start | bytes 294920 | tf_op jit(solution)/shard_map/ppermute | solution.py:26
  118.8 4.5 %collective-permute-start.7 = (bf16[4,48,128]{2,1,0:T(8,128)(2,1)S(1)}, bf16[4,48,128]{2,1,0:T(8,128)(2,1)S(1)}, u32[]{:S(2)}, u32[]{:S(2)}) collective-permute-start(bf16[4,48,128]{2,1,0:T(8,128)(2,1)S(1)} %get-tuple-element.51), channel_id=1, source_target_pairs={{0,64},{32,96},{64,0},{96,32},{128,192},{160,224},{192,128},{224,1... | collective-permute-start | bytes 147464 | tf_op jit(solution)/shard_map/ppermute | solution.py:26
  125.1 6.1 %collective-permute-start.8 = (bf16[2,48,128]{2,1,0:T(8,128)(2,1)S(1)}, bf16[2,48,128]{2,1,0:T(8,128)(2,1)S(1)}, u32[]{:S(2)}, u32[]{:S(2)}) collective-permute-start(bf16[2,48,128]{2,1,0:T(8,128)(2,1)S(1)} %get-tuple-element.53), channel_id=1, source_target_pairs={{0,128},{32,160},{64,192},{96,224},{128,0},{160,32},{192,64},{224,... | collective-permute-start | bytes 73736 | tf_op jit(solution)/shard_map/ppermute | solution.py:26
  131.2 2.6 %collective-permute-done.8.got = bf16[2,48,128]{2,1,0:T(8,128)(2,1)S(1)} collective-permute-done((bf16[2,48,128]{2,1,0:T(8,128)(2,1)S(1)}, bf16[2,48,128]{2,1,0:T(8,128)(2,1)S(1)}, u32[]{:S(2)}, u32[]{:S(2)}) %collective-permute-start.8) | collective-permute-done | bytes 24608 | tf_op jit(solution)/shard_map/ppermute | solution.py:26
  135.9 8.8 %collective-permute-start.10 = (bf16[8,1104,128]{2,1,0:T(8,128)(2,1)}, bf16[8,1104,128]{2,1,0:T(8,128)(2,1)S(1)}, u32[]{:S(2)}, u32[]{:S(2)}) collective-permute-start(bf16[8,1104,128]{2,1,0:T(8,128)(2,1)} %shard_map.142.own.own_grad.vals), channel_id=1, source_target_pairs={{0,8},{8,0},{1,9},{9,1},{2,10},{10,2},{3,11},{11,3},{4,12},{12,4},... | collective-permute-start | bytes 6782984 | tf_op jit(solution)/shard_map/ppermute | solution.py:21
  144.6 4.2 %collective-permute-done.10.other.other_grad = bf16[8,1104,128]{2,1,0:T(8,128)(2,1)S(1)} collective-permute-done((bf16[8,1104,128]{2,1,0:T(8,128)(2,1)}, bf16[8,1104,128]{2,1,0:T(8,128)(2,1)S(1)}, u32[]{:S(2)}, u32[]{:S(2)}) %collective-permute-start.10) | collective-permute-done | bytes 2261024 | tf_op jit(solution)/shard_map/ppermute | solution.py:21
  153.3 6.9 %all-to-all-start.4 = ((bf16[8,64,128]{2,1,0:T(8,128)(2,1)}), bf16[8,64,128]{2,1,0:T(8,128)(2,1)S(1)}, u32[]{:S(2)}, u32[]{:S(2)}) async-start(bf16[8,64,128]{2,1,0:T(8,128)(2,1)} %shard_map.143), calls=%async_computation.4 | async-start | bytes 262144 | tf_op jit(solution)/shard_map/all_to_all | solution.py:17
  160.2 8.5 %collective-permute-start.9 = (bf16[1,48,128]{2,1,0:T(8,128)(2,1)S(1)}, bf16[1,48,128]{2,1,0:T(8,128)(2,1)S(1)}, u32[]{:S(2)}, u32[]{:S(2)}) collective-permute-start(bf16[1,48,128]{2,1,0:T(8,128)(2,1)S(1)} %copy-done.19), channel_id=1, source_target_pairs={{0,256},{32,288},{64,320},{96,352},{128,384},{160,416},{192,448},{... | collective-permute-start | bytes 36872 | tf_op jit(solution)/shard_map/ppermute | solution.py:26
  168.7 4.7 %collective-permute-done.9.got = bf16[1,48,128]{2,1,0:T(8,128)(2,1)S(1)} collective-permute-done((bf16[1,48,128]{2,1,0:T(8,128)(2,1)S(1)}, bf16[1,48,128]{2,1,0:T(8,128)(2,1)S(1)}, u32[]{:S(2)}, u32[]{:S(2)}) %collective-permute-start.9) | collective-permute-done | bytes 12320 | tf_op jit(solution)/shard_map/ppermute | solution.py:26
  177.7 14.3 %all_to_all.31 = bf16[16,64,128]{2,1,0:T(8,128)(2,1)S(1)} all-to-all(bf16[16,64,128]{2,1,0:T(8,128)(2,1)S(1)} %bitcast.3), channel_id=1, replica_groups=mesh['z'=16,'xl'=2,'c'=2,'t'=8] {'xl','t'}, dimensions={0} | all-to-all | bytes 524288 | tf_op jit(solution)/shard_map/all_to_all | solution.py:17
  192.0 5.3 %collective-permute-start.11 = (bf16[2,8,64,128]{3,2,1,0:T(8,128)(2,1)S(1)}, bf16[2,8,64,128]{3,2,1,0:T(8,128)(2,1)S(1)}, u32[]{:S(2)}, u32[]{:S(2)}) collective-permute-start(bf16[2,8,64,128]{3,2,1,0:T(8,128)(2,1)S(1)} %bitcast.4), channel_id=1, source_target_pairs={{0,8},{8,0},{1,9},{9,1},{2,10},{10,2},{3,11},{11,3},{4,12},{12,4},... | collective-permute-start | bytes 786440 | tf_op jit(solution)/shard_map/ppermute | solution.py:21
  199.5 3.9 %shard_map.145 = (bf16[1024,2,128]{2,1,0:T(2,128)(2,1)}, bf16[1,1024,128]{2,1,0:T(8,128)(2,1)}) custom-call(s32[64]{0:T(128)S(1)} %copy-done.22, bf16[8,1104,128]{2,1,0:T(8,128)(2,1)S(1)} %copy-done.2, bf16[8,1104,128]{2,1,0:T(8,128)(2,1)S(1)} %copy-done.5, bf16[2,8,64,128]{3,2,1,0:T(8,128)(2,1)S(1)} %bitcast.5, ...), custom_call_target="tpu_custom_call" | custom-call | flops 536870912 | bytes 5832704 | tf_op jit(solution)/shard_map/pallas_call | solution.py:42
  (75 shorter events, 34.2 us)
Async XLA Ops:
  0.6 16.2 %copy-start.9 = (bf16[512,128]{1,0:T(8,128)(2,1)S(1)}, bf16[512,128]{1,0:T(8,128)(2,1)}, u32[]{:S(2)}) copy-start(bf16[512,128]{1,0:T(8,128)(2,1)} %act.5) | copy-start | bytes 393220
  4.3 16.3 %copy-start.21 = (s32[3]{0:T(128)S(1)}, s32[3]{0:T(128)}, u32[]{:S(2)}) copy-start(s32[3]{0:T(128)} %owners.5) | copy-start | bytes 40
  4.3 29.8 %all-to-all-start = ((bf16[8,512,128]{2,1,0:T(8,128)(2,1)}), bf16[8,512,128]{2,1,0:T(8,128)(2,1)S(1)}, u32[]{:S(2)}, u32[]{:S(2)}) async-start(bf16[8,512,128]{2,1,0:T(8,128)(2,1)} %get-tuple-element.41), calls=%async_computation | async-start | bytes 2097152 | tf_op jit(solution)/shard_map/all_to_all | solution.py:17
  11.8 8.8 %collective-permute-start.2 = (bf16[1552,128]{1,0:T(8,128)(2,1)}, bf16[1552,128]{1,0:T(8,128)(2,1)S(1)}, u32[]{:S(2)}, u32[]{:S(2)}) collective-permute-start(bf16[1552,128]{1,0:T(8,128)(2,1)} %get-tuple-element.38), channel_id=1, source_target_pairs={{0,8},{8,0},{1,9},{9,1},{2,10},{10,2},{3,11},{11,3},{4,12},{12,4},... | collective-permute-start | bytes 1191944 | tf_op jit(solution)/shard_map/ppermute | solution.py:21
  18.6 4.6 %collective-permute-start = (bf16[2,512,128]{2,1,0:T(8,128)(2,1)S(1)}, bf16[2,512,128]{2,1,0:T(8,128)(2,1)S(1)}, u32[]{:S(2)}, u32[]{:S(2)}) collective-permute-start(bf16[2,512,128]{2,1,0:T(8,128)(2,1)S(1)} %get-tuple-element.34), channel_id=1, source_target_pairs={{0,8},{8,0},{1,9},{9,1},{2,10},{10,2},{3,11},{11,3},{4,12},{12,4},... | collective-permute-start | bytes 786440 | tf_op jit(solution)/shard_map/ppermute | solution.py:21
  21.3 12.2 %collective-permute-start.3 = (bf16[1040,128]{1,0:T(8,128)(2,1)S(1)}, bf16[1040,128]{1,0:T(8,128)(2,1)S(1)}, u32[]{:S(2)}, u32[]{:S(2)}) collective-permute-start(bf16[1040,128]{1,0:T(8,128)(2,1)S(1)} %get-tuple-element.40), channel_id=1, source_target_pairs={{0,16},{16,0},{1,17},{17,1},{2,18},{18,2},{3,19},{19,3},{4,20},{20... | collective-permute-start | bytes 798728 | tf_op jit(solution)/shard_map/ppermute | solution.py:21
  24.0 9.5 %collective-permute-start.1 = (bf16[512,128]{1,0:T(8,128)(2,1)S(1)}, bf16[512,128]{1,0:T(8,128)(2,1)S(1)}, u32[]{:S(2)}, u32[]{:S(2)}) collective-permute-start(bf16[512,128]{1,0:T(8,128)(2,1)S(1)} %get-tuple-element.36), channel_id=1, source_target_pairs={{0,16},{16,0},{1,17},{17,1},{2,18},{18,2},{3,19},{19,3},{4,20},{20... | collective-permute-start | bytes 393224 | tf_op jit(solution)/shard_map/ppermute | solution.py:21
  72.3 29.8 %all-to-all-start.2 = ((bf16[16,96,128]{2,1,0:T(8,128)(2,1)}), bf16[16,96,128]{2,1,0:T(8,128)(2,1)S(1)}, u32[]{:S(2)}, u32[]{:S(2)}) async-start(bf16[16,96,128]{2,1,0:T(8,128)(2,1)} %copy-done.13), calls=%async_computation.2 | async-start | bytes 786432 | tf_op jit(solution)/shard_map/all_to_all | solution.py:17
  86.8 4.4 %collective-permute-start.4 = (bf16[16,2,48,128]{3,2,1,0:T(8,128)(2,1)S(1)}, bf16[16,2,48,128]{3,2,1,0:T(8,128)(2,1)S(1)}, u32[]{:S(2)}, u32[]{:S(2)}) collective-permute-start(bf16[16,2,48,128]{3,2,1,0:T(8,128)(2,1)S(1)} %get-tuple-element.45), channel_id=1, source_target_pairs={{0,8},{8,0},{1,9},{9,1},{2,10},{10,2},{3,11},{11,3},{4,12},{12,4},... | collective-permute-start | bytes 1179656 | tf_op jit(solution)/shard_map/ppermute | solution.py:21
  91.3 8.0 %collective-permute-start.5 = (bf16[16,48,128]{2,1,0:T(8,128)(2,1)S(1)}, bf16[16,48,128]{2,1,0:T(8,128)(2,1)S(1)}, u32[]{:S(2)}, u32[]{:S(2)}) collective-permute-start(bf16[16,48,128]{2,1,0:T(8,128)(2,1)S(1)} %get-tuple-element.47), channel_id=1, source_target_pairs={{0,16},{16,0},{1,17},{17,1},{2,18},{18,2},{3,19},{19,3},{4,20},{20... | collective-permute-start | bytes 589832 | tf_op jit(solution)/shard_map/ppermute | solution.py:21
  103.9 30.6 %all-to-all-start.3 = ((bf16[8,1104,128]{2,1,0:T(8,128)(2,1)}), bf16[8,1104,128]{2,1,0:T(8,128)(2,1)S(1)}, u32[]{:S(2)}, u32[]{:S(2)}) async-start(bf16[8,1104,128]{2,1,0:T(8,128)(2,1)} %copy-done.8), calls=%async_computation.3 | async-start | bytes 4521984 | tf_op jit(solution)/shard_map/all_to_all | solution.py:17
  109.2 9.6 %collective-permute-start.6 = (bf16[8,48,128]{2,1,0:T(8,128)(2,1)S(1)}, bf16[8,48,128]{2,1,0:T(8,128)(2,1)S(1)}, u32[]{:S(2)}, u32[]{:S(2)}) collective-permute-start(bf16[8,48,128]{2,1,0:T(8,128)(2,1)S(1)} %get-tuple-element.49), channel_id=1, source_target_pairs={{0,32},{32,0},{64,96},{96,64},{128,160},{160,128},{192,224},{224,1... | collective-permute-start | bytes 294920 | tf_op jit(solution)/shard_map/ppermute | solution.py:26
  118.8 6.3 %collective-permute-start.7 = (bf16[4,48,128]{2,1,0:T(8,128)(2,1)S(1)}, bf16[4,48,128]{2,1,0:T(8,128)(2,1)S(1)}, u32[]{:S(2)}, u32[]{:S(2)}) collective-permute-start(bf16[4,48,128]{2,1,0:T(8,128)(2,1)S(1)} %get-tuple-element.51), channel_id=1, source_target_pairs={{0,64},{32,96},{64,0},{96,32},{128,192},{160,224},{192,128},{224,1... | collective-permute-start | bytes 147464 | tf_op jit(solution)/shard_map/ppermute | solution.py:26
  125.1 8.8 %collective-permute-start.8 = (bf16[2,48,128]{2,1,0:T(8,128)(2,1)S(1)}, bf16[2,48,128]{2,1,0:T(8,128)(2,1)S(1)}, u32[]{:S(2)}, u32[]{:S(2)}) collective-permute-start(bf16[2,48,128]{2,1,0:T(8,128)(2,1)S(1)} %get-tuple-element.53), channel_id=1, source_target_pairs={{0,128},{32,160},{64,192},{96,224},{128,0},{160,32},{192,64},{224,... | collective-permute-start | bytes 73736 | tf_op jit(solution)/shard_map/ppermute | solution.py:26
  135.9 24.3 %copy-start.19 = (bf16[1,48,128]{2,1,0:T(8,128)(2,1)S(1)}, bf16[1,48,128]{2,1,0:T(8,128)(2,1)}, u32[]{:S(2)}) copy-start(bf16[1,48,128]{2,1,0:T(8,128)(2,1)} %copy-done.18) | copy-start | bytes 36868
  135.9 13.0 %collective-permute-start.10 = (bf16[8,1104,128]{2,1,0:T(8,128)(2,1)}, bf16[8,1104,128]{2,1,0:T(8,128)(2,1)S(1)}, u32[]{:S(2)}, u32[]{:S(2)}) collective-permute-start(bf16[8,1104,128]{2,1,0:T(8,128)(2,1)} %shard_map.142.own.own_grad.vals), channel_id=1, source_target_pairs={{0,8},{8,0},{1,9},{9,1},{2,10},{10,2},{3,11},{11,3},{4,12},{12,4},... | collective-permute-start | bytes 6782984 | tf_op jit(solution)/shard_map/ppermute | solution.py:21
  150.5 23.5 %copy-start.2 = (bf16[8,1104,128]{2,1,0:T(8,128)(2,1)S(1)}, bf16[8,1104,128]{2,1,0:T(8,128)(2,1)}, u32[]{:S(2)}) copy-start(bf16[8,1104,128]{2,1,0:T(8,128)(2,1)} %shard_map.142.own.own_grad.vals) | copy-start | bytes 6782980
  153.3 20.7 %all-to-all-start.4 = ((bf16[8,64,128]{2,1,0:T(8,128)(2,1)}), bf16[8,64,128]{2,1,0:T(8,128)(2,1)S(1)}, u32[]{:S(2)}, u32[]{:S(2)}) async-start(bf16[8,64,128]{2,1,0:T(8,128)(2,1)} %shard_map.143), calls=%async_computation.4 | async-start | bytes 262144 | tf_op jit(solution)/shard_map/all_to_all | solution.py:17
  160.2 13.2 %collective-permute-start.9 = (bf16[1,48,128]{2,1,0:T(8,128)(2,1)S(1)}, bf16[1,48,128]{2,1,0:T(8,128)(2,1)S(1)}, u32[]{:S(2)}, u32[]{:S(2)}) collective-permute-start(bf16[1,48,128]{2,1,0:T(8,128)(2,1)S(1)} %copy-done.19), channel_id=1, source_target_pairs={{0,256},{32,288},{64,320},{96,352},{128,384},{160,416},{192,448},{... | collective-permute-start | bytes 36872 | tf_op jit(solution)/shard_map/ppermute | solution.py:26
  176.3 21.0 %copy-start.7 = (bf16[512,2,1024]{2,1,0:T(2,128)(2,1)S(1)}, bf16[512,2,1024]{2,1,0:T(2,128)(2,1)}, u32[]{:S(2)}) copy-start(bf16[512,2,1024]{2,1,0:T(2,128)(2,1)} %cot.5) | copy-start | bytes 6291460
  176.3 21.0 %copy-start.11 = (bf16[128,2,1024]{2,1,0:T(2,128)(2,1)S(1)}, bf16[128,2,1024]{2,1,0:T(2,128)(2,1)}, u32[]{:S(2)}) copy-start(bf16[128,2,1024]{2,1,0:T(2,128)(2,1)} %weight.1) | copy-start | bytes 1572868
  177.7 21.9 %copy-start.5 = (bf16[8,1104,128]{2,1,0:T(8,128)(2,1)S(1)}, bf16[8,1104,128]{2,1,0:T(8,128)(2,1)}, u32[]{:S(2)}) copy-start(bf16[8,1104,128]{2,1,0:T(8,128)(2,1)} %copy-done.3) | copy-start | bytes 6782980
  177.7 21.9 %copy-start.22 = (s32[64]{0:T(128)S(1)}, s32[64]{0:T(128)}, u32[]{:S(2)}) copy-start(s32[64]{0:T(128)} %groups.1) | copy-start | bytes 772
  192.0 7.6 %collective-permute-start.11 = (bf16[2,8,64,128]{3,2,1,0:T(8,128)(2,1)S(1)}, bf16[2,8,64,128]{3,2,1,0:T(8,128)(2,1)S(1)}, u32[]{:S(2)}, u32[]{:S(2)}) collective-permute-start(bf16[2,8,64,128]{3,2,1,0:T(8,128)(2,1)S(1)} %bitcast.4), channel_id=1, source_target_pairs={{0,8},{8,0},{1,9},{9,1},{2,10},{10,2},{3,11},{11,3},{4,12},{12,4},... | collective-permute-start | bytes 786440 | tf_op jit(solution)/shard_map/ppermute | solution.py:21
  (15 other events, 38.7 us)

commit v9 on v8

--- a/solution.py
+++ b/solution.py
@@ -26,17 +26,20 @@
     return lax.ppermute(array, axis, pairs)
 
 
+def full_block(array):
+    return pl.BlockSpec(array.shape, lambda i: (0,) * array.ndim)
+
+
 def call(body, outs, scalars, args, places=None, scratch=(), flops=0, limit=20):
-    places = places or [pltpu.VMEM] * len(args)
     specs, arrays = [], []
-    for arg, place in zip(args, places):
+    for arg, place in zip(args, places or [None] * len(args)):
         if isinstance(arg, tuple):
             array, rows, block = arg
             shape = (array.shape[0], rows, array.shape[2])
             specs.append(pl.BlockSpec(shape, functools.partial(lambda k, i: (0, k, 0), block)))
         else:
             array = arg
-            specs.append(pl.BlockSpec(memory_space=place))
+            specs.append(pl.BlockSpec(memory_space=place) if place else full_block(array))
         arrays.append(array)
     bytes_all = sum(a.size * a.dtype.itemsize for a in arrays + list(outs))
     return pl.pallas_call(
@@ -44,7 +47,7 @@
         grid=(1,),
         out_shape=outs,
         in_specs=[pl.BlockSpec(memory_space=pltpu.SMEM)] * len(scalars) + specs,
-        out_specs=[pl.BlockSpec(memory_space=pltpu.VMEM)] * len(outs),
+        out_specs=[full_block(o) for o in outs],
         scratch_shapes=list(scratch),
         compiler_params=pltpu.CompilerParams(vmem_limit_bytes=limit * 1024 * 1024),
         cost_estimate=pl.CostEstimate(flops=flops, bytes_accessed=bytes_all, transcendentals=0),
@@ -185,7 +188,7 @@
         sent[k, 3 * per :] = vals
 
 
-def reduce_z(owners, got, sent, vals):
+def reduce_z(owners, got, keep, f_got, sent, vals, f_sent, f_rest):
     nz, height, _ = sent.shape
     per = height // 3
     xl = lax.axis_index("xl")
@@ -204,6 +207,7 @@
     for i in (1, 2):
         chosen = jnp.where(place == i, got[source[i], 3 * per :].astype(f32), chosen)
     vals[...] = chosen.astype(bf16)
+    factor_z(1, keep, f_got, f_sent, f_rest)
 
 
 def factor_terms(cot, act, whole, sent, keep, flat, both):
@@ -267,7 +271,7 @@
             sent[k, i * half : (i + 1) * half] = rows
         sent[k, 2 * half + piece :] = vals[...]
     sent[:, 2 * half : 2 * half + piece] = got[:, 0:per].reshape(nt, piece, slab)
-    factor_z(1, keep, f_got, f_sent, f_rest)
+    factor_z(4, keep, f_got, f_sent, f_rest)
 
 
 def factor_out(keep, got, factor_a, factor_g):
@@ -297,7 +301,7 @@
         sent[2 * i + 1] = turned[piece:]
 
 
-def scale_rows(rows, own, other, vals, after, sent, rot, scaled, column):
+def scale_rows(rows, own, other, vals, sent, rot, scaled, column):
     nt, piece, slab = rows.shape
     half = own.shape[1]
     core, xl, t = lax.axis_index("c"), lax.axis_index("xl"), lax.axis_index("t")
@@ -370,7 +374,7 @@
         [out(shape), out(shape), out((nt, tok, slab))],
         [],
         [basis_a, basis_g, values_a, values_g, act],
-        [pl.ANY, pl.ANY, pltpu.VMEM, pltpu.VMEM, pltpu.VMEM],
+        [pl.ANY, pl.ANY, None, None, None],
         scratch=[pltpu.SemaphoreType.DMA((2, 3))],
         limit=56,
     )
@@ -399,17 +403,13 @@
         [out((nz, 3 * per + VALS, slab))],
         [owners],
         [keep, got, base, base_got, whole_act],
-        [pltpu.VMEM] * 4 + [pl.ANY],
-    )
-    got = exchange(sent, "z")
-    sent, vals = call(
-        reduce_z, [out((nz, 3 * per, slab)), out((VALS, slab))], [owners], [got]
+        [None] * 4 + [pl.ANY],
     )
     got = exchange(sent, "z")
 
     height = (blocks + 1) * group
     shape = (nz, 2, height, slab)
-    sent, keep = call(
+    sent, f_keep = call(
         factor_terms,
         [out(shape), out(shape, f32)],
         [],
@@ -419,34 +419,46 @@
     )
     f_got = swap(sent, "c")
     shape = (nz, height, slab)
-    sent, keep = call(factor_core, [out(shape), out(shape, f32)], [], [keep, f_got])
+    sent, f_keep = call(factor_core, [out(shape), out(shape, f32)], [], [f_keep, f_got])
     f_got = swap(sent, "xl")
 
+    shape = (nz // 2, height, slab)
+    sent, vals, f_sent, f_keep = call(
+        reduce_z,
+        [out((nz, 3 * per, slab)), out((VALS, slab)), out(shape), out(shape, f32)],
+        [owners],
+        [got, f_keep, f_got],
+    )
+    got = exchange(sent, "z")
+    f_got = across(f_sent, "z", 1)
+    shape = (nz // 4, height, slab)
+    f_sent, f_keep = call(
+        functools.partial(factor_z, 2), [out(shape), out(shape, f32)], [], [f_keep, f_got]
+    )
+    f_got = across(f_sent, "z", 2)
+
     width = piece + 2 * half + VALS
-    shape = (nz // 2, height, slab)
+    shape = (nz // 8, height, slab)
     sent, f_sent, f_keep = call(
         pack_t,
         [out((nt, width, slab)), out(shape), out(shape, f32)],
         [],
-        [got, vals, keep, f_got],
+        [got, vals, f_keep, f_got],
     )
     own = exchange(sent, "t")
-    f_got = across(f_sent, "z", 1)
-    bit = 2
-    while bit < nz:
-        shape = (nz // 2 // bit, height, slab)
-        f_sent, f_keep = call(
-            functools.partial(factor_z, bit), [out(shape), out(shape, f32)], [], [f_keep, f_got]
-        )
-        f_got = across(f_sent, "z", bit)
-        bit *= 2
+    f_got = across(f_sent, "z", 4)
+    shape = (nz // 16, height, slab)
+    f_sent, f_keep = call(
+        functools.partial(factor_z, 8), [out(shape), out(shape, f32)], [], [f_keep, f_got]
+    )
+    f_got = across(f_sent, "z", 8)
     factor_a, factor_g = call(
         factor_out,
         [out((group, slab), f32), out((blocks, group, slab), f32)],
         [],
         [f_keep, f_got],
     )
-    own = follow(own, f_sent)
+    own = follow(own, factor_a)
     other = swap(own, "c")
     qa, qa_other = (own, half, 0), (other, half, 0)
     qg, qg_other = (own, half, 1), (other, half, 1)
@@ -465,8 +477,7 @@
         scale_rows,
         [out((blocks, nt, piece, slab))],
         [],
-        [rows, qg, qg_other, vals, factor_a],
-        [pltpu.VMEM] * 4 + [pl.ANY],
+        [rows, qg, qg_other, vals],
         scratch=[
             pltpu.VMEM((piece, full), bf16),
             pltpu.VMEM((nt, piece, slab), bf16),

time: 205 us -> 197 us (0.961)
  blocking collectives: 48.6 us -> 22.1 us
  waiting for transfers between devices: 30.7 us -> 46.9 us
  starting transfers between devices: 90.3 us -> 96.2 us
  local copies, waits for them, and re-layouts: 14.3 us -> 10.7 us
    all_to_all x2, blocking collectives: 48.6 us -> 22.1 us  [exchange(): return lax.all_to_all(array, axis, 0, 0, tiled=True)]
    ppermute x4, waiting for transfers between devices: 11.1 us -> 21.5 us  [across(): return lax.ppermute(array, axis, pairs)]
    all_to_all x4, starting transfers between devices: 31.4 us -> 39.2 us  [exchange(): return lax.all_to_all(array, axis, 0, 0, tiled=True)]
    all_to_all x4, waiting for transfers between devices: 2.84 us -> 8.66 us  [exchange(): return lax.all_to_all(array, axis, 0, 0, tiled=True)]
    unnamed x47 -> x37, local copies, waits for them, and re-layouts: 14.3 us -> 10.7 us
    pallas_call x17 -> x16, Pallas kernels: 18.4 us -> 19 us  [call(): pl.pallas_call(body, grid=(1,), out_shape=outs, in_specs=[pl.BlockSpec(me...]
  transfers between devices with their start and end apart: 16 -> 16, of which waited for: 9 -> 10; matrix products, arithmetic and copies ran while one was open for 0% -> 0% of each run, Pallas kernels for 3% -> 3%
where the time goes in v9:
time: 197 us; the launch traced here: 196 us
  starting transfers between devices  96.2 us (49%)
  waiting for transfers between devices  46.9 us (24%)
  blocking collectives  22.1 us (11%)
  Pallas kernels  19 us (10%)
  local copies, waits for them, and re-layouts  10.7 us (5%)
    all_to_all x4, starting transfers between devices, exchange(): return lax.all_to_all(array, axis, 0, 0, tiled=True)  39.2 us
    ppermute x8, starting transfers between devices, swap(): return lax.ppermute(array, axis, [(0, 1), (1, 0)])  30.4 us
    ppermute x4, starting transfers between devices, across(): return lax.ppermute(array, axis, pairs)  26.5 us
    all_to_all x2, blocking collectives, exchange(): return lax.all_to_all(array, axis, 0, 0, tiled=True)  22.1 us
    ppermute x4, waiting for transfers between devices, across(): return lax.ppermute(array, axis, pairs)  21.5 us
    pallas_call x16, Pallas kernels, call(): pl.pallas_call(body, grid=(1,), out_shape=outs, in_specs=[pl.BlockSpec(me...  19 us
    ppermute x8, waiting for transfers between devices, swap(): return lax.ppermute(array, axis, [(0, 1), (1, 0)])  16.7 us
    unnamed x37, local copies, waits for them, and re-layouts  10.7 us
  transfers between devices with their start and end apart: 16, of which 10 were waited for; matrix products, arithmetic and copies ran while one was open for 0% of the time, Pallas kernels for 3%

profile of v9, /device:TPU:1, one launch (start us, length us, event | category | flops | bytes accessed | tf_op | source)
XLA Modules:
  0.0 195.9 jit_solution(6905259788474132610)
XLA Ops:
  0.7 3.6 %shard_map.131 = (bf16[1552,128]{1,0:T(8,128)(2,1)}, bf16[1552,128]{1,0:T(8,128)(2,1)}, bf16[8,512,128]{2,1,0:T(8,128)(2,1)}) custom-call(bf16[1,1024,128]{2,1,0:T(8,128)(2,1)} %ba.1, bf16[1,2,1024,128]{3,2,1,0:T(8,128)(2,1)} %bg.1, bf16[1,128]{1,0:T(2,128)(2,1)} %va.1, bf16[1,2,128]{2,1,0:T(2,128)(2,1)} %vg.1, bf16[512,128]{1,0:T(8,128)(2,1)} %act.5), custom_call_target="tpu_custom_call" | custom-call | bytes 2761472 | tf_op jit(solution)/shard_map/pallas_call | solution.py:45
  4.3 7.5 %all-to-all-start = ((bf16[8,512,128]{2,1,0:T(8,128)(2,1)}), bf16[8,512,128]{2,1,0:T(8,128)(2,1)S(1)}, u32[]{:S(2)}, u32[]{:S(2)}) async-start(bf16[8,512,128]{2,1,0:T(8,128)(2,1)} %get-tuple-element.41), calls=%async_computation | async-start | bytes 2097152 | tf_op jit(solution)/shard_map/all_to_all | solution.py:17
  11.8 5.0 %collective-permute-start.2 = (bf16[1552,128]{1,0:T(8,128)(2,1)}, bf16[1552,128]{1,0:T(8,128)(2,1)S(1)}, u32[]{:S(2)}, u32[]{:S(2)}) collective-permute-start(bf16[1552,128]{1,0:T(8,128)(2,1)} %get-tuple-element.38), channel_id=1, source_target_pairs={{0,8},{8,0},{1,9},{9,1},{2,10},{10,2},{3,11},{11,3},{4,12},{12,4},... | collective-permute-start | bytes 1191944 | tf_op jit(solution)/shard_map/ppermute | solution.py:21
  24.0 3.4 %collective-permute-start.1 = (bf16[512,128]{1,0:T(8,128)(2,1)S(1)}, bf16[512,128]{1,0:T(8,128)(2,1)S(1)}, u32[]{:S(2)}, u32[]{:S(2)}) collective-permute-start(bf16[512,128]{1,0:T(8,128)(2,1)S(1)} %get-tuple-element.36), channel_id=1, source_target_pairs={{0,16},{16,0},{1,17},{17,1},{2,18},{18,2},{3,19},{19,3},{4,20},{20... | collective-permute-start | bytes 393224 | tf_op jit(solution)/shard_map/ppermute | solution.py:21
  27.3 6.1 %collective-permute-done.1.got = bf16[512,128]{1,0:T(8,128)(2,1)S(1)} collective-permute-done((bf16[512,128]{1,0:T(8,128)(2,1)S(1)}, bf16[512,128]{1,0:T(8,128)(2,1)S(1)}, u32[]{:S(2)}, u32[]{:S(2)}) %collective-permute-start.1) | collective-permute-done | bytes 131104 | tf_op jit(solution)/shard_map/ppermute | solution.py:21
  39.0 14.0 %all-to-all-start.1 = ((bf16[16,112,128]{2,1,0:T(8,128)(2,1)}), bf16[16,112,128]{2,1,0:T(8,128)(2,1)}, u32[]{:S(2)}, u32[]{:S(2)}) async-start(bf16[16,112,128]{2,1,0:T(8,128)(2,1)} %copy-done.6), calls=%async_computation.1 | async-start | bytes 917504 | tf_op jit(solution)/shard_map/all_to_all | solution.py:17
  54.8 3.5 %collective-permute-start.4 = (bf16[16,2,48,128]{3,2,1,0:T(8,128)(2,1)S(1)}, bf16[16,2,48,128]{3,2,1,0:T(8,128)(2,1)S(1)}, u32[]{:S(2)}, u32[]{:S(2)}) collective-permute-start(bf16[16,2,48,128]{3,2,1,0:T(8,128)(2,1)S(1)} %get-tuple-element.43), channel_id=1, source_target_pairs={{0,8},{8,0},{1,9},{9,1},{2,10},{10,2},{3,11},{11,3},{4,12},{12,4},... | collective-permute-start | bytes 1179656 | tf_op jit(solution)/shard_map/ppermute | solution.py:21
  59.7 3.1 %collective-permute-start.5 = (bf16[16,48,128]{2,1,0:T(8,128)(2,1)S(1)}, bf16[16,48,128]{2,1,0:T(8,128)(2,1)S(1)}, u32[]{:S(2)}, u32[]{:S(2)}) collective-permute-start(bf16[16,48,128]{2,1,0:T(8,128)(2,1)S(1)} %get-tuple-element.45), channel_id=1, source_target_pairs={{0,16},{16,0},{1,17},{17,1},{2,18},{18,2},{3,19},{19,3},{4,20},{20... | collective-permute-start | bytes 589832 | tf_op jit(solution)/shard_map/ppermute | solution.py:21
  62.8 5.0 %collective-permute-done.5.f_got = bf16[16,48,128]{2,1,0:T(8,128)(2,1)S(1)} collective-permute-done((bf16[16,48,128]{2,1,0:T(8,128)(2,1)S(1)}, bf16[16,48,128]{2,1,0:T(8,128)(2,1)S(1)}, u32[]{:S(2)}, u32[]{:S(2)}) %collective-permute-start.5) | collective-permute-done | bytes 196640 | tf_op jit(solution)/shard_map/ppermute | solution.py:21
  67.8 5.8 %all-to-all-done.1.got = bf16[16,112,128]{2,1,0:T(8,128)(2,1)} async-done(((bf16[16,112,128]{2,1,0:T(8,128)(2,1)}), bf16[16,112,128]{2,1,0:T(8,128)(2,1)}, u32[]{:S(2)}, u32[]{:S(2)}) %all-to-all-start.1) | async-done | bytes 458784 | tf_op jit(solution)/shard_map/all_to_all | solution.py:17
  75.5 11.7 %all-to-all-start.2 = ((bf16[16,96,128]{2,1,0:T(8,128)(2,1)}), bf16[16,96,128]{2,1,0:T(8,128)(2,1)S(1)}, u32[]{:S(2)}, u32[]{:S(2)}) async-start(bf16[16,96,128]{2,1,0:T(8,128)(2,1)} %get-tuple-element.46), calls=%async_computation.2 | async-start | bytes 786432 | tf_op jit(solution)/shard_map/all_to_all | solution.py:17
  87.3 3.3 %collective-permute-start.6 = (bf16[8,48,128]{2,1,0:T(8,128)(2,1)S(1)}, bf16[8,48,128]{2,1,0:T(8,128)(2,1)S(1)}, u32[]{:S(2)}, u32[]{:S(2)}) collective-permute-start(bf16[8,48,128]{2,1,0:T(8,128)(2,1)S(1)} %get-tuple-element.49), channel_id=1, source_target_pairs={{0,32},{32,0},{64,96},{96,64},{128,160},{160,128},{192,224},{224,1... | collective-permute-start | bytes 294920 | tf_op jit(solution)/shard_map/ppermute | solution.py:26
  90.5 16.5 %collective-permute-done.6.got = bf16[8,48,128]{2,1,0:T(8,128)(2,1)S(1)} collective-permute-done((bf16[8,48,128]{2,1,0:T(8,128)(2,1)S(1)}, bf16[8,48,128]{2,1,0:T(8,128)(2,1)S(1)}, u32[]{:S(2)}, u32[]{:S(2)}) %collective-permute-start.6) | collective-permute-done | bytes 98336 | tf_op jit(solution)/shard_map/ppermute | solution.py:26
  107.1 2.9 %collective-permute-start.7 = (bf16[4,48,128]{2,1,0:T(8,128)(2,1)S(1)}, bf16[4,48,128]{2,1,0:T(8,128)(2,1)S(1)}, u32[]{:S(2)}, u32[]{:S(2)}) collective-permute-start(bf16[4,48,128]{2,1,0:T(8,128)(2,1)S(1)} %get-tuple-element.51), channel_id=1, source_target_pairs={{0,64},{32,96},{64,0},{96,32},{128,192},{160,224},{192,128},{224,1... | collective-permute-start | bytes 147464 | tf_op jit(solution)/shard_map/ppermute | solution.py:26
  114.5 6.0 %all-to-all-start.3 = ((bf16[8,1104,128]{2,1,0:T(8,128)(2,1)}), bf16[8,1104,128]{2,1,0:T(8,128)(2,1)S(1)}, u32[]{:S(2)}, u32[]{:S(2)}) async-start(bf16[8,1104,128]{2,1,0:T(8,128)(2,1)} %copy-done.5), calls=%async_computation.3 | async-start | bytes 4521984 | tf_op jit(solution)/shard_map/all_to_all | solution.py:17
  120.5 7.5 %collective-permute-start.8 = (bf16[2,48,128]{2,1,0:T(8,128)(2,1)S(1)}, bf16[2,48,128]{2,1,0:T(8,128)(2,1)S(1)}, u32[]{:S(2)}, u32[]{:S(2)}) collective-permute-start(bf16[2,48,128]{2,1,0:T(8,128)(2,1)S(1)} %get-tuple-element.53), channel_id=1, source_target_pairs={{0,128},{32,160},{64,192},{96,224},{128,0},{160,32},{192,64},{224,... | collective-permute-start | bytes 73736 | tf_op jit(solution)/shard_map/ppermute | solution.py:26
  129.3 12.8 %collective-permute-start.9 = (bf16[1,48,128]{2,1,0:T(8,128)(2,1)S(1)}, bf16[1,48,128]{2,1,0:T(8,128)(2,1)S(1)}, u32[]{:S(2)}, u32[]{:S(2)}) collective-permute-start(bf16[1,48,128]{2,1,0:T(8,128)(2,1)S(1)} %get-tuple-element.55), channel_id=1, source_target_pairs={{0,256},{32,288},{64,320},{96,352},{128,384},{160,416},{192,448},{... | collective-permute-start | bytes 36872 | tf_op jit(solution)/shard_map/ppermute | solution.py:26
  143.7 2.8 %all-to-all-done.3.refs_0_ = bf16[8,1104,128]{2,1,0:T(8,128)(2,1)S(1)} async-done(((bf16[8,1104,128]{2,1,0:T(8,128)(2,1)}), bf16[8,1104,128]{2,1,0:T(8,128)(2,1)S(1)}, u32[]{:S(2)}, u32[]{:S(2)}) %all-to-all-start.3) | async-done | bytes 2261024 | tf_op jit(solution)/shard_map/all_to_all | solution.py:17
  148.0 7.0 %collective-permute-start.10 = (bf16[8,1104,128]{2,1,0:T(8,128)(2,1)}, bf16[8,1104,128]{2,1,0:T(8,128)(2,1)S(1)}, u32[]{:S(2)}, u32[]{:S(2)}) collective-permute-start(bf16[8,1104,128]{2,1,0:T(8,128)(2,1)} %shard_map.141.own.own_grad.vals), channel_id=1, source_target_pairs={{0,8},{8,0},{1,9},{9,1},{2,10},{10,2},{3,11},{11,3},{4,12},{12,4},... | collective-permute-start | bytes 6782984 | tf_op jit(solution)/shard_map/ppermute | solution.py:21
  155.0 4.2 %collective-permute-done.10.other.other_grad = bf16[8,1104,128]{2,1,0:T(8,128)(2,1)S(1)} collective-permute-done((bf16[8,1104,128]{2,1,0:T(8,128)(2,1)}, bf16[8,1104,128]{2,1,0:T(8,128)(2,1)S(1)}, u32[]{:S(2)}, u32[]{:S(2)}) %collective-permute-start.10) | collective-permute-done | bytes 2261024 | tf_op jit(solution)/shard_map/ppermute | solution.py:21
  161.6 11.4 %all_to_all.30.rows = bf16[8,64,128]{2,1,0:T(8,128)(2,1)S(1)} all-to-all(bf16[8,64,128]{2,1,0:T(8,128)(2,1)S(1)} %shard_map.142), channel_id=1, replica_groups=mesh['z'=16,'xl'=2,'c'=2,'t'=8] {'t'}, dimensions={0} | all-to-all | bytes 262144 | tf_op jit(solution)/shard_map/all_to_all | solution.py:17
  174.4 10.7 %all_to_all.31 = bf16[16,64,128]{2,1,0:T(8,128)(2,1)S(1)} all-to-all(bf16[16,64,128]{2,1,0:T(8,128)(2,1)S(1)} %bitcast.3), channel_id=1, replica_groups=mesh['z'=16,'xl'=2,'c'=2,'t'=8] {'xl','t'}, dimensions={0} | all-to-all | bytes 524288 | tf_op jit(solution)/shard_map/all_to_all | solution.py:17
  185.1 4.7 %collective-permute-start.11 = (bf16[2,8,64,128]{3,2,1,0:T(8,128)(2,1)S(1)}, bf16[2,8,64,128]{3,2,1,0:T(8,128)(2,1)S(1)}, u32[]{:S(2)}, u32[]{:S(2)}) collective-permute-start(bf16[2,8,64,128]{3,2,1,0:T(8,128)(2,1)S(1)} %bitcast.4), channel_id=1, source_target_pairs={{0,8},{8,0},{1,9},{9,1},{2,10},{10,2},{3,11},{11,3},{4,12},{12,4},... | collective-permute-start | bytes 786440 | tf_op jit(solution)/shard_map/ppermute | solution.py:21
  192.0 3.9 %shard_map.144 = (bf16[1024,2,128]{2,1,0:T(2,128)(2,1)}, bf16[1,1024,128]{2,1,0:T(8,128)(2,1)}) custom-call(s32[64]{0:T(128)S(1)} %copy-done.17, bf16[8,1104,128]{2,1,0:T(8,128)(2,1)S(1)} %copy-done.2, bf16[8,1104,128]{2,1,0:T(8,128)(2,1)S(1)} %collective-permute-done.10.other.other_grad, bf16[2,8,64,128]{3,2,1,0:T(8,128)(2,1)S(1)} %bitcast.5, ...), custom_call_target="tpu_custom_call" | custom-call | flops 536870912 | bytes 5832704 | tf_op jit(solution)/shard_map/pallas_call | solution.py:45
  (64 shorter events, 32.5 us)
Async XLA Ops:
  0.6 16.2 %copy-start.7 = (bf16[512,128]{1,0:T(8,128)(2,1)S(1)}, bf16[512,128]{1,0:T(8,128)(2,1)}, u32[]{:S(2)}) copy-start(bf16[512,128]{1,0:T(8,128)(2,1)} %act.5) | copy-start | bytes 393220
  0.6 16.2 %copy-start.3 = (bf16[512,2,1024]{2,1,0:T(2,128)(2,1)S(1)}, bf16[512,2,1024]{2,1,0:T(2,128)(2,1)}, u32[]{:S(2)}) copy-start(bf16[512,2,1024]{2,1,0:T(2,128)(2,1)} %cot.5) | copy-start | bytes 6291460
  4.3 16.3 %copy-start.16 = (s32[3]{0:T(128)S(1)}, s32[3]{0:T(128)}, u32[]{:S(2)}) copy-start(s32[3]{0:T(128)} %owners.5) | copy-start | bytes 40
  4.3 30.5 %all-to-all-start = ((bf16[8,512,128]{2,1,0:T(8,128)(2,1)}), bf16[8,512,128]{2,1,0:T(8,128)(2,1)S(1)}, u32[]{:S(2)}, u32[]{:S(2)}) async-start(bf16[8,512,128]{2,1,0:T(8,128)(2,1)} %get-tuple-element.41), calls=%async_computation | async-start | bytes 2097152 | tf_op jit(solution)/shard_map/all_to_all | solution.py:17
  11.8 8.8 %copy-start.9 = (bf16[1552,128]{1,0:T(8,128)(2,1)S(1)}, bf16[1552,128]{1,0:T(8,128)(2,1)}, u32[]{:S(2)}) copy-start(bf16[1552,128]{1,0:T(8,128)(2,1)} %get-tuple-element.37.own) | copy-start | bytes 1191940
  11.8 8.8 %collective-permute-start.2 = (bf16[1552,128]{1,0:T(8,128)(2,1)}, bf16[1552,128]{1,0:T(8,128)(2,1)S(1)}, u32[]{:S(2)}, u32[]{:S(2)}) collective-permute-start(bf16[1552,128]{1,0:T(8,128)(2,1)} %get-tuple-element.38), channel_id=1, source_target_pairs={{0,8},{8,0},{1,9},{9,1},{2,10},{10,2},{3,11},{11,3},{4,12},{12,4},... | collective-permute-start | bytes 1191944 | tf_op jit(solution)/shard_map/ppermute | solution.py:21
  18.6 4.5 %collective-permute-start = (bf16[2,512,128]{2,1,0:T(8,128)(2,1)S(1)}, bf16[2,512,128]{2,1,0:T(8,128)(2,1)S(1)}, u32[]{:S(2)}, u32[]{:S(2)}) collective-permute-start(bf16[2,512,128]{2,1,0:T(8,128)(2,1)S(1)} %get-tuple-element.34), channel_id=1, source_target_pairs={{0,8},{8,0},{1,9},{9,1},{2,10},{10,2},{3,11},{11,3},{4,12},{12,4},... | collective-permute-start | bytes 786440 | tf_op jit(solution)/shard_map/ppermute | solution.py:21
  21.2 12.8 %collective-permute-start.3 = (bf16[1040,128]{1,0:T(8,128)(2,1)S(1)}, bf16[1040,128]{1,0:T(8,128)(2,1)S(1)}, u32[]{:S(2)}, u32[]{:S(2)}) collective-permute-start(bf16[1040,128]{1,0:T(8,128)(2,1)S(1)} %get-tuple-element.40), channel_id=1, source_target_pairs={{0,16},{16,0},{1,17},{17,1},{2,18},{18,2},{3,19},{19,3},{4,20},{20... | collective-permute-start | bytes 798728 | tf_op jit(solution)/shard_map/ppermute | solution.py:21
  24.0 9.5 %collective-permute-start.1 = (bf16[512,128]{1,0:T(8,128)(2,1)S(1)}, bf16[512,128]{1,0:T(8,128)(2,1)S(1)}, u32[]{:S(2)}, u32[]{:S(2)}) collective-permute-start(bf16[512,128]{1,0:T(8,128)(2,1)S(1)} %get-tuple-element.36), channel_id=1, source_target_pairs={{0,16},{16,0},{1,17},{17,1},{2,18},{18,2},{3,19},{19,3},{4,20},{20... | collective-permute-start | bytes 393224 | tf_op jit(solution)/shard_map/ppermute | solution.py:21
  39.0 34.7 %all-to-all-start.1 = ((bf16[16,112,128]{2,1,0:T(8,128)(2,1)}), bf16[16,112,128]{2,1,0:T(8,128)(2,1)}, u32[]{:S(2)}, u32[]{:S(2)}) async-start(bf16[16,112,128]{2,1,0:T(8,128)(2,1)} %copy-done.6), calls=%async_computation.1 | async-start | bytes 917504 | tf_op jit(solution)/shard_map/all_to_all | solution.py:17
  54.8 4.8 %collective-permute-start.4 = (bf16[16,2,48,128]{3,2,1,0:T(8,128)(2,1)S(1)}, bf16[16,2,48,128]{3,2,1,0:T(8,128)(2,1)S(1)}, u32[]{:S(2)}, u32[]{:S(2)}) collective-permute-start(bf16[16,2,48,128]{3,2,1,0:T(8,128)(2,1)S(1)} %get-tuple-element.43), channel_id=1, source_target_pairs={{0,8},{8,0},{1,9},{9,1},{2,10},{10,2},{3,11},{11,3},{4,12},{12,4},... | collective-permute-start | bytes 1179656 | tf_op jit(solution)/shard_map/ppermute | solution.py:21
  59.7 8.1 %collective-permute-start.5 = (bf16[16,48,128]{2,1,0:T(8,128)(2,1)S(1)}, bf16[16,48,128]{2,1,0:T(8,128)(2,1)S(1)}, u32[]{:S(2)}, u32[]{:S(2)}) collective-permute-start(bf16[16,48,128]{2,1,0:T(8,128)(2,1)S(1)} %get-tuple-element.45), channel_id=1, source_target_pairs={{0,16},{16,0},{1,17},{17,1},{2,18},{18,2},{3,19},{19,3},{4,20},{20... | collective-permute-start | bytes 589832 | tf_op jit(solution)/shard_map/ppermute | solution.py:21
  75.5 37.3 %all-to-all-start.2 = ((bf16[16,96,128]{2,1,0:T(8,128)(2,1)}), bf16[16,96,128]{2,1,0:T(8,128)(2,1)S(1)}, u32[]{:S(2)}, u32[]{:S(2)}) async-start(bf16[16,96,128]{2,1,0:T(8,128)(2,1)} %get-tuple-element.46), calls=%async_computation.2 | async-start | bytes 786432 | tf_op jit(solution)/shard_map/all_to_all | solution.py:17
  87.3 19.8 %collective-permute-start.6 = (bf16[8,48,128]{2,1,0:T(8,128)(2,1)S(1)}, bf16[8,48,128]{2,1,0:T(8,128)(2,1)S(1)}, u32[]{:S(2)}, u32[]{:S(2)}) collective-permute-start(bf16[8,48,128]{2,1,0:T(8,128)(2,1)S(1)} %get-tuple-element.49), channel_id=1, source_target_pairs={{0,32},{32,0},{64,96},{96,64},{128,160},{160,128},{192,224},{224,1... | collective-permute-start | bytes 294920 | tf_op jit(solution)/shard_map/ppermute | solution.py:26
  107.1 5.7 %collective-permute-start.7 = (bf16[4,48,128]{2,1,0:T(8,128)(2,1)S(1)}, bf16[4,48,128]{2,1,0:T(8,128)(2,1)S(1)}, u32[]{:S(2)}, u32[]{:S(2)}) collective-permute-start(bf16[4,48,128]{2,1,0:T(8,128)(2,1)S(1)} %get-tuple-element.51), channel_id=1, source_target_pairs={{0,64},{32,96},{64,0},{96,32},{128,192},{160,224},{192,128},{224,1... | collective-permute-start | bytes 147464 | tf_op jit(solution)/shard_map/ppermute | solution.py:26
  114.5 32.0 %all-to-all-start.3 = ((bf16[8,1104,128]{2,1,0:T(8,128)(2,1)}), bf16[8,1104,128]{2,1,0:T(8,128)(2,1)S(1)}, u32[]{:S(2)}, u32[]{:S(2)}) async-start(bf16[8,1104,128]{2,1,0:T(8,128)(2,1)} %copy-done.5), calls=%async_computation.3 | async-start | bytes 4521984 | tf_op jit(solution)/shard_map/all_to_all | solution.py:17
  120.5 8.7 %collective-permute-start.8 = (bf16[2,48,128]{2,1,0:T(8,128)(2,1)S(1)}, bf16[2,48,128]{2,1,0:T(8,128)(2,1)S(1)}, u32[]{:S(2)}, u32[]{:S(2)}) collective-permute-start(bf16[2,48,128]{2,1,0:T(8,128)(2,1)S(1)} %get-tuple-element.53), channel_id=1, source_target_pairs={{0,128},{32,160},{64,192},{96,224},{128,0},{160,32},{192,64},{224,... | collective-permute-start | bytes 73736 | tf_op jit(solution)/shard_map/ppermute | solution.py:26
  129.3 13.9 %collective-permute-start.9 = (bf16[1,48,128]{2,1,0:T(8,128)(2,1)S(1)}, bf16[1,48,128]{2,1,0:T(8,128)(2,1)S(1)}, u32[]{:S(2)}, u32[]{:S(2)}) collective-permute-start(bf16[1,48,128]{2,1,0:T(8,128)(2,1)S(1)} %get-tuple-element.55), channel_id=1, source_target_pairs={{0,256},{32,288},{64,320},{96,352},{128,384},{160,416},{192,448},{... | collective-permute-start | bytes 36872 | tf_op jit(solution)/shard_map/ppermute | solution.py:26
  148.0 11.3 %collective-permute-start.10 = (bf16[8,1104,128]{2,1,0:T(8,128)(2,1)}, bf16[8,1104,128]{2,1,0:T(8,128)(2,1)S(1)}, u32[]{:S(2)}, u32[]{:S(2)}) collective-permute-start(bf16[8,1104,128]{2,1,0:T(8,128)(2,1)} %shard_map.141.own.own_grad.vals), channel_id=1, source_target_pairs={{0,8},{8,0},{1,9},{9,1},{2,10},{10,2},{3,11},{11,3},{4,12},{12,4},... | collective-permute-start | bytes 6782984 | tf_op jit(solution)/shard_map/ppermute | solution.py:21
  173.0 16.8 %copy-start.4 = (bf16[512,2,1024]{2,1,0:T(2,128)(2,1)S(1)}, bf16[512,2,1024]{2,1,0:T(2,128)(2,1)}, u32[]{:S(2)}) copy-start(bf16[512,2,1024]{2,1,0:T(2,128)(2,1)} %cot.5) | copy-start | bytes 6291460
  173.0 16.8 %copy-start.8 = (bf16[128,2,1024]{2,1,0:T(2,128)(2,1)S(1)}, bf16[128,2,1024]{2,1,0:T(2,128)(2,1)}, u32[]{:S(2)}) copy-start(bf16[128,2,1024]{2,1,0:T(2,128)(2,1)} %weight.1) | copy-start | bytes 1572868
  174.3 17.7 %copy-start.2 = (bf16[8,1104,128]{2,1,0:T(8,128)(2,1)S(1)}, bf16[8,1104,128]{2,1,0:T(8,128)(2,1)}, u32[]{:S(2)}) copy-start(bf16[8,1104,128]{2,1,0:T(8,128)(2,1)} %shard_map.141.own.own_grad.vals) | copy-start | bytes 6782980
  174.3 17.7 %copy-start.17 = (s32[64]{0:T(128)S(1)}, s32[64]{0:T(128)}, u32[]{:S(2)}) copy-start(s32[64]{0:T(128)} %groups.1) | copy-start | bytes 772
  185.1 6.9 %collective-permute-start.11 = (bf16[2,8,64,128]{3,2,1,0:T(8,128)(2,1)S(1)}, bf16[2,8,64,128]{3,2,1,0:T(8,128)(2,1)S(1)}, u32[]{:S(2)}, u32[]{:S(2)}) collective-permute-start(bf16[2,8,64,128]{3,2,1,0:T(8,128)(2,1)S(1)} %bitcast.4), channel_id=1, source_target_pairs={{0,8},{8,0},{1,9},{9,1},{2,10},{10,2},{3,11},{11,3},{4,12},{12,4},... | collective-permute-start | bytes 786440 | tf_op jit(solution)/shard_map/ppermute | solution.py:21
  (10 other events, 10.1 us)

commit v10 on v9

--- a/solution.py
+++ b/solution.py
@@ -61,6 +61,7 @@
         in_specs=[pl.BlockSpec(memory_space=pl.ANY)] * 2,
         out_specs=pl.BlockSpec(memory_space=pl.ANY),
         input_output_aliases={0: 0},
+        compiler_params=pltpu.CompilerParams(vmem_limit_bytes=56 * 1024 * 1024),
     )(array, after)
 
 
@@ -165,7 +166,7 @@
     rest[...] = keep[xl] + got[xl].astype(f32)
 
 
-def pack_z(owners, keep, got, own, other, after, sent):
+def pack_z(owners, keep, got, own, other, sent):
     nz, _, slab = sent.shape
     half = (own.shape[0] - VALS) // 2
     per = half // nz
@@ -271,7 +272,7 @@
             sent[k, i * half : (i + 1) * half] = rows
         sent[k, 2 * half + piece :] = vals[...]
     sent[:, 2 * half : 2 * half + piece] = got[:, 0:per].reshape(nt, piece, slab)
-    factor_z(4, keep, f_got, f_sent, f_rest)
+    factor_z(2, keep, f_got, f_sent, f_rest)
 
 
 def factor_out(keep, got, factor_a, factor_g):
@@ -336,11 +337,13 @@
     for side, ref in ((core, own), (1 - core, other)):
         total = jnp.zeros((half, blocks * slab), f32)
         for part, mixed in ((core, own_mixed), (1 - core, other_mixed)):
-            for i in range(nt // 2):
+            for i in range(nt // 4):
+                k = part * (nt // 2) + 2 * i
+                left = jnp.concatenate([ref[k], ref[k + 1]], 1)
                 right = jnp.concatenate(
-                    [mixed[j, 2 * i : 2 * i + 2].reshape(2 * piece, slab) for j in range(blocks)], 1
+                    [mixed[j, 4 * i : 4 * i + 4].reshape(4 * piece, slab) for j in range(blocks)], 1
                 )
-                total = total + dot(ref[part * (nt // 2) + i], right)
+                total = total + dot(left, right)
         total = total.astype(bf16)
         place = pl.ds(pl.multiple_of(side * half, half), half)
         pre[place] = total.reshape(half, blocks, slab)
@@ -402,10 +405,9 @@
         pack_z,
         [out((nz, 3 * per + VALS, slab))],
         [owners],
-        [keep, got, base, base_got, whole_act],
-        [None] * 4 + [pl.ANY],
-    )
-    got = exchange(sent, "z")
+        [keep, got, base, base_got],
+    )
+    got = exchange(follow(sent, whole_act), "z")
 
     height = (blocks + 1) * group
     shape = (nz, 2, height, slab)
@@ -431,27 +433,24 @@
     )
     got = exchange(sent, "z")
     f_got = across(f_sent, "z", 1)
+
+    width = piece + 2 * half + VALS
     shape = (nz // 4, height, slab)
-    f_sent, f_keep = call(
-        functools.partial(factor_z, 2), [out(shape), out(shape, f32)], [], [f_keep, f_got]
-    )
-    f_got = across(f_sent, "z", 2)
-
-    width = piece + 2 * half + VALS
-    shape = (nz // 8, height, slab)
     sent, f_sent, f_keep = call(
         pack_t,
         [out((nt, width, slab)), out(shape), out(shape, f32)],
         [],
         [got, vals, f_keep, f_got],
+        limit=56,
     )
     own = exchange(sent, "t")
-    f_got = across(f_sent, "z", 4)
-    shape = (nz // 16, height, slab)
-    f_sent, f_keep = call(
-        functools.partial(factor_z, 8), [out(shape), out(shape, f32)], [], [f_keep, f_got]
-    )
-    f_got = across(f_sent, "z", 8)
+    f_got = across(f_sent, "z", 2)
+    for bit in (4, 8):
+        shape = (nz // 2 // bit, height, slab)
+        f_sent, f_keep = call(
+            functools.partial(factor_z, bit), [out(shape), out(shape, f32)], [], [f_keep, f_got]
+        )
+        f_got = across(f_sent, "z", bit)
     factor_a, factor_g = call(
         factor_out,
         [out((group, slab), f32), out((blocks, group, slab), f32)],
@@ -471,6 +470,7 @@
         [qa, qa_other, columns, columns_other],
         scratch=[pltpu.VMEM((slab, full), bf16)],
         flops=2 * slab * full * half,
+        limit=56,
     )
     rows = exchange(sent, "t")
     (sent,) = call(
@@ -484,6 +484,7 @@
             pltpu.VMEM((slab, slab), f32),
         ],
         flops=4 * piece * full * full,
+        limit=56,
     )
     own_mixed = exchange(sent.reshape(blocks * nt, piece, slab), ("xl", "t"))
     own_mixed = own_mixed.reshape(blocks, nt, piece, slab)
@@ -494,6 +495,7 @@
         [worker_group],
         [qa, qa_other, own_mixed, other_mixed],
         flops=4 * full * full * slab,
+        limit=56,
     )
 
     (grad_input,) = call(

time: 197 us -> 204 us (1.036)
  Pallas kernels: 19 us -> 25.8 us
  local copies, waits for them, and re-layouts: 10.7 us -> 7.17 us
  starting transfers between devices: 96.2 us -> 99.7 us
  waiting for transfers between devices: 46.9 us -> 43.4 us
  blocking collectives: 22.1 us -> 25.2 us
    pallas_call x16, Pallas kernels: 19 us -> 25.8 us  [call(): pl.pallas_call(body, grid=(1,), out_shape=outs, in_specs=[pl.BlockSpec(me...]
    all_to_all x4, waiting for transfers between devices: 8.66 us -> 4.63 us  [exchange(): return lax.all_to_all(array, axis, 0, 0, tiled=True)]
    unnamed x37 -> x35, local copies, waits for them, and re-layouts: 10.7 us -> 7.17 us
    all_to_all x2, blocking collectives: 22.1 us -> 25.2 us  [exchange(): return lax.all_to_all(array, axis, 0, 0, tiled=True)]
    ppermute x8, starting transfers between devices: 30.4 us -> 33.1 us  [swap(): return lax.ppermute(array, axis, [(0, 1), (1, 0)])]
  transfers between devices with their start and end apart: 16 -> 16, of which waited for: 10 -> 9; matrix products, arithmetic and copies ran while one was open for 0% -> 0% of each run, Pallas kernels for 3% -> 4%
where the time goes in v10:
time: 204 us; the launch traced here: 202 us
  starting transfers between devices  99.7 us (49%)
  waiting for transfers between devices  43.4 us (21%)
  Pallas kernels  25.8 us (13%)
  blocking collectives  25.2 us (12%)
  local copies, waits for them, and re-layouts  7.17 us (4%)
    all_to_all x4, starting transfers between devices, exchange(): return lax.all_to_all(array, axis, 0, 0, tiled=True)  39.3 us
    ppermute x8, starting transfers between devices, swap(): return lax.ppermute(array, axis, [(0, 1), (1, 0)])  33.1 us
    ppermute x4, starting transfers between devices, across(): return lax.ppermute(array, axis, pairs)  27.3 us
    pallas_call x16, Pallas kernels, call(): pl.pallas_call(body, grid=(1,), out_shape=outs, in_specs=[pl.BlockSpec(me...  25.8 us
    all_to_all x2, blocking collectives, exchange(): return lax.all_to_all(array, axis, 0, 0, tiled=True)  25.2 us
    ppermute x4, waiting for transfers between devices, across(): return lax.ppermute(array, axis, pairs)  21.4 us
    ppermute x8, waiting for transfers between devices, swap(): return lax.ppermute(array, axis, [(0, 1), (1, 0)])  17.4 us
    unnamed x35, local copies, waits for them, and re-layouts  7.17 us
  transfers between devices with their start and end apart: 16, of which 9 were waited for; matrix products, arithmetic and copies ran while one was open for 0% of the time, Pallas kernels for 4%

profile of v10, /device:TPU:1, one launch (start us, length us, event | category | flops | bytes accessed | tf_op | source)
XLA Modules:
  0.0 202.2 jit_solution(2642727403169688691)
XLA Ops:
  0.7 3.6 %shard_map.131 = (bf16[1552,128]{1,0:T(8,128)(2,1)}, bf16[1552,128]{1,0:T(8,128)(2,1)}, bf16[8,512,128]{2,1,0:T(8,128)(2,1)}) custom-call(bf16[1,1024,128]{2,1,0:T(8,128)(2,1)} %ba.1, bf16[1,2,1024,128]{3,2,1,0:T(8,128)(2,1)} %bg.1, bf16[1,128]{1,0:T(2,128)(2,1)} %va.1, bf16[1,2,128]{2,1,0:T(2,128)(2,1)} %vg.1, bf16[512,128]{1,0:T(8,128)(2,1)} %act.5), custom_call_target="tpu_custom_call" | custom-call | bytes 2761472 | tf_op jit(solution)/shard_map/pallas_call | solution.py:45
  4.3 7.5 %all-to-all-start = ((bf16[8,512,128]{2,1,0:T(8,128)(2,1)}), bf16[8,512,128]{2,1,0:T(8,128)(2,1)S(1)}, u32[]{:S(2)}, u32[]{:S(2)}) async-start(bf16[8,512,128]{2,1,0:T(8,128)(2,1)} %get-tuple-element.41), calls=%async_computation | async-start | bytes 2097152 | tf_op jit(solution)/shard_map/all_to_all | solution.py:17
  11.8 5.0 %collective-permute-start.2 = (bf16[1552,128]{1,0:T(8,128)(2,1)}, bf16[1552,128]{1,0:T(8,128)(2,1)S(1)}, u32[]{:S(2)}, u32[]{:S(2)}) collective-permute-start(bf16[1552,128]{1,0:T(8,128)(2,1)} %get-tuple-element.38), channel_id=1, source_target_pairs={{0,8},{8,0},{1,9},{9,1},{2,10},{10,2},{3,11},{11,3},{4,12},{12,4},... | collective-permute-start | bytes 1191944 | tf_op jit(solution)/shard_map/ppermute | solution.py:21
  23.3 3.4 %collective-permute-start.1 = (bf16[512,128]{1,0:T(8,128)(2,1)S(1)}, bf16[512,128]{1,0:T(8,128)(2,1)S(1)}, u32[]{:S(2)}, u32[]{:S(2)}) collective-permute-start(bf16[512,128]{1,0:T(8,128)(2,1)S(1)} %get-tuple-element.36), channel_id=1, source_target_pairs={{0,16},{16,0},{1,17},{17,1},{2,18},{18,2},{3,19},{19,3},{4,20},{20... | collective-permute-start | bytes 393224 | tf_op jit(solution)/shard_map/ppermute | solution.py:21
  26.6 6.8 %collective-permute-done.1.got = bf16[512,128]{1,0:T(8,128)(2,1)S(1)} collective-permute-done((bf16[512,128]{1,0:T(8,128)(2,1)S(1)}, bf16[512,128]{1,0:T(8,128)(2,1)S(1)}, u32[]{:S(2)}, u32[]{:S(2)}) %collective-permute-start.1) | collective-permute-done | bytes 131104 | tf_op jit(solution)/shard_map/ppermute | solution.py:21
  35.8 13.9 %all-to-all-start.1 = ((bf16[16,112,128]{2,1,0:T(8,128)(2,1)}), bf16[16,112,128]{2,1,0:T(8,128)(2,1)}, u32[]{:S(2)}, u32[]{:S(2)}) async-start(bf16[16,112,128]{2,1,0:T(8,128)(2,1)} %shard_map.134), calls=%async_computation.1 | async-start | bytes 917504 | tf_op jit(solution)/shard_map/all_to_all | solution.py:17
  52.8 3.5 %collective-permute-start.4 = (bf16[16,2,48,128]{3,2,1,0:T(8,128)(2,1)S(1)}, bf16[16,2,48,128]{3,2,1,0:T(8,128)(2,1)S(1)}, u32[]{:S(2)}, u32[]{:S(2)}) collective-permute-start(bf16[16,2,48,128]{3,2,1,0:T(8,128)(2,1)S(1)} %get-tuple-element.43), channel_id=1, source_target_pairs={{0,8},{8,0},{1,9},{9,1},{2,10},{10,2},{3,11},{11,3},{4,12},{12,4},... | collective-permute-start | bytes 1179656 | tf_op jit(solution)/shard_map/ppermute | solution.py:21
  57.7 3.1 %collective-permute-start.5 = (bf16[16,48,128]{2,1,0:T(8,128)(2,1)S(1)}, bf16[16,48,128]{2,1,0:T(8,128)(2,1)S(1)}, u32[]{:S(2)}, u32[]{:S(2)}) collective-permute-start(bf16[16,48,128]{2,1,0:T(8,128)(2,1)S(1)} %get-tuple-element.45), channel_id=1, source_target_pairs={{0,16},{16,0},{1,17},{17,1},{2,18},{18,2},{3,19},{19,3},{4,20},{20... | collective-permute-start | bytes 589832 | tf_op jit(solution)/shard_map/ppermute | solution.py:21
  60.8 5.0 %collective-permute-done.5.f_got = bf16[16,48,128]{2,1,0:T(8,128)(2,1)S(1)} collective-permute-done((bf16[16,48,128]{2,1,0:T(8,128)(2,1)S(1)}, bf16[16,48,128]{2,1,0:T(8,128)(2,1)S(1)}, u32[]{:S(2)}, u32[]{:S(2)}) %collective-permute-start.5) | collective-permute-done | bytes 196640 | tf_op jit(solution)/shard_map/ppermute | solution.py:21
  65.9 4.6 %all-to-all-done.1.got = bf16[16,112,128]{2,1,0:T(8,128)(2,1)} async-done(((bf16[16,112,128]{2,1,0:T(8,128)(2,1)}), bf16[16,112,128]{2,1,0:T(8,128)(2,1)}, u32[]{:S(2)}, u32[]{:S(2)}) %all-to-all-start.1) | async-done | bytes 458784 | tf_op jit(solution)/shard_map/all_to_all | solution.py:17
  73.0 11.7 %all-to-all-start.2 = ((bf16[16,96,128]{2,1,0:T(8,128)(2,1)}), bf16[16,96,128]{2,1,0:T(8,128)(2,1)S(1)}, u32[]{:S(2)}, u32[]{:S(2)}) async-start(bf16[16,96,128]{2,1,0:T(8,128)(2,1)} %get-tuple-element.46), calls=%async_computation.2 | async-start | bytes 786432 | tf_op jit(solution)/shard_map/all_to_all | solution.py:17
  84.8 3.3 %collective-permute-start.6 = (bf16[8,48,128]{2,1,0:T(8,128)(2,1)S(1)}, bf16[8,48,128]{2,1,0:T(8,128)(2,1)S(1)}, u32[]{:S(2)}, u32[]{:S(2)}) collective-permute-start(bf16[8,48,128]{2,1,0:T(8,128)(2,1)S(1)} %get-tuple-element.49), channel_id=1, source_target_pairs={{0,32},{32,0},{64,96},{96,64},{128,160},{160,128},{192,224},{224,1... | collective-permute-start | bytes 294920 | tf_op jit(solution)/shard_map/ppermute | solution.py:26
  88.1 16.5 %collective-permute-done.6.f_got = bf16[8,48,128]{2,1,0:T(8,128)(2,1)S(1)} collective-permute-done((bf16[8,48,128]{2,1,0:T(8,128)(2,1)S(1)}, bf16[8,48,128]{2,1,0:T(8,128)(2,1)S(1)}, u32[]{:S(2)}, u32[]{:S(2)}) %collective-permute-start.6) | collective-permute-done | bytes 98336 | tf_op jit(solution)/shard_map/ppermute | solution.py:26
  108.2 6.2 %all-to-all-start.3 = ((bf16[8,1104,128]{2,1,0:T(8,128)(2,1)}), bf16[8,1104,128]{2,1,0:T(8,128)(2,1)}, u32[]{:S(2)}, u32[]{:S(2)}) async-start(bf16[8,1104,128]{2,1,0:T(8,128)(2,1)} %get-tuple-element.58), calls=%async_computation.3 | async-start | bytes 4521984 | tf_op jit(solution)/shard_map/all_to_all | solution.py:17
  114.3 3.2 %collective-permute-start.7 = (bf16[4,48,128]{2,1,0:T(8,128)(2,1)S(1)}, bf16[4,48,128]{2,1,0:T(8,128)(2,1)S(1)}, u32[]{:S(2)}, u32[]{:S(2)}) collective-permute-start(bf16[4,48,128]{2,1,0:T(8,128)(2,1)S(1)} %copy-done.16), channel_id=1, source_target_pairs={{0,64},{32,96},{64,0},{96,32},{128,192},{160,224},{192,128},{224,1... | collective-permute-start | bytes 147464 | tf_op jit(solution)/shard_map/ppermute | solution.py:26
  120.1 7.5 %collective-permute-start.8 = (bf16[2,48,128]{2,1,0:T(8,128)(2,1)S(1)}, bf16[2,48,128]{2,1,0:T(8,128)(2,1)S(1)}, u32[]{:S(2)}, u32[]{:S(2)}) collective-permute-start(bf16[2,48,128]{2,1,0:T(8,128)(2,1)S(1)} %get-tuple-element.53), channel_id=1, source_target_pairs={{0,128},{32,160},{64,192},{96,224},{128,0},{160,32},{192,64},{224,... | collective-permute-start | bytes 73736 | tf_op jit(solution)/shard_map/ppermute | solution.py:26
  128.9 13.3 %collective-permute-start.9 = (bf16[1,48,128]{2,1,0:T(8,128)(2,1)S(1)}, bf16[1,48,128]{2,1,0:T(8,128)(2,1)S(1)}, u32[]{:S(2)}, u32[]{:S(2)}) collective-permute-start(bf16[1,48,128]{2,1,0:T(8,128)(2,1)S(1)} %get-tuple-element.55), channel_id=1, source_target_pairs={{0,256},{32,288},{64,320},{96,352},{128,384},{160,416},{192,448},{... | collective-permute-start | bytes 36872 | tf_op jit(solution)/shard_map/ppermute | solution.py:26
  143.9 9.6 %collective-permute-start.10 = (bf16[8,1104,128]{2,1,0:T(8,128)(2,1)}, bf16[8,1104,128]{2,1,0:T(8,128)(2,1)S(1)}, u32[]{:S(2)}, u32[]{:S(2)}) collective-permute-start(bf16[8,1104,128]{2,1,0:T(8,128)(2,1)} %shard_map.142.own.own_grad.vals), channel_id=1, source_target_pairs={{0,8},{8,0},{1,9},{9,1},{2,10},{10,2},{3,11},{11,3},{4,12},{12,4},... | collective-permute-start | bytes 6782984 | tf_op jit(solution)/shard_map/ppermute | solution.py:21
  153.5 4.2 %collective-permute-done.10.other.other_grad = bf16[8,1104,128]{2,1,0:T(8,128)(2,1)S(1)} collective-permute-done((bf16[8,1104,128]{2,1,0:T(8,128)(2,1)}, bf16[8,1104,128]{2,1,0:T(8,128)(2,1)S(1)}, u32[]{:S(2)}, u32[]{:S(2)}) %collective-permute-start.10) | collective-permute-done | bytes 2261024 | tf_op jit(solution)/shard_map/ppermute | solution.py:21
  161.9 14.1 %all_to_all.30.rows = bf16[8,64,128]{2,1,0:T(8,128)(2,1)} all-to-all(bf16[8,64,128]{2,1,0:T(8,128)(2,1)} %shard_map.143), channel_id=1, replica_groups=mesh['z'=16,'xl'=2,'c'=2,'t'=8] {'t'}, dimensions={0} | all-to-all | bytes 262144 | tf_op jit(solution)/shard_map/all_to_all | solution.py:17
  176.0 3.5 %shard_map.144 = bf16[2,8,64,128]{3,2,1,0:T(8,128)(2,1)} custom-call(bf16[8,64,128]{2,1,0:T(8,128)(2,1)} %all_to_all.30.rows, bf16[8,1104,128]{2,1,0:T(8,128)(2,1)} %shard_map.142.own.own_grad.vals, bf16[8,1104,128]{2,1,0:T(8,128)(2,1)} %copy-done.11, bf16[8,1104,128]{2,1,0:T(8,128)(2,1)} %shard_map.142.own.own_grad.vals), custom_call_target="tpu_custom_call" | custom-call | flops 268435456 | bytes 7176192 | tf_op jit(solution)/shard_map/pallas_call | solution.py:45
  179.5 11.1 %all_to_all.31 = bf16[16,64,128]{2,1,0:T(8,128)(2,1)S(1)} all-to-all(bf16[16,64,128]{2,1,0:T(8,128)(2,1)} %bitcast.4), channel_id=1, replica_groups=mesh['z'=16,'xl'=2,'c'=2,'t'=8] {'xl','t'}, dimensions={0} | all-to-all | bytes 524288 | tf_op jit(solution)/shard_map/all_to_all | solution.py:17
  190.6 4.7 %collective-permute-start.11 = (bf16[2,8,64,128]{3,2,1,0:T(8,128)(2,1)S(1)}, bf16[2,8,64,128]{3,2,1,0:T(8,128)(2,1)S(1)}, u32[]{:S(2)}, u32[]{:S(2)}) collective-permute-start(bf16[2,8,64,128]{3,2,1,0:T(8,128)(2,1)S(1)} %bitcast.5), channel_id=1, source_target_pairs={{0,8},{8,0},{1,9},{9,1},{2,10},{10,2},{3,11},{11,3},{4,12},{12,4},... | collective-permute-start | bytes 786440 | tf_op jit(solution)/shard_map/ppermute | solution.py:21
  198.2 4.0 %shard_map.145 = (bf16[1024,2,128]{2,1,0:T(2,128)(2,1)}, bf16[1,1024,128]{2,1,0:T(8,128)(2,1)}) custom-call(s32[64]{0:T(128)} %groups.1, bf16[8,1104,128]{2,1,0:T(8,128)(2,1)} %shard_map.142.own.own_grad.vals, bf16[8,1104,128]{2,1,0:T(8,128)(2,1)} %copy-done.11, bf16[2,8,64,128]{3,2,1,0:T(8,128)(2,1)} %bitcast.6, bf16[2,8,64,128]{3,2,1,0:T(8,128)(2,1)} %copy-done.14), custom_call_target="tpu_custom_call" | custom-call | flops 536870912 | bytes 5832704 | tf_op jit(solution)/shard_map/pallas_call | solution.py:45
  (63 shorter events, 32.0 us)
Async XLA Ops:
  0.6 16.2 %copy-start.4 = (bf16[512,128]{1,0:T(8,128)(2,1)S(1)}, bf16[512,128]{1,0:T(8,128)(2,1)}, u32[]{:S(2)}) copy-start(bf16[512,128]{1,0:T(8,128)(2,1)} %act.5) | copy-start | bytes 393220
  0.6 16.2 %copy-start = (bf16[512,2,1024]{2,1,0:T(2,128)(2,1)S(1)}, bf16[512,2,1024]{2,1,0:T(2,128)(2,1)}, u32[]{:S(2)}) copy-start(bf16[512,2,1024]{2,1,0:T(2,128)(2,1)} %cot.5) | copy-start | bytes 6291460
  4.3 16.3 %copy-start.9 = (s32[3]{0:T(128)S(1)}, s32[3]{0:T(128)}, u32[]{:S(2)}) copy-start(s32[3]{0:T(128)} %owners.5) | copy-start | bytes 40
  4.3 30.5 %all-to-all-start = ((bf16[8,512,128]{2,1,0:T(8,128)(2,1)}), bf16[8,512,128]{2,1,0:T(8,128)(2,1)S(1)}, u32[]{:S(2)}, u32[]{:S(2)}) async-start(bf16[8,512,128]{2,1,0:T(8,128)(2,1)} %get-tuple-element.41), calls=%async_computation | async-start | bytes 2097152 | tf_op jit(solution)/shard_map/all_to_all | solution.py:17
  11.8 8.8 %copy-start.6 = (bf16[1552,128]{1,0:T(8,128)(2,1)S(1)}, bf16[1552,128]{1,0:T(8,128)(2,1)}, u32[]{:S(2)}) copy-start(bf16[1552,128]{1,0:T(8,128)(2,1)} %get-tuple-element.37.own) | copy-start | bytes 1191940
  11.8 8.8 %collective-permute-start.2 = (bf16[1552,128]{1,0:T(8,128)(2,1)}, bf16[1552,128]{1,0:T(8,128)(2,1)S(1)}, u32[]{:S(2)}, u32[]{:S(2)}) collective-permute-start(bf16[1552,128]{1,0:T(8,128)(2,1)} %get-tuple-element.38), channel_id=1, source_target_pairs={{0,8},{8,0},{1,9},{9,1},{2,10},{10,2},{3,11},{11,3},{4,12},{12,4},... | collective-permute-start | bytes 1191944 | tf_op jit(solution)/shard_map/ppermute | solution.py:21
  18.6 4.6 %collective-permute-start = (bf16[2,512,128]{2,1,0:T(8,128)(2,1)S(1)}, bf16[2,512,128]{2,1,0:T(8,128)(2,1)S(1)}, u32[]{:S(2)}, u32[]{:S(2)}) collective-permute-start(bf16[2,512,128]{2,1,0:T(8,128)(2,1)S(1)} %get-tuple-element.34), channel_id=1, source_target_pairs={{0,8},{8,0},{1,9},{9,1},{2,10},{10,2},{3,11},{11,3},{4,12},{12,4},... | collective-permute-start | bytes 786440 | tf_op jit(solution)/shard_map/ppermute | solution.py:21
  21.3 12.2 %collective-permute-start.3 = (bf16[1040,128]{1,0:T(8,128)(2,1)S(1)}, bf16[1040,128]{1,0:T(8,128)(2,1)S(1)}, u32[]{:S(2)}, u32[]{:S(2)}) collective-permute-start(bf16[1040,128]{1,0:T(8,128)(2,1)S(1)} %get-tuple-element.40), channel_id=1, source_target_pairs={{0,16},{16,0},{1,17},{17,1},{2,18},{18,2},{3,19},{19,3},{4,20},{20... | collective-permute-start | bytes 798728 | tf_op jit(solution)/shard_map/ppermute | solution.py:21
  23.3 10.2 %collective-permute-start.1 = (bf16[512,128]{1,0:T(8,128)(2,1)S(1)}, bf16[512,128]{1,0:T(8,128)(2,1)S(1)}, u32[]{:S(2)}, u32[]{:S(2)}) collective-permute-start(bf16[512,128]{1,0:T(8,128)(2,1)S(1)} %get-tuple-element.36), channel_id=1, source_target_pairs={{0,16},{16,0},{1,17},{17,1},{2,18},{18,2},{3,19},{19,3},{4,20},{20... | collective-permute-start | bytes 393224 | tf_op jit(solution)/shard_map/ppermute | solution.py:21
  35.8 34.6 %all-to-all-start.1 = ((bf16[16,112,128]{2,1,0:T(8,128)(2,1)}), bf16[16,112,128]{2,1,0:T(8,128)(2,1)}, u32[]{:S(2)}, u32[]{:S(2)}) async-start(bf16[16,112,128]{2,1,0:T(8,128)(2,1)} %shard_map.134), calls=%async_computation.1 | async-start | bytes 917504 | tf_op jit(solution)/shard_map/all_to_all | solution.py:17
  52.8 4.8 %collective-permute-start.4 = (bf16[16,2,48,128]{3,2,1,0:T(8,128)(2,1)S(1)}, bf16[16,2,48,128]{3,2,1,0:T(8,128)(2,1)S(1)}, u32[]{:S(2)}, u32[]{:S(2)}) collective-permute-start(bf16[16,2,48,128]{3,2,1,0:T(8,128)(2,1)S(1)} %get-tuple-element.43), channel_id=1, source_target_pairs={{0,8},{8,0},{1,9},{9,1},{2,10},{10,2},{3,11},{11,3},{4,12},{12,4},... | collective-permute-start | bytes 1179656 | tf_op jit(solution)/shard_map/ppermute | solution.py:21
  57.7 8.1 %collective-permute-start.5 = (bf16[16,48,128]{2,1,0:T(8,128)(2,1)S(1)}, bf16[16,48,128]{2,1,0:T(8,128)(2,1)S(1)}, u32[]{:S(2)}, u32[]{:S(2)}) collective-permute-start(bf16[16,48,128]{2,1,0:T(8,128)(2,1)S(1)} %get-tuple-element.45), channel_id=1, source_target_pairs={{0,16},{16,0},{1,17},{17,1},{2,18},{18,2},{3,19},{19,3},{4,20},{20... | collective-permute-start | bytes 589832 | tf_op jit(solution)/shard_map/ppermute | solution.py:21
  73.0 31.5 %copy-start.10 = (bf16[16,128]{1,0:T(8,128)(2,1)}, bf16[16,128]{1,0:T(8,128)(2,1)S(1)}, u32[]{:S(2)}) copy-start(bf16[16,128]{1,0:T(8,128)(2,1)S(1)} %get-tuple-element.47.vals) | copy-start | bytes 12292
  73.0 31.5 %all-to-all-start.2 = ((bf16[16,96,128]{2,1,0:T(8,128)(2,1)}), bf16[16,96,128]{2,1,0:T(8,128)(2,1)S(1)}, u32[]{:S(2)}, u32[]{:S(2)}) async-start(bf16[16,96,128]{2,1,0:T(8,128)(2,1)} %get-tuple-element.46), calls=%async_computation.2 | async-start | bytes 786432 | tf_op jit(solution)/shard_map/all_to_all | solution.py:17
  84.8 19.8 %collective-permute-start.6 = (bf16[8,48,128]{2,1,0:T(8,128)(2,1)S(1)}, bf16[8,48,128]{2,1,0:T(8,128)(2,1)S(1)}, u32[]{:S(2)}, u32[]{:S(2)}) collective-permute-start(bf16[8,48,128]{2,1,0:T(8,128)(2,1)S(1)} %get-tuple-element.49), channel_id=1, source_target_pairs={{0,32},{32,0},{64,96},{96,64},{128,160},{160,128},{192,224},{224,1... | collective-permute-start | bytes 294920 | tf_op jit(solution)/shard_map/ppermute | solution.py:26
  108.2 11.9 %copy-start.8 = (f32[4,48,128]{2,1,0:T(8,128)S(1)}, f32[4,48,128]{2,1,0:T(8,128)}, u32[]{:S(2)}) copy-start(f32[4,48,128]{2,1,0:T(8,128)} %get-tuple-element.50.keep) | copy-start | bytes 294916
  108.2 35.7 %all-to-all-start.3 = ((bf16[8,1104,128]{2,1,0:T(8,128)(2,1)}), bf16[8,1104,128]{2,1,0:T(8,128)(2,1)}, u32[]{:S(2)}, u32[]{:S(2)}) async-start(bf16[8,1104,128]{2,1,0:T(8,128)(2,1)} %get-tuple-element.58), calls=%async_computation.3 | async-start | bytes 4521984 | tf_op jit(solution)/shard_map/all_to_all | solution.py:17
  114.3 5.7 %collective-permute-start.7 = (bf16[4,48,128]{2,1,0:T(8,128)(2,1)S(1)}, bf16[4,48,128]{2,1,0:T(8,128)(2,1)S(1)}, u32[]{:S(2)}, u32[]{:S(2)}) collective-permute-start(bf16[4,48,128]{2,1,0:T(8,128)(2,1)S(1)} %copy-done.16), channel_id=1, source_target_pairs={{0,64},{32,96},{64,0},{96,32},{128,192},{160,224},{192,128},{224,1... | collective-permute-start | bytes 147464 | tf_op jit(solution)/shard_map/ppermute | solution.py:26
  120.1 8.8 %collective-permute-start.8 = (bf16[2,48,128]{2,1,0:T(8,128)(2,1)S(1)}, bf16[2,48,128]{2,1,0:T(8,128)(2,1)S(1)}, u32[]{:S(2)}, u32[]{:S(2)}) collective-permute-start(bf16[2,48,128]{2,1,0:T(8,128)(2,1)S(1)} %get-tuple-element.53), channel_id=1, source_target_pairs={{0,128},{32,160},{64,192},{96,224},{128,0},{160,32},{192,64},{224,... | collective-permute-start | bytes 73736 | tf_op jit(solution)/shard_map/ppermute | solution.py:26
  128.9 14.3 %collective-permute-start.9 = (bf16[1,48,128]{2,1,0:T(8,128)(2,1)S(1)}, bf16[1,48,128]{2,1,0:T(8,128)(2,1)S(1)}, u32[]{:S(2)}, u32[]{:S(2)}) collective-permute-start(bf16[1,48,128]{2,1,0:T(8,128)(2,1)S(1)} %get-tuple-element.55), channel_id=1, source_target_pairs={{0,256},{32,288},{64,320},{96,352},{128,384},{160,416},{192,448},{... | collective-permute-start | bytes 36872 | tf_op jit(solution)/shard_map/ppermute | solution.py:26
  143.9 13.8 %collective-permute-start.10 = (bf16[8,1104,128]{2,1,0:T(8,128)(2,1)}, bf16[8,1104,128]{2,1,0:T(8,128)(2,1)S(1)}, u32[]{:S(2)}, u32[]{:S(2)}) collective-permute-start(bf16[8,1104,128]{2,1,0:T(8,128)(2,1)} %shard_map.142.own.own_grad.vals), channel_id=1, source_target_pairs={{0,8},{8,0},{1,9},{9,1},{2,10},{10,2},{3,11},{11,3},{4,12},{12,4},... | collective-permute-start | bytes 6782984 | tf_op jit(solution)/shard_map/ppermute | solution.py:21
  176.0 19.3 %copy-start.5 = (bf16[128,2,1024]{2,1,0:T(2,128)(2,1)S(1)}, bf16[128,2,1024]{2,1,0:T(2,128)(2,1)}, u32[]{:S(2)}) copy-start(bf16[128,2,1024]{2,1,0:T(2,128)(2,1)} %weight.1) | copy-start | bytes 1572868
  190.6 6.9 %copy-start.13 = (bf16[16,64,128]{2,1,0:T(8,128)(2,1)}, bf16[16,64,128]{2,1,0:T(8,128)(2,1)S(1)}, u32[]{:S(2)}) copy-start(bf16[16,64,128]{2,1,0:T(8,128)(2,1)S(1)} %all_to_all.31) | copy-start | bytes 786436
  190.6 6.9 %collective-permute-start.11 = (bf16[2,8,64,128]{3,2,1,0:T(8,128)(2,1)S(1)}, bf16[2,8,64,128]{3,2,1,0:T(8,128)(2,1)S(1)}, u32[]{:S(2)}, u32[]{:S(2)}) collective-permute-start(bf16[2,8,64,128]{3,2,1,0:T(8,128)(2,1)S(1)} %bitcast.5), channel_id=1, source_target_pairs={{0,8},{8,0},{1,9},{9,1},{2,10},{10,2},{3,11},{11,3},{4,12},{12,4},... | collective-permute-start | bytes 786440 | tf_op jit(solution)/shard_map/ppermute | solution.py:21
  (9 other events, 13.4 us)

commit v11 on v10

--- a/solution.py
+++ b/solution.py
@@ -54,14 +54,14 @@
     )(*scalars, *arrays)
 
 
-def follow(array, after):
+def follow(array, after, limit):
     return pl.pallas_call(
         lambda *refs: None,
         out_shape=jax.ShapeDtypeStruct(array.shape, array.dtype),
         in_specs=[pl.BlockSpec(memory_space=pl.ANY)] * 2,
         out_specs=pl.BlockSpec(memory_space=pl.ANY),
         input_output_aliases={0: 0},
-        compiler_params=pltpu.CompilerParams(vmem_limit_bytes=56 * 1024 * 1024),
+        compiler_params=pltpu.CompilerParams(vmem_limit_bytes=limit * 1024 * 1024),
     )(array, after)
 
 
@@ -166,7 +166,7 @@
     rest[...] = keep[xl] + got[xl].astype(f32)
 
 
-def pack_z(owners, keep, got, own, other, sent):
+def pack_z(owners, keep, got, own, other, sent, vals):
     nz, _, slab = sent.shape
     half = (own.shape[0] - VALS) // 2
     per = half // nz
@@ -184,31 +184,52 @@
             lambda: own[rows].reshape(nz, per, slab),
             lambda: other[rows].reshape(nz, per, slab),
         )
-    vals = value_rows(here, own[2 * half :], other[2 * half :])
-    for k in range(nz):
-        sent[k, 3 * per :] = vals
-
-
-def reduce_z(owners, got, keep, f_got, sent, vals, f_sent, f_rest):
+    vals[...] = value_rows(here, own[2 * half :], other[2 * half :])
+
+
+def halve(bit, total, vals, sent, rest):
+    count, height, slab = total.shape
+    total = total.reshape(count // 2, 2, height, slab)
+    rows = count // 2 * height
+    mine = (lax.axis_index("z") // bit) % 2
+    for side in range(2):
+
+        @pl.when(mine == side)
+        def _():
+            rest[...] = total[:, side]
+            sent[0:rows] = total[:, 1 - side].astype(bf16).reshape(rows, slab)
+
+    sent[rows:] = vals
+
+
+def join(bit, owners, keep, got, vals):
+    count, height, slab = keep.shape
+    rows = count * height
+    z = lax.axis_index("z")
+    flags = [(owners[i] // 4 // bit) % 2 == (z // bit) % 2 for i in range(3)]
+    total = keep[...] + got[0:rows].astype(f32).reshape(count, height, slab)
+    return total, value_rows(flags, vals[...], got[rows:])
+
+
+def factor_z(bit, owners, keep, got, vals, sent, rest, chosen):
+    total, chosen[...] = join(bit // 2, owners, keep, got, vals)
+    halve(bit, total, chosen[...], sent, rest)
+
+
+def reduce_z(owners, got, keep, f_got, vals, sent, f_sent, f_rest):
     nz, height, _ = sent.shape
     per = height // 3
     xl = lax.axis_index("xl")
-    source = [owners[i] // 4 for i in range(3)]
     total = got[0, 0:per].astype(f32)
     for k in range(1, nz):
         total = total + got[k, 0:per].astype(f32)
     parts = [total.astype(bf16)]
-    for i, src in enumerate((source[0], owners[1 + xl] // 4)):
-        parts.append(got[src, (1 + i) * per : (2 + i) * per])
+    for i, owner in enumerate((owners[0], owners[1 + xl])):
+        parts.append(got[owner // 4, (1 + i) * per : (2 + i) * per])
     for i, part in enumerate(parts):
         for k in range(nz):
             sent[k, i * per : (i + 1) * per] = part
-    chosen = got[source[0], 3 * per :].astype(f32)
-    place = lax.broadcasted_iota(jnp.int32, chosen.shape, 0)
-    for i in (1, 2):
-        chosen = jnp.where(place == i, got[source[i], 3 * per :].astype(f32), chosen)
-    vals[...] = chosen.astype(bf16)
-    factor_z(1, keep, f_got, f_sent, f_rest)
+    halve(1, keep[...] + f_got[...].astype(f32), vals[...], f_sent, f_rest)
 
 
 def factor_terms(cot, act, whole, sent, keep, flat, both):
@@ -244,23 +265,7 @@
     rest[...] = keep[:, xl] + got[:, xl].astype(f32)
 
 
-def factor_z(bit, keep, got, sent, rest):
-    count, height, slab = keep.shape
-    total = keep[...] + got[...].astype(f32)
-    if count == 1:
-        rest[...] = total
-    else:
-        mine = (lax.axis_index("z") // bit) % 2
-        total = total.reshape(count // 2, 2, height, slab)
-        for side in range(2):
-
-            @pl.when(mine == side)
-            def _():
-                rest[...] = total[:, side]
-                sent[...] = total[:, 1 - side].astype(bf16)
-
-
-def pack_t(got, vals, keep, f_got, sent, f_sent, f_rest):
+def pack_t(owners, got, keep, f_got, vals, sent, f_sent, f_rest, chosen):
     nz, height, slab = got.shape
     nt = sent.shape[0]
     per = height // 3
@@ -270,20 +275,19 @@
         for i in range(2):
             rows = got[:, (1 + i) * per : (2 + i) * per].reshape(half, slab)
             sent[k, i * half : (i + 1) * half] = rows
-        sent[k, 2 * half + piece :] = vals[...]
-    sent[:, 2 * half : 2 * half + piece] = got[:, 0:per].reshape(nt, piece, slab)
-    factor_z(2, keep, f_got, f_sent, f_rest)
-
-
-def factor_out(keep, got, factor_a, factor_g):
+    sent[:, 2 * half :] = got[:, 0:per].reshape(nt, piece, slab)
+    factor_z(2, owners, keep, f_got, vals, f_sent, f_rest, chosen)
+
+
+def factor_out(bit, owners, keep, got, vals, factor_a, factor_g, chosen):
     group = factor_a.shape[0]
-    total = keep[0] + got[0].astype(f32)
+    total, chosen[...] = join(bit, owners, keep, got, vals)
     for j in range(2):
-        factor_g[j] = total[j * group : (j + 1) * group]
-    factor_a[...] = total[2 * group :]
-
-
-def rotate(own, other, own_grad, other_grad, sent, grad):
+        factor_g[j] = total[0, j * group : (j + 1) * group]
+    factor_a[...] = total[0, 2 * group :]
+
+
+def rotate(own, other, own_grad, other_grad, vals, sent, grad):
     nt, half, slab = own.shape
     piece = slab // 2
     core = lax.axis_index("c")
@@ -298,24 +302,27 @@
         k = core * (nt // 2) + i
         turned = dot(near, own[k]) + dot(far, other[k])
         turned = turned.T.astype(bf16)
-        sent[2 * i] = turned[0:piece]
-        sent[2 * i + 1] = turned[piece:]
-
-
-def scale_rows(rows, own, other, vals, sent, rot, scaled, column):
-    nt, piece, slab = rows.shape
+        sent[2 * i, 0:piece] = turned[0:piece]
+        sent[2 * i + 1, 0:piece] = turned[piece:]
+    for k in range(nt):
+        sent[k, piece:] = vals[...]
+
+
+def scale_rows(rows, own, other, sent, rot, scaled, column):
+    nt, height, slab = rows.shape
+    piece = height - VALS
     half = own.shape[1]
     core, xl, t = lax.axis_index("c"), lax.axis_index("xl"), lax.axis_index("t")
-    row = vals[core * (nt // 2) + t // 2].astype(f32)[0:1]
+    row = rows[core * (nt // 2) + t // 2, piece:].astype(f32)[0:1]
     column[...] = jnp.broadcast_to(row, (slab, slab)).T
     la = column[pl.ds(pl.multiple_of((t % 2) * piece, piece), piece)]
     for k in range(nt):
-        rot[:, k * slab : (k + 1) * slab] = rows[k]
+        rot[:, k * slab : (k + 1) * slab] = rows[k, 0:piece]
     near = rot[:, pl.ds(pl.multiple_of(core * half, half), half)]
     far = rot[:, pl.ds(pl.multiple_of((1 - core) * half, half), half)]
     for k in range(nt):
         spectral = dot(near, own[k]) + dot(far, other[k])
-        values = vals[k].astype(f32)
+        values = rows[k, piece:].astype(f32)
         lg = jnp.where(xl == 0, values[1:2], values[2:3])
         scaled[k] = (spectral / (la * lg + damping)).astype(bf16)
     for side, ref in ((core, own), (1 - core, other)):
@@ -401,13 +408,13 @@
     sent, keep = call(add_core, [out(shape[1:]), out(shape[1:], f32)], [], [keep, got])
     got = swap(sent, "xl")
 
-    (sent,) = call(
+    sent, vals = call(
         pack_z,
-        [out((nz, 3 * per + VALS, slab))],
+        [out((nz, 3 * per, slab)), out((VALS, slab))],
         [owners],
         [keep, got, base, base_got],
     )
-    got = exchange(follow(sent, whole_act), "z")
+    got = exchange(follow(sent, whole_act, 56), "z")
 
     height = (blocks + 1) * group
     shape = (nz, 2, height, slab)
@@ -424,67 +431,68 @@
     sent, f_keep = call(factor_core, [out(shape), out(shape, f32)], [], [f_keep, f_got])
     f_got = swap(sent, "xl")
 
-    shape = (nz // 2, height, slab)
-    sent, vals, f_sent, f_keep = call(
+    def step_outs(count):
+        return [out((count * height + VALS, slab)), out((count, height, slab), f32)]
+
+    sent, f_sent, f_keep = call(
         reduce_z,
-        [out((nz, 3 * per, slab)), out((VALS, slab)), out(shape), out(shape, f32)],
+        [out((nz, 3 * per, slab))] + step_outs(nz // 2),
         [owners],
-        [got, f_keep, f_got],
+        [got, f_keep, f_got, vals],
     )
     got = exchange(sent, "z")
     f_got = across(f_sent, "z", 1)
 
-    width = piece + 2 * half + VALS
-    shape = (nz // 4, height, slab)
-    sent, f_sent, f_keep = call(
+    chosen = out((VALS, slab))
+    sent, f_sent, f_keep, vals = call(
         pack_t,
-        [out((nt, width, slab)), out(shape), out(shape, f32)],
-        [],
-        [got, vals, f_keep, f_got],
-        limit=56,
+        [out((nt, 2 * half + piece, slab))] + step_outs(nz // 4) + [chosen],
+        [owners],
+        [got, f_keep, f_got, vals],
     )
     own = exchange(sent, "t")
     f_got = across(f_sent, "z", 2)
-    for bit in (4, 8):
-        shape = (nz // 2 // bit, height, slab)
-        f_sent, f_keep = call(
-            functools.partial(factor_z, bit), [out(shape), out(shape, f32)], [], [f_keep, f_got]
+    bit = 4
+    while bit < nz:
+        f_sent, f_keep, vals = call(
+            functools.partial(factor_z, bit),
+            step_outs(nz // 2 // bit) + [chosen],
+            [owners],
+            [f_keep, f_got, vals],
         )
         f_got = across(f_sent, "z", bit)
-    factor_a, factor_g = call(
-        factor_out,
-        [out((group, slab), f32), out((blocks, group, slab), f32)],
-        [],
-        [f_keep, f_got],
-    )
-    own = follow(own, factor_a)
+        bit *= 2
+    factor_a, factor_g, vals = call(
+        functools.partial(factor_out, nz // 2),
+        [out((group, slab), f32), out((blocks, group, slab), f32), chosen],
+        [owners],
+        [f_keep, f_got, vals],
+    )
+    own = follow(own, factor_a, 20)
     other = swap(own, "c")
     qa, qa_other = (own, half, 0), (other, half, 0)
     qg, qg_other = (own, half, 1), (other, half, 1)
     columns, columns_other = (own, piece, 2 * half // piece), (other, piece, 2 * half // piece)
-    vals = (own, VALS, (2 * half + piece) // VALS)
     (sent,) = call(
         rotate,
-        [out((nt, piece, slab))],
+        [out((nt, piece + VALS, slab))],
         [],
-        [qa, qa_other, columns, columns_other],
+        [qa, qa_other, columns, columns_other, vals],
         scratch=[pltpu.VMEM((slab, full), bf16)],
         flops=2 * slab * full * half,
-        limit=56,
     )
     rows = exchange(sent, "t")
     (sent,) = call(
         scale_rows,
         [out((blocks, nt, piece, slab))],
         [],
-        [rows, qg, qg_other, vals],
+        [rows, qg, qg_other],
         scratch=[
             pltpu.VMEM((piece, full), bf16),
             pltpu.VMEM((nt, piece, slab), bf16),
             pltpu.VMEM((slab, slab), f32),
         ],
         flops=4 * piece * full * full,
-        limit=56,
     )
     own_mixed = exchange(sent.reshape(blocks * nt, piece, slab), ("xl", "t"))
     own_mixed = own_mixed.reshape(blocks, nt, piece, slab)
@@ -495,7 +503,6 @@
         [worker_group],
         [qa, qa_other, own_mixed, other_mixed],
         flops=4 * full * full * slab,
-        limit=56,
     )
 
     (grad_input,) = call(

time: 204 us -> 192 us (0.941)
  Pallas kernels: 25.8 us -> 19.7 us
  waiting for transfers between devices: 43.4 us -> 39.5 us
    pallas_call x16, Pallas kernels: 25.8 us -> 19.7 us  [call(): pl.pallas_call(body, grid=(1,), out_shape=outs, in_specs=[pl.BlockSpec(me...]
    all_to_all x4, waiting for transfers between devices: 4.63 us -> 0.83 us  [exchange(): return lax.all_to_all(array, axis, 0, 0, tiled=True)]
    unnamed x35 -> x25, local copies, waits for them, and re-layouts: 7.17 us -> 5.66 us
  transfers between devices with their start and end apart: 16 -> 16, of which waited for: 9 -> 9; matrix products, arithmetic and copies ran while one was open for 0% -> 0% of each run, Pallas kernels for 4% -> 5%
where the time goes in v11:
time: 192 us; the launch traced here: 191 us
  starting transfers between devices  101 us (53%)
  waiting for transfers between devices  39.5 us (21%)
  blocking collectives  24.7 us (13%)
  Pallas kernels  19.7 us (10%)
  local copies, waits for them, and re-layouts  5.66 us (3%)
    all_to_all x4, starting transfers between devices, exchange(): return lax.all_to_all(array, axis, 0, 0, tiled=True)  40.6 us
    ppermute x8, starting transfers between devices, swap(): return lax.ppermute(array, axis, [(0, 1), (1, 0)])  33.2 us
    ppermute x4, starting transfers between devices, across(): return lax.ppermute(array, axis, pairs)  26.8 us
    all_to_all x2, blocking collectives, exchange(): return lax.all_to_all(array, axis, 0, 0, tiled=True)  24.7 us
    ppermute x4, waiting for transfers between devices, across(): return lax.ppermute(array, axis, pairs)  21.6 us
    pallas_call x16, Pallas kernels, call(): pl.pallas_call(body, grid=(1,), out_shape=outs, in_specs=[pl.BlockSpec(me...  19.7 us
    ppermute x8, waiting for transfers between devices, swap(): return lax.ppermute(array, axis, [(0, 1), (1, 0)])  17 us
    unnamed x25, local copies, waits for them, and re-layouts  5.66 us
  transfers between devices with their start and end apart: 16, of which 9 were waited for; matrix products, arithmetic and copies ran while one was open for 0% of the time, Pallas kernels for 5%

profile of v11, /device:TPU:1, one launch (start us, length us, event | category | flops | bytes accessed | tf_op | source)
XLA Modules:
  0.0 191.1 jit_solution(855324561997060208)
XLA Ops:
  0.7 3.6 %shard_map.131 = (bf16[1552,128]{1,0:T(8,128)(2,1)}, bf16[1552,128]{1,0:T(8,128)(2,1)}, bf16[8,512,128]{2,1,0:T(8,128)(2,1)}) custom-call(bf16[1,1024,128]{2,1,0:T(8,128)(2,1)} %ba.1, bf16[1,2,1024,128]{3,2,1,0:T(8,128)(2,1)} %bg.1, bf16[1,128]{1,0:T(2,128)(2,1)} %va.1, bf16[1,2,128]{2,1,0:T(2,128)(2,1)} %vg.1, bf16[512,128]{1,0:T(8,128)(2,1)} %act.5), custom_call_target="tpu_custom_call" | custom-call | bytes 2761472 | tf_op jit(solution)/shard_map/pallas_call | solution.py:45
  4.3 7.5 %all-to-all-start = ((bf16[8,512,128]{2,1,0:T(8,128)(2,1)}), bf16[8,512,128]{2,1,0:T(8,128)(2,1)S(1)}, u32[]{:S(2)}, u32[]{:S(2)}) async-start(bf16[8,512,128]{2,1,0:T(8,128)(2,1)} %get-tuple-element.47), calls=%async_computation | async-start | bytes 2097152 | tf_op jit(solution)/shard_map/all_to_all | solution.py:17
  11.8 5.0 %collective-permute-start.2 = (bf16[1552,128]{1,0:T(8,128)(2,1)}, bf16[1552,128]{1,0:T(8,128)(2,1)S(1)}, u32[]{:S(2)}, u32[]{:S(2)}) collective-permute-start(bf16[1552,128]{1,0:T(8,128)(2,1)} %get-tuple-element.43), channel_id=1, source_target_pairs={{0,8},{8,0},{1,9},{9,1},{2,10},{10,2},{3,11},{11,3},{4,12},{12,4},... | collective-permute-start | bytes 1191944 | tf_op jit(solution)/shard_map/ppermute | solution.py:21
  18.6 1.9 %collective-permute-start = (bf16[2,512,128]{2,1,0:T(8,128)(2,1)S(1)}, bf16[2,512,128]{2,1,0:T(8,128)(2,1)S(1)}, u32[]{:S(2)}, u32[]{:S(2)}) collective-permute-start(bf16[2,512,128]{2,1,0:T(8,128)(2,1)S(1)} %get-tuple-element.39), channel_id=1, source_target_pairs={{0,8},{8,0},{1,9},{9,1},{2,10},{10,2},{3,11},{11,3},{4,12},{12,4},... | collective-permute-start | bytes 786440 | tf_op jit(solution)/shard_map/ppermute | solution.py:21
  23.2 3.4 %collective-permute-start.1 = (bf16[512,128]{1,0:T(8,128)(2,1)S(1)}, bf16[512,128]{1,0:T(8,128)(2,1)S(1)}, u32[]{:S(2)}, u32[]{:S(2)}) collective-permute-start(bf16[512,128]{1,0:T(8,128)(2,1)S(1)} %get-tuple-element.41), channel_id=1, source_target_pairs={{0,16},{16,0},{1,17},{17,1},{2,18},{18,2},{3,19},{19,3},{4,20},{20... | collective-permute-start | bytes 393224 | tf_op jit(solution)/shard_map/ppermute | solution.py:21
  26.6 6.8 %collective-permute-done.1.got = bf16[512,128]{1,0:T(8,128)(2,1)S(1)} collective-permute-done((bf16[512,128]{1,0:T(8,128)(2,1)S(1)}, bf16[512,128]{1,0:T(8,128)(2,1)S(1)}, u32[]{:S(2)}, u32[]{:S(2)}) %collective-permute-start.1) | collective-permute-done | bytes 131104 | tf_op jit(solution)/shard_map/ppermute | solution.py:21
  35.8 13.9 %all-to-all-start.1 = ((bf16[16,96,128]{2,1,0:T(8,128)(2,1)}), bf16[16,96,128]{2,1,0:T(8,128)(2,1)S(1)}, u32[]{:S(2)}, u32[]{:S(2)}) async-start(bf16[16,96,128]{2,1,0:T(8,128)(2,1)} %shard_map.134), calls=%async_computation.1 | async-start | bytes 786432 | tf_op jit(solution)/shard_map/all_to_all | solution.py:17
  52.8 3.5 %collective-permute-start.4 = (bf16[16,2,48,128]{3,2,1,0:T(8,128)(2,1)S(1)}, bf16[16,2,48,128]{3,2,1,0:T(8,128)(2,1)S(1)}, u32[]{:S(2)}, u32[]{:S(2)}) collective-permute-start(bf16[16,2,48,128]{3,2,1,0:T(8,128)(2,1)S(1)} %get-tuple-element.49), channel_id=1, source_target_pairs={{0,8},{8,0},{1,9},{9,1},{2,10},{10,2},{3,11},{11,3},{4,12},{12,4},... | collective-permute-start | bytes 1179656 | tf_op jit(solution)/shard_map/ppermute | solution.py:21
  57.7 3.0 %collective-permute-start.5 = (bf16[16,48,128]{2,1,0:T(8,128)(2,1)S(1)}, bf16[16,48,128]{2,1,0:T(8,128)(2,1)S(1)}, u32[]{:S(2)}, u32[]{:S(2)}) collective-permute-start(bf16[16,48,128]{2,1,0:T(8,128)(2,1)S(1)} %get-tuple-element.51), channel_id=1, source_target_pairs={{0,16},{16,0},{1,17},{17,1},{2,18},{18,2},{3,19},{19,3},{4,20},{20... | collective-permute-start | bytes 589832 | tf_op jit(solution)/shard_map/ppermute | solution.py:21
  60.7 5.0 %collective-permute-done.5.f_got = bf16[16,48,128]{2,1,0:T(8,128)(2,1)S(1)} collective-permute-done((bf16[16,48,128]{2,1,0:T(8,128)(2,1)S(1)}, bf16[16,48,128]{2,1,0:T(8,128)(2,1)S(1)}, u32[]{:S(2)}, u32[]{:S(2)}) %collective-permute-start.5) | collective-permute-done | bytes 196640 | tf_op jit(solution)/shard_map/ppermute | solution.py:21
  67.9 12.8 %all-to-all-start.2 = ((bf16[16,96,128]{2,1,0:T(8,128)(2,1)}), bf16[16,96,128]{2,1,0:T(8,128)(2,1)S(1)}, u32[]{:S(2)}, u32[]{:S(2)}) async-start(bf16[16,96,128]{2,1,0:T(8,128)(2,1)} %get-tuple-element.53), calls=%async_computation.2 | async-start | bytes 786432 | tf_op jit(solution)/shard_map/all_to_all | solution.py:17
  80.7 3.3 %collective-permute-start.6 = (bf16[400,128]{1,0:T(8,128)(2,1)S(1)}, bf16[400,128]{1,0:T(8,128)(2,1)S(1)}, u32[]{:S(2)}, u32[]{:S(2)}) collective-permute-start(bf16[400,128]{1,0:T(8,128)(2,1)S(1)} %get-tuple-element.55), channel_id=1, source_target_pairs={{0,32},{32,0},{64,96},{96,64},{128,160},{160,128},{192,224},{224,1... | collective-permute-start | bytes 307208 | tf_op jit(solution)/shard_map/ppermute | solution.py:26
  83.9 16.6 %collective-permute-done.6.f_got = bf16[400,128]{1,0:T(8,128)(2,1)S(1)} collective-permute-done((bf16[400,128]{1,0:T(8,128)(2,1)S(1)}, bf16[400,128]{1,0:T(8,128)(2,1)S(1)}, u32[]{:S(2)}, u32[]{:S(2)}) %collective-permute-start.6) | collective-permute-done | bytes 102432 | tf_op jit(solution)/shard_map/ppermute | solution.py:26
  102.8 6.4 %all-to-all-start.3 = ((bf16[8,1088,128]{2,1,0:T(8,128)(2,1)}), bf16[8,1088,128]{2,1,0:T(8,128)(2,1)S(1)}, u32[]{:S(2)}, u32[]{:S(2)}) async-start(bf16[8,1088,128]{2,1,0:T(8,128)(2,1)} %copy-done.4), calls=%async_computation.3 | async-start | bytes 4456448 | tf_op jit(solution)/shard_map/all_to_all | solution.py:17
  109.2 3.2 %collective-permute-start.7 = (bf16[208,128]{1,0:T(8,128)(2,1)S(1)}, bf16[208,128]{1,0:T(8,128)(2,1)S(1)}, u32[]{:S(2)}, u32[]{:S(2)}) collective-permute-start(bf16[208,128]{1,0:T(8,128)(2,1)S(1)} %get-tuple-element.57), channel_id=1, source_target_pairs={{0,64},{32,96},{64,0},{96,32},{128,192},{160,224},{192,128},{224,1... | collective-permute-start | bytes 159752 | tf_op jit(solution)/shard_map/ppermute | solution.py:26
  112.4 2.6 %collective-permute-done.7.got = bf16[208,128]{1,0:T(8,128)(2,1)S(1)} collective-permute-done((bf16[208,128]{1,0:T(8,128)(2,1)S(1)}, bf16[208,128]{1,0:T(8,128)(2,1)S(1)}, u32[]{:S(2)}, u32[]{:S(2)}) %collective-permute-start.7) | collective-permute-done | bytes 53280 | tf_op jit(solution)/shard_map/ppermute | solution.py:26
  115.6 7.3 %collective-permute-start.8 = (bf16[112,128]{1,0:T(8,128)(2,1)S(1)}, bf16[112,128]{1,0:T(8,128)(2,1)S(1)}, u32[]{:S(2)}, u32[]{:S(2)}) collective-permute-start(bf16[112,128]{1,0:T(8,128)(2,1)S(1)} %get-tuple-element.60), channel_id=1, source_target_pairs={{0,128},{32,160},{64,192},{96,224},{128,0},{160,32},{192,64},{224,... | collective-permute-start | bytes 86024 | tf_op jit(solution)/shard_map/ppermute | solution.py:26
  124.7 13.1 %collective-permute-start.9 = (bf16[64,128]{1,0:T(8,128)(2,1)S(1)}, bf16[64,128]{1,0:T(8,128)(2,1)S(1)}, u32[]{:S(2)}, u32[]{:S(2)}) collective-permute-start(bf16[64,128]{1,0:T(8,128)(2,1)S(1)} %get-tuple-element.63), channel_id=1, source_target_pairs={{0,256},{32,288},{64,320},{96,352},{128,384},{160,416},{192,448},{... | collective-permute-start | bytes 49160 | tf_op jit(solution)/shard_map/ppermute | solution.py:26
  140.8 9.8 %collective-permute-start.10 = (bf16[8,1088,128]{2,1,0:T(8,128)(2,1)S(1)}, bf16[8,1088,128]{2,1,0:T(8,128)(2,1)S(1)}, u32[]{:S(2)}, u32[]{:S(2)}) collective-permute-start(bf16[8,1088,128]{2,1,0:T(8,128)(2,1)S(1)} %shard_map.142.own.own_grad), channel_id=1, source_target_pairs={{0,8},{8,0},{1,9},{9,1},{2,10},{10,2},{3,11},{11,3},{4,12},{12,4},... | collective-permute-start | bytes 6684680 | tf_op jit(solution)/shard_map/ppermute | solution.py:21
  150.6 4.0 %collective-permute-done.10.other.other_grad = bf16[8,1088,128]{2,1,0:T(8,128)(2,1)S(1)} collective-permute-done((bf16[8,1088,128]{2,1,0:T(8,128)(2,1)S(1)}, bf16[8,1088,128]{2,1,0:T(8,128)(2,1)S(1)}, u32[]{:S(2)}, u32[]{:S(2)}) %collective-permute-start.10) | collective-permute-done | bytes 2228256 | tf_op jit(solution)/shard_map/ppermute | solution.py:21
  155.3 13.9 %all_to_all.30.rows = bf16[8,80,128]{2,1,0:T(8,128)(2,1)S(1)} all-to-all(bf16[8,80,128]{2,1,0:T(8,128)(2,1)S(1)} %shard_map.143), channel_id=1, replica_groups=mesh['z'=16,'xl'=2,'c'=2,'t'=8] {'t'}, dimensions={0} | all-to-all | bytes 327680 | tf_op jit(solution)/shard_map/all_to_all | solution.py:17
  170.6 10.8 %all_to_all.31 = bf16[16,64,128]{2,1,0:T(8,128)(2,1)S(1)} all-to-all(bf16[16,64,128]{2,1,0:T(8,128)(2,1)S(1)} %bitcast.5), channel_id=1, replica_groups=mesh['z'=16,'xl'=2,'c'=2,'t'=8] {'xl','t'}, dimensions={0} | all-to-all | bytes 524288 | tf_op jit(solution)/shard_map/all_to_all | solution.py:17
  181.4 4.7 %collective-permute-start.11 = (bf16[2,8,64,128]{3,2,1,0:T(8,128)(2,1)S(1)}, bf16[2,8,64,128]{3,2,1,0:T(8,128)(2,1)S(1)}, u32[]{:S(2)}, u32[]{:S(2)}) collective-permute-start(bf16[2,8,64,128]{3,2,1,0:T(8,128)(2,1)S(1)} %bitcast.3), channel_id=1, source_target_pairs={{0,8},{8,0},{1,9},{9,1},{2,10},{10,2},{3,11},{11,3},{4,12},{12,4},... | collective-permute-start | bytes 786440 | tf_op jit(solution)/shard_map/ppermute | solution.py:21
  188.3 2.8 %shard_map.145 = (bf16[1024,2,128]{2,1,0:T(2,128)(2,1)}, bf16[1,1024,128]{2,1,0:T(8,128)(2,1)}) custom-call(s32[64]{0:T(128)S(1)} %copy-done.11, bf16[8,1088,128]{2,1,0:T(8,128)(2,1)S(1)} %shard_map.142.own.own_grad, bf16[8,1088,128]{2,1,0:T(8,128)(2,1)S(1)} %collective-permute-done.10.other.other_grad, bf16[2,8,64,128]{3,2,1,0:T(8,128)(2,1)S(1)} %bitcast.4, ...), custom_call_target="tpu_custom_call" | custom-call | flops 536870912 | bytes 5767168 | tf_op jit(solution)/shard_map/pallas_call | solution.py:45
  (53 shorter events, 25.4 us)
Async XLA Ops:
  0.6 16.2 %copy-start.6 = (bf16[512,128]{1,0:T(8,128)(2,1)S(1)}, bf16[512,128]{1,0:T(8,128)(2,1)}, u32[]{:S(2)}) copy-start(bf16[512,128]{1,0:T(8,128)(2,1)} %act.5) | copy-start | bytes 393220
  0.6 16.2 %copy-start = (bf16[512,2,1024]{2,1,0:T(2,128)(2,1)S(1)}, bf16[512,2,1024]{2,1,0:T(2,128)(2,1)}, u32[]{:S(2)}) copy-start(bf16[512,2,1024]{2,1,0:T(2,128)(2,1)} %cot.5) | copy-start | bytes 6291460
  4.3 16.3 %copy-start.9 = (s32[3]{0:T(128)S(1)}, s32[3]{0:T(128)}, u32[]{:S(2)}) copy-start(s32[3]{0:T(128)} %owners.13) | copy-start | bytes 40
  4.3 30.5 %all-to-all-start = ((bf16[8,512,128]{2,1,0:T(8,128)(2,1)}), bf16[8,512,128]{2,1,0:T(8,128)(2,1)S(1)}, u32[]{:S(2)}, u32[]{:S(2)}) async-start(bf16[8,512,128]{2,1,0:T(8,128)(2,1)} %get-tuple-element.47), calls=%async_computation | async-start | bytes 2097152 | tf_op jit(solution)/shard_map/all_to_all | solution.py:17
  11.8 8.8 %copy-start.8 = (bf16[1552,128]{1,0:T(8,128)(2,1)S(1)}, bf16[1552,128]{1,0:T(8,128)(2,1)}, u32[]{:S(2)}) copy-start(bf16[1552,128]{1,0:T(8,128)(2,1)} %get-tuple-element.42.own) | copy-start | bytes 1191940
  11.8 8.8 %collective-permute-start.2 = (bf16[1552,128]{1,0:T(8,128)(2,1)}, bf16[1552,128]{1,0:T(8,128)(2,1)S(1)}, u32[]{:S(2)}, u32[]{:S(2)}) collective-permute-start(bf16[1552,128]{1,0:T(8,128)(2,1)} %get-tuple-element.43), channel_id=1, source_target_pairs={{0,8},{8,0},{1,9},{9,1},{2,10},{10,2},{3,11},{11,3},{4,12},{12,4},... | collective-permute-start | bytes 1191944 | tf_op jit(solution)/shard_map/ppermute | solution.py:21
  18.6 4.5 %collective-permute-start = (bf16[2,512,128]{2,1,0:T(8,128)(2,1)S(1)}, bf16[2,512,128]{2,1,0:T(8,128)(2,1)S(1)}, u32[]{:S(2)}, u32[]{:S(2)}) collective-permute-start(bf16[2,512,128]{2,1,0:T(8,128)(2,1)S(1)} %get-tuple-element.39), channel_id=1, source_target_pairs={{0,8},{8,0},{1,9},{9,1},{2,10},{10,2},{3,11},{11,3},{4,12},{12,4},... | collective-permute-start | bytes 786440 | tf_op jit(solution)/shard_map/ppermute | solution.py:21
  21.2 12.2 %collective-permute-start.3 = (bf16[1040,128]{1,0:T(8,128)(2,1)S(1)}, bf16[1040,128]{1,0:T(8,128)(2,1)S(1)}, u32[]{:S(2)}, u32[]{:S(2)}) collective-permute-start(bf16[1040,128]{1,0:T(8,128)(2,1)S(1)} %get-tuple-element.45), channel_id=1, source_target_pairs={{0,16},{16,0},{1,17},{17,1},{2,18},{18,2},{3,19},{19,3},{4,20},{20... | collective-permute-start | bytes 798728 | tf_op jit(solution)/shard_map/ppermute | solution.py:21
  23.2 10.2 %collective-permute-start.1 = (bf16[512,128]{1,0:T(8,128)(2,1)S(1)}, bf16[512,128]{1,0:T(8,128)(2,1)S(1)}, u32[]{:S(2)}, u32[]{:S(2)}) collective-permute-start(bf16[512,128]{1,0:T(8,128)(2,1)S(1)} %get-tuple-element.41), channel_id=1, source_target_pairs={{0,16},{16,0},{1,17},{17,1},{2,18},{18,2},{3,19},{19,3},{4,20},{20... | collective-permute-start | bytes 393224 | tf_op jit(solution)/shard_map/ppermute | solution.py:21
  35.8 30.7 %all-to-all-start.1 = ((bf16[16,96,128]{2,1,0:T(8,128)(2,1)}), bf16[16,96,128]{2,1,0:T(8,128)(2,1)S(1)}, u32[]{:S(2)}, u32[]{:S(2)}) async-start(bf16[16,96,128]{2,1,0:T(8,128)(2,1)} %shard_map.134), calls=%async_computation.1 | async-start | bytes 786432 | tf_op jit(solution)/shard_map/all_to_all | solution.py:17
  52.8 4.8 %collective-permute-start.4 = (bf16[16,2,48,128]{3,2,1,0:T(8,128)(2,1)S(1)}, bf16[16,2,48,128]{3,2,1,0:T(8,128)(2,1)S(1)}, u32[]{:S(2)}, u32[]{:S(2)}) collective-permute-start(bf16[16,2,48,128]{3,2,1,0:T(8,128)(2,1)S(1)} %get-tuple-element.49), channel_id=1, source_target_pairs={{0,8},{8,0},{1,9},{9,1},{2,10},{10,2},{3,11},{11,3},{4,12},{12,4},... | collective-permute-start | bytes 1179656 | tf_op jit(solution)/shard_map/ppermute | solution.py:21
  57.7 8.0 %collective-permute-start.5 = (bf16[16,48,128]{2,1,0:T(8,128)(2,1)S(1)}, bf16[16,48,128]{2,1,0:T(8,128)(2,1)S(1)}, u32[]{:S(2)}, u32[]{:S(2)}) collective-permute-start(bf16[16,48,128]{2,1,0:T(8,128)(2,1)S(1)} %get-tuple-element.51), channel_id=1, source_target_pairs={{0,16},{16,0},{1,17},{17,1},{2,18},{18,2},{3,19},{19,3},{4,20},{20... | collective-permute-start | bytes 589832 | tf_op jit(solution)/shard_map/ppermute | solution.py:21
  67.9 32.7 %all-to-all-start.2 = ((bf16[16,96,128]{2,1,0:T(8,128)(2,1)}), bf16[16,96,128]{2,1,0:T(8,128)(2,1)S(1)}, u32[]{:S(2)}, u32[]{:S(2)}) async-start(bf16[16,96,128]{2,1,0:T(8,128)(2,1)} %get-tuple-element.53), calls=%async_computation.2 | async-start | bytes 786432 | tf_op jit(solution)/shard_map/all_to_all | solution.py:17
  80.7 19.9 %collective-permute-start.6 = (bf16[400,128]{1,0:T(8,128)(2,1)S(1)}, bf16[400,128]{1,0:T(8,128)(2,1)S(1)}, u32[]{:S(2)}, u32[]{:S(2)}) collective-permute-start(bf16[400,128]{1,0:T(8,128)(2,1)S(1)} %get-tuple-element.55), channel_id=1, source_target_pairs={{0,32},{32,0},{64,96},{96,64},{128,160},{160,128},{192,224},{224,1... | collective-permute-start | bytes 307208 | tf_op jit(solution)/shard_map/ppermute | solution.py:26
  101.4 1.4 copy-start.4
  102.8 37.3 %all-to-all-start.3 = ((bf16[8,1088,128]{2,1,0:T(8,128)(2,1)}), bf16[8,1088,128]{2,1,0:T(8,128)(2,1)S(1)}, u32[]{:S(2)}, u32[]{:S(2)}) async-start(bf16[8,1088,128]{2,1,0:T(8,128)(2,1)} %copy-done.4), calls=%async_computation.3 | async-start | bytes 4456448 | tf_op jit(solution)/shard_map/all_to_all | solution.py:17
  109.2 5.8 %collective-permute-start.7 = (bf16[208,128]{1,0:T(8,128)(2,1)S(1)}, bf16[208,128]{1,0:T(8,128)(2,1)S(1)}, u32[]{:S(2)}, u32[]{:S(2)}) collective-permute-start(bf16[208,128]{1,0:T(8,128)(2,1)S(1)} %get-tuple-element.57), channel_id=1, source_target_pairs={{0,64},{32,96},{64,0},{96,32},{128,192},{160,224},{192,128},{224,1... | collective-permute-start | bytes 159752 | tf_op jit(solution)/shard_map/ppermute | solution.py:26
  115.6 8.6 %collective-permute-start.8 = (bf16[112,128]{1,0:T(8,128)(2,1)S(1)}, bf16[112,128]{1,0:T(8,128)(2,1)S(1)}, u32[]{:S(2)}, u32[]{:S(2)}) collective-permute-start(bf16[112,128]{1,0:T(8,128)(2,1)S(1)} %get-tuple-element.60), channel_id=1, source_target_pairs={{0,128},{32,160},{64,192},{96,224},{128,0},{160,32},{192,64},{224,... | collective-permute-start | bytes 86024 | tf_op jit(solution)/shard_map/ppermute | solution.py:26
  124.7 14.2 %collective-permute-start.9 = (bf16[64,128]{1,0:T(8,128)(2,1)S(1)}, bf16[64,128]{1,0:T(8,128)(2,1)S(1)}, u32[]{:S(2)}, u32[]{:S(2)}) collective-permute-start(bf16[64,128]{1,0:T(8,128)(2,1)S(1)} %get-tuple-element.63), channel_id=1, source_target_pairs={{0,256},{32,288},{64,320},{96,352},{128,384},{160,416},{192,448},{... | collective-permute-start | bytes 49160 | tf_op jit(solution)/shard_map/ppermute | solution.py:26
  140.8 13.8 %collective-permute-start.10 = (bf16[8,1088,128]{2,1,0:T(8,128)(2,1)S(1)}, bf16[8,1088,128]{2,1,0:T(8,128)(2,1)S(1)}, u32[]{:S(2)}, u32[]{:S(2)}) collective-permute-start(bf16[8,1088,128]{2,1,0:T(8,128)(2,1)S(1)} %shard_map.142.own.own_grad), channel_id=1, source_target_pairs={{0,8},{8,0},{1,9},{9,1},{2,10},{10,2},{3,11},{11,3},{4,12},{12,4},... | collective-permute-start | bytes 6684680 | tf_op jit(solution)/shard_map/ppermute | solution.py:21
  169.2 16.8 %copy-start.1 = (bf16[512,2,1024]{2,1,0:T(2,128)(2,1)S(1)}, bf16[512,2,1024]{2,1,0:T(2,128)(2,1)}, u32[]{:S(2)}) copy-start(bf16[512,2,1024]{2,1,0:T(2,128)(2,1)} %cot.5) | copy-start | bytes 6291460
  169.2 16.9 %copy-start.7 = (bf16[128,2,1024]{2,1,0:T(2,128)(2,1)S(1)}, bf16[128,2,1024]{2,1,0:T(2,128)(2,1)}, u32[]{:S(2)}) copy-start(bf16[128,2,1024]{2,1,0:T(2,128)(2,1)} %weight.1) | copy-start | bytes 1572868
  170.6 17.7 %copy-start.11 = (s32[64]{0:T(128)S(1)}, s32[64]{0:T(128)}, u32[]{:S(2)}) copy-start(s32[64]{0:T(128)} %groups.1) | copy-start | bytes 772
  181.4 6.9 %collective-permute-start.11 = (bf16[2,8,64,128]{3,2,1,0:T(8,128)(2,1)S(1)}, bf16[2,8,64,128]{3,2,1,0:T(8,128)(2,1)S(1)}, u32[]{:S(2)}, u32[]{:S(2)}) collective-permute-start(bf16[2,8,64,128]{3,2,1,0:T(8,128)(2,1)S(1)} %bitcast.3), channel_id=1, source_target_pairs={{0,8},{8,0},{1,9},{9,1},{2,10},{10,2},{3,11},{11,3},{4,12},{12,4},... | collective-permute-start | bytes 786440 | tf_op jit(solution)/shard_map/ppermute | solution.py:21
  (4 other events, 3.7 us)

commit v12 on v11

--- a/solution.py
+++ b/solution.py
@@ -91,7 +91,7 @@
         ref[place] = other()
 
 
-def pack_bases(ba, bg, va, vg, act, sent, keep, every, sem):
+def pack_bases(ba, bg, va, vg, sent, keep, sem):
     half = ba.shape[1] // 2
     core = lax.axis_index("c")
     place = lax.broadcasted_iota(jnp.int32, (VALS, ba.shape[2]), 0)
@@ -110,8 +110,6 @@
             copies[-1].start()
     sent[3 * half :] = vals.astype(bf16)
     keep[3 * half :] = vals.astype(bf16)
-    for k in range(every.shape[0]):
-        every[k] = act[...]
     for copy in copies:
         copy.wait()
 
@@ -216,7 +214,7 @@
     halve(bit, total, chosen[...], sent, rest)
 
 
-def reduce_z(owners, got, keep, f_got, vals, sent, f_sent, f_rest):
+def reduce_z(owners, got, after, sent):
     nz, height, _ = sent.shape
     per = height // 3
     xl = lax.axis_index("xl")
@@ -229,10 +227,15 @@
     for i, part in enumerate(parts):
         for k in range(nz):
             sent[k, i * per : (i + 1) * per] = part
-    halve(1, keep[...] + f_got[...].astype(f32), vals[...], f_sent, f_rest)
-
-
-def factor_terms(cot, act, whole, sent, keep, flat, both):
+
+
+def factor_first(keep, got, vals, sent, rest):
+    halve(1, keep[...] + got[...].astype(f32), vals[...], sent, rest)
+
+
+def factor_terms(cot, *refs):
+    pieces, (sent, keep, flat, both) = refs[:-4], refs[-4:]
+    act = pieces[0]
     nz, _, height, slab = keep.shape
     group = height // 3
     tok, blocks, full = cot.shape
@@ -243,8 +246,9 @@
     for j in range(blocks):
         own = flat[:, pl.ds(pl.multiple_of(j * full + t * slab, slab), slab)]
         both[j] = dot(flat[:, j * full : (j + 1) * full], own, ((0,), (0,))) * scale
-    for k in range(nt):
-        both[blocks, k * slab : (k + 1) * slab] = dot(whole[k], act[...], ((0,), (0,))) * scale
+    for k, piece in enumerate(pieces):
+        rows = pl.ds(pl.multiple_of((t ^ k) * slab, slab), slab)
+        both[blocks, rows] = dot(piece[...], act[...], ((0,), (0,))) * scale
     for i in range(blocks + 1):
         term = both[i].reshape(nz, 2, 2, group, slab)
         rows = slice(i * group, (i + 1) * group)
@@ -379,17 +383,16 @@
     per = half // nz
 
     shape = (3 * half + VALS, slab)
-    sent, keep, every = call(
+    sent, keep = call(
         pack_bases,
-        [out(shape), out(shape), out((nt, tok, slab))],
+        [out(shape), out(shape)],
         [],
-        [basis_a, basis_g, values_a, values_g, act],
-        [pl.ANY, pl.ANY, None, None, None],
+        [basis_a, basis_g, values_a, values_g],
+        [pl.ANY, pl.ANY, None, None],
         scratch=[pltpu.SemaphoreType.DMA((2, 3))],
         limit=56,
     )
     got = swap(sent, "c")
-    whole_act = exchange(every, "t")
     shape = (2 * half + VALS, slab)
     sent, base = call(select_core, [out(shape), out(shape)], [owners], [keep, got])
     base_got = swap(sent, "xl")
@@ -414,33 +417,36 @@
         [owners],
         [keep, got, base, base_got],
     )
-    got = exchange(follow(sent, whole_act, 56), "z")
+    got = exchange(sent, "z")
 
     height = (blocks + 1) * group
     shape = (nz, 2, height, slab)
-    sent, f_keep = call(
+    pieces = [act] + [across(act, "t", k) for k in range(1, nt)]
+    sent_f, f_keep = call(
         factor_terms,
         [out(shape), out(shape, f32)],
         [],
-        [cot, act, whole_act],
+        [cot] + pieces,
         scratch=[flat, pltpu.VMEM((blocks + 1, full, slab), f32)],
         flops=6 * tok * full * slab,
     )
-    f_got = swap(sent, "c")
-    shape = (nz, height, slab)
-    sent, f_keep = call(factor_core, [out(shape), out(shape, f32)], [], [f_keep, f_got])
-    f_got = swap(sent, "xl")
 
     def step_outs(count):
         return [out((count * height + VALS, slab)), out((count, height, slab), f32)]
 
-    sent, f_sent, f_keep = call(
+    (sent,) = call(
         reduce_z,
-        [out((nz, 3 * per, slab))] + step_outs(nz // 2),
+        [out((nz, 3 * per, slab))],
         [owners],
-        [got, f_keep, f_got, vals],
+        [got, sent_f],
+        [None, pl.ANY],
     )
     got = exchange(sent, "z")
+    f_got = swap(sent_f, "c")
+    shape = (nz, height, slab)
+    f_sent, f_keep = call(factor_core, [out(shape), out(shape, f32)], [], [f_keep, f_got])
+    f_got = swap(f_sent, "xl")
+    f_sent, f_keep = call(factor_first, step_outs(nz // 2), [], [f_keep, f_got, vals])
     f_got = across(f_sent, "z", 1)
 
     chosen = out((VALS, slab))

time: 192 us -> 200 us (1.042)
  starting transfers between devices: 101 us -> 114 us
  waiting for transfers between devices: 39.5 us -> 31 us
  local copies, waits for them, and re-layouts: 5.66 us -> 7.92 us
    ppermute x4 -> x11, starting transfers between devices: 26.8 us -> 52.5 us  [across(): return lax.ppermute(array, axis, pairs)]
    all_to_all x4 -> x3, starting transfers between devices: 40.6 us -> 24.9 us  [exchange(): return lax.all_to_all(array, axis, 0, 0, tiled=True)]
    ppermute x4 -> x11, waiting for transfers between devices: 21.6 us -> 14 us  [across(): return lax.ppermute(array, axis, pairs)]
    ppermute x8, starting transfers between devices: 33.2 us -> 37 us  [swap(): return lax.ppermute(array, axis, [(0, 1), (1, 0)])]
    unnamed x25 -> x27, local copies, waits for them, and re-layouts: 5.66 us -> 7.92 us
    pallas_call x16 -> x17, Pallas kernels: 19.7 us -> 19.6 us  [call(): pl.pallas_call(body, grid=(1,), out_shape=outs, in_specs=[pl.BlockSpec(me...]
  transfers between devices with their start and end apart: 16 -> 22, of which waited for: 9 -> 10; matrix products, arithmetic and copies ran while one was open for 0% -> 0% of each run, Pallas kernels for 5% -> 4%
where the time goes in v12:
time: 200 us; the launch traced here: 199 us
  starting transfers between devices  114 us (57%)
  waiting for transfers between devices  31 us (16%)
  blocking collectives  24.8 us (12%)
  Pallas kernels  19.6 us (10%)
  local copies, waits for them, and re-layouts  7.92 us (4%)
    ppermute x11, starting transfers between devices, across(): return lax.ppermute(array, axis, pairs)  52.5 us
    ppermute x8, starting transfers between devices, swap(): return lax.ppermute(array, axis, [(0, 1), (1, 0)])  37 us
    all_to_all x3, starting transfers between devices, exchange(): return lax.all_to_all(array, axis, 0, 0, tiled=True)  24.9 us
    all_to_all x2, blocking collectives, exchange(): return lax.all_to_all(array, axis, 0, 0, tiled=True)  24.8 us
    pallas_call x17, Pallas kernels, call(): pl.pallas_call(body, grid=(1,), out_shape=outs, in_specs=[pl.BlockSpec(me...  19.6 us
    ppermute x8, waiting for transfers between devices, swap(): return lax.ppermute(array, axis, [(0, 1), (1, 0)])  17 us
    ppermute x11, waiting for transfers between devices, across(): return lax.ppermute(array, axis, pairs)  14 us
    unnamed x27, local copies, waits for them, and re-layouts  7.92 us
  transfers between devices with their start and end apart: 22, of which 10 were waited for; matrix products, arithmetic and copies ran while one was open for 0% of the time, Pallas kernels for 4%

profile of v12, /device:TPU:1, one launch (start us, length us, event | category | flops | bytes accessed | tf_op | source)
XLA Modules:
  0.0 198.6 jit_solution(5768295949245993199)
XLA Ops:
  0.6 2.8 %shard_map.131 = (bf16[1552,128]{1,0:T(8,128)(2,1)}, bf16[1552,128]{1,0:T(8,128)(2,1)}) custom-call(bf16[1,1024,128]{2,1,0:T(8,128)(2,1)} %ba.1, bf16[1,2,1024,128]{3,2,1,0:T(8,128)(2,1)} %bg.1, bf16[1,128]{1,0:T(2,128)(2,1)} %va.1, bf16[1,2,128]{2,1,0:T(2,128)(2,1)} %vg.1), custom_call_target="tpu_custom_call" | custom-call | bytes 1581824 | tf_op jit(solution)/shard_map/pallas_call | solution.py:45
  3.5 8.8 %collective-permute-start.2 = (bf16[1552,128]{1,0:T(8,128)(2,1)}, bf16[1552,128]{1,0:T(8,128)(2,1)S(1)}, u32[]{:S(2)}, u32[]{:S(2)}) collective-permute-start(bf16[1552,128]{1,0:T(8,128)(2,1)} %get-tuple-element.41), channel_id=1, source_target_pairs={{0,8},{8,0},{1,9},{9,1},{2,10},{10,2},{3,11},{11,3},{4,12},{12,4},... | collective-permute-start | bytes 1191944 | tf_op jit(solution)/shard_map/ppermute | solution.py:21
  22.1 3.4 %collective-permute-start.1 = (bf16[512,128]{1,0:T(8,128)(2,1)S(1)}, bf16[512,128]{1,0:T(8,128)(2,1)S(1)}, u32[]{:S(2)}, u32[]{:S(2)}) collective-permute-start(bf16[512,128]{1,0:T(8,128)(2,1)S(1)} %get-tuple-element.39), channel_id=1, source_target_pairs={{0,16},{16,0},{1,17},{17,1},{2,18},{18,2},{3,19},{19,3},{4,20},{20... | collective-permute-start | bytes 393224 | tf_op jit(solution)/shard_map/ppermute | solution.py:21
  25.5 6.8 %collective-permute-done.1.got = bf16[512,128]{1,0:T(8,128)(2,1)S(1)} collective-permute-done((bf16[512,128]{1,0:T(8,128)(2,1)S(1)}, bf16[512,128]{1,0:T(8,128)(2,1)S(1)}, u32[]{:S(2)}, u32[]{:S(2)}) %collective-permute-start.1) | collective-permute-done | bytes 131104 | tf_op jit(solution)/shard_map/ppermute | solution.py:21
  33.7 9.5 %all-to-all-start = ((bf16[16,96,128]{2,1,0:T(8,128)(2,1)}), bf16[16,96,128]{2,1,0:T(8,128)(2,1)S(1)}, u32[]{:S(2)}, u32[]{:S(2)}) async-start(bf16[16,96,128]{2,1,0:T(8,128)(2,1)} %get-tuple-element.44), calls=%async_computation | async-start | bytes 786432 | tf_op jit(solution)/shard_map/all_to_all | solution.py:17
  43.2 7.1 %collective-permute-start.10 = (bf16[512,128]{1,0:T(8,128)(2,1)S(1)}, bf16[512,128]{1,0:T(8,128)(2,1)S(1)}, u32[]{:S(2)}, u32[]{:S(2)}) collective-permute-start(bf16[512,128]{1,0:T(8,128)(2,1)S(1)} %copy-done.5), channel_id=1, source_target_pairs={{0,7},{1,6},{2,5},{3,4},{4,3},{5,2},{6,1},{7,0},{8,15},{9,14},{10,... | collective-permute-start | bytes 393224 | tf_op jit(solution)/shard_map/ppermute | solution.py:26
  54.4 5.8 %collective-permute-start.6 = (bf16[512,128]{1,0:T(8,128)(2,1)S(1)}, bf16[512,128]{1,0:T(8,128)(2,1)S(1)}, u32[]{:S(2)}, u32[]{:S(2)}) collective-permute-start(bf16[512,128]{1,0:T(8,128)(2,1)S(1)} %copy-done.5), channel_id=1, source_target_pairs={{0,3},{1,2},{2,1},{3,0},{4,7},{5,6},{6,5},{7,4},{8,11},{9,10},{10,... | collective-permute-start | bytes 393224 | tf_op jit(solution)/shard_map/ppermute | solution.py:26
  62.5 4.5 %collective-permute-start.8 = (bf16[512,128]{1,0:T(8,128)(2,1)S(1)}, bf16[512,128]{1,0:T(8,128)(2,1)S(1)}, u32[]{:S(2)}, u32[]{:S(2)}) collective-permute-start(bf16[512,128]{1,0:T(8,128)(2,1)S(1)} %copy-done.5), channel_id=1, source_target_pairs={{0,5},{1,4},{2,7},{3,6},{4,1},{5,0},{6,3},{7,2},{8,13},{9,12},{10,... | collective-permute-start | bytes 393224 | tf_op jit(solution)/shard_map/ppermute | solution.py:26
  69.0 3.1 %collective-permute-done.8.refs_5_ = bf16[512,128]{1,0:T(8,128)(2,1)S(1)} collective-permute-done((bf16[512,128]{1,0:T(8,128)(2,1)S(1)}, bf16[512,128]{1,0:T(8,128)(2,1)S(1)}, u32[]{:S(2)}, u32[]{:S(2)}) %collective-permute-start.8) | collective-permute-done | bytes 131104 | tf_op jit(solution)/shard_map/ppermute | solution.py:26
  79.1 11.2 %all-to-all-start.1 = ((bf16[16,96,128]{2,1,0:T(8,128)(2,1)}), bf16[16,96,128]{2,1,0:T(8,128)(2,1)S(1)}, u32[]{:S(2)}, u32[]{:S(2)}) async-start(bf16[16,96,128]{2,1,0:T(8,128)(2,1)} %shard_map.135), calls=%async_computation.1 | async-start | bytes 786432 | tf_op jit(solution)/shard_map/all_to_all | solution.py:17
  90.3 6.9 %collective-permute-start.11 = (bf16[16,2,48,128]{3,2,1,0:T(8,128)(2,1)S(1)}, bf16[16,2,48,128]{3,2,1,0:T(8,128)(2,1)S(1)}, u32[]{:S(2)}, u32[]{:S(2)}) collective-permute-start(bf16[16,2,48,128]{3,2,1,0:T(8,128)(2,1)S(1)} %copy-done.9), channel_id=1, source_target_pairs={{0,8},{8,0},{1,9},{9,1},{2,10},{10,2},{3,11},{11,3},{4,12},{12,4},... | collective-permute-start | bytes 1179656 | tf_op jit(solution)/shard_map/ppermute | solution.py:21
  98.7 3.1 %collective-permute-start.12 = (bf16[16,48,128]{2,1,0:T(8,128)(2,1)S(1)}, bf16[16,48,128]{2,1,0:T(8,128)(2,1)S(1)}, u32[]{:S(2)}, u32[]{:S(2)}) collective-permute-start(bf16[16,48,128]{2,1,0:T(8,128)(2,1)S(1)} %get-tuple-element.48), channel_id=1, source_target_pairs={{0,16},{16,0},{1,17},{17,1},{2,18},{18,2},{3,19},{19,3},{4,20},{20... | collective-permute-start | bytes 589832 | tf_op jit(solution)/shard_map/ppermute | solution.py:21
  101.8 4.9 %collective-permute-done.12.got = bf16[16,48,128]{2,1,0:T(8,128)(2,1)S(1)} collective-permute-done((bf16[16,48,128]{2,1,0:T(8,128)(2,1)S(1)}, bf16[16,48,128]{2,1,0:T(8,128)(2,1)S(1)}, u32[]{:S(2)}, u32[]{:S(2)}) %collective-permute-start.12) | collective-permute-done | bytes 196640 | tf_op jit(solution)/shard_map/ppermute | solution.py:21
  106.7 3.5 %collective-permute-start.13 = (bf16[400,128]{1,0:T(8,128)(2,1)S(1)}, bf16[400,128]{1,0:T(8,128)(2,1)S(1)}, u32[]{:S(2)}, u32[]{:S(2)}) collective-permute-start(bf16[400,128]{1,0:T(8,128)(2,1)S(1)} %get-tuple-element.51), channel_id=1, source_target_pairs={{0,32},{32,0},{64,96},{96,64},{128,160},{160,128},{192,224},{224,1... | collective-permute-start | bytes 307208 | tf_op jit(solution)/shard_map/ppermute | solution.py:26
  115.3 4.2 %all-to-all-start.2 = ((bf16[8,1088,128]{2,1,0:T(8,128)(2,1)}), bf16[8,1088,128]{2,1,0:T(8,128)(2,1)S(1)}, u32[]{:S(2)}, u32[]{:S(2)}) async-start(bf16[8,1088,128]{2,1,0:T(8,128)(2,1)} %copy-done.3), calls=%async_computation.2 | async-start | bytes 4456448 | tf_op jit(solution)/shard_map/all_to_all | solution.py:17
  119.4 4.1 %collective-permute-start.14 = (bf16[208,128]{1,0:T(8,128)(2,1)S(1)}, bf16[208,128]{1,0:T(8,128)(2,1)S(1)}, u32[]{:S(2)}, u32[]{:S(2)}) collective-permute-start(bf16[208,128]{1,0:T(8,128)(2,1)S(1)} %get-tuple-element.53), channel_id=1, source_target_pairs={{0,64},{32,96},{64,0},{96,32},{128,192},{160,224},{192,128},{224,1... | collective-permute-start | bytes 159752 | tf_op jit(solution)/shard_map/ppermute | solution.py:26
  125.8 8.5 %collective-permute-start.15 = (bf16[112,128]{1,0:T(8,128)(2,1)S(1)}, bf16[112,128]{1,0:T(8,128)(2,1)S(1)}, u32[]{:S(2)}, u32[]{:S(2)}) collective-permute-start(bf16[112,128]{1,0:T(8,128)(2,1)S(1)} %get-tuple-element.56), channel_id=1, source_target_pairs={{0,128},{32,160},{64,192},{96,224},{128,0},{160,32},{192,64},{224,... | collective-permute-start | bytes 86024 | tf_op jit(solution)/shard_map/ppermute | solution.py:26
  136.7 10.7 %collective-permute-start.16 = (bf16[64,128]{1,0:T(8,128)(2,1)S(1)}, bf16[64,128]{1,0:T(8,128)(2,1)S(1)}, u32[]{:S(2)}, u32[]{:S(2)}) collective-permute-start(bf16[64,128]{1,0:T(8,128)(2,1)S(1)} %get-tuple-element.59), channel_id=1, source_target_pairs={{0,256},{32,288},{64,320},{96,352},{128,384},{160,416},{192,448},{... | collective-permute-start | bytes 49160 | tf_op jit(solution)/shard_map/ppermute | solution.py:26
  151.8 6.3 %collective-permute-start.17 = (bf16[8,1088,128]{2,1,0:T(8,128)(2,1)S(1)}, bf16[8,1088,128]{2,1,0:T(8,128)(2,1)S(1)}, u32[]{:S(2)}, u32[]{:S(2)}) collective-permute-start(bf16[8,1088,128]{2,1,0:T(8,128)(2,1)S(1)} %shard_map.142.own.own_grad), channel_id=1, source_target_pairs={{0,8},{8,0},{1,9},{9,1},{2,10},{10,2},{3,11},{11,3},{4,12},{12,4},... | collective-permute-start | bytes 6684680 | tf_op jit(solution)/shard_map/ppermute | solution.py:21
  158.1 4.0 %collective-permute-done.17.other.other_grad = bf16[8,1088,128]{2,1,0:T(8,128)(2,1)S(1)} collective-permute-done((bf16[8,1088,128]{2,1,0:T(8,128)(2,1)S(1)}, bf16[8,1088,128]{2,1,0:T(8,128)(2,1)S(1)}, u32[]{:S(2)}, u32[]{:S(2)}) %collective-permute-start.17) | collective-permute-done | bytes 2228256 | tf_op jit(solution)/shard_map/ppermute | solution.py:21
  162.7 13.9 %all_to_all.25.rows = bf16[8,80,128]{2,1,0:T(8,128)(2,1)S(1)} all-to-all(bf16[8,80,128]{2,1,0:T(8,128)(2,1)S(1)} %shard_map.143), channel_id=1, replica_groups=mesh['z'=16,'xl'=2,'c'=2,'t'=8] {'t'}, dimensions={0} | all-to-all | bytes 327680 | tf_op jit(solution)/shard_map/all_to_all | solution.py:17
  178.0 10.9 %all_to_all.26 = bf16[16,64,128]{2,1,0:T(8,128)(2,1)S(1)} all-to-all(bf16[16,64,128]{2,1,0:T(8,128)(2,1)S(1)} %bitcast.5), channel_id=1, replica_groups=mesh['z'=16,'xl'=2,'c'=2,'t'=8] {'xl','t'}, dimensions={0} | all-to-all | bytes 524288 | tf_op jit(solution)/shard_map/all_to_all | solution.py:17
  188.9 4.6 %collective-permute-start.18 = (bf16[2,8,64,128]{3,2,1,0:T(8,128)(2,1)S(1)}, bf16[2,8,64,128]{3,2,1,0:T(8,128)(2,1)S(1)}, u32[]{:S(2)}, u32[]{:S(2)}) collective-permute-start(bf16[2,8,64,128]{3,2,1,0:T(8,128)(2,1)S(1)} %bitcast.3), channel_id=1, source_target_pairs={{0,8},{8,0},{1,9},{9,1},{2,10},{10,2},{3,11},{11,3},{4,12},{12,4},... | collective-permute-start | bytes 786440 | tf_op jit(solution)/shard_map/ppermute | solution.py:21
  195.8 2.8 %shard_map.145 = (bf16[1024,2,128]{2,1,0:T(2,128)(2,1)}, bf16[1,1024,128]{2,1,0:T(8,128)(2,1)}) custom-call(s32[64]{0:T(128)S(1)} %copy-done.12, bf16[8,1088,128]{2,1,0:T(8,128)(2,1)S(1)} %shard_map.142.own.own_grad, bf16[8,1088,128]{2,1,0:T(8,128)(2,1)S(1)} %collective-permute-done.17.other.other_grad, bf16[2,8,64,128]{3,2,1,0:T(8,128)(2,1)S(1)} %bitcast.4, ...), custom_call_target="tpu_custom_call" | custom-call | flops 536870912 | bytes 5767168 | tf_op jit(solution)/shard_map/pallas_call | solution.py:45
  (67 shorter events, 46.3 us)
Async XLA Ops:
  3.5 15.0 %collective-permute-start.2 = (bf16[1552,128]{1,0:T(8,128)(2,1)}, bf16[1552,128]{1,0:T(8,128)(2,1)S(1)}, u32[]{:S(2)}, u32[]{:S(2)}) collective-permute-start(bf16[1552,128]{1,0:T(8,128)(2,1)} %get-tuple-element.41), channel_id=1, source_target_pairs={{0,8},{8,0},{1,9},{9,1},{2,10},{10,2},{3,11},{11,3},{4,12},{12,4},... | collective-permute-start | bytes 1191944 | tf_op jit(solution)/shard_map/ppermute | solution.py:21
  14.7 28.5 %copy-start.5 = (bf16[512,128]{1,0:T(8,128)(2,1)S(1)}, bf16[512,128]{1,0:T(8,128)(2,1)}, u32[]{:S(2)}) copy-start(bf16[512,128]{1,0:T(8,128)(2,1)} %refs_0_.1) | copy-start | bytes 393220
  14.7 59.5 %copy-start.1 = (bf16[512,2,1024]{2,1,0:T(2,128)(2,1)S(1)}, bf16[512,2,1024]{2,1,0:T(2,128)(2,1)}, u32[]{:S(2)}) copy-start(bf16[512,2,1024]{2,1,0:T(2,128)(2,1)} %cot.5) | copy-start | bytes 6291460
  16.5 5.5 %collective-permute-start = (bf16[2,512,128]{2,1,0:T(8,128)(2,1)S(1)}, bf16[2,512,128]{2,1,0:T(8,128)(2,1)S(1)}, u32[]{:S(2)}, u32[]{:S(2)}) collective-permute-start(bf16[2,512,128]{2,1,0:T(8,128)(2,1)S(1)} %get-tuple-element.37), channel_id=1, source_target_pairs={{0,8},{8,0},{1,9},{9,1},{2,10},{10,2},{3,11},{11,3},{4,12},{12,4},... | collective-permute-start | bytes 786440 | tf_op jit(solution)/shard_map/ppermute | solution.py:21
  20.1 12.2 %collective-permute-start.3 = (bf16[1040,128]{1,0:T(8,128)(2,1)S(1)}, bf16[1040,128]{1,0:T(8,128)(2,1)S(1)}, u32[]{:S(2)}, u32[]{:S(2)}) collective-permute-start(bf16[1040,128]{1,0:T(8,128)(2,1)S(1)} %get-tuple-element.43), channel_id=1, source_target_pairs={{0,16},{16,0},{1,17},{17,1},{2,18},{18,2},{3,19},{19,3},{4,20},{20... | collective-permute-start | bytes 798728 | tf_op jit(solution)/shard_map/ppermute | solution.py:21
  22.1 10.2 %collective-permute-start.1 = (bf16[512,128]{1,0:T(8,128)(2,1)S(1)}, bf16[512,128]{1,0:T(8,128)(2,1)S(1)}, u32[]{:S(2)}, u32[]{:S(2)}) collective-permute-start(bf16[512,128]{1,0:T(8,128)(2,1)S(1)} %get-tuple-element.39), channel_id=1, source_target_pairs={{0,16},{16,0},{1,17},{17,1},{2,18},{18,2},{3,19},{19,3},{4,20},{20... | collective-permute-start | bytes 393224 | tf_op jit(solution)/shard_map/ppermute | solution.py:21
  33.7 43.1 %all-to-all-start = ((bf16[16,96,128]{2,1,0:T(8,128)(2,1)}), bf16[16,96,128]{2,1,0:T(8,128)(2,1)S(1)}, u32[]{:S(2)}, u32[]{:S(2)}) async-start(bf16[16,96,128]{2,1,0:T(8,128)(2,1)} %get-tuple-element.44), calls=%async_computation | async-start | bytes 786432 | tf_op jit(solution)/shard_map/all_to_all | solution.py:17
  43.2 19.3 %collective-permute-start.10 = (bf16[512,128]{1,0:T(8,128)(2,1)S(1)}, bf16[512,128]{1,0:T(8,128)(2,1)S(1)}, u32[]{:S(2)}, u32[]{:S(2)}) collective-permute-start(bf16[512,128]{1,0:T(8,128)(2,1)S(1)} %copy-done.5), channel_id=1, source_target_pairs={{0,7},{1,6},{2,5},{3,4},{4,3},{5,2},{6,1},{7,0},{8,15},{9,14},{10,... | collective-permute-start | bytes 393224 | tf_op jit(solution)/shard_map/ppermute | solution.py:26
  50.3 16.7 %collective-permute-start.4 = (bf16[512,128]{1,0:T(8,128)(2,1)S(1)}, bf16[512,128]{1,0:T(8,128)(2,1)S(1)}, u32[]{:S(2)}, u32[]{:S(2)}) collective-permute-start(bf16[512,128]{1,0:T(8,128)(2,1)S(1)} %copy-done.5), channel_id=1, source_target_pairs={{0,1},{1,0},{2,3},{3,2},{4,5},{5,4},{6,7},{7,6},{8,9},{9,8},{10,11... | collective-permute-start | bytes 393224 | tf_op jit(solution)/shard_map/ppermute | solution.py:26
  52.5 16.5 %collective-permute-start.5 = (bf16[512,128]{1,0:T(8,128)(2,1)S(1)}, bf16[512,128]{1,0:T(8,128)(2,1)S(1)}, u32[]{:S(2)}, u32[]{:S(2)}) collective-permute-start(bf16[512,128]{1,0:T(8,128)(2,1)S(1)} %copy-done.5), channel_id=1, source_target_pairs={{0,2},{1,3},{2,0},{3,1},{4,6},{5,7},{6,4},{7,5},{8,10},{9,11},{10,... | collective-permute-start | bytes 393224 | tf_op jit(solution)/shard_map/ppermute | solution.py:26
  54.4 14.6 %collective-permute-start.6 = (bf16[512,128]{1,0:T(8,128)(2,1)S(1)}, bf16[512,128]{1,0:T(8,128)(2,1)S(1)}, u32[]{:S(2)}, u32[]{:S(2)}) collective-permute-start(bf16[512,128]{1,0:T(8,128)(2,1)S(1)} %copy-done.5), channel_id=1, source_target_pairs={{0,3},{1,2},{2,1},{3,0},{4,7},{5,6},{6,5},{7,4},{8,11},{9,10},{10,... | collective-permute-start | bytes 393224 | tf_op jit(solution)/shard_map/ppermute | solution.py:26
  60.2 8.8 %collective-permute-start.7 = (bf16[512,128]{1,0:T(8,128)(2,1)S(1)}, bf16[512,128]{1,0:T(8,128)(2,1)S(1)}, u32[]{:S(2)}, u32[]{:S(2)}) collective-permute-start(bf16[512,128]{1,0:T(8,128)(2,1)S(1)} %copy-done.5), channel_id=1, source_target_pairs={{0,4},{1,5},{2,6},{3,7},{4,0},{5,1},{6,2},{7,3},{8,12},{9,13},{10,... | collective-permute-start | bytes 393224 | tf_op jit(solution)/shard_map/ppermute | solution.py:26
  62.5 9.6 %collective-permute-start.8 = (bf16[512,128]{1,0:T(8,128)(2,1)S(1)}, bf16[512,128]{1,0:T(8,128)(2,1)S(1)}, u32[]{:S(2)}, u32[]{:S(2)}) collective-permute-start(bf16[512,128]{1,0:T(8,128)(2,1)S(1)} %copy-done.5), channel_id=1, source_target_pairs={{0,5},{1,4},{2,7},{3,6},{4,1},{5,0},{6,3},{7,2},{8,13},{9,12},{10,... | collective-permute-start | bytes 393224 | tf_op jit(solution)/shard_map/ppermute | solution.py:26
  67.0 7.2 %collective-permute-start.9 = (bf16[512,128]{1,0:T(8,128)(2,1)S(1)}, bf16[512,128]{1,0:T(8,128)(2,1)S(1)}, u32[]{:S(2)}, u32[]{:S(2)}) collective-permute-start(bf16[512,128]{1,0:T(8,128)(2,1)S(1)} %copy-done.5), channel_id=1, source_target_pairs={{0,6},{1,7},{2,4},{3,5},{4,2},{5,3},{6,0},{7,1},{8,14},{9,15},{10,... | collective-permute-start | bytes 393224 | tf_op jit(solution)/shard_map/ppermute | solution.py:26
  79.1 33.9 %all-to-all-start.1 = ((bf16[16,96,128]{2,1,0:T(8,128)(2,1)}), bf16[16,96,128]{2,1,0:T(8,128)(2,1)S(1)}, u32[]{:S(2)}, u32[]{:S(2)}) async-start(bf16[16,96,128]{2,1,0:T(8,128)(2,1)} %shard_map.135), calls=%async_computation.1 | async-start | bytes 786432 | tf_op jit(solution)/shard_map/all_to_all | solution.py:17
  90.3 8.3 %collective-permute-start.11 = (bf16[16,2,48,128]{3,2,1,0:T(8,128)(2,1)S(1)}, bf16[16,2,48,128]{3,2,1,0:T(8,128)(2,1)S(1)}, u32[]{:S(2)}, u32[]{:S(2)}) collective-permute-start(bf16[16,2,48,128]{3,2,1,0:T(8,128)(2,1)S(1)} %copy-done.9), channel_id=1, source_target_pairs={{0,8},{8,0},{1,9},{9,1},{2,10},{10,2},{3,11},{11,3},{4,12},{12,4},... | collective-permute-start | bytes 1179656 | tf_op jit(solution)/shard_map/ppermute | solution.py:21
  98.7 8.0 %collective-permute-start.12 = (bf16[16,48,128]{2,1,0:T(8,128)(2,1)S(1)}, bf16[16,48,128]{2,1,0:T(8,128)(2,1)S(1)}, u32[]{:S(2)}, u32[]{:S(2)}) collective-permute-start(bf16[16,48,128]{2,1,0:T(8,128)(2,1)S(1)} %get-tuple-element.48), channel_id=1, source_target_pairs={{0,16},{16,0},{1,17},{17,1},{2,18},{18,2},{3,19},{19,3},{4,20},{20... | collective-permute-start | bytes 589832 | tf_op jit(solution)/shard_map/ppermute | solution.py:21
  106.7 6.3 %collective-permute-start.13 = (bf16[400,128]{1,0:T(8,128)(2,1)S(1)}, bf16[400,128]{1,0:T(8,128)(2,1)S(1)}, u32[]{:S(2)}, u32[]{:S(2)}) collective-permute-start(bf16[400,128]{1,0:T(8,128)(2,1)S(1)} %get-tuple-element.51), channel_id=1, source_target_pairs={{0,32},{32,0},{64,96},{96,64},{128,160},{160,128},{192,224},{224,1... | collective-permute-start | bytes 307208 | tf_op jit(solution)/shard_map/ppermute | solution.py:26
  115.3 35.8 %all-to-all-start.2 = ((bf16[8,1088,128]{2,1,0:T(8,128)(2,1)}), bf16[8,1088,128]{2,1,0:T(8,128)(2,1)S(1)}, u32[]{:S(2)}, u32[]{:S(2)}) async-start(bf16[8,1088,128]{2,1,0:T(8,128)(2,1)} %copy-done.3), calls=%async_computation.2 | async-start | bytes 4456448 | tf_op jit(solution)/shard_map/all_to_all | solution.py:17
  119.4 5.8 %collective-permute-start.14 = (bf16[208,128]{1,0:T(8,128)(2,1)S(1)}, bf16[208,128]{1,0:T(8,128)(2,1)S(1)}, u32[]{:S(2)}, u32[]{:S(2)}) collective-permute-start(bf16[208,128]{1,0:T(8,128)(2,1)S(1)} %get-tuple-element.53), channel_id=1, source_target_pairs={{0,64},{32,96},{64,0},{96,32},{128,192},{160,224},{192,128},{224,1... | collective-permute-start | bytes 159752 | tf_op jit(solution)/shard_map/ppermute | solution.py:26
  125.8 10.3 %collective-permute-start.15 = (bf16[112,128]{1,0:T(8,128)(2,1)S(1)}, bf16[112,128]{1,0:T(8,128)(2,1)S(1)}, u32[]{:S(2)}, u32[]{:S(2)}) collective-permute-start(bf16[112,128]{1,0:T(8,128)(2,1)S(1)} %get-tuple-element.56), channel_id=1, source_target_pairs={{0,128},{32,160},{64,192},{96,224},{128,0},{160,32},{192,64},{224,... | collective-permute-start | bytes 86024 | tf_op jit(solution)/shard_map/ppermute | solution.py:26
  136.7 13.2 %collective-permute-start.16 = (bf16[64,128]{1,0:T(8,128)(2,1)S(1)}, bf16[64,128]{1,0:T(8,128)(2,1)S(1)}, u32[]{:S(2)}, u32[]{:S(2)}) collective-permute-start(bf16[64,128]{1,0:T(8,128)(2,1)S(1)} %get-tuple-element.59), channel_id=1, source_target_pairs={{0,256},{32,288},{64,320},{96,352},{128,384},{160,416},{192,448},{... | collective-permute-start | bytes 49160 | tf_op jit(solution)/shard_map/ppermute | solution.py:26
  151.8 10.2 %collective-permute-start.17 = (bf16[8,1088,128]{2,1,0:T(8,128)(2,1)S(1)}, bf16[8,1088,128]{2,1,0:T(8,128)(2,1)S(1)}, u32[]{:S(2)}, u32[]{:S(2)}) collective-permute-start(bf16[8,1088,128]{2,1,0:T(8,128)(2,1)S(1)} %shard_map.142.own.own_grad), channel_id=1, source_target_pairs={{0,8},{8,0},{1,9},{9,1},{2,10},{10,2},{3,11},{11,3},{4,12},{12,4},... | collective-permute-start | bytes 6684680 | tf_op jit(solution)/shard_map/ppermute | solution.py:21
  188.9 6.9 %collective-permute-start.18 = (bf16[2,8,64,128]{3,2,1,0:T(8,128)(2,1)S(1)}, bf16[2,8,64,128]{3,2,1,0:T(8,128)(2,1)S(1)}, u32[]{:S(2)}, u32[]{:S(2)}) collective-permute-start(bf16[2,8,64,128]{3,2,1,0:T(8,128)(2,1)S(1)} %bitcast.3), channel_id=1, source_target_pairs={{0,8},{8,0},{1,9},{9,1},{2,10},{10,2},{3,11},{11,3},{4,12},{12,4},... | collective-permute-start | bytes 786440 | tf_op jit(solution)/shard_map/ppermute | solution.py:21
  (11 other events, 76.7 us)

commit v13 on v11

--- a/solution.py
+++ b/solution.py
@@ -216,7 +216,11 @@
     halve(bit, total, chosen[...], sent, rest)
 
 
-def reduce_z(owners, got, keep, f_got, vals, sent, f_sent, f_rest):
+def factor_first(keep, got, vals, sent, rest):
+    halve(1, keep[...] + got[...].astype(f32), vals[...], sent, rest)
+
+
+def reduce_z(owners, got, keep, f_got, vals, sent, f_sent, f_rest, chosen):
     nz, height, _ = sent.shape
     per = height // 3
     xl = lax.axis_index("xl")
@@ -229,7 +233,7 @@
     for i, part in enumerate(parts):
         for k in range(nz):
             sent[k, i * per : (i + 1) * per] = part
-    halve(1, keep[...] + f_got[...].astype(f32), vals[...], f_sent, f_rest)
+    factor_z(2, owners, keep, f_got, vals, f_sent, f_rest, chosen)
 
 
 def factor_terms(cot, act, whole, sent, keep, flat, both):
@@ -276,7 +280,7 @@
             rows = got[:, (1 + i) * per : (2 + i) * per].reshape(half, slab)
             sent[k, i * half : (i + 1) * half] = rows
     sent[:, 2 * half :] = got[:, 0:per].reshape(nt, piece, slab)
-    factor_z(2, owners, keep, f_got, vals, f_sent, f_rest, chosen)
+    factor_z(4, owners, keep, f_got, vals, f_sent, f_rest, chosen)
 
 
 def factor_out(bit, owners, keep, got, vals, factor_a, factor_g, chosen):
@@ -434,41 +438,41 @@
     def step_outs(count):
         return [out((count * height + VALS, slab)), out((count, height, slab), f32)]
 
-    sent, f_sent, f_keep = call(
+    f_sent, f_keep = call(factor_first, step_outs(nz // 2), [], [f_keep, f_got, vals])
+    f_got = across(f_sent, "z", 1)
+
+    chosen = out((VALS, slab))
+    sent, f_sent, f_keep, vals = call(
         reduce_z,
-        [out((nz, 3 * per, slab))] + step_outs(nz // 2),
+        [out((nz, 3 * per, slab))] + step_outs(nz // 4) + [chosen],
         [owners],
         [got, f_keep, f_got, vals],
     )
     got = exchange(sent, "z")
-    f_got = across(f_sent, "z", 1)
-
-    chosen = out((VALS, slab))
+    f_got = across(f_sent, "z", 2)
+
     sent, f_sent, f_keep, vals = call(
         pack_t,
-        [out((nt, 2 * half + piece, slab))] + step_outs(nz // 4) + [chosen],
+        [out((nt, 2 * half + piece, slab))] + step_outs(nz // 8) + [chosen],
         [owners],
         [got, f_keep, f_got, vals],
     )
     own = exchange(sent, "t")
-    f_got = across(f_sent, "z", 2)
-    bit = 4
-    while bit < nz:
-        f_sent, f_keep, vals = call(
-            functools.partial(factor_z, bit),
-            step_outs(nz // 2 // bit) + [chosen],
-            [owners],
-            [f_keep, f_got, vals],
-        )
-        f_got = across(f_sent, "z", bit)
-        bit *= 2
+    f_got = across(f_sent, "z", 4)
+    f_sent, f_keep, vals = call(
+        functools.partial(factor_z, 8),
+        step_outs(nz // 16) + [chosen],
+        [owners],
+        [f_keep, f_got, vals],
+    )
+    f_got = across(f_sent, "z", 8)
     factor_a, factor_g, vals = call(
         functools.partial(factor_out, nz // 2),
         [out((group, slab), f32), out((blocks, group, slab), f32), chosen],
         [owners],
         [f_keep, f_got, vals],
     )
-    own = follow(own, factor_a, 20)
+    own = follow(own, vals, 20)
     other = swap(own, "c")
     qa, qa_other = (own, half, 0), (other, half, 0)
     qg, qg_other = (own, half, 1), (other, half, 1)

time: 192 us -> 188 us (0.979)
    unnamed x25 -> x23, local copies, waits for them, and re-layouts: 5.66 us -> 4.97 us
  transfers between devices with their start and end apart: 16 -> 16, of which waited for: 9 -> 8; matrix products, arithmetic and copies ran while one was open for 0% -> 0% of each run, Pallas kernels for 5% -> 4%
where the time goes in v13:
time: 188 us; the launch traced here: 187 us
  starting transfers between devices  99.8 us (53%)
  waiting for transfers between devices  38.3 us (20%)
  blocking collectives  24.1 us (13%)
  Pallas kernels  19.2 us (10%)
  local copies, waits for them, and re-layouts  4.97 us (3%)
    all_to_all x4, starting transfers between devices, exchange(): return lax.all_to_all(array, axis, 0, 0, tiled=True)  39.7 us
    ppermute x8, starting transfers between devices, swap(): return lax.ppermute(array, axis, [(0, 1), (1, 0)])  33.3 us
    ppermute x4, starting transfers between devices, across(): return lax.ppermute(array, axis, pairs)  26.9 us
    all_to_all x2, blocking collectives, exchange(): return lax.all_to_all(array, axis, 0, 0, tiled=True)  24.1 us
    ppermute x4, waiting for transfers between devices, across(): return lax.ppermute(array, axis, pairs)  21.2 us
    pallas_call x16, Pallas kernels, call(): pl.pallas_call(body, grid=(1,), out_shape=outs, in_specs=[pl.BlockSpec(me...  19.2 us
    ppermute x8, waiting for transfers between devices, swap(): return lax.ppermute(array, axis, [(0, 1), (1, 0)])  17 us
    unnamed x23, local copies, waits for them, and re-layouts  4.97 us
  transfers between devices with their start and end apart: 16, of which 8 were waited for; matrix products, arithmetic and copies ran while one was open for 0% of the time, Pallas kernels for 4%

profile of v13, /device:TPU:1, one launch (start us, length us, event | category | flops | bytes accessed | tf_op | source)
XLA Modules:
  0.0 187.4 jit_solution(4997796569652908044)
XLA Ops:
  0.7 3.6 %shard_map.131 = (bf16[1552,128]{1,0:T(8,128)(2,1)}, bf16[1552,128]{1,0:T(8,128)(2,1)}, bf16[8,512,128]{2,1,0:T(8,128)(2,1)}) custom-call(bf16[1,1024,128]{2,1,0:T(8,128)(2,1)} %ba.1, bf16[1,2,1024,128]{3,2,1,0:T(8,128)(2,1)} %bg.1, bf16[1,128]{1,0:T(2,128)(2,1)} %va.1, bf16[1,2,128]{2,1,0:T(2,128)(2,1)} %vg.1, bf16[512,128]{1,0:T(8,128)(2,1)} %act.5), custom_call_target="tpu_custom_call" | custom-call | bytes 2761472 | tf_op jit(solution)/shard_map/pallas_call | solution.py:45
  4.3 7.5 %all-to-all-start = ((bf16[8,512,128]{2,1,0:T(8,128)(2,1)}), bf16[8,512,128]{2,1,0:T(8,128)(2,1)S(1)}, u32[]{:S(2)}, u32[]{:S(2)}) async-start(bf16[8,512,128]{2,1,0:T(8,128)(2,1)} %get-tuple-element.47), calls=%async_computation | async-start | bytes 2097152 | tf_op jit(solution)/shard_map/all_to_all | solution.py:17
  11.8 5.0 %collective-permute-start.2 = (bf16[1552,128]{1,0:T(8,128)(2,1)}, bf16[1552,128]{1,0:T(8,128)(2,1)S(1)}, u32[]{:S(2)}, u32[]{:S(2)}) collective-permute-start(bf16[1552,128]{1,0:T(8,128)(2,1)} %get-tuple-element.43), channel_id=1, source_target_pairs={{0,8},{8,0},{1,9},{9,1},{2,10},{10,2},{3,11},{11,3},{4,12},{12,4},... | collective-permute-start | bytes 1191944 | tf_op jit(solution)/shard_map/ppermute | solution.py:21
  23.3 3.4 %collective-permute-start.1 = (bf16[512,128]{1,0:T(8,128)(2,1)S(1)}, bf16[512,128]{1,0:T(8,128)(2,1)S(1)}, u32[]{:S(2)}, u32[]{:S(2)}) collective-permute-start(bf16[512,128]{1,0:T(8,128)(2,1)S(1)} %get-tuple-element.41), channel_id=1, source_target_pairs={{0,16},{16,0},{1,17},{17,1},{2,18},{18,2},{3,19},{19,3},{4,20},{20... | collective-permute-start | bytes 393224 | tf_op jit(solution)/shard_map/ppermute | solution.py:21
  26.6 6.8 %collective-permute-done.1.got = bf16[512,128]{1,0:T(8,128)(2,1)S(1)} collective-permute-done((bf16[512,128]{1,0:T(8,128)(2,1)S(1)}, bf16[512,128]{1,0:T(8,128)(2,1)S(1)}, u32[]{:S(2)}, u32[]{:S(2)}) %collective-permute-start.1) | collective-permute-done | bytes 131104 | tf_op jit(solution)/shard_map/ppermute | solution.py:21
  35.8 13.9 %all-to-all-start.1 = ((bf16[16,96,128]{2,1,0:T(8,128)(2,1)}), bf16[16,96,128]{2,1,0:T(8,128)(2,1)S(1)}, u32[]{:S(2)}, u32[]{:S(2)}) async-start(bf16[16,96,128]{2,1,0:T(8,128)(2,1)} %shard_map.134), calls=%async_computation.1 | async-start | bytes 786432 | tf_op jit(solution)/shard_map/all_to_all | solution.py:17
  52.7 3.5 %collective-permute-start.4 = (bf16[16,2,48,128]{3,2,1,0:T(8,128)(2,1)S(1)}, bf16[16,2,48,128]{3,2,1,0:T(8,128)(2,1)S(1)}, u32[]{:S(2)}, u32[]{:S(2)}) collective-permute-start(bf16[16,2,48,128]{3,2,1,0:T(8,128)(2,1)S(1)} %get-tuple-element.49), channel_id=1, source_target_pairs={{0,8},{8,0},{1,9},{9,1},{2,10},{10,2},{3,11},{11,3},{4,12},{12,4},... | collective-permute-start | bytes 1179656 | tf_op jit(solution)/shard_map/ppermute | solution.py:21
  57.6 3.1 %collective-permute-start.5 = (bf16[16,48,128]{2,1,0:T(8,128)(2,1)S(1)}, bf16[16,48,128]{2,1,0:T(8,128)(2,1)S(1)}, u32[]{:S(2)}, u32[]{:S(2)}) collective-permute-start(bf16[16,48,128]{2,1,0:T(8,128)(2,1)S(1)} %get-tuple-element.51), channel_id=1, source_target_pairs={{0,16},{16,0},{1,17},{17,1},{2,18},{18,2},{3,19},{19,3},{4,20},{20... | collective-permute-start | bytes 589832 | tf_op jit(solution)/shard_map/ppermute | solution.py:21
  60.7 4.9 %collective-permute-done.5.got = bf16[16,48,128]{2,1,0:T(8,128)(2,1)S(1)} collective-permute-done((bf16[16,48,128]{2,1,0:T(8,128)(2,1)S(1)}, bf16[16,48,128]{2,1,0:T(8,128)(2,1)S(1)}, u32[]{:S(2)}, u32[]{:S(2)}) %collective-permute-start.5) | collective-permute-done | bytes 196640 | tf_op jit(solution)/shard_map/ppermute | solution.py:21
  65.7 3.6 %collective-permute-start.6 = (bf16[400,128]{1,0:T(8,128)(2,1)S(1)}, bf16[400,128]{1,0:T(8,128)(2,1)S(1)}, u32[]{:S(2)}, u32[]{:S(2)}) collective-permute-start(bf16[400,128]{1,0:T(8,128)(2,1)S(1)} %get-tuple-element.54), channel_id=1, source_target_pairs={{0,32},{32,0},{64,96},{96,64},{128,160},{160,128},{192,224},{224,1... | collective-permute-start | bytes 307208 | tf_op jit(solution)/shard_map/ppermute | solution.py:26
  69.3 2.6 %collective-permute-done.6.f_got = bf16[400,128]{1,0:T(8,128)(2,1)S(1)} collective-permute-done((bf16[400,128]{1,0:T(8,128)(2,1)S(1)}, bf16[400,128]{1,0:T(8,128)(2,1)S(1)}, u32[]{:S(2)}, u32[]{:S(2)}) %collective-permute-start.6) | collective-permute-done | bytes 102432 | tf_op jit(solution)/shard_map/ppermute | solution.py:26
  73.2 11.0 %all-to-all-start.2 = ((bf16[16,96,128]{2,1,0:T(8,128)(2,1)}), bf16[16,96,128]{2,1,0:T(8,128)(2,1)S(1)}, u32[]{:S(2)}, u32[]{:S(2)}) async-start(bf16[16,96,128]{2,1,0:T(8,128)(2,1)} %get-tuple-element.55), calls=%async_computation.2 | async-start | bytes 786432 | tf_op jit(solution)/shard_map/all_to_all | solution.py:17
  84.3 4.2 %collective-permute-start.7 = (bf16[208,128]{1,0:T(8,128)(2,1)S(1)}, bf16[208,128]{1,0:T(8,128)(2,1)S(1)}, u32[]{:S(2)}, u32[]{:S(2)}) collective-permute-start(bf16[208,128]{1,0:T(8,128)(2,1)S(1)} %get-tuple-element.57), channel_id=1, source_target_pairs={{0,64},{32,96},{64,0},{96,32},{128,192},{160,224},{192,128},{224,1... | collective-permute-start | bytes 159752 | tf_op jit(solution)/shard_map/ppermute | solution.py:26
  88.4 15.1 %collective-permute-done.7.f_got = bf16[208,128]{1,0:T(8,128)(2,1)S(1)} collective-permute-done((bf16[208,128]{1,0:T(8,128)(2,1)S(1)}, bf16[208,128]{1,0:T(8,128)(2,1)S(1)}, u32[]{:S(2)}, u32[]{:S(2)}) %collective-permute-start.7) | collective-permute-done | bytes 53280 | tf_op jit(solution)/shard_map/ppermute | solution.py:26
  105.8 7.2 %all-to-all-start.3 = ((bf16[8,1088,128]{2,1,0:T(8,128)(2,1)}), bf16[8,1088,128]{2,1,0:T(8,128)(2,1)S(1)}, u32[]{:S(2)}, u32[]{:S(2)}) async-start(bf16[8,1088,128]{2,1,0:T(8,128)(2,1)} %copy-done.4), calls=%async_computation.3 | async-start | bytes 4456448 | tf_op jit(solution)/shard_map/all_to_all | solution.py:17
  113.1 6.1 %collective-permute-start.8 = (bf16[112,128]{1,0:T(8,128)(2,1)S(1)}, bf16[112,128]{1,0:T(8,128)(2,1)S(1)}, u32[]{:S(2)}, u32[]{:S(2)}) collective-permute-start(bf16[112,128]{1,0:T(8,128)(2,1)S(1)} %get-tuple-element.60), channel_id=1, source_target_pairs={{0,128},{32,160},{64,192},{96,224},{128,0},{160,32},{192,64},{224,... | collective-permute-start | bytes 86024 | tf_op jit(solution)/shard_map/ppermute | solution.py:26
  119.2 2.4 %collective-permute-done.8.got = bf16[112,128]{1,0:T(8,128)(2,1)S(1)} collective-permute-done((bf16[112,128]{1,0:T(8,128)(2,1)S(1)}, bf16[112,128]{1,0:T(8,128)(2,1)S(1)}, u32[]{:S(2)}, u32[]{:S(2)}) %collective-permute-start.8) | collective-permute-done | bytes 28704 | tf_op jit(solution)/shard_map/ppermute | solution.py:26
  122.2 13.1 %collective-permute-start.9 = (bf16[64,128]{1,0:T(8,128)(2,1)S(1)}, bf16[64,128]{1,0:T(8,128)(2,1)S(1)}, u32[]{:S(2)}, u32[]{:S(2)}) collective-permute-start(bf16[64,128]{1,0:T(8,128)(2,1)S(1)} %get-tuple-element.63), channel_id=1, source_target_pairs={{0,256},{32,288},{64,320},{96,352},{128,384},{160,416},{192,448},{... | collective-permute-start | bytes 49160 | tf_op jit(solution)/shard_map/ppermute | solution.py:26
  137.6 9.8 %collective-permute-start.10 = (bf16[8,1088,128]{2,1,0:T(8,128)(2,1)S(1)}, bf16[8,1088,128]{2,1,0:T(8,128)(2,1)S(1)}, u32[]{:S(2)}, u32[]{:S(2)}) collective-permute-start(bf16[8,1088,128]{2,1,0:T(8,128)(2,1)S(1)} %shard_map.142.own.own_grad), channel_id=1, source_target_pairs={{0,8},{8,0},{1,9},{9,1},{2,10},{10,2},{3,11},{11,3},{4,12},{12,4},... | collective-permute-start | bytes 6684680 | tf_op jit(solution)/shard_map/ppermute | solution.py:21
  147.4 4.0 %collective-permute-done.10.other.other_grad = bf16[8,1088,128]{2,1,0:T(8,128)(2,1)S(1)} collective-permute-done((bf16[8,1088,128]{2,1,0:T(8,128)(2,1)S(1)}, bf16[8,1088,128]{2,1,0:T(8,128)(2,1)S(1)}, u32[]{:S(2)}, u32[]{:S(2)}) %collective-permute-start.10) | collective-permute-done | bytes 2228256 | tf_op jit(solution)/shard_map/ppermute | solution.py:21
  152.1 13.9 %all_to_all.30.rows = bf16[8,80,128]{2,1,0:T(8,128)(2,1)S(1)} all-to-all(bf16[8,80,128]{2,1,0:T(8,128)(2,1)S(1)} %shard_map.143), channel_id=1, replica_groups=mesh['z'=16,'xl'=2,'c'=2,'t'=8] {'t'}, dimensions={0} | all-to-all | bytes 327680 | tf_op jit(solution)/shard_map/all_to_all | solution.py:17
  167.4 10.2 %all_to_all.31 = bf16[16,64,128]{2,1,0:T(8,128)(2,1)S(1)} all-to-all(bf16[16,64,128]{2,1,0:T(8,128)(2,1)S(1)} %bitcast.5), channel_id=1, replica_groups=mesh['z'=16,'xl'=2,'c'=2,'t'=8] {'xl','t'}, dimensions={0} | all-to-all | bytes 524288 | tf_op jit(solution)/shard_map/all_to_all | solution.py:17
  177.7 4.7 %collective-permute-start.11 = (bf16[2,8,64,128]{3,2,1,0:T(8,128)(2,1)S(1)}, bf16[2,8,64,128]{3,2,1,0:T(8,128)(2,1)S(1)}, u32[]{:S(2)}, u32[]{:S(2)}) collective-permute-start(bf16[2,8,64,128]{3,2,1,0:T(8,128)(2,1)S(1)} %bitcast.3), channel_id=1, source_target_pairs={{0,8},{8,0},{1,9},{9,1},{2,10},{10,2},{3,11},{11,3},{4,12},{12,4},... | collective-permute-start | bytes 786440 | tf_op jit(solution)/shard_map/ppermute | solution.py:21
  184.6 2.8 %shard_map.145 = (bf16[1024,2,128]{2,1,0:T(2,128)(2,1)}, bf16[1,1024,128]{2,1,0:T(8,128)(2,1)}) custom-call(s32[64]{0:T(128)S(1)} %copy-done.10, bf16[8,1088,128]{2,1,0:T(8,128)(2,1)S(1)} %shard_map.142.own.own_grad, bf16[8,1088,128]{2,1,0:T(8,128)(2,1)S(1)} %collective-permute-done.10.other.other_grad, bf16[2,8,64,128]{3,2,1,0:T(8,128)(2,1)S(1)} %bitcast.4, ...), custom_call_target="tpu_custom_call" | custom-call | flops 536870912 | bytes 5767168 | tf_op jit(solution)/shard_map/pallas_call | solution.py:45
  (51 shorter events, 24.0 us)
Async XLA Ops:
  0.6 16.2 %copy-start.6 = (bf16[512,128]{1,0:T(8,128)(2,1)S(1)}, bf16[512,128]{1,0:T(8,128)(2,1)}, u32[]{:S(2)}) copy-start(bf16[512,128]{1,0:T(8,128)(2,1)} %act.5) | copy-start | bytes 393220
  0.6 16.2 %copy-start = (bf16[512,2,1024]{2,1,0:T(2,128)(2,1)S(1)}, bf16[512,2,1024]{2,1,0:T(2,128)(2,1)}, u32[]{:S(2)}) copy-start(bf16[512,2,1024]{2,1,0:T(2,128)(2,1)} %cot.5) | copy-start | bytes 6291460
  4.3 16.3 %copy-start.9 = (s32[3]{0:T(128)S(1)}, s32[3]{0:T(128)}, u32[]{:S(2)}) copy-start(s32[3]{0:T(128)} %owners.11) | copy-start | bytes 40
  4.3 30.5 %all-to-all-start = ((bf16[8,512,128]{2,1,0:T(8,128)(2,1)}), bf16[8,512,128]{2,1,0:T(8,128)(2,1)S(1)}, u32[]{:S(2)}, u32[]{:S(2)}) async-start(bf16[8,512,128]{2,1,0:T(8,128)(2,1)} %get-tuple-element.47), calls=%async_computation | async-start | bytes 2097152 | tf_op jit(solution)/shard_map/all_to_all | solution.py:17
  11.8 8.8 %copy-start.8 = (bf16[1552,128]{1,0:T(8,128)(2,1)S(1)}, bf16[1552,128]{1,0:T(8,128)(2,1)}, u32[]{:S(2)}) copy-start(bf16[1552,128]{1,0:T(8,128)(2,1)} %get-tuple-element.42.own) | copy-start | bytes 1191940
  11.8 8.8 %collective-permute-start.2 = (bf16[1552,128]{1,0:T(8,128)(2,1)}, bf16[1552,128]{1,0:T(8,128)(2,1)S(1)}, u32[]{:S(2)}, u32[]{:S(2)}) collective-permute-start(bf16[1552,128]{1,0:T(8,128)(2,1)} %get-tuple-element.43), channel_id=1, source_target_pairs={{0,8},{8,0},{1,9},{9,1},{2,10},{10,2},{3,11},{11,3},{4,12},{12,4},... | collective-permute-start | bytes 1191944 | tf_op jit(solution)/shard_map/ppermute | solution.py:21
  18.6 4.6 %collective-permute-start = (bf16[2,512,128]{2,1,0:T(8,128)(2,1)S(1)}, bf16[2,512,128]{2,1,0:T(8,128)(2,1)S(1)}, u32[]{:S(2)}, u32[]{:S(2)}) collective-permute-start(bf16[2,512,128]{2,1,0:T(8,128)(2,1)S(1)} %get-tuple-element.39), channel_id=1, source_target_pairs={{0,8},{8,0},{1,9},{9,1},{2,10},{10,2},{3,11},{11,3},{4,12},{12,4},... | collective-permute-start | bytes 786440 | tf_op jit(solution)/shard_map/ppermute | solution.py:21
  21.2 12.2 %collective-permute-start.3 = (bf16[1040,128]{1,0:T(8,128)(2,1)S(1)}, bf16[1040,128]{1,0:T(8,128)(2,1)S(1)}, u32[]{:S(2)}, u32[]{:S(2)}) collective-permute-start(bf16[1040,128]{1,0:T(8,128)(2,1)S(1)} %get-tuple-element.45), channel_id=1, source_target_pairs={{0,16},{16,0},{1,17},{17,1},{2,18},{18,2},{3,19},{19,3},{4,20},{20... | collective-permute-start | bytes 798728 | tf_op jit(solution)/shard_map/ppermute | solution.py:21
  23.3 10.2 %collective-permute-start.1 = (bf16[512,128]{1,0:T(8,128)(2,1)S(1)}, bf16[512,128]{1,0:T(8,128)(2,1)S(1)}, u32[]{:S(2)}, u32[]{:S(2)}) collective-permute-start(bf16[512,128]{1,0:T(8,128)(2,1)S(1)} %get-tuple-element.41), channel_id=1, source_target_pairs={{0,16},{16,0},{1,17},{17,1},{2,18},{18,2},{3,19},{19,3},{4,20},{20... | collective-permute-start | bytes 393224 | tf_op jit(solution)/shard_map/ppermute | solution.py:21
  35.8 36.1 %all-to-all-start.1 = ((bf16[16,96,128]{2,1,0:T(8,128)(2,1)}), bf16[16,96,128]{2,1,0:T(8,128)(2,1)S(1)}, u32[]{:S(2)}, u32[]{:S(2)}) async-start(bf16[16,96,128]{2,1,0:T(8,128)(2,1)} %shard_map.134), calls=%async_computation.1 | async-start | bytes 786432 | tf_op jit(solution)/shard_map/all_to_all | solution.py:17
  52.7 4.8 %collective-permute-start.4 = (bf16[16,2,48,128]{3,2,1,0:T(8,128)(2,1)S(1)}, bf16[16,2,48,128]{3,2,1,0:T(8,128)(2,1)S(1)}, u32[]{:S(2)}, u32[]{:S(2)}) collective-permute-start(bf16[16,2,48,128]{3,2,1,0:T(8,128)(2,1)S(1)} %get-tuple-element.49), channel_id=1, source_target_pairs={{0,8},{8,0},{1,9},{9,1},{2,10},{10,2},{3,11},{11,3},{4,12},{12,4},... | collective-permute-start | bytes 1179656 | tf_op jit(solution)/shard_map/ppermute | solution.py:21
  57.6 8.0 %collective-permute-start.5 = (bf16[16,48,128]{2,1,0:T(8,128)(2,1)S(1)}, bf16[16,48,128]{2,1,0:T(8,128)(2,1)S(1)}, u32[]{:S(2)}, u32[]{:S(2)}) collective-permute-start(bf16[16,48,128]{2,1,0:T(8,128)(2,1)S(1)} %get-tuple-element.51), channel_id=1, source_target_pairs={{0,16},{16,0},{1,17},{17,1},{2,18},{18,2},{3,19},{19,3},{4,20},{20... | collective-permute-start | bytes 589832 | tf_op jit(solution)/shard_map/ppermute | solution.py:21
  65.7 6.1 %collective-permute-start.6 = (bf16[400,128]{1,0:T(8,128)(2,1)S(1)}, bf16[400,128]{1,0:T(8,128)(2,1)S(1)}, u32[]{:S(2)}, u32[]{:S(2)}) collective-permute-start(bf16[400,128]{1,0:T(8,128)(2,1)S(1)} %get-tuple-element.54), channel_id=1, source_target_pairs={{0,32},{32,0},{64,96},{96,64},{128,160},{160,128},{192,224},{224,1... | collective-permute-start | bytes 307208 | tf_op jit(solution)/shard_map/ppermute | solution.py:26
  73.2 30.4 %all-to-all-start.2 = ((bf16[16,96,128]{2,1,0:T(8,128)(2,1)}), bf16[16,96,128]{2,1,0:T(8,128)(2,1)S(1)}, u32[]{:S(2)}, u32[]{:S(2)}) async-start(bf16[16,96,128]{2,1,0:T(8,128)(2,1)} %get-tuple-element.55), calls=%async_computation.2 | async-start | bytes 786432 | tf_op jit(solution)/shard_map/all_to_all | solution.py:17
  84.3 19.3 %collective-permute-start.7 = (bf16[208,128]{1,0:T(8,128)(2,1)S(1)}, bf16[208,128]{1,0:T(8,128)(2,1)S(1)}, u32[]{:S(2)}, u32[]{:S(2)}) collective-permute-start(bf16[208,128]{1,0:T(8,128)(2,1)S(1)} %get-tuple-element.57), channel_id=1, source_target_pairs={{0,64},{32,96},{64,0},{96,32},{128,192},{160,224},{192,128},{224,1... | collective-permute-start | bytes 159752 | tf_op jit(solution)/shard_map/ppermute | solution.py:26
  104.5 1.4 copy-start.4
  105.8 31.8 %all-to-all-start.3 = ((bf16[8,1088,128]{2,1,0:T(8,128)(2,1)}), bf16[8,1088,128]{2,1,0:T(8,128)(2,1)S(1)}, u32[]{:S(2)}, u32[]{:S(2)}) async-start(bf16[8,1088,128]{2,1,0:T(8,128)(2,1)} %copy-done.4), calls=%async_computation.3 | async-start | bytes 4456448 | tf_op jit(solution)/shard_map/all_to_all | solution.py:17
  113.1 8.5 %collective-permute-start.8 = (bf16[112,128]{1,0:T(8,128)(2,1)S(1)}, bf16[112,128]{1,0:T(8,128)(2,1)S(1)}, u32[]{:S(2)}, u32[]{:S(2)}) collective-permute-start(bf16[112,128]{1,0:T(8,128)(2,1)S(1)} %get-tuple-element.60), channel_id=1, source_target_pairs={{0,128},{32,160},{64,192},{96,224},{128,0},{160,32},{192,64},{224,... | collective-permute-start | bytes 86024 | tf_op jit(solution)/shard_map/ppermute | solution.py:26
  122.2 14.2 %collective-permute-start.9 = (bf16[64,128]{1,0:T(8,128)(2,1)S(1)}, bf16[64,128]{1,0:T(8,128)(2,1)S(1)}, u32[]{:S(2)}, u32[]{:S(2)}) collective-permute-start(bf16[64,128]{1,0:T(8,128)(2,1)S(1)} %get-tuple-element.63), channel_id=1, source_target_pairs={{0,256},{32,288},{64,320},{96,352},{128,384},{160,416},{192,448},{... | collective-permute-start | bytes 49160 | tf_op jit(solution)/shard_map/ppermute | solution.py:26
  137.6 13.8 %collective-permute-start.10 = (bf16[8,1088,128]{2,1,0:T(8,128)(2,1)S(1)}, bf16[8,1088,128]{2,1,0:T(8,128)(2,1)S(1)}, u32[]{:S(2)}, u32[]{:S(2)}) collective-permute-start(bf16[8,1088,128]{2,1,0:T(8,128)(2,1)S(1)} %shard_map.142.own.own_grad), channel_id=1, source_target_pairs={{0,8},{8,0},{1,9},{9,1},{2,10},{10,2},{3,11},{11,3},{4,12},{12,4},... | collective-permute-start | bytes 6684680 | tf_op jit(solution)/shard_map/ppermute | solution.py:21
  166.0 16.3 %copy-start.1 = (bf16[512,2,1024]{2,1,0:T(2,128)(2,1)S(1)}, bf16[512,2,1024]{2,1,0:T(2,128)(2,1)}, u32[]{:S(2)}) copy-start(bf16[512,2,1024]{2,1,0:T(2,128)(2,1)} %cot.5) | copy-start | bytes 6291460
  166.0 16.3 %copy-start.7 = (bf16[128,2,1024]{2,1,0:T(2,128)(2,1)S(1)}, bf16[128,2,1024]{2,1,0:T(2,128)(2,1)}, u32[]{:S(2)}) copy-start(bf16[128,2,1024]{2,1,0:T(2,128)(2,1)} %weight.1) | copy-start | bytes 1572868
  167.4 17.2 %copy-start.10 = (s32[64]{0:T(128)S(1)}, s32[64]{0:T(128)}, u32[]{:S(2)}) copy-start(s32[64]{0:T(128)} %groups.1) | copy-start | bytes 772
  177.7 6.9 %collective-permute-start.11 = (bf16[2,8,64,128]{3,2,1,0:T(8,128)(2,1)S(1)}, bf16[2,8,64,128]{3,2,1,0:T(8,128)(2,1)S(1)}, u32[]{:S(2)}, u32[]{:S(2)}) collective-permute-start(bf16[2,8,64,128]{3,2,1,0:T(8,128)(2,1)S(1)} %bitcast.3), channel_id=1, source_target_pairs={{0,8},{8,0},{1,9},{9,1},{2,10},{10,2},{3,11},{11,3},{4,12},{12,4},... | collective-permute-start | bytes 786440 | tf_op jit(solution)/shard_map/ppermute | solution.py:21
  (3 other events, 3.0 us)

commit v14 on v13

--- a/solution.py
+++ b/solution.py
@@ -55,10 +55,15 @@
 
 
 def follow(array, after, limit):
+    block = (1,) * (after.ndim - 2) + (16, after.shape[-1])
     return pl.pallas_call(
         lambda *refs: None,
+        grid=(1,),
         out_shape=jax.ShapeDtypeStruct(array.shape, array.dtype),
-        in_specs=[pl.BlockSpec(memory_space=pl.ANY)] * 2,
+        in_specs=[
+            pl.BlockSpec(memory_space=pl.ANY),
+            pl.BlockSpec(block, lambda i: (0,) * after.ndim),
+        ],
         out_specs=pl.BlockSpec(memory_space=pl.ANY),
         input_output_aliases={0: 0},
         compiler_params=pltpu.CompilerParams(vmem_limit_bytes=limit * 1024 * 1024),
@@ -287,7 +292,7 @@
     group = factor_a.shape[0]
     total, chosen[...] = join(bit, owners, keep, got, vals)
     for j in range(2):
-        factor_g[j] = total[0, j * group : (j + 1) * group]
+        factor_g[:, j] = total[0, j * group : (j + 1) * group]
     factor_a[...] = total[0, 2 * group :]
 
 
@@ -429,6 +434,7 @@
         [cot, act, whole_act],
         scratch=[flat, pltpu.VMEM((blocks + 1, full, slab), f32)],
         flops=6 * tok * full * slab,
+        limit=56,
     )
     f_got = swap(sent, "c")
     shape = (nz, height, slab)
@@ -468,7 +474,7 @@
     f_got = across(f_sent, "z", 8)
     factor_a, factor_g, vals = call(
         functools.partial(factor_out, nz // 2),
-        [out((group, slab), f32), out((blocks, group, slab), f32), chosen],
+        [out((group, slab), f32), out((group, blocks, slab), f32), chosen],
         [owners],
         [f_keep, f_got, vals],
     )
@@ -512,7 +518,7 @@
     (grad_input,) = call(
         input_grad, [out((tok, slab))], [], [cot, weight], flops=4 * tok * full * slab
     )
-    return grad_input, factor_a, factor_g.transpose(1, 0, 2), pre, worker
+    return grad_input, factor_a, factor_g, pre, worker
 
 
 def solution(mesh):

time: 188 us -> 191 us (1.016)
  Pallas kernels: 19.2 us -> 22.8 us
    pallas_call x16, Pallas kernels: 19.2 us -> 22.1 us  [call(): pl.pallas_call(body, grid=(1,), out_shape=outs, in_specs=[pl.BlockSpec(me...]
    unnamed x23 -> x20, local copies, waits for them, and re-layouts: 4.97 us -> 3.29 us
  transfers between devices with their start and end apart: 16 -> 16, of which waited for: 8 -> 8; matrix products, arithmetic and copies ran while one was open for 0% -> 0% of each run, Pallas kernels for 4% -> 6%
where the time goes in v14:
time: 191 us; the launch traced here: 190 us
  starting transfers between devices  100 us (52%)
  waiting for transfers between devices  38 us (20%)
  blocking collectives  24.1 us (13%)
  Pallas kernels  22.8 us (12%)
  local copies, waits for them, and re-layouts  3.29 us (2%)
    all_to_all x4, starting transfers between devices, exchange(): return lax.all_to_all(array, axis, 0, 0, tiled=True)  39.6 us
    ppermute x8, starting transfers between devices, swap(): return lax.ppermute(array, axis, [(0, 1), (1, 0)])  33.9 us
    ppermute x4, starting transfers between devices, across(): return lax.ppermute(array, axis, pairs)  26.9 us
    all_to_all x2, blocking collectives, exchange(): return lax.all_to_all(array, axis, 0, 0, tiled=True)  24.1 us
    pallas_call x16, Pallas kernels, call(): pl.pallas_call(body, grid=(1,), out_shape=outs, in_specs=[pl.BlockSpec(me...  22.1 us
    ppermute x4, waiting for transfers between devices, across(): return lax.ppermute(array, axis, pairs)  20.7 us
    ppermute x8, waiting for transfers between devices, swap(): return lax.ppermute(array, axis, [(0, 1), (1, 0)])  17.2 us
  transfers between devices with their start and end apart: 16, of which 8 were waited for; matrix products, arithmetic and copies ran while one was open for 0% of the time, Pallas kernels for 6%

profile of v14, /device:TPU:1, one launch (start us, length us, event | category | flops | bytes accessed | tf_op | source)
XLA Modules:
  0.0 189.6 jit_solution(51875576427333662)
XLA Ops:
  0.7 3.6 %shard_map.131 = (bf16[1552,128]{1,0:T(8,128)(2,1)}, bf16[1552,128]{1,0:T(8,128)(2,1)}, bf16[8,512,128]{2,1,0:T(8,128)(2,1)}) custom-call(bf16[1,1024,128]{2,1,0:T(8,128)(2,1)} %ba.1, bf16[1,2,1024,128]{3,2,1,0:T(8,128)(2,1)} %bg.1, bf16[1,128]{1,0:T(2,128)(2,1)} %va.1, bf16[1,2,128]{2,1,0:T(2,128)(2,1)} %vg.1, bf16[512,128]{1,0:T(8,128)(2,1)} %act.5), custom_call_target="tpu_custom_call" | custom-call | bytes 2761472 | tf_op jit(solution)/shard_map/pallas_call | solution.py:45
  4.3 7.6 %all-to-all-start = ((bf16[8,512,128]{2,1,0:T(8,128)(2,1)}), bf16[8,512,128]{2,1,0:T(8,128)(2,1)}, u32[]{:S(2)}, u32[]{:S(2)}) async-start(bf16[8,512,128]{2,1,0:T(8,128)(2,1)} %get-tuple-element.47), calls=%async_computation | async-start | bytes 2097152 | tf_op jit(solution)/shard_map/all_to_all | solution.py:17
  11.9 5.5 %collective-permute-start.2 = (bf16[1552,128]{1,0:T(8,128)(2,1)}, bf16[1552,128]{1,0:T(8,128)(2,1)S(1)}, u32[]{:S(2)}, u32[]{:S(2)}) collective-permute-start(bf16[1552,128]{1,0:T(8,128)(2,1)} %get-tuple-element.43), channel_id=1, source_target_pairs={{0,8},{8,0},{1,9},{9,1},{2,10},{10,2},{3,11},{11,3},{4,12},{12,4},... | collective-permute-start | bytes 1191944 | tf_op jit(solution)/shard_map/ppermute | solution.py:21
  23.9 3.4 %collective-permute-start.1 = (bf16[512,128]{1,0:T(8,128)(2,1)S(1)}, bf16[512,128]{1,0:T(8,128)(2,1)S(1)}, u32[]{:S(2)}, u32[]{:S(2)}) collective-permute-start(bf16[512,128]{1,0:T(8,128)(2,1)S(1)} %get-tuple-element.41), channel_id=1, source_target_pairs={{0,16},{16,0},{1,17},{17,1},{2,18},{18,2},{3,19},{19,3},{4,20},{20... | collective-permute-start | bytes 393224 | tf_op jit(solution)/shard_map/ppermute | solution.py:21
  27.3 6.8 %collective-permute-done.1.got = bf16[512,128]{1,0:T(8,128)(2,1)S(1)} collective-permute-done((bf16[512,128]{1,0:T(8,128)(2,1)S(1)}, bf16[512,128]{1,0:T(8,128)(2,1)S(1)}, u32[]{:S(2)}, u32[]{:S(2)}) %collective-permute-start.1) | collective-permute-done | bytes 131104 | tf_op jit(solution)/shard_map/ppermute | solution.py:21
  36.1 13.2 %all-to-all-start.1 = ((bf16[16,96,128]{2,1,0:T(8,128)(2,1)}), bf16[16,96,128]{2,1,0:T(8,128)(2,1)S(1)}, u32[]{:S(2)}, u32[]{:S(2)}) async-start(bf16[16,96,128]{2,1,0:T(8,128)(2,1)} %shard_map.134), calls=%async_computation.1 | async-start | bytes 786432 | tf_op jit(solution)/shard_map/all_to_all | solution.py:17
  49.4 4.7 %shard_map.135 = (bf16[16,2,48,128]{3,2,1,0:T(8,128)(2,1)}, f32[16,2,48,128]{3,2,1,0:T(8,128)}) custom-call(bf16[512,2,1024]{2,1,0:T(2,128)(2,1)} %cot.5, bf16[512,128]{1,0:T(8,128)(2,1)} %act.5, bf16[8,512,128]{2,1,0:T(8,128)(2,1)} %all-to-all-done.refs_1_.whole), custom_call_target="tpu_custom_call" | custom-call | flops 402653184 | bytes 4456448 | tf_op jit(solution)/shard_map/pallas_call | solution.py:45
  54.1 3.6 %collective-permute-start.4 = (bf16[16,2,48,128]{3,2,1,0:T(8,128)(2,1)}, bf16[16,2,48,128]{3,2,1,0:T(8,128)(2,1)S(1)}, u32[]{:S(2)}, u32[]{:S(2)}) collective-permute-start(bf16[16,2,48,128]{3,2,1,0:T(8,128)(2,1)} %get-tuple-element.49), channel_id=1, source_target_pairs={{0,8},{8,0},{1,9},{9,1},{2,10},{10,2},{3,11},{11,3},{4,12},{12,4},... | collective-permute-start | bytes 1179656 | tf_op jit(solution)/shard_map/ppermute | solution.py:21
  60.5 3.1 %collective-permute-start.5 = (bf16[16,48,128]{2,1,0:T(8,128)(2,1)S(1)}, bf16[16,48,128]{2,1,0:T(8,128)(2,1)S(1)}, u32[]{:S(2)}, u32[]{:S(2)}) collective-permute-start(bf16[16,48,128]{2,1,0:T(8,128)(2,1)S(1)} %get-tuple-element.51), channel_id=1, source_target_pairs={{0,16},{16,0},{1,17},{17,1},{2,18},{18,2},{3,19},{19,3},{4,20},{20... | collective-permute-start | bytes 589832 | tf_op jit(solution)/shard_map/ppermute | solution.py:21
  63.5 5.0 %collective-permute-done.5.got = bf16[16,48,128]{2,1,0:T(8,128)(2,1)S(1)} collective-permute-done((bf16[16,48,128]{2,1,0:T(8,128)(2,1)S(1)}, bf16[16,48,128]{2,1,0:T(8,128)(2,1)S(1)}, u32[]{:S(2)}, u32[]{:S(2)}) %collective-permute-start.5) | collective-permute-done | bytes 196640 | tf_op jit(solution)/shard_map/ppermute | solution.py:21
  68.5 3.6 %collective-permute-start.6 = (bf16[400,128]{1,0:T(8,128)(2,1)S(1)}, bf16[400,128]{1,0:T(8,128)(2,1)S(1)}, u32[]{:S(2)}, u32[]{:S(2)}) collective-permute-start(bf16[400,128]{1,0:T(8,128)(2,1)S(1)} %get-tuple-element.54), channel_id=1, source_target_pairs={{0,32},{32,0},{64,96},{96,64},{128,160},{160,128},{192,224},{224,1... | collective-permute-start | bytes 307208 | tf_op jit(solution)/shard_map/ppermute | solution.py:26
  75.5 11.5 %all-to-all-start.2 = ((bf16[16,96,128]{2,1,0:T(8,128)(2,1)}), bf16[16,96,128]{2,1,0:T(8,128)(2,1)S(1)}, u32[]{:S(2)}, u32[]{:S(2)}) async-start(bf16[16,96,128]{2,1,0:T(8,128)(2,1)} %get-tuple-element.55), calls=%async_computation.2 | async-start | bytes 786432 | tf_op jit(solution)/shard_map/all_to_all | solution.py:17
  87.1 4.2 %collective-permute-start.7 = (bf16[208,128]{1,0:T(8,128)(2,1)S(1)}, bf16[208,128]{1,0:T(8,128)(2,1)S(1)}, u32[]{:S(2)}, u32[]{:S(2)}) collective-permute-start(bf16[208,128]{1,0:T(8,128)(2,1)S(1)} %get-tuple-element.57), channel_id=1, source_target_pairs={{0,64},{32,96},{64,0},{96,32},{128,192},{160,224},{192,128},{224,1... | collective-permute-start | bytes 159752 | tf_op jit(solution)/shard_map/ppermute | solution.py:26
  91.2 15.1 %collective-permute-done.7.f_got = bf16[208,128]{1,0:T(8,128)(2,1)S(1)} collective-permute-done((bf16[208,128]{1,0:T(8,128)(2,1)S(1)}, bf16[208,128]{1,0:T(8,128)(2,1)S(1)}, u32[]{:S(2)}, u32[]{:S(2)}) %collective-permute-start.7) | collective-permute-done | bytes 53280 | tf_op jit(solution)/shard_map/ppermute | solution.py:26
  108.6 7.2 %all-to-all-start.3 = ((bf16[8,1088,128]{2,1,0:T(8,128)(2,1)}), bf16[8,1088,128]{2,1,0:T(8,128)(2,1)S(1)}, u32[]{:S(2)}, u32[]{:S(2)}) async-start(bf16[8,1088,128]{2,1,0:T(8,128)(2,1)} %copy-done.2), calls=%async_computation.3 | async-start | bytes 4456448 | tf_op jit(solution)/shard_map/all_to_all | solution.py:17
  115.9 6.1 %collective-permute-start.8 = (bf16[112,128]{1,0:T(8,128)(2,1)S(1)}, bf16[112,128]{1,0:T(8,128)(2,1)S(1)}, u32[]{:S(2)}, u32[]{:S(2)}) collective-permute-start(bf16[112,128]{1,0:T(8,128)(2,1)S(1)} %get-tuple-element.60), channel_id=1, source_target_pairs={{0,128},{32,160},{64,192},{96,224},{128,0},{160,32},{192,64},{224,... | collective-permute-start | bytes 86024 | tf_op jit(solution)/shard_map/ppermute | solution.py:26
  122.0 2.4 %collective-permute-done.8.got = bf16[112,128]{1,0:T(8,128)(2,1)S(1)} collective-permute-done((bf16[112,128]{1,0:T(8,128)(2,1)S(1)}, bf16[112,128]{1,0:T(8,128)(2,1)S(1)}, u32[]{:S(2)}, u32[]{:S(2)}) %collective-permute-start.8) | collective-permute-done | bytes 28704 | tf_op jit(solution)/shard_map/ppermute | solution.py:26
  125.0 13.1 %collective-permute-start.9 = (bf16[64,128]{1,0:T(8,128)(2,1)S(1)}, bf16[64,128]{1,0:T(8,128)(2,1)S(1)}, u32[]{:S(2)}, u32[]{:S(2)}) collective-permute-start(bf16[64,128]{1,0:T(8,128)(2,1)S(1)} %get-tuple-element.63), channel_id=1, source_target_pairs={{0,256},{32,288},{64,320},{96,352},{128,384},{160,416},{192,448},{... | collective-permute-start | bytes 49160 | tf_op jit(solution)/shard_map/ppermute | solution.py:26
  140.5 9.8 %collective-permute-start.10 = (bf16[8,1088,128]{2,1,0:T(8,128)(2,1)S(1)}, bf16[8,1088,128]{2,1,0:T(8,128)(2,1)S(1)}, u32[]{:S(2)}, u32[]{:S(2)}) collective-permute-start(bf16[8,1088,128]{2,1,0:T(8,128)(2,1)S(1)} %shard_map.142.own.own_grad), channel_id=1, source_target_pairs={{0,8},{8,0},{1,9},{9,1},{2,10},{10,2},{3,11},{11,3},{4,12},{12,4},... | collective-permute-start | bytes 6684680 | tf_op jit(solution)/shard_map/ppermute | solution.py:21
  150.3 4.0 %collective-permute-done.10.other.other_grad = bf16[8,1088,128]{2,1,0:T(8,128)(2,1)S(1)} collective-permute-done((bf16[8,1088,128]{2,1,0:T(8,128)(2,1)S(1)}, bf16[8,1088,128]{2,1,0:T(8,128)(2,1)S(1)}, u32[]{:S(2)}, u32[]{:S(2)}) %collective-permute-start.10) | collective-permute-done | bytes 2228256 | tf_op jit(solution)/shard_map/ppermute | solution.py:21
  155.0 13.9 %all_to_all.30.rows = bf16[8,80,128]{2,1,0:T(8,128)(2,1)S(1)} all-to-all(bf16[8,80,128]{2,1,0:T(8,128)(2,1)S(1)} %shard_map.143), channel_id=1, replica_groups=mesh['z'=16,'xl'=2,'c'=2,'t'=8] {'t'}, dimensions={0} | all-to-all | bytes 327680 | tf_op jit(solution)/shard_map/all_to_all | solution.py:17
  170.3 10.2 %all_to_all.31 = bf16[16,64,128]{2,1,0:T(8,128)(2,1)S(1)} all-to-all(bf16[16,64,128]{2,1,0:T(8,128)(2,1)S(1)} %bitcast.4), channel_id=1, replica_groups=mesh['z'=16,'xl'=2,'c'=2,'t'=8] {'xl','t'}, dimensions={0} | all-to-all | bytes 524288 | tf_op jit(solution)/shard_map/all_to_all | solution.py:17
  180.5 4.7 %collective-permute-start.11 = (bf16[2,8,64,128]{3,2,1,0:T(8,128)(2,1)S(1)}, bf16[2,8,64,128]{3,2,1,0:T(8,128)(2,1)S(1)}, u32[]{:S(2)}, u32[]{:S(2)}) collective-permute-start(bf16[2,8,64,128]{3,2,1,0:T(8,128)(2,1)S(1)} %bitcast.2), channel_id=1, source_target_pairs={{0,8},{8,0},{1,9},{9,1},{2,10},{10,2},{3,11},{11,3},{4,12},{12,4},... | collective-permute-start | bytes 786440 | tf_op jit(solution)/shard_map/ppermute | solution.py:21
  186.8 2.8 %shard_map.145 = (bf16[1024,2,128]{2,1,0:T(2,128)(2,1)}, bf16[1,1024,128]{2,1,0:T(8,128)(2,1)}) custom-call(s32[64]{0:T(128)S(1)} %copy-done.9, bf16[8,1088,128]{2,1,0:T(8,128)(2,1)S(1)} %shard_map.142.own.own_grad, bf16[8,1088,128]{2,1,0:T(8,128)(2,1)S(1)} %collective-permute-done.10.other.other_grad, bf16[2,8,64,128]{3,2,1,0:T(8,128)(2,1)S(1)} %bitcast.3, ...), custom_call_target="tpu_custom_call" | custom-call | flops 536870912 | bytes 5767168 | tf_op jit(solution)/shard_map/pallas_call | solution.py:45
  (48 shorter events, 23.5 us)
Async XLA Ops:
  0.6 16.8 %copy-start.4 = (bf16[512,128]{1,0:T(8,128)(2,1)S(1)}, bf16[512,128]{1,0:T(8,128)(2,1)}, u32[]{:S(2)}) copy-start(bf16[512,128]{1,0:T(8,128)(2,1)} %act.5) | copy-start | bytes 393220
  0.6 16.8 %copy-start = (bf16[512,2,1024]{2,1,0:T(2,128)(2,1)S(1)}, bf16[512,2,1024]{2,1,0:T(2,128)(2,1)}, u32[]{:S(2)}) copy-start(bf16[512,2,1024]{2,1,0:T(2,128)(2,1)} %cot.5) | copy-start | bytes 6291460
  4.3 17.0 %copy-start.7 = (bf16[1552,128]{1,0:T(8,128)(2,1)S(1)}, bf16[1552,128]{1,0:T(8,128)(2,1)}, u32[]{:S(2)}) copy-start(bf16[1552,128]{1,0:T(8,128)(2,1)} %get-tuple-element.42.own) | copy-start | bytes 1191940
  4.3 17.0 %copy-start.8 = (s32[3]{0:T(128)S(1)}, s32[3]{0:T(128)}, u32[]{:S(2)}) copy-start(s32[3]{0:T(128)} %owners.11) | copy-start | bytes 40
  4.3 31.2 %all-to-all-start = ((bf16[8,512,128]{2,1,0:T(8,128)(2,1)}), bf16[8,512,128]{2,1,0:T(8,128)(2,1)}, u32[]{:S(2)}, u32[]{:S(2)}) async-start(bf16[8,512,128]{2,1,0:T(8,128)(2,1)} %get-tuple-element.47), calls=%async_computation | async-start | bytes 2097152 | tf_op jit(solution)/shard_map/all_to_all | solution.py:17
  11.9 9.3 %collective-permute-start.2 = (bf16[1552,128]{1,0:T(8,128)(2,1)}, bf16[1552,128]{1,0:T(8,128)(2,1)S(1)}, u32[]{:S(2)}, u32[]{:S(2)}) collective-permute-start(bf16[1552,128]{1,0:T(8,128)(2,1)} %get-tuple-element.43), channel_id=1, source_target_pairs={{0,8},{8,0},{1,9},{9,1},{2,10},{10,2},{3,11},{11,3},{4,12},{12,4},... | collective-permute-start | bytes 1191944 | tf_op jit(solution)/shard_map/ppermute | solution.py:21
  19.3 4.6 %collective-permute-start = (bf16[2,512,128]{2,1,0:T(8,128)(2,1)S(1)}, bf16[2,512,128]{2,1,0:T(8,128)(2,1)S(1)}, u32[]{:S(2)}, u32[]{:S(2)}) collective-permute-start(bf16[2,512,128]{2,1,0:T(8,128)(2,1)S(1)} %get-tuple-element.39), channel_id=1, source_target_pairs={{0,8},{8,0},{1,9},{9,1},{2,10},{10,2},{3,11},{11,3},{4,12},{12,4},... | collective-permute-start | bytes 786440 | tf_op jit(solution)/shard_map/ppermute | solution.py:21
  21.9 12.2 %collective-permute-start.3 = (bf16[1040,128]{1,0:T(8,128)(2,1)S(1)}, bf16[1040,128]{1,0:T(8,128)(2,1)S(1)}, u32[]{:S(2)}, u32[]{:S(2)}) collective-permute-start(bf16[1040,128]{1,0:T(8,128)(2,1)S(1)} %get-tuple-element.45), channel_id=1, source_target_pairs={{0,16},{16,0},{1,17},{17,1},{2,18},{18,2},{3,19},{19,3},{4,20},{20... | collective-permute-start | bytes 798728 | tf_op jit(solution)/shard_map/ppermute | solution.py:21
  23.9 10.2 %collective-permute-start.1 = (bf16[512,128]{1,0:T(8,128)(2,1)S(1)}, bf16[512,128]{1,0:T(8,128)(2,1)S(1)}, u32[]{:S(2)}, u32[]{:S(2)}) collective-permute-start(bf16[512,128]{1,0:T(8,128)(2,1)S(1)} %get-tuple-element.41), channel_id=1, source_target_pairs={{0,16},{16,0},{1,17},{17,1},{2,18},{18,2},{3,19},{19,3},{4,20},{20... | collective-permute-start | bytes 393224 | tf_op jit(solution)/shard_map/ppermute | solution.py:21
  36.1 38.0 %all-to-all-start.1 = ((bf16[16,96,128]{2,1,0:T(8,128)(2,1)}), bf16[16,96,128]{2,1,0:T(8,128)(2,1)S(1)}, u32[]{:S(2)}, u32[]{:S(2)}) async-start(bf16[16,96,128]{2,1,0:T(8,128)(2,1)} %shard_map.134), calls=%async_computation.1 | async-start | bytes 786432 | tf_op jit(solution)/shard_map/all_to_all | solution.py:17
  54.1 5.1 %collective-permute-start.4 = (bf16[16,2,48,128]{3,2,1,0:T(8,128)(2,1)}, bf16[16,2,48,128]{3,2,1,0:T(8,128)(2,1)S(1)}, u32[]{:S(2)}, u32[]{:S(2)}) collective-permute-start(bf16[16,2,48,128]{3,2,1,0:T(8,128)(2,1)} %get-tuple-element.49), channel_id=1, source_target_pairs={{0,8},{8,0},{1,9},{9,1},{2,10},{10,2},{3,11},{11,3},{4,12},{12,4},... | collective-permute-start | bytes 1179656 | tf_op jit(solution)/shard_map/ppermute | solution.py:21
  60.5 8.0 %collective-permute-start.5 = (bf16[16,48,128]{2,1,0:T(8,128)(2,1)S(1)}, bf16[16,48,128]{2,1,0:T(8,128)(2,1)S(1)}, u32[]{:S(2)}, u32[]{:S(2)}) collective-permute-start(bf16[16,48,128]{2,1,0:T(8,128)(2,1)S(1)} %get-tuple-element.51), channel_id=1, source_target_pairs={{0,16},{16,0},{1,17},{17,1},{2,18},{18,2},{3,19},{19,3},{4,20},{20... | collective-permute-start | bytes 589832 | tf_op jit(solution)/shard_map/ppermute | solution.py:21
  68.5 5.6 %collective-permute-start.6 = (bf16[400,128]{1,0:T(8,128)(2,1)S(1)}, bf16[400,128]{1,0:T(8,128)(2,1)S(1)}, u32[]{:S(2)}, u32[]{:S(2)}) collective-permute-start(bf16[400,128]{1,0:T(8,128)(2,1)S(1)} %get-tuple-element.54), channel_id=1, source_target_pairs={{0,32},{32,0},{64,96},{96,64},{128,160},{160,128},{192,224},{224,1... | collective-permute-start | bytes 307208 | tf_op jit(solution)/shard_map/ppermute | solution.py:26
  75.5 30.9 %all-to-all-start.2 = ((bf16[16,96,128]{2,1,0:T(8,128)(2,1)}), bf16[16,96,128]{2,1,0:T(8,128)(2,1)S(1)}, u32[]{:S(2)}, u32[]{:S(2)}) async-start(bf16[16,96,128]{2,1,0:T(8,128)(2,1)} %get-tuple-element.55), calls=%async_computation.2 | async-start | bytes 786432 | tf_op jit(solution)/shard_map/all_to_all | solution.py:17
  87.1 19.3 %collective-permute-start.7 = (bf16[208,128]{1,0:T(8,128)(2,1)S(1)}, bf16[208,128]{1,0:T(8,128)(2,1)S(1)}, u32[]{:S(2)}, u32[]{:S(2)}) collective-permute-start(bf16[208,128]{1,0:T(8,128)(2,1)S(1)} %get-tuple-element.57), channel_id=1, source_target_pairs={{0,64},{32,96},{64,0},{96,32},{128,192},{160,224},{192,128},{224,1... | collective-permute-start | bytes 159752 | tf_op jit(solution)/shard_map/ppermute | solution.py:26
  107.3 1.4 copy-start.2
  108.6 31.8 %all-to-all-start.3 = ((bf16[8,1088,128]{2,1,0:T(8,128)(2,1)}), bf16[8,1088,128]{2,1,0:T(8,128)(2,1)S(1)}, u32[]{:S(2)}, u32[]{:S(2)}) async-start(bf16[8,1088,128]{2,1,0:T(8,128)(2,1)} %copy-done.2), calls=%async_computation.3 | async-start | bytes 4456448 | tf_op jit(solution)/shard_map/all_to_all | solution.py:17
  115.9 8.5 %collective-permute-start.8 = (bf16[112,128]{1,0:T(8,128)(2,1)S(1)}, bf16[112,128]{1,0:T(8,128)(2,1)S(1)}, u32[]{:S(2)}, u32[]{:S(2)}) collective-permute-start(bf16[112,128]{1,0:T(8,128)(2,1)S(1)} %get-tuple-element.60), channel_id=1, source_target_pairs={{0,128},{32,160},{64,192},{96,224},{128,0},{160,32},{192,64},{224,... | collective-permute-start | bytes 86024 | tf_op jit(solution)/shard_map/ppermute | solution.py:26
  125.0 14.2 %collective-permute-start.9 = (bf16[64,128]{1,0:T(8,128)(2,1)S(1)}, bf16[64,128]{1,0:T(8,128)(2,1)S(1)}, u32[]{:S(2)}, u32[]{:S(2)}) collective-permute-start(bf16[64,128]{1,0:T(8,128)(2,1)S(1)} %get-tuple-element.63), channel_id=1, source_target_pairs={{0,256},{32,288},{64,320},{96,352},{128,384},{160,416},{192,448},{... | collective-permute-start | bytes 49160 | tf_op jit(solution)/shard_map/ppermute | solution.py:26
  140.5 13.8 %collective-permute-start.10 = (bf16[8,1088,128]{2,1,0:T(8,128)(2,1)S(1)}, bf16[8,1088,128]{2,1,0:T(8,128)(2,1)S(1)}, u32[]{:S(2)}, u32[]{:S(2)}) collective-permute-start(bf16[8,1088,128]{2,1,0:T(8,128)(2,1)S(1)} %shard_map.142.own.own_grad), channel_id=1, source_target_pairs={{0,8},{8,0},{1,9},{9,1},{2,10},{10,2},{3,11},{11,3},{4,12},{12,4},... | collective-permute-start | bytes 6684680 | tf_op jit(solution)/shard_map/ppermute | solution.py:21
  168.9 16.3 %copy-start.1 = (bf16[512,2,1024]{2,1,0:T(2,128)(2,1)S(1)}, bf16[512,2,1024]{2,1,0:T(2,128)(2,1)}, u32[]{:S(2)}) copy-start(bf16[512,2,1024]{2,1,0:T(2,128)(2,1)} %cot.5) | copy-start | bytes 6291460
  168.9 16.3 %copy-start.6 = (bf16[128,2,1024]{2,1,0:T(2,128)(2,1)S(1)}, bf16[128,2,1024]{2,1,0:T(2,128)(2,1)}, u32[]{:S(2)}) copy-start(bf16[128,2,1024]{2,1,0:T(2,128)(2,1)} %weight.1) | copy-start | bytes 1572868
  170.3 16.5 %copy-start.9 = (s32[64]{0:T(128)S(1)}, s32[64]{0:T(128)}, u32[]{:S(2)}) copy-start(s32[64]{0:T(128)} %groups.1) | copy-start | bytes 772
  180.5 6.3 %collective-permute-start.11 = (bf16[2,8,64,128]{3,2,1,0:T(8,128)(2,1)S(1)}, bf16[2,8,64,128]{3,2,1,0:T(8,128)(2,1)S(1)}, u32[]{:S(2)}, u32[]{:S(2)}) collective-permute-start(bf16[2,8,64,128]{3,2,1,0:T(8,128)(2,1)S(1)} %bitcast.2), channel_id=1, source_target_pairs={{0,8},{8,0},{1,9},{9,1},{2,10},{10,2},{3,11},{11,3},{4,12},{12,4},... | collective-permute-start | bytes 786440 | tf_op jit(solution)/shard_map/ppermute | solution.py:21
  (2 other events, 1.9 us)

commit v15 on v13

--- a/solution.py
+++ b/solution.py
@@ -287,7 +287,7 @@
     group = factor_a.shape[0]
     total, chosen[...] = join(bit, owners, keep, got, vals)
     for j in range(2):
-        factor_g[j] = total[0, j * group : (j + 1) * group]
+        factor_g[:, j] = total[0, j * group : (j + 1) * group]
     factor_a[...] = total[0, 2 * group :]
 
 
@@ -418,7 +418,7 @@
         [owners],
         [keep, got, base, base_got],
     )
-    got = exchange(follow(sent, whole_act, 56), "z")
+    got = exchange(sent, "z")
 
     height = (blocks + 1) * group
     shape = (nz, 2, height, slab)
@@ -468,7 +468,7 @@
     f_got = across(f_sent, "z", 8)
     factor_a, factor_g, vals = call(
         functools.partial(factor_out, nz // 2),
-        [out((group, slab), f32), out((blocks, group, slab), f32), chosen],
+        [out((group, slab), f32), out((group, blocks, slab), f32), chosen],
         [owners],
         [f_keep, f_got, vals],
     )
@@ -512,7 +512,7 @@
     (grad_input,) = call(
         input_grad, [out((tok, slab))], [], [cot, weight], flops=4 * tok * full * slab
     )
-    return grad_input, factor_a, factor_g.transpose(1, 0, 2), pre, worker
+    return grad_input, factor_a, factor_g, pre, worker
 
 
 def solution(mesh):

time: 188 us -> 186 us (0.989)
  local copies, waits for them, and re-layouts: 4.97 us -> 3.05 us
    unnamed x23 -> x20, local copies, waits for them, and re-layouts: 4.97 us -> 3.05 us
  transfers between devices with their start and end apart: 16 -> 16, of which waited for: 8 -> 8; matrix products, arithmetic and copies ran while one was open for 0% -> 0% of each run, Pallas kernels for 4% -> 5%
where the time goes in v15:
time: 186 us
  starting transfers between devices  99.7 us (54%)
  waiting for transfers between devices  38.4 us (21%)
  blocking collectives  24.1 us (13%)
  Pallas kernels  19.2 us (10%)
  local copies, waits for them, and re-layouts  3.05 us (2%)
    all_to_all x4, starting transfers between devices, exchange(): return lax.all_to_all(array, axis, 0, 0, tiled=True)  39.5 us
    ppermute x8, starting transfers between devices, swap(): return lax.ppermute(array, axis, [(0, 1), (1, 0)])  33.2 us
    ppermute x4, starting transfers between devices, across(): return lax.ppermute(array, axis, pairs)  26.9 us
    all_to_all x2, blocking collectives, exchange(): return lax.all_to_all(array, axis, 0, 0, tiled=True)  24.1 us
    ppermute x4, waiting for transfers between devices, across(): return lax.ppermute(array, axis, pairs)  21.4 us
    pallas_call x16, Pallas kernels, call(): pl.pallas_call(body, grid=(1,), out_shape=outs, in_specs=[pl.BlockSpec(me...  19.2 us
    ppermute x8, waiting for transfers between devices, swap(): return lax.ppermute(array, axis, [(0, 1), (1, 0)])  17 us
  transfers between devices with their start and end apart: 16, of which 8 were waited for; matrix products, arithmetic and copies ran while one was open for 0% of the time, Pallas kernels for 5%

profile of v15, /device:TPU:1, one launch (start us, length us, event | category | flops | bytes accessed | tf_op | source)
XLA Modules:
  0.0 185.5 jit_solution(5453825518592454732)
XLA Ops:
  0.7 3.6 %shard_map.131 = (bf16[1552,128]{1,0:T(8,128)(2,1)}, bf16[1552,128]{1,0:T(8,128)(2,1)}, bf16[8,512,128]{2,1,0:T(8,128)(2,1)}) custom-call(bf16[1,1024,128]{2,1,0:T(8,128)(2,1)} %ba.1, bf16[1,2,1024,128]{3,2,1,0:T(8,128)(2,1)} %bg.1, bf16[1,128]{1,0:T(2,128)(2,1)} %va.1, bf16[1,2,128]{2,1,0:T(2,128)(2,1)} %vg.1, bf16[512,128]{1,0:T(8,128)(2,1)} %act.5), custom_call_target="tpu_custom_call" | custom-call | bytes 2761472 | tf_op jit(solution)/shard_map/pallas_call | solution.py:45
  4.3 7.5 %all-to-all-start.1 = ((bf16[8,512,128]{2,1,0:T(8,128)(2,1)}), bf16[8,512,128]{2,1,0:T(8,128)(2,1)S(1)}, u32[]{:S(2)}, u32[]{:S(2)}) async-start(bf16[8,512,128]{2,1,0:T(8,128)(2,1)} %get-tuple-element.47), calls=%async_computation.1 | async-start | bytes 2097152 | tf_op jit(solution)/shard_map/all_to_all | solution.py:17
  11.8 5.0 %collective-permute-start.2 = (bf16[1552,128]{1,0:T(8,128)(2,1)}, bf16[1552,128]{1,0:T(8,128)(2,1)S(1)}, u32[]{:S(2)}, u32[]{:S(2)}) collective-permute-start(bf16[1552,128]{1,0:T(8,128)(2,1)} %get-tuple-element.43), channel_id=1, source_target_pairs={{0,8},{8,0},{1,9},{9,1},{2,10},{10,2},{3,11},{11,3},{4,12},{12,4},... | collective-permute-start | bytes 1191944 | tf_op jit(solution)/shard_map/ppermute | solution.py:21
  23.3 3.4 %collective-permute-start.1 = (bf16[512,128]{1,0:T(8,128)(2,1)S(1)}, bf16[512,128]{1,0:T(8,128)(2,1)S(1)}, u32[]{:S(2)}, u32[]{:S(2)}) collective-permute-start(bf16[512,128]{1,0:T(8,128)(2,1)S(1)} %get-tuple-element.41), channel_id=1, source_target_pairs={{0,16},{16,0},{1,17},{17,1},{2,18},{18,2},{3,19},{19,3},{4,20},{20... | collective-permute-start | bytes 393224 | tf_op jit(solution)/shard_map/ppermute | solution.py:21
  26.6 6.8 %collective-permute-done.1.got = bf16[512,128]{1,0:T(8,128)(2,1)S(1)} collective-permute-done((bf16[512,128]{1,0:T(8,128)(2,1)S(1)}, bf16[512,128]{1,0:T(8,128)(2,1)S(1)}, u32[]{:S(2)}, u32[]{:S(2)}) %collective-permute-start.1) | collective-permute-done | bytes 131104 | tf_op jit(solution)/shard_map/ppermute | solution.py:21
  34.8 13.9 %all-to-all-start = ((bf16[16,96,128]{2,1,0:T(8,128)(2,1)}), bf16[16,96,128]{2,1,0:T(8,128)(2,1)S(1)}, u32[]{:S(2)}, u32[]{:S(2)}) async-start(bf16[16,96,128]{2,1,0:T(8,128)(2,1)} %copy-done.7), calls=%async_computation | async-start | bytes 786432 | tf_op jit(solution)/shard_map/all_to_all | solution.py:17
  51.4 3.5 %collective-permute-start.4 = (bf16[16,2,48,128]{3,2,1,0:T(8,128)(2,1)S(1)}, bf16[16,2,48,128]{3,2,1,0:T(8,128)(2,1)S(1)}, u32[]{:S(2)}, u32[]{:S(2)}) collective-permute-start(bf16[16,2,48,128]{3,2,1,0:T(8,128)(2,1)S(1)} %get-tuple-element.49), channel_id=1, source_target_pairs={{0,8},{8,0},{1,9},{9,1},{2,10},{10,2},{3,11},{11,3},{4,12},{12,4},... | collective-permute-start | bytes 1179656 | tf_op jit(solution)/shard_map/ppermute | solution.py:21
  56.3 3.1 %collective-permute-start.5 = (bf16[16,48,128]{2,1,0:T(8,128)(2,1)S(1)}, bf16[16,48,128]{2,1,0:T(8,128)(2,1)S(1)}, u32[]{:S(2)}, u32[]{:S(2)}) collective-permute-start(bf16[16,48,128]{2,1,0:T(8,128)(2,1)S(1)} %get-tuple-element.51), channel_id=1, source_target_pairs={{0,16},{16,0},{1,17},{17,1},{2,18},{18,2},{3,19},{19,3},{4,20},{20... | collective-permute-start | bytes 589832 | tf_op jit(solution)/shard_map/ppermute | solution.py:21
  59.4 5.0 %collective-permute-done.5.got = bf16[16,48,128]{2,1,0:T(8,128)(2,1)S(1)} collective-permute-done((bf16[16,48,128]{2,1,0:T(8,128)(2,1)S(1)}, bf16[16,48,128]{2,1,0:T(8,128)(2,1)S(1)}, u32[]{:S(2)}, u32[]{:S(2)}) %collective-permute-start.5) | collective-permute-done | bytes 196640 | tf_op jit(solution)/shard_map/ppermute | solution.py:21
  64.4 3.6 %collective-permute-start.6 = (bf16[400,128]{1,0:T(8,128)(2,1)S(1)}, bf16[400,128]{1,0:T(8,128)(2,1)S(1)}, u32[]{:S(2)}, u32[]{:S(2)}) collective-permute-start(bf16[400,128]{1,0:T(8,128)(2,1)S(1)} %get-tuple-element.54), channel_id=1, source_target_pairs={{0,32},{32,0},{64,96},{96,64},{128,160},{160,128},{192,224},{224,1... | collective-permute-start | bytes 307208 | tf_op jit(solution)/shard_map/ppermute | solution.py:26
  68.0 2.7 %collective-permute-done.6.f_got = bf16[400,128]{1,0:T(8,128)(2,1)S(1)} collective-permute-done((bf16[400,128]{1,0:T(8,128)(2,1)S(1)}, bf16[400,128]{1,0:T(8,128)(2,1)S(1)}, u32[]{:S(2)}, u32[]{:S(2)}) %collective-permute-start.6) | collective-permute-done | bytes 102432 | tf_op jit(solution)/shard_map/ppermute | solution.py:26
  72.1 10.9 %all-to-all-start.2 = ((bf16[16,96,128]{2,1,0:T(8,128)(2,1)}), bf16[16,96,128]{2,1,0:T(8,128)(2,1)S(1)}, u32[]{:S(2)}, u32[]{:S(2)}) async-start(bf16[16,96,128]{2,1,0:T(8,128)(2,1)} %get-tuple-element.55), calls=%async_computation.2 | async-start | bytes 786432 | tf_op jit(solution)/shard_map/all_to_all | solution.py:17
  82.9 4.2 %collective-permute-start.7 = (bf16[208,128]{1,0:T(8,128)(2,1)S(1)}, bf16[208,128]{1,0:T(8,128)(2,1)S(1)}, u32[]{:S(2)}, u32[]{:S(2)}) collective-permute-start(bf16[208,128]{1,0:T(8,128)(2,1)S(1)} %get-tuple-element.57), channel_id=1, source_target_pairs={{0,64},{32,96},{64,0},{96,32},{128,192},{160,224},{192,128},{224,1... | collective-permute-start | bytes 159752 | tf_op jit(solution)/shard_map/ppermute | solution.py:26
  87.1 15.1 %collective-permute-done.7.f_got = bf16[208,128]{1,0:T(8,128)(2,1)S(1)} collective-permute-done((bf16[208,128]{1,0:T(8,128)(2,1)S(1)}, bf16[208,128]{1,0:T(8,128)(2,1)S(1)}, u32[]{:S(2)}, u32[]{:S(2)}) %collective-permute-start.7) | collective-permute-done | bytes 53280 | tf_op jit(solution)/shard_map/ppermute | solution.py:26
  104.5 7.2 %all-to-all-start.3 = ((bf16[8,1088,128]{2,1,0:T(8,128)(2,1)}), bf16[8,1088,128]{2,1,0:T(8,128)(2,1)S(1)}, u32[]{:S(2)}, u32[]{:S(2)}) async-start(bf16[8,1088,128]{2,1,0:T(8,128)(2,1)} %copy-done.2), calls=%async_computation.3 | async-start | bytes 4456448 | tf_op jit(solution)/shard_map/all_to_all | solution.py:17
  111.8 6.1 %collective-permute-start.8 = (bf16[112,128]{1,0:T(8,128)(2,1)S(1)}, bf16[112,128]{1,0:T(8,128)(2,1)S(1)}, u32[]{:S(2)}, u32[]{:S(2)}) collective-permute-start(bf16[112,128]{1,0:T(8,128)(2,1)S(1)} %get-tuple-element.60), channel_id=1, source_target_pairs={{0,128},{32,160},{64,192},{96,224},{128,0},{160,32},{192,64},{224,... | collective-permute-start | bytes 86024 | tf_op jit(solution)/shard_map/ppermute | solution.py:26
  117.9 2.4 %collective-permute-done.8.got = bf16[112,128]{1,0:T(8,128)(2,1)S(1)} collective-permute-done((bf16[112,128]{1,0:T(8,128)(2,1)S(1)}, bf16[112,128]{1,0:T(8,128)(2,1)S(1)}, u32[]{:S(2)}, u32[]{:S(2)}) %collective-permute-start.8) | collective-permute-done | bytes 28704 | tf_op jit(solution)/shard_map/ppermute | solution.py:26
  120.9 13.1 %collective-permute-start.9 = (bf16[64,128]{1,0:T(8,128)(2,1)S(1)}, bf16[64,128]{1,0:T(8,128)(2,1)S(1)}, u32[]{:S(2)}, u32[]{:S(2)}) collective-permute-start(bf16[64,128]{1,0:T(8,128)(2,1)S(1)} %get-tuple-element.63), channel_id=1, source_target_pairs={{0,256},{32,288},{64,320},{96,352},{128,384},{160,416},{192,448},{... | collective-permute-start | bytes 49160 | tf_op jit(solution)/shard_map/ppermute | solution.py:26
  136.3 9.8 %collective-permute-start.10 = (bf16[8,1088,128]{2,1,0:T(8,128)(2,1)S(1)}, bf16[8,1088,128]{2,1,0:T(8,128)(2,1)S(1)}, u32[]{:S(2)}, u32[]{:S(2)}) collective-permute-start(bf16[8,1088,128]{2,1,0:T(8,128)(2,1)S(1)} %shard_map.141.own.own_grad), channel_id=1, source_target_pairs={{0,8},{8,0},{1,9},{9,1},{2,10},{10,2},{3,11},{11,3},{4,12},{12,4},... | collective-permute-start | bytes 6684680 | tf_op jit(solution)/shard_map/ppermute | solution.py:21
  146.2 4.0 %collective-permute-done.10.other.other_grad = bf16[8,1088,128]{2,1,0:T(8,128)(2,1)S(1)} collective-permute-done((bf16[8,1088,128]{2,1,0:T(8,128)(2,1)S(1)}, bf16[8,1088,128]{2,1,0:T(8,128)(2,1)S(1)}, u32[]{:S(2)}, u32[]{:S(2)}) %collective-permute-start.10) | collective-permute-done | bytes 2228256 | tf_op jit(solution)/shard_map/ppermute | solution.py:21
  150.9 13.9 %all_to_all.30.rows = bf16[8,80,128]{2,1,0:T(8,128)(2,1)S(1)} all-to-all(bf16[8,80,128]{2,1,0:T(8,128)(2,1)S(1)} %shard_map.142), channel_id=1, replica_groups=mesh['z'=16,'xl'=2,'c'=2,'t'=8] {'t'}, dimensions={0} | all-to-all | bytes 327680 | tf_op jit(solution)/shard_map/all_to_all | solution.py:17
  166.2 10.2 %all_to_all.31 = bf16[16,64,128]{2,1,0:T(8,128)(2,1)S(1)} all-to-all(bf16[16,64,128]{2,1,0:T(8,128)(2,1)S(1)} %bitcast.4), channel_id=1, replica_groups=mesh['z'=16,'xl'=2,'c'=2,'t'=8] {'xl','t'}, dimensions={0} | all-to-all | bytes 524288 | tf_op jit(solution)/shard_map/all_to_all | solution.py:17
  176.4 4.7 %collective-permute-start.11 = (bf16[2,8,64,128]{3,2,1,0:T(8,128)(2,1)S(1)}, bf16[2,8,64,128]{3,2,1,0:T(8,128)(2,1)S(1)}, u32[]{:S(2)}, u32[]{:S(2)}) collective-permute-start(bf16[2,8,64,128]{3,2,1,0:T(8,128)(2,1)S(1)} %bitcast.2), channel_id=1, source_target_pairs={{0,8},{8,0},{1,9},{9,1},{2,10},{10,2},{3,11},{11,3},{4,12},{12,4},... | collective-permute-start | bytes 786440 | tf_op jit(solution)/shard_map/ppermute | solution.py:21
  182.7 2.8 %shard_map.144 = (bf16[1024,2,128]{2,1,0:T(2,128)(2,1)}, bf16[1,1024,128]{2,1,0:T(8,128)(2,1)}) custom-call(s32[64]{0:T(128)S(1)} %copy-done.9, bf16[8,1088,128]{2,1,0:T(8,128)(2,1)S(1)} %shard_map.141.own.own_grad, bf16[8,1088,128]{2,1,0:T(8,128)(2,1)S(1)} %collective-permute-done.10.other.other_grad, bf16[2,8,64,128]{3,2,1,0:T(8,128)(2,1)S(1)} %bitcast.3, ...), custom_call_target="tpu_custom_call" | custom-call | flops 536870912 | bytes 5767168 | tf_op jit(solution)/shard_map/pallas_call | solution.py:45
  (47 shorter events, 22.2 us)
Async XLA Ops:
  0.6 16.2 %copy-start.3 = (bf16[512,128]{1,0:T(8,128)(2,1)S(1)}, bf16[512,128]{1,0:T(8,128)(2,1)}, u32[]{:S(2)}) copy-start(bf16[512,128]{1,0:T(8,128)(2,1)} %act.5) | copy-start | bytes 393220
  0.6 16.2 %copy-start = (bf16[512,2,1024]{2,1,0:T(2,128)(2,1)S(1)}, bf16[512,2,1024]{2,1,0:T(2,128)(2,1)}, u32[]{:S(2)}) copy-start(bf16[512,2,1024]{2,1,0:T(2,128)(2,1)} %cot.5) | copy-start | bytes 6291460
  4.3 16.3 %copy-start.8 = (s32[3]{0:T(128)S(1)}, s32[3]{0:T(128)}, u32[]{:S(2)}) copy-start(s32[3]{0:T(128)} %owners.11) | copy-start | bytes 40
  4.3 30.5 %all-to-all-start.1 = ((bf16[8,512,128]{2,1,0:T(8,128)(2,1)}), bf16[8,512,128]{2,1,0:T(8,128)(2,1)S(1)}, u32[]{:S(2)}, u32[]{:S(2)}) async-start(bf16[8,512,128]{2,1,0:T(8,128)(2,1)} %get-tuple-element.47), calls=%async_computation.1 | async-start | bytes 2097152 | tf_op jit(solution)/shard_map/all_to_all | solution.py:17
  11.8 8.8 %copy-start.6 = (bf16[1552,128]{1,0:T(8,128)(2,1)S(1)}, bf16[1552,128]{1,0:T(8,128)(2,1)}, u32[]{:S(2)}) copy-start(bf16[1552,128]{1,0:T(8,128)(2,1)} %get-tuple-element.42.own) | copy-start | bytes 1191940
  11.8 8.8 %collective-permute-start.2 = (bf16[1552,128]{1,0:T(8,128)(2,1)}, bf16[1552,128]{1,0:T(8,128)(2,1)S(1)}, u32[]{:S(2)}, u32[]{:S(2)}) collective-permute-start(bf16[1552,128]{1,0:T(8,128)(2,1)} %get-tuple-element.43), channel_id=1, source_target_pairs={{0,8},{8,0},{1,9},{9,1},{2,10},{10,2},{3,11},{11,3},{4,12},{12,4},... | collective-permute-start | bytes 1191944 | tf_op jit(solution)/shard_map/ppermute | solution.py:21
  18.6 4.5 %collective-permute-start = (bf16[2,512,128]{2,1,0:T(8,128)(2,1)S(1)}, bf16[2,512,128]{2,1,0:T(8,128)(2,1)S(1)}, u32[]{:S(2)}, u32[]{:S(2)}) collective-permute-start(bf16[2,512,128]{2,1,0:T(8,128)(2,1)S(1)} %get-tuple-element.39), channel_id=1, source_target_pairs={{0,8},{8,0},{1,9},{9,1},{2,10},{10,2},{3,11},{11,3},{4,12},{12,4},... | collective-permute-start | bytes 786440 | tf_op jit(solution)/shard_map/ppermute | solution.py:21
  21.2 12.2 %collective-permute-start.3 = (bf16[1040,128]{1,0:T(8,128)(2,1)S(1)}, bf16[1040,128]{1,0:T(8,128)(2,1)S(1)}, u32[]{:S(2)}, u32[]{:S(2)}) collective-permute-start(bf16[1040,128]{1,0:T(8,128)(2,1)S(1)} %get-tuple-element.45), channel_id=1, source_target_pairs={{0,16},{16,0},{1,17},{17,1},{2,18},{18,2},{3,19},{19,3},{4,20},{20... | collective-permute-start | bytes 798728 | tf_op jit(solution)/shard_map/ppermute | solution.py:21
  23.3 10.2 %collective-permute-start.1 = (bf16[512,128]{1,0:T(8,128)(2,1)S(1)}, bf16[512,128]{1,0:T(8,128)(2,1)S(1)}, u32[]{:S(2)}, u32[]{:S(2)}) collective-permute-start(bf16[512,128]{1,0:T(8,128)(2,1)S(1)} %get-tuple-element.41), channel_id=1, source_target_pairs={{0,16},{16,0},{1,17},{17,1},{2,18},{18,2},{3,19},{19,3},{4,20},{20... | collective-permute-start | bytes 393224 | tf_op jit(solution)/shard_map/ppermute | solution.py:21
  34.8 35.9 %all-to-all-start = ((bf16[16,96,128]{2,1,0:T(8,128)(2,1)}), bf16[16,96,128]{2,1,0:T(8,128)(2,1)S(1)}, u32[]{:S(2)}, u32[]{:S(2)}) async-start(bf16[16,96,128]{2,1,0:T(8,128)(2,1)} %copy-done.7), calls=%async_computation | async-start | bytes 786432 | tf_op jit(solution)/shard_map/all_to_all | solution.py:17
  51.4 4.8 %collective-permute-start.4 = (bf16[16,2,48,128]{3,2,1,0:T(8,128)(2,1)S(1)}, bf16[16,2,48,128]{3,2,1,0:T(8,128)(2,1)S(1)}, u32[]{:S(2)}, u32[]{:S(2)}) collective-permute-start(bf16[16,2,48,128]{3,2,1,0:T(8,128)(2,1)S(1)} %get-tuple-element.49), channel_id=1, source_target_pairs={{0,8},{8,0},{1,9},{9,1},{2,10},{10,2},{3,11},{11,3},{4,12},{12,4},... | collective-permute-start | bytes 1179656 | tf_op jit(solution)/shard_map/ppermute | solution.py:21
  56.3 8.0 %collective-permute-start.5 = (bf16[16,48,128]{2,1,0:T(8,128)(2,1)S(1)}, bf16[16,48,128]{2,1,0:T(8,128)(2,1)S(1)}, u32[]{:S(2)}, u32[]{:S(2)}) collective-permute-start(bf16[16,48,128]{2,1,0:T(8,128)(2,1)S(1)} %get-tuple-element.51), channel_id=1, source_target_pairs={{0,16},{16,0},{1,17},{17,1},{2,18},{18,2},{3,19},{19,3},{4,20},{20... | collective-permute-start | bytes 589832 | tf_op jit(solution)/shard_map/ppermute | solution.py:21
  64.4 6.3 %collective-permute-start.6 = (bf16[400,128]{1,0:T(8,128)(2,1)S(1)}, bf16[400,128]{1,0:T(8,128)(2,1)S(1)}, u32[]{:S(2)}, u32[]{:S(2)}) collective-permute-start(bf16[400,128]{1,0:T(8,128)(2,1)S(1)} %get-tuple-element.54), channel_id=1, source_target_pairs={{0,32},{32,0},{64,96},{96,64},{128,160},{160,128},{192,224},{224,1... | collective-permute-start | bytes 307208 | tf_op jit(solution)/shard_map/ppermute | solution.py:26
  72.1 30.2 %all-to-all-start.2 = ((bf16[16,96,128]{2,1,0:T(8,128)(2,1)}), bf16[16,96,128]{2,1,0:T(8,128)(2,1)S(1)}, u32[]{:S(2)}, u32[]{:S(2)}) async-start(bf16[16,96,128]{2,1,0:T(8,128)(2,1)} %get-tuple-element.55), calls=%async_computation.2 | async-start | bytes 786432 | tf_op jit(solution)/shard_map/all_to_all | solution.py:17
  82.9 19.3 %collective-permute-start.7 = (bf16[208,128]{1,0:T(8,128)(2,1)S(1)}, bf16[208,128]{1,0:T(8,128)(2,1)S(1)}, u32[]{:S(2)}, u32[]{:S(2)}) collective-permute-start(bf16[208,128]{1,0:T(8,128)(2,1)S(1)} %get-tuple-element.57), channel_id=1, source_target_pairs={{0,64},{32,96},{64,0},{96,32},{128,192},{160,224},{192,128},{224,1... | collective-permute-start | bytes 159752 | tf_op jit(solution)/shard_map/ppermute | solution.py:26
  103.1 1.4 copy-start.2
  104.5 31.8 %all-to-all-start.3 = ((bf16[8,1088,128]{2,1,0:T(8,128)(2,1)}), bf16[8,1088,128]{2,1,0:T(8,128)(2,1)S(1)}, u32[]{:S(2)}, u32[]{:S(2)}) async-start(bf16[8,1088,128]{2,1,0:T(8,128)(2,1)} %copy-done.2), calls=%async_computation.3 | async-start | bytes 4456448 | tf_op jit(solution)/shard_map/all_to_all | solution.py:17
  111.8 8.5 %collective-permute-start.8 = (bf16[112,128]{1,0:T(8,128)(2,1)S(1)}, bf16[112,128]{1,0:T(8,128)(2,1)S(1)}, u32[]{:S(2)}, u32[]{:S(2)}) collective-permute-start(bf16[112,128]{1,0:T(8,128)(2,1)S(1)} %get-tuple-element.60), channel_id=1, source_target_pairs={{0,128},{32,160},{64,192},{96,224},{128,0},{160,32},{192,64},{224,... | collective-permute-start | bytes 86024 | tf_op jit(solution)/shard_map/ppermute | solution.py:26
  120.9 14.2 %collective-permute-start.9 = (bf16[64,128]{1,0:T(8,128)(2,1)S(1)}, bf16[64,128]{1,0:T(8,128)(2,1)S(1)}, u32[]{:S(2)}, u32[]{:S(2)}) collective-permute-start(bf16[64,128]{1,0:T(8,128)(2,1)S(1)} %get-tuple-element.63), channel_id=1, source_target_pairs={{0,256},{32,288},{64,320},{96,352},{128,384},{160,416},{192,448},{... | collective-permute-start | bytes 49160 | tf_op jit(solution)/shard_map/ppermute | solution.py:26
  136.3 13.8 %collective-permute-start.10 = (bf16[8,1088,128]{2,1,0:T(8,128)(2,1)S(1)}, bf16[8,1088,128]{2,1,0:T(8,128)(2,1)S(1)}, u32[]{:S(2)}, u32[]{:S(2)}) collective-permute-start(bf16[8,1088,128]{2,1,0:T(8,128)(2,1)S(1)} %shard_map.141.own.own_grad), channel_id=1, source_target_pairs={{0,8},{8,0},{1,9},{9,1},{2,10},{10,2},{3,11},{11,3},{4,12},{12,4},... | collective-permute-start | bytes 6684680 | tf_op jit(solution)/shard_map/ppermute | solution.py:21
  164.8 16.3 %copy-start.1 = (bf16[512,2,1024]{2,1,0:T(2,128)(2,1)S(1)}, bf16[512,2,1024]{2,1,0:T(2,128)(2,1)}, u32[]{:S(2)}) copy-start(bf16[512,2,1024]{2,1,0:T(2,128)(2,1)} %cot.5) | copy-start | bytes 6291460
  164.8 16.3 %copy-start.5 = (bf16[128,2,1024]{2,1,0:T(2,128)(2,1)S(1)}, bf16[128,2,1024]{2,1,0:T(2,128)(2,1)}, u32[]{:S(2)}) copy-start(bf16[128,2,1024]{2,1,0:T(2,128)(2,1)} %weight.1) | copy-start | bytes 1572868
  166.2 16.5 %copy-start.9 = (s32[64]{0:T(128)S(1)}, s32[64]{0:T(128)}, u32[]{:S(2)}) copy-start(s32[64]{0:T(128)} %groups.1) | copy-start | bytes 772
  176.4 6.3 %collective-permute-start.11 = (bf16[2,8,64,128]{3,2,1,0:T(8,128)(2,1)S(1)}, bf16[2,8,64,128]{3,2,1,0:T(8,128)(2,1)S(1)}, u32[]{:S(2)}, u32[]{:S(2)}) collective-permute-start(bf16[2,8,64,128]{3,2,1,0:T(8,128)(2,1)S(1)} %bitcast.2), channel_id=1, source_target_pairs={{0,8},{8,0},{1,9},{9,1},{2,10},{10,2},{3,11},{11,3},{4,12},{12,4},... | collective-permute-start | bytes 786440 | tf_op jit(solution)/shard_map/ppermute | solution.py:21
  (2 other events, 1.7 us)
